TPU v7x, 32 devices: a whole 2x2x4 slice. The times are simulated.
32 devices in a mesh: group: 2 (over y), ep: 8 (over z, core), tp: 2 (over x).
Axes of the slice: x: 2, y: 2, z: 4, core: 2. Of those that a mesh axis runs over, the one named last changes fastest.
Arguments:
- layer_input: bfloat16 [2048, 4096], P(('group', 'ep'), 'tp'), parts along dimension 0, may hold values from -6 to 6
- stream: bfloat16 [2048, 4096], P(('group', 'ep'), 'tp'), parts along dimension 0, may hold values from -6 to 6
- expert_ids: int32 [2048, 8], P(('group', 'ep')), parts along dimension 0, may hold values from 0 to 15, all different within a row; in each aligned block of 128 rows (0 to 127, 128 to 255, ...) at most 96 rows name the same one
- kv_owner: int32 [2048, 1], P(('group', 'ep')), parts along dimension 0, may hold values from 0 to 1; in each aligned block of 128 rows (0 to 127, 128 to 255, ...) at most 128 rows name the same one
- attn_norm: bfloat16 [4096], P('tp'), may hold values from 0.099609375 to 1.8984375
- moe_norm: bfloat16 [4096], P('tp'), may hold values from 0.099609375 to 1.8984375
- k_norm: bfloat16 [128], replicated, may hold values from 0.099609375 to 1.8984375
- w_kv: bfloat16 [4096, 1024], P('tp'), may hold values from -0.09375 to 0.09375
- router: bfloat16 [4096, 16], P('tp')
- w_gate: bfloat16 [16, 4096, 1536], P('ep', None, 'tp'), may hold values from -0.09375 to 0.09375
- w_up: bfloat16 [16, 4096, 1536], P('ep', None, 'tp'), may hold values from -0.09375 to 0.09375
- w_down: bfloat16 [16, 1536, 4096], P('ep', 'tp'), may hold values from -0.21875 to 0.21875
Outputs:
- moe_out: bfloat16 [2048, 4096], P(('group', 'ep'), 'tp'), parts along dimension 0
- kv_cache: bfloat16 [16, 2, 128, 1024], P(('group', 'ep'), 'tp'), parts along dimension 0
There are 2 independent parts, one for each index of `group`. A program takes and returns all parts, laid end to end along the dimension named above; an argument that names none is the same for every part. Nothing has to cross between parts.
Inputs may be any that keep to these rules, and one draw needn't show every extreme that they name: `expert_ids`: each row names 8 different experts. Among the 128 rows of one index of ep no expert is named more than 96 times, a bound that some block reaches. `kv_owner`: among the 128 rows of one index of ep no owner is named more than 128 times, a bound that some block reaches.
All inputs are finite; a program needn't handle non-finite values.
Results may differ from a plain program's by a relative error of at most 0.012.
Values may be sent and summed in bfloat16 or wider, within the bound.
No kernel may reach another device: no remote copies, remote signals or barrier semaphores. Data moves between devices by JAX's collectives and lax.ppermute only.
A program may use at most 192 MiB of HBM per device.

v0:
```python
import jax
import jax.numpy as jnp
from jax import lax
from jax.sharding import PartitionSpec as P

D = 4096
KVH = 4
HD = 128
TOPK = 8


EPS = 1e-06


def key_norm(heads, k_norm, is_key):
    scaled = (
        heads
        * lax.rsqrt(jnp.mean(heads * heads, 1, keepdims=True) + EPS)
        * k_norm.astype(jnp.float32)[None, :, None]
    )
    return jnp.where(is_key[:, None, None], scaled, heads)


def per_device(
    layer_input,
    stream,
    expert_ids,
    kv_owner,
    attn_norm,
    moe_norm,
    k_norm,
    w_kv,
    router,
    w_gate,
    w_up,
    w_down,
):
    tok_rows = layer_input.shape[0]
    tp_count = lax.axis_size("tp")
    ep_count = lax.axis_size("ep")
    columns = 2 * KVH * HD
    first = layer_input.astype(jnp.float32)
    second = stream.astype(jnp.float32)
    squares = lax.psum((jnp.sum(first * first, 1), jnp.sum(second * second, 1)), "tp")
    first_scale = lax.rsqrt(squares[0] / D + EPS)[:, None]
    second_scale = lax.rsqrt(squares[1] / D + EPS)[:, None]
    attn_in = (first * first_scale * attn_norm.astype(jnp.float32)).astype(jnp.bfloat16)
    owner_cap = 2 * tok_rows // tp_count
    owner = kv_owner[:, 0]
    owner_hot = (owner[:, None] == jnp.arange(tp_count, dtype=jnp.int32)[None, :]).astype(jnp.int32)
    owner_slot = jnp.sum(
        (jnp.cumsum(owner_hot, 0, dtype=jnp.int32) - owner_hot) * owner_hot, 1, dtype=jnp.int32
    )
    target = owner * owner_cap + owner_slot
    placing = (
        target[None, :] == jnp.arange(tp_count * owner_cap, dtype=jnp.int32)[:, None]
    ).astype(jnp.float32)
    width = columns // tp_count
    mine = lax.psum_scatter(
        lax.dot_general(
            w_kv, attn_in, (((0,), (1,)), ((), ())), preferred_element_type=jnp.float32
        ).astype(jnp.bfloat16),
        "tp",
        scatter_dimension=0,
        tiled=True,
    ).astype(jnp.float32)
    heads = mine.reshape(width // HD, HD, tok_rows)
    head_index = lax.axis_index("tp") * (width // HD) + jnp.arange(width // HD, dtype=jnp.int32)
    normed = key_norm(heads, k_norm, head_index < KVH).reshape(width, tok_rows).astype(jnp.bfloat16)
    outgoing = lax.dot_general(
        placing.astype(jnp.bfloat16),
        normed,
        (((1,), (1,)), ((), ())),
        preferred_element_type=jnp.float32,
    )
    outgoing = outgoing.astype(jnp.bfloat16).reshape(tp_count, owner_cap, width)
    arrived = lax.all_to_all(outgoing, "tp", split_axis=0, concat_axis=2, tiled=True)
    kv_cache = arrived[0]
    kv_cache = kv_cache.reshape(1, 1, owner_cap, columns)
    moe_in = (second * second_scale * moe_norm.astype(jnp.float32)).astype(jnp.bfloat16)
    expert_count = router.shape[1]
    exp_local = w_gate.shape[0]
    capacity = min(tok_rows, 3 * tok_rows * TOPK // (2 * expert_count))
    expert_range = jnp.arange(expert_count, dtype=jnp.int32)
    expert_hot = (expert_ids[:, :, None] == expert_range[None, None, :]).astype(jnp.int32)
    counts = jnp.sum(expert_hot, 1, dtype=jnp.int32)
    earlier = jnp.cumsum(counts, 0, dtype=jnp.int32) - counts
    slots = jnp.sum(earlier[:, None, :] * expert_hot, 2, dtype=jnp.int32)
    send_place = expert_ids * capacity + slots
    sending = jnp.any(
        send_place[None, :, :]
        == jnp.arange(expert_count * capacity, dtype=jnp.int32)[:, None, None],
        2,
    )
    sending = sending.astype(jnp.bfloat16)
    total_rows = ep_count * capacity
    full_rows, full_router = (
        lax.all_gather(moe_in, "tp", axis=1, tiled=True),
        lax.all_gather(router, "tp", axis=0, tiled=True),
    )
    logits = jnp.dot(full_rows, full_router, preferred_element_type=jnp.float32)
    packed = jnp.dot(sending, full_rows, preferred_element_type=jnp.float32).astype(jnp.bfloat16)
    packed = packed.reshape(ep_count, exp_local, capacity, D)
    received = lax.all_to_all(packed, "ep", split_axis=0, concat_axis=2, tiled=True)[0]
    gate = jnp.einsum("erd,edf->erf", received, w_gate, preferred_element_type=jnp.float32)
    up = jnp.einsum("erd,edf->erf", received, w_up, preferred_element_type=jnp.float32)
    hidden = (jax.nn.silu(gate) * up).astype(jnp.bfloat16)
    partial_out = jnp.einsum("erf,efd->erd", hidden, w_down, preferred_element_type=jnp.float32)
    summed = lax.psum_scatter(
        partial_out.astype(jnp.bfloat16), "tp", scatter_dimension=2, tiled=True
    )
    returning = summed.reshape(exp_local, ep_count, capacity, summed.shape[2])
    returned = lax.all_to_all(returning, "ep", split_axis=1, concat_axis=1, tiled=True)
    returned = returned.reshape(exp_local * ep_count * capacity, summed.shape[2])
    chosen = jnp.sum(jnp.where(expert_hot == 1, logits[:, None, :], 0.0), 2)
    gates = jax.nn.softmax(chosen, -1)
    position = expert_ids % exp_local * total_rows + expert_ids // exp_local * capacity + slots
    picked = jnp.take(returned, position.reshape(-1), axis=0)
    picked = picked.reshape(tok_rows, TOPK, summed.shape[2]).astype(jnp.float32)
    moe_out = jnp.sum(gates[:, :, None] * picked, 1).astype(jnp.bfloat16)
    return (moe_out, kv_cache)


def solution(mesh):
    placed = (
        P(("group", "ep"), "tp"),
        P(("group", "ep"), "tp"),
        P(("group", "ep"), None),
        P(("group", "ep"), None),
        P("tp"),
        P("tp"),
        P(),
        P("tp", None),
        P("tp", None),
        P("ep", None, "tp"),
        P("ep", None, "tp"),
        P("ep", "tp", None),
    )
    return jax.shard_map(
        per_device,
        mesh=mesh,
        in_specs=placed,
        out_specs=(P(("group", "ep"), "tp"), P(("group", "ep"), "tp", None, None)),
        check_vma=False,
    )
```

profile of v0, /device:TPU:0, one launch (start us, length us, event | category | flops | bytes accessed | tf_op | source)
XLA Modules:
  0.0 706.5 jit_solution(5155169532917432954)
XLA Ops:
  7.2 1.5 fusion.2
  8.7 5.8 all-reduce
  14.5 0.7 convert_element_type.66
  15.2 2.0 fusion.4
  17.3 0.7 convert_reduce_fusion
  18.0 0.1 copy.58
  18.1 0.2 reduce_window_sum.22
  18.3 0.1 copy.60
  18.3 0.7 select_reduce_fusion.1
  19.1 0.7 multiply_add_fusion
  19.8 5.6 fusion
  25.3 15.2 %all-gather.2.cloned.1.call-done = bf16[128,4096]{1,0:T(8,128)(2,1)} async-done(((bf16[128,2048]{1,0:T(8,128)(2,1)}), bf16[128,4096]{1,0:T(8,128)(2,1)}) %all-gather.2.cloned.1.call-update) | async-done | bytes 1048592 | tf_op jit(solution)/shard_map/all_gather | solution.py:98
  40.6 7.5 %convolution_convert_fusion = bf16[1536,4096]{1,0:T(8,128)(2,1)} fusion(pred[1536,128]{1,0:T(8,128)(4,1)S(1)} %fusion, bf16[128,4096]{1,0:T(8,128)(2,1)} %all-gather.2.cloned.1.call-done), kind=kOutput, calls=%fused_computation.1 | convolution fusion | flops 1616904192 | bytes 13828096 | tf_op jit(solution)/shard_map/dot_general | solution.py:102
  48.0 5.5 all-to-all-start
  53.5 0.0 reduce-scatter.5.cloned.1.call-start
  53.6 3.7 fusion.1
  57.3 0.2 reduce-scatter.3.cloned.1.call-start
  57.5 269.8 %all-to-all-done = bf16[8,2,96,4096]{3,2,1,0:T(8,128)(2,1)} async-done(((bf16[8,2,96,4096]{3,2,1,0:T(8,128)(2,1)}), bf16[8,2,96,4096]{3,2,1,0:T(8,128)(2,1)}, u32[]{:S(2)}, u32[]{:S(2)}) %all-to-all-start) | async-done | bytes 12582944 | tf_op jit(solution)/shard_map/all_to_all | solution.py:104
  327.3 6.3 copy.62
  333.6 14.3 %fusion.30 = f32[2,768,768]{2,1,0:T(8,128)} fusion(bf16[2,768,4096]{2,1,0:T(8,128)(2,1)S(1)} %bitcast.45, bf16[2,4096,768]{2,1,0:T(8,128)(2,1)} %param.21), kind=kOutput, calls=%fused_computation.71 | convolution fusion | flops 9663676416 | bytes 29884416 | tf_op jit(solution)/shard_map/erd,edf->erf/dot_general | solution.py:105
  347.8 13.9 %multiply_convert_fusion = bf16[2,768,768]{2,1,0:T(8,128)(2,1)S(1)} fusion(f32[2,768,768]{2,1,0:T(8,128)} %fusion.30, bf16[2,768,4096]{2,1,0:T(8,128)(2,1)S(1)} %bitcast.46, bf16[2,4096,768]{2,1,0:T(8,128)(2,1)} %param.22), kind=kOutput, calls=%fused_computation.6 | convolution fusion | flops 9670754304 | bytes 32243712 | tf_op jit(solution)/shard_map/erd,edf->erf/dot_general | solution.py:106
  361.8 17.2 %convolution_convert_fusion.1 = bf16[2,768,4096]{2,1,0:T(8,128)(2,1)} fusion(bf16[2,768,768]{2,1,0:T(8,128)(2,1)S(1)} %multiply_convert_fusion, bf16[2,768,4096]{2,1,0:T(8,128)(2,1)} %param.23), kind=kOutput, calls=%fused_computation.2 | convolution fusion | flops 9669967872 | bytes 27525120 | tf_op jit(solution)/shard_map/erf,efd->erd/dot_general | solution.py:108
  379.0 0.6 copy-done.5
  379.6 0.1 fusion.17
  379.7 0.2 reduce_window_sum.23
  379.9 0.2 select_reduce_fusion
  380.1 0.1 broadcast_bitcast_fusion.1
  380.1 0.9 convert_multiply_fusion.5
  381.1 0.1 mul.144
  381.2 0.2 reduce_sum.89
  381.4 0.2 mul.145
  381.6 1.9 convolution_convert_fusion.2
  383.5 3.7 all-to-all-start.2
  387.1 137.2 %reduce-scatter.3.cloned.1.call-done = bf16[2,768,2048]{2,1,0:T(8,128)(2,1)} async-done(((bf16[2,768,4096]{2,1,0:T(8,128)(2,1)}), bf16[2,768,2048]{2,1,0:T(8,128)(2,1)}) %reduce-scatter.3.cloned.1.call-update) | async-done | bytes 6291472 | tf_op jit(solution)/shard_map/reduce_scatter | solution.py:109
  524.3 6.6 copy.63
  530.9 4.9 all-to-all-start.1
  535.8 0.1 copy.65
  535.9 0.1 reshape.143
  536.0 0.1 copy.61
  536.1 5.0 all_gather.7
  541.2 0.3 copy.68
  541.5 0.9 reshape_squeeze.3
  542.4 0.4 fusion.29
  542.8 0.1 copy.57
  542.9 131.8 %all-to-all-done.1 = bf16[2,8,96,2048]{3,2,0,1:T(8,128)(2,1)} async-done(((bf16[2,8,96,2048]{3,2,0,1:T(8,128)(2,1)}), bf16[2,8,96,2048]{3,2,0,1:T(8,128)(2,1)}, u32[]{:S(2)}, u32[]{:S(2)}) %all-to-all-start.1) | async-done | bytes 6291488 | tf_op jit(solution)/shard_map/all_to_all | solution.py:113
  674.7 6.6 copy.64
  681.3 12.4 %gather_fusion = bf16[1024,2048]{1,0:T(8,128)(2,1)} fusion(bf16[1536,2048]{1,0:T(8,128)(2,1)} %bitcast.43, s32[1024]{0:T(1024)S(1)} %broadcast_clamp_fusion), kind=kCustom, calls=%fused_computation | custom fusion | bytes 8392704 | tf_op jit(solution)/shard_map/jit(_take)/gather | solution.py:118
  693.7 6.3 multiply_reduce_fusion
  (35 shorter events, 0.3 us)
Async XLA Ops:
  7.2 33.4 %all-gather.2.cloned.1.call-start = ((), (), s32[]{:S(2)}) async-start(), calls=%async_computation.5 | async-start | bytes 1572864 | tf_op jit(solution)/shard_map/all_gather | solution.py:98
  48.0 5.5 copy-start.4
  48.0 5.6 copy-start.1
  48.0 279.3 %all-to-all-start = ((bf16[8,2,96,4096]{3,2,1,0:T(8,128)(2,1)}), bf16[8,2,96,4096]{3,2,1,0:T(8,128)(2,1)}, u32[]{:S(2)}, u32[]{:S(2)}) async-start(bf16[8,2,96,4096]{3,2,1,0:T(8,128)(2,1)} %bitcast.44), calls=%async_computation | async-start | bytes 25165824 | tf_op jit(solution)/shard_map/all_to_all | solution.py:104
  53.5 326.6 %reduce-scatter.5.cloned.1.call-start = ((), (), s32[]{:S(2)}) async-start(), calls=%async_computation.7 | async-start | bytes 393216 | tf_op jit(solution)/shard_map/reduce_scatter | solution.py:59
  57.3 467.0 %reduce-scatter.3.cloned.1.call-start = ((), (), s32[]{:S(2)}) async-start(), calls=%async_computation.6 | async-start | bytes 18874368 | tf_op jit(solution)/shard_map/reduce_scatter | solution.py:109
  378.9 0.7 copy-start.5
  378.9 0.9 copy-start.6
  383.5 147.4 %all-to-all-start.2 = ((bf16[2,128,512]{2,1,0:T(8,128)(2,1)}), bf16[2,128,512]{2,1,0:T(8,128)(2,1)S(1)}, u32[]{:S(2)}, u32[]{:S(2)}) async-start(bf16[2,128,512]{2,1,0:T(8,128)(2,1)} %bitcast.12), calls=%async_computation.4 | async-start | bytes 524288 | tf_op jit(solution)/shard_map/all_to_all | solution.py:77
  530.9 4.9 copy-start.2
  530.9 5.3 copy-start.3
  530.9 11.5 %copy-start = (bf16[128,4096]{1,0:T(8,128)(2,1)S(1)}, bf16[128,4096]{1,0:T(8,128)(2,1)}, u32[]{:S(2)}) copy-start(bf16[128,4096]{1,0:T(8,128)(2,1)} %all-gather.2.cloned.1.call-done) | copy-start | bytes 3145732
  530.9 143.8 %all-to-all-start.1 = ((bf16[2,8,96,2048]{3,2,0,1:T(8,128)(2,1)}), bf16[2,8,96,2048]{3,2,0,1:T(8,128)(2,1)}, u32[]{:S(2)}, u32[]{:S(2)}) async-start(bf16[2,8,96,2048]{3,2,0,1:T(8,128)(2,1)} %copy.63), calls=%async_computation.2 | async-start | bytes 12582912 | tf_op jit(solution)/shard_map/all_to_all | solution.py:113
Sparse Core Ops, SparseCore 0:
  17.4 23.0 all-gather.1
  57.4 12.0 reduce-scatter.4
  379.1 145.1 reduce-scatter.2
where the time goes:
time: 707 us
  waiting for transfers between devices  554 us (78%)
  matrix products  58.7 us (8%)
  local copies, waits for them, and re-layouts  34.6 us (5%)
  other arithmetic  20 us (3%)
  starting transfers between devices  14.3 us (2%)
  between operations  13.9 us (2%)
  blocking collectives  10.9 us (2%)
    all_to_all x1, waiting for transfers between devices, per_device(): lax.all_to_all(packed, 'ep', split_axis=0, concat_axis=2, tiled=True)[0]  270 us
    reduce_scatter x1, waiting for transfers between devices, per_device(): lax.psum_scatter(partial_out.astype(jnp.bfloat16), 'tp', scatter_dimensio...  137 us
    all_to_all x1, waiting for transfers between devices, per_device(): lax.all_to_all(returning, 'ep', split_axis=1, concat_axis=1, tiled=True)  132 us
    dot_general x1, matrix products, per_device(): jnp.einsum('erf,efd->erd', hidden, w_down, preferred_element_type=jnp.flo...  17.2 us
    all_gather x1, waiting for transfers between devices, per_device(): lax.all_gather(moe_in, 'tp', axis=1, tiled=True)  15.2 us
    dot_general x1, matrix products, per_device(): jnp.einsum('erd,edf->erf', received, w_gate, preferred_element_type=jnp.f...  14.3 us
  transfers between devices with their start and end apart: 6, of which 4 were waited for; matrix products, arithmetic and copies ran while one was open for 11% of the time, Pallas kernels for 0%

commit v1 on v0

v1 whole, which is shorter than its diff:
```python
import functools

import jax
import jax.numpy as jnp
from jax import lax
from jax.experimental import pallas as pl
from jax.experimental.pallas import tpu as pltpu
from jax.sharding import PartitionSpec as P

D = 4096
KVH = 4
HD = 128
TOPK = 8


EPS = 1e-06
VMEM_LIMIT = 56 * 1024 * 1024


def tile_of(size, most):
    tile = size
    while tile > most and tile % 2 == 0 and (tile // 2) % 128 == 0:
        tile //= 2
    for candidate in range(most, 127, -128):
        if size % candidate == 0:
            return candidate
    return tile


def hidden_kernel(x_ref, wg_ref, wu_ref, scale_ref, weight_ref, out_ref):
    blocks, parts, rows, width = x_ref.shape
    gate = up = None
    for part in range(parts):
        x = x_ref[:, part].reshape(blocks * rows, width)
        depth = pl.ds(part * width, width)
        g = jnp.dot(x, wg_ref[0, depth], preferred_element_type=jnp.float32)
        u = jnp.dot(x, wu_ref[0, depth], preferred_element_type=jnp.float32)
        gate = g if gate is None else gate + g
        up = u if up is None else up + u
    scale = scale_ref[...]
    gate = gate * scale
    up = up * scale
    value = gate / (1.0 + jnp.exp(-gate)) * up * weight_ref[0]
    out_ref[0] = value.astype(jnp.bfloat16)


def hidden_of(x, w_gate, w_up, scale, weight):
    blocks, parts, rows, width = x.shape
    experts, depth, units = w_gate.shape
    tokens = blocks * rows
    tile = tile_of(units, 256)
    tiles = units // tile
    wspec = pl.BlockSpec((1, depth, tile), lambda e, f: (e, 0, f))
    return pl.pallas_call(
        hidden_kernel,
        grid=(experts, tiles),
        in_specs=[
            pl.BlockSpec(x.shape, lambda e, f: (0, 0, 0, 0)),
            wspec,
            wspec,
            pl.BlockSpec((tokens, 1), lambda e, f: (0, 0)),
            pl.BlockSpec((1, tokens, 1), lambda e, f: (e, 0, 0)),
        ],
        out_specs=pl.BlockSpec((1, tokens, tile), lambda e, f: (e, 0, f)),
        out_shape=jax.ShapeDtypeStruct((experts, tokens, units), jnp.bfloat16),
        compiler_params=pltpu.CompilerParams(vmem_limit_bytes=VMEM_LIMIT),
        cost_estimate=pl.CostEstimate(
            flops=4 * tokens * depth * units * experts,
            bytes_accessed=4 * experts * depth * units + 2 * tokens * depth,
            transcendentals=tokens * units * experts,
        ),
    )(x, w_gate, w_up, scale, weight)


def down_kernel(h_ref, w_ref, out_ref):
    blocks, _, rows, tile = out_ref.shape
    y = None
    for e in range(h_ref.shape[0]):
        term = jnp.dot(h_ref[e], w_ref[e], preferred_element_type=jnp.float32)
        y = term if y is None else y + term
    out_ref[:, 0] = y.astype(jnp.bfloat16).reshape(blocks, rows, tile)


def down_of(hidden, w_down, blocks, parts):
    experts, tokens, units = hidden.shape
    width = w_down.shape[2] // parts
    rows = tokens // blocks
    tile = tile_of(width, 512)
    tiles = width // tile
    return pl.pallas_call(
        down_kernel,
        grid=(parts * tiles,),
        in_specs=[
            pl.BlockSpec((experts, tokens, units), lambda n: (0, 0, 0)),
            pl.BlockSpec((experts, units, tile), lambda n: (0, 0, n)),
        ],
        out_specs=pl.BlockSpec(
            (blocks, 1, rows, tile), lambda n: (0, n // tiles, 0, n % tiles)
        ),
        out_shape=jax.ShapeDtypeStruct((blocks, parts, rows, width), jnp.bfloat16),
        compiler_params=pltpu.CompilerParams(vmem_limit_bytes=VMEM_LIMIT),
        cost_estimate=pl.CostEstimate(
            flops=2 * experts * tokens * units * width * parts,
            bytes_accessed=2 * (experts * units + tokens) * width * parts,
            transcendentals=0,
        ),
    )(hidden, w_down)


def per_device(
    layer_input,
    stream,
    expert_ids,
    kv_owner,
    attn_norm,
    moe_norm,
    k_norm,
    w_kv,
    router,
    w_gate,
    w_up,
    w_down,
):
    rows = layer_input.shape[0]
    tp_count = lax.axis_size("tp")
    ep_count = lax.axis_size("ep")
    columns = 2 * KVH * HD
    expert_count = router.shape[1]
    exp_local = w_gate.shape[0]
    first = layer_input.astype(jnp.float32)
    second = stream.astype(jnp.float32)

    rows_out = (second * moe_norm.astype(jnp.float32)).astype(jnp.bfloat16)
    gathered = lax.all_gather(rows_out, ("ep", "tp"), axis=0, tiled=False)
    gathered = gathered.reshape(ep_count, tp_count, rows, rows_out.shape[1])

    partial_logits = jnp.dot(rows_out, router, preferred_element_type=jnp.float32)
    squares = jnp.stack([jnp.sum(first * first, 1), jnp.sum(second * second, 1)], 1)
    small = lax.psum(jnp.concatenate([squares, partial_logits], 1), "tp")
    first_scale = lax.rsqrt(small[:, 0:1] / D + EPS)
    second_scale = lax.rsqrt(small[:, 1:2] / D + EPS)
    logits = small[:, 2:] * second_scale
    expert_range = jnp.arange(expert_count, dtype=jnp.int32)
    chosen = jnp.any(expert_ids[:, :, None] == expert_range[None, None, :], 1)
    top = jnp.max(jnp.where(chosen, logits, -jnp.inf), 1, keepdims=True)
    weights = jnp.where(chosen, jnp.exp(jnp.where(chosen, logits - top, 0.0)), 0.0)
    weights = weights / jnp.sum(weights, 1, keepdims=True)
    side = lax.all_gather(
        jnp.concatenate([second_scale, weights], 1), "ep", axis=0, tiled=True
    )
    scale = side[:, 0:1]
    mine = lax.dynamic_slice_in_dim(side, 1 + lax.axis_index("ep") * exp_local, exp_local, 1)
    weight = mine.T[:, :, None]

    attn_in = (first * attn_norm.astype(jnp.float32)).astype(jnp.bfloat16)
    kv = jnp.dot(attn_in, w_kv, preferred_element_type=jnp.float32) * first_scale
    owner_cap = 2 * rows // tp_count
    owner = kv_owner[:, 0]
    owner_hot = (owner[:, None] == jnp.arange(tp_count, dtype=jnp.int32)[None, :]).astype(jnp.int32)
    owner_slot = jnp.sum(
        (jnp.cumsum(owner_hot, 0, dtype=jnp.int32) - owner_hot) * owner_hot, 1, dtype=jnp.int32
    )
    target = owner * owner_cap + owner_slot
    placing = target[None, :] == jnp.arange(tp_count * owner_cap, dtype=jnp.int32)[:, None]
    placed = jnp.dot(
        placing.astype(jnp.bfloat16), kv.astype(jnp.bfloat16), preferred_element_type=jnp.float32
    )
    placed = placed.astype(jnp.bfloat16).reshape(tp_count, owner_cap, columns)
    arrived = lax.all_to_all(placed, "tp", split_axis=0, concat_axis=0, tiled=True)
    heads = jnp.sum(arrived.astype(jnp.float32), 0).reshape(owner_cap, 2 * KVH, HD)
    keys = heads[:, :KVH]
    keys = keys * lax.rsqrt(jnp.mean(keys * keys, 2, keepdims=True) + EPS)
    keys = keys * k_norm.astype(jnp.float32)
    kv_cache = jnp.concatenate([keys, heads[:, KVH:]], 1).astype(jnp.bfloat16)
    kv_cache = kv_cache.reshape(1, 1, owner_cap, columns)

    hidden = hidden_of(gathered, w_gate, w_up, scale, weight)
    partial = down_of(hidden, w_down, ep_count, tp_count)
    partial = partial.reshape(ep_count * tp_count, rows, -1)
    moe_out = lax.psum_scatter(partial, ("ep", "tp"), scatter_dimension=0, tiled=False)
    return (moe_out, kv_cache)


def solution(mesh):
    placed = (
        P(("group", "ep"), "tp"),
        P(("group", "ep"), "tp"),
        P(("group", "ep"), None),
        P(("group", "ep"), None),
        P("tp"),
        P("tp"),
        P(),
        P("tp", None),
        P("tp", None),
        P("ep", None, "tp"),
        P("ep", None, "tp"),
        P("ep", "tp", None),
    )
    return jax.shard_map(
        per_device,
        mesh=mesh,
        in_specs=placed,
        out_specs=(P(("group", "ep"), "tp"), P(("group", "ep"), "tp", None, None)),
        check_vma=False,
    )
```

time: 707 us -> 255 us (0.36)
  waiting for transfers between devices: 554 us -> 137 us
  matrix products: 58.7 us -> 5.27 us
  Pallas kernels: 0 us -> 52.2 us
  local copies, waits for them, and re-layouts: 34.6 us -> 9.51 us
  blocking collectives: 10.9 us -> 27.1 us
  other arithmetic: 20 us -> 5.8 us
  starting transfers between devices: 14.3 us -> 3.59 us
    all_to_all x3 -> x1, waiting for transfers between devices: 402 us -> 8.67 us  [per_device(): lax.all_to_all(placed, 'tp', split_axis=0, concat_axis=0, tiled=True)]
    dot_general x7 -> x2, matrix products: 58.7 us -> 5.27 us  [the longest x1 3.99 us: per_device(): jnp.dot(placing.astype(jnp.bfloat16), kv.astype(jnp.bfloat16), preferred_...]
    reduce_scatter x2 -> x1, waiting for transfers between devices: 137 us -> 84.1 us  [per_device(): lax.psum_scatter(partial, ('ep', 'tp'), scatter_dimension=0, tiled=False)]
    pallas_call x0 -> x2, Pallas kernels: none -> 52.2 us  [the longest x1 34.2 us: hidden_of(): pl.pallas_call(hidden_kernel, grid=(experts, tiles), in_specs=[pl.BlockSp...]
    all_gather x1, waiting for transfers between devices: 15.2 us -> 44.4 us  [per_device(): gathered = lax.all_gather(rows_out, ('ep', 'tp'), axis=0, tiled=False)]
    all_to_all x3 -> x0, local copies, waits for them, and re-layouts: 13.1 us -> none  [the longest x1 6.57 us: per_device(): lax.all_to_all(returning, 'ep', split_axis=1, concat_axis=1, tiled=True)]
    gather x1 -> x0, local copies, waits for them, and re-layouts: 12.4 us -> none  [per_device(): picked = jnp.take(returned, position.reshape(-1), axis=0)]
    all_gather x1, blocking collectives: 5.04 us -> 17.5 us  [per_device(): lax.all_gather(jnp.concatenate([second_scale, weights], 1), 'ep', axis=0,...]
  transfers between devices with their start and end apart: 6 -> 3, of which waited for: 4 -> 3; matrix products, arithmetic and copies ran while one was open for 11% -> 7% of each run, Pallas kernels for 0% -> 0%
where the time goes in v1:
time: 255 us
  waiting for transfers between devices  137 us (54%)
  Pallas kernels  52.2 us (20%)
  blocking collectives  27.1 us (11%)
  between operations  14.2 us (6%)
  local copies, waits for them, and re-layouts  9.51 us (4%)
  other arithmetic  5.8 us (2%)
  matrix products  5.27 us (2%)
  starting transfers between devices  3.59 us (1%)
    reduce_scatter x1, waiting for transfers between devices, per_device(): lax.psum_scatter(partial, ('ep', 'tp'), scatter_dimension=0, tiled=False)  84.1 us
    all_gather x1, waiting for transfers between devices, per_device(): gathered = lax.all_gather(rows_out, ('ep', 'tp'), axis=0, tiled=False)  44.4 us
    pallas_call x1, Pallas kernels, hidden_of(): pl.pallas_call(hidden_kernel, grid=(experts, tiles), in_specs=[pl.BlockSp...  34.2 us
    pallas_call x1, Pallas kernels, down_of(): pl.pallas_call(down_kernel, grid=(parts * tiles,), in_specs=[pl.BlockSpec...  18 us
    all_gather x1, blocking collectives, per_device(): lax.all_gather(jnp.concatenate([second_scale, weights], 1), 'ep', axis=0,...  17.5 us
    psum x1, blocking collectives, per_device(): small = lax.psum(jnp.concatenate([squares, partial_logits], 1), 'tp')  9.59 us
    all_to_all x1, waiting for transfers between devices, per_device(): lax.all_to_all(placed, 'tp', split_axis=0, concat_axis=0, tiled=True)  8.67 us
    broadcast_in_dim x2, local copies, waits for them, and re-layouts, per_device(): weight = mine.T[:, :, None]  7.78 us
  transfers between devices with their start and end apart: 3, of which 3 were waited for; matrix products, arithmetic and copies ran while one was open for 7% of the time, Pallas kernels for 0%

profile of v1, /device:TPU:0, one launch (start us, length us, event | category | flops | bytes accessed | tf_op | source)
XLA Modules:
  0.0 254.8 jit_solution(11974602117178947771)
XLA Ops:
  7.2 0.0 copy-start
  7.2 0.0 all-gather.3.cloned.1.call-start
  7.2 0.7 convert_element_type.46
  7.9 2.0 fusion.2
  9.9 0.0 all-gather.3.cloned.1.call-update
  9.9 0.0 reduce-scatter.2.cloned.1.call-start
  10.0 1.2 fusion.3
  11.2 0.0 copy-done
  11.2 1.3 fusion.20
  12.5 9.6 %psum.7 = f32[128,18]{0,1:T(8,128)S(1)} all-reduce(f32[128,18]{0,1:T(8,128)S(1)} %pad_maximum_fusion.1), channel_id=1, replica_groups=mesh['group'=2,'ep'=8,'tp'=2] {'tp'}, use_global_device_ids=true, to_apply=%region_2.0 | all-reduce | flops 2304 | bytes 18432 | tf_op jit(solution)/shard_map/psum | solution.py:139
  22.1 0.7 fusion.12
  22.9 0.1 copy.39
  23.0 17.5 %all_gather.11 = f32[1024,17]{1,0:T(8,128)S(1)} all-gather(f32[128,17]{1,0:T(8,128)S(1)} %copy.39), channel_id=1, replica_groups=mesh['group'=2,'ep'=8,'tp'=2] {'ep'}, dimensions={0}, use_global_device_ids=true | all-gather | bytes 78336 | tf_op jit(solution)/shard_map/all_gather | solution.py:148
  40.5 0.0 copy-start.3
  40.5 0.2 dynamic-slice_bitcast_fusion
  40.7 7.6 %copy.41.weight_ref = f32[2,1024,1]{2,1,0:T(8,128)} copy(f32[2,1024,1]{0,1,2:T(8,128)S(1)} %dynamic-slice_bitcast_fusion) | data formatting | bytes 16384 | tf_op jit(solution)/shard_map/broadcast_in_dim | solution.py:153
  48.3 44.4 %all-gather.3.cloned.1.call-done = bf16[2048,2048]{1,0:T(8,128)(2,1)} async-done(((bf16[128,2048]{1,0:T(8,128)(2,1)}), bf16[2048,2048]{1,0:T(8,128)(2,1)}) %all-gather.3.cloned.1.call-update) | async-done | bytes 8388624 | tf_op jit(solution)/shard_map/all_gather | solution.py:134
  92.6 0.0 copy-done.3
  92.6 34.2 %shard_map.131.h_ref = bf16[2,1024,768]{2,1,0:T(8,128)(2,1)} custom-call(bf16[8,2,128,2048]{3,2,1,0:T(8,128)(2,1)} %bitcast.34, bf16[2,4096,768]{2,1,0:T(8,128)(2,1)} %wg_ref.1, bf16[2,4096,768]{2,1,0:T(8,128)(2,1)} %wu_ref.1, f32[1024,1]{1,0:T(8,128)} %bitcast.25, f32[2,1024,1]{2,1,0:T(8,128)} %copy.41.weight_ref), custom_call_target="tpu_custom_call" | custom-call | flops 25769803776 | bytes 33554432 | tf_op jit(solution)/shard_map/pallas_call | solution.py:54
  126.8 18.0 %shard_map.132 = bf16[8,2,128,2048]{3,2,1,0:T(8,128)(2,1)} custom-call(bf16[2,1024,768]{2,1,0:T(8,128)(2,1)} %shard_map.131.h_ref, bf16[2,768,4096]{2,1,0:T(8,128)(2,1)} %w_ref.1), custom_call_target="tpu_custom_call" | custom-call | flops 12884901888 | bytes 20971520 | tf_op jit(solution)/shard_map/pallas_call | solution.py:90
  144.8 0.0 copy-start.5
  144.8 0.0 copy-start.4
  144.8 0.0 copy-start.2
  144.8 0.0 reduce-scatter.2.cloned.1.call-update
  144.9 0.0 copy-start.6
  144.9 0.6 copy-done.5
  145.5 0.1 fusion.11
  145.6 0.2 reduce_window_sum.11
  145.7 0.0 copy-done.4
  145.7 0.2 select_reduce_fusion
  145.9 0.0 copy-start.1
  145.9 0.0 copy-done.2
  146.0 4.0 %convolution_convert_fusion = bf16[256,1024]{1,0:T(8,128)(2,1)} fusion(bf16[2048,1024]{1,0:T(8,128)(2,1)} %param.19, bf16[128,2048]{1,0:T(8,128)(2,1)S(1)} %copy-done.2, f32[2048]{0:T(1024)S(1)} %convert_element_type.50, f32[128]{0:T(128)S(1)} %get-tuple-element.4, s32[128]{0:T(128)S(1)} %multiply_add_fusion), kind=kOutput, calls=%fused_computation.4 | convolution fusion | flops 605323264 | bytes 5252096 | tf_op jit(solution)/shard_map/dot_general | solution.py:165
  150.0 3.5 %all-to-all-start = ((bf16[2,128,1024]{2,1,0:T(8,128)(2,1)}), bf16[2,128,1024]{2,1,0:T(8,128)(2,1)S(1)}, u32[]{:S(2)}, u32[]{:S(2)}) async-start(bf16[2,128,1024]{2,1,0:T(8,128)(2,1)} %bitcast.10), calls=%async_computation.1 | async-start | bytes 1048576 | tf_op jit(solution)/shard_map/all_to_all | solution.py:169
  153.5 0.0 copy-done.6
  153.5 8.7 %all-to-all-done = bf16[2,128,1024]{2,1,0:T(8,128)(2,1)S(1)} async-done(((bf16[2,128,1024]{2,1,0:T(8,128)(2,1)}), bf16[2,128,1024]{2,1,0:T(8,128)(2,1)S(1)}, u32[]{:S(2)}, u32[]{:S(2)}) %all-to-all-start) | async-done | bytes 524320 | tf_op jit(solution)/shard_map/all_to_all | solution.py:169
  162.2 0.1 convert_reduce_fusion
  162.3 0.1 copy.46
  162.4 0.1 slice.55
  162.4 0.2 multiply_reduce_fusion
  162.7 0.2 multiply_convert_fusion
  162.9 0.1 pad_maximum_fusion
  163.0 0.8 convert_element_type.56
  163.8 84.1 %reduce-scatter.2.cloned.1.call-done = bf16[1,128,2048]{2,1,0:T(8,128)(2,1)} async-done(((bf16[16,128,2048]{2,1,0:T(8,128)(2,1)}), bf16[1,128,2048]{2,1,0:T(8,128)(2,1)}) %reduce-scatter.2.cloned.1.call-update) | async-done | bytes 524304 | tf_op jit(solution)/shard_map/reduce_scatter | solution.py:180
  247.9 0.0 copy-done.1
  (10 shorter events, 0.1 us)
Async XLA Ops:
  7.2 4.1 %copy-start = (bf16[2048,16]{0,1:T(8,128)(2,1)S(1)}, bf16[2048,16]{0,1:T(8,128)(2,1)}, u32[]{:S(2)}) copy-start(bf16[2048,16]{0,1:T(8,128)(2,1)} %param.20) | copy-start | bytes 196612
  7.2 85.5 %all-gather.3.cloned.1.call-start = ((), (), s32[]{:S(2)}) async-start(), calls=%async_computation.3 | async-start | bytes 8912896 | tf_op jit(solution)/shard_map/all_gather | solution.py:134
  9.9 238.0 %reduce-scatter.2.cloned.1.call-start = ((), (), s32[]{:S(2)}) async-start(), calls=%async_computation.2 | async-start | bytes 8912896 | tf_op jit(solution)/shard_map/reduce_scatter | solution.py:180
  40.5 52.1 %copy-start.3 = (f32[1024,17]{1,0:T(8,128)}, f32[1024,17]{1,0:T(8,128)S(1)}, u32[]{:S(2)}) copy-start(f32[1024,17]{1,0:T(8,128)S(1)} %all_gather.11) | copy-start | bytes 208900
  144.8 0.7 copy-start.5
  144.8 0.9 copy-start.4
  144.8 1.1 copy-start.2
  144.9 8.6 %copy-start.6 = (bf16[128]{0:T(256)(128)(2,1)S(1)}, bf16[128]{0:T(256)(128)(2,1)}, u32[]{:S(2)}) copy-start(bf16[128]{0:T(256)(128)(2,1)} %param.18) | copy-start | bytes 772
  145.9 102.0 %copy-start.1 = (bf16[2048,16]{0,1:T(8,128)(2,1)S(1)}, bf16[2048,16]{0,1:T(8,128)(2,1)}, u32[]{:S(2)}) copy-start(bf16[2048,16]{0,1:T(8,128)(2,1)} %param.20) | copy-start | bytes 196612
  150.0 12.2 %all-to-all-start = ((bf16[2,128,1024]{2,1,0:T(8,128)(2,1)}), bf16[2,128,1024]{2,1,0:T(8,128)(2,1)S(1)}, u32[]{:S(2)}, u32[]{:S(2)}) async-start(bf16[2,128,1024]{2,1,0:T(8,128)(2,1)} %bitcast.10), calls=%async_computation.1 | async-start | bytes 1048576 | tf_op jit(solution)/shard_map/all_to_all | solution.py:169
Sparse Core Ops, SparseCore 0:
  10.8 81.7 all-gather.2
  145.0 102.9 reduce-scatter.1

commit v2 on v1

v2 whole, which is shorter than its diff:
```python
import functools

import jax
import jax.numpy as jnp
from jax import lax
from jax.experimental import pallas as pl
from jax.experimental.pallas import tpu as pltpu
from jax.sharding import PartitionSpec as P

D = 4096
KVH = 4
HD = 128
TOPK = 8


EPS = 1e-06
VMEM_LIMIT = 56 * 1024 * 1024


def tile_of(size, most):
    for candidate in range(most, 127, -128):
        if size % candidate == 0:
            return candidate
    return size


def silu_up(gate, up, scale, weight):
    gate = gate * scale
    up = up * scale
    return (gate / (1.0 + jnp.exp(-gate)) * up * weight).astype(jnp.bfloat16)


def column_of(side, index):
    lane = lax.broadcasted_iota(jnp.int32, side.shape, 1)
    return jnp.sum(jnp.where(lane == index, side, 0.0), 1, keepdims=True)


def gained_kernel(x_ref, gain_ref, out_ref):
    gained = x_ref[...].astype(jnp.float32) * gain_ref[...].astype(jnp.float32)
    out_ref[...] = gained.astype(jnp.bfloat16)


def gained(x, gain):
    return pl.pallas_call(
        gained_kernel, out_shape=jax.ShapeDtypeStruct(x.shape, jnp.bfloat16)
    )(x, gain[None])


def block_hidden_kernel(
    where_ref, own_ref, other_ref, sib_own_ref, sib_other_ref, side_ref, wg_ref, wu_ref,
    out_ref, x_ref, gates_ref,
):
    rows, width = own_ref.shape
    expert = pl.program_id(0)

    @pl.when((expert == 0) & (pl.program_id(1) == 0))
    def _():
        mine = pl.ds(pl.multiple_of(where_ref[0] * width, width), width)
        theirs = pl.ds(pl.multiple_of((1 - where_ref[0]) * width, width), width)
        x_ref[0:rows, mine] = own_ref[...]
        x_ref[0:rows, theirs] = other_ref[...]
        x_ref[rows : 2 * rows, mine] = sib_own_ref[...]
        x_ref[rows : 2 * rows, theirs] = sib_other_ref[...]
        gates_ref[...] = jnp.transpose(side_ref[...])

    x = x_ref[...]
    gate = jnp.dot(x, wg_ref[0], preferred_element_type=jnp.float32)
    up = jnp.dot(x, wu_ref[0], preferred_element_type=jnp.float32)
    side = gates_ref[...]
    weight = column_of(side, 1 + where_ref[1] + expert)
    out_ref[0] = silu_up(gate, up, column_of(side, 0), weight)


def block_hidden(where, chunks, side, w_gate, w_up):
    rows, width = chunks[0].shape
    experts, depth, units = w_gate.shape
    tile = tile_of(units, 256)
    chunk_spec = pl.BlockSpec((rows, width), lambda e, f, s: (0, 0))
    weight_spec = pl.BlockSpec((1, depth, tile), lambda e, f, s: (e, 0, f))
    return pl.pallas_call(
        block_hidden_kernel,
        grid_spec=pltpu.PrefetchScalarGridSpec(
            num_scalar_prefetch=1,
            grid=(experts, units // tile),
            in_specs=[chunk_spec] * 4
            + [pl.BlockSpec(side.shape, lambda e, f, s: (0, 0)), weight_spec, weight_spec],
            out_specs=pl.BlockSpec((1, 2 * rows, tile), lambda e, f, s: (e, 0, f)),
            scratch_shapes=[
                pltpu.VMEM((2 * rows, depth), jnp.bfloat16),
                pltpu.VMEM((2 * rows, side.shape[0]), jnp.float32),
            ],
        ),
        out_shape=jax.ShapeDtypeStruct((experts, 2 * rows, units), jnp.bfloat16),
        compiler_params=pltpu.CompilerParams(vmem_limit_bytes=VMEM_LIMIT),
        cost_estimate=pl.CostEstimate(
            flops=8 * rows * depth * units * experts,
            bytes_accessed=4 * experts * depth * units + 4 * rows * depth,
            transcendentals=2 * rows * units * experts,
        ),
    )(where, *chunks, side, w_gate, w_up)


def block_down_kernel(where_ref, h_ref, w_ref, own_ref, sib_ref):
    rows = own_ref.shape[1]
    y = None
    for e in range(h_ref.shape[0]):
        term = jnp.dot(h_ref[e], w_ref[e], preferred_element_type=jnp.float32)
        y = term if y is None else y + term
    own_ref[0] = y[:rows].astype(jnp.bfloat16)
    sib_ref[0] = y[rows:].astype(jnp.bfloat16)


def block_down(where, hidden, w_down):
    experts, tokens, units = hidden.shape
    rows, width = tokens // 2, w_down.shape[2] // 2
    tile = tile_of(width, 512)
    tiles = width // tile
    out_spec = pl.BlockSpec((1, rows, tile), lambda h, n, s: (h, 0, n))
    out = jax.ShapeDtypeStruct((2, rows, width), jnp.bfloat16)
    return pl.pallas_call(
        block_down_kernel,
        grid_spec=pltpu.PrefetchScalarGridSpec(
            num_scalar_prefetch=1,
            grid=(2, tiles),
            in_specs=[
                pl.BlockSpec((experts, tokens, units), lambda h, n, s: (0, 0, 0)),
                pl.BlockSpec(
                    (experts, units, tile),
                    lambda h, n, s: (0, 0, (h + s[0] - 2 * h * s[0]) * tiles + n),
                ),
            ],
            out_specs=[out_spec, out_spec],
        ),
        out_shape=[out, out],
        compiler_params=pltpu.CompilerParams(vmem_limit_bytes=VMEM_LIMIT),
        cost_estimate=pl.CostEstimate(
            flops=4 * experts * tokens * units * width,
            bytes_accessed=4 * (experts * units + tokens) * width,
            transcendentals=0,
        ),
    )(where, hidden, w_down)


def total(*terms):
    return sum(term.astype(jnp.float32) for term in terms).astype(jnp.bfloat16)


def ring_experts(rows_out, side, w_gate, w_up, w_down):
    ep_count = lax.axis_size("ep")
    chips = ep_count // 2
    forward = [(d, (d + 2) % ep_count) for d in range(ep_count)]
    siblings = [(d, d ^ 1) for d in range(ep_count)]
    along = functools.partial(lax.ppermute, axis_name="ep", perm=forward)
    beside = functools.partial(lax.ppermute, axis_name="ep", perm=siblings)
    across = functools.partial(lax.ppermute, axis_name="tp", perm=[(0, 1), (1, 0)])
    where = jnp.stack([lax.axis_index("tp"), lax.axis_index("ep") * w_gate.shape[0]])
    where = where.astype(jnp.int32)

    lane, sides = [rows_out], [jnp.concatenate([side, beside(side)], 1)]
    for _ in range(chips - 1):
        lane.append(along(lane[-1]))
        sides.append(along(sides[-1]))
    crossed = [across(chunk) for chunk in lane]
    hidden = []
    for s in range(chips):
        chunks = (lane[s], crossed[s], beside(lane[s]), beside(crossed[s]))
        hidden.append(block_hidden(where, chunks, sides[s], w_gate, w_up))

    travelling = None
    for s in list(range(1, chips)) + [0]:
        own, sib = block_down(where, hidden[s], w_down)
        back = beside(sib)
        swapped = across(total(own[1], back[1]))
        terms = (own[0], back[0], swapped)
        travelling = total(*terms) if travelling is None else total(along(travelling), *terms)
    return travelling


def hidden_kernel(x_ref, wg_ref, wu_ref, scale_ref, weight_ref, out_ref):
    blocks, parts, rows, width = x_ref.shape
    gate = up = None
    for part in range(parts):
        x = x_ref[:, part].reshape(blocks * rows, width)
        depth = pl.ds(part * width, width)
        g = jnp.dot(x, wg_ref[0, depth], preferred_element_type=jnp.float32)
        u = jnp.dot(x, wu_ref[0, depth], preferred_element_type=jnp.float32)
        gate = g if gate is None else gate + g
        up = u if up is None else up + u
    out_ref[0] = silu_up(gate, up, scale_ref[...], weight_ref[0])


def hidden_of(x, w_gate, w_up, scale, weight):
    blocks, parts, rows, width = x.shape
    experts, depth, units = w_gate.shape
    tokens = blocks * rows
    tile = tile_of(units, 256)
    tiles = units // tile
    wspec = pl.BlockSpec((1, depth, tile), lambda e, f: (e, 0, f))
    return pl.pallas_call(
        hidden_kernel,
        grid=(experts, tiles),
        in_specs=[
            pl.BlockSpec(x.shape, lambda e, f: (0, 0, 0, 0)),
            wspec,
            wspec,
            pl.BlockSpec((tokens, 1), lambda e, f: (0, 0)),
            pl.BlockSpec((1, tokens, 1), lambda e, f: (e, 0, 0)),
        ],
        out_specs=pl.BlockSpec((1, tokens, tile), lambda e, f: (e, 0, f)),
        out_shape=jax.ShapeDtypeStruct((experts, tokens, units), jnp.bfloat16),
        compiler_params=pltpu.CompilerParams(vmem_limit_bytes=VMEM_LIMIT),
    )(x, w_gate, w_up, scale, weight)


def down_kernel(h_ref, w_ref, out_ref):
    blocks, _, rows, tile = out_ref.shape
    y = None
    for e in range(h_ref.shape[0]):
        term = jnp.dot(h_ref[e], w_ref[e], preferred_element_type=jnp.float32)
        y = term if y is None else y + term
    out_ref[:, 0] = y.astype(jnp.bfloat16).reshape(blocks, rows, tile)


def down_of(hidden, w_down, blocks, parts):
    experts, tokens, units = hidden.shape
    width = w_down.shape[2] // parts
    rows = tokens // blocks
    tile = tile_of(width, 512)
    tiles = width // tile
    return pl.pallas_call(
        down_kernel,
        grid=(parts * tiles,),
        in_specs=[
            pl.BlockSpec((experts, tokens, units), lambda n: (0, 0, 0)),
            pl.BlockSpec((experts, units, tile), lambda n: (0, 0, n)),
        ],
        out_specs=pl.BlockSpec(
            (blocks, 1, rows, tile), lambda n: (0, n // tiles, 0, n % tiles)
        ),
        out_shape=jax.ShapeDtypeStruct((blocks, parts, rows, width), jnp.bfloat16),
        compiler_params=pltpu.CompilerParams(vmem_limit_bytes=VMEM_LIMIT),
    )(hidden, w_down)


def plain_experts(rows_out, side, w_gate, w_up, w_down):
    tp_count, ep_count = lax.axis_size("tp"), lax.axis_size("ep")
    rows, width = rows_out.shape
    exp_local = w_gate.shape[0]
    gathered = lax.all_gather(rows_out, ("ep", "tp"), axis=0, tiled=False)
    gathered = gathered.reshape(ep_count, tp_count, rows, width)
    side = lax.all_gather(side, "ep", axis=1, tiled=True)
    first_expert = 1 + lax.axis_index("ep") * exp_local
    weight = lax.dynamic_slice_in_dim(side, first_expert, exp_local, 0)[:, :, None]
    hidden = hidden_of(gathered, w_gate, w_up, side[0][:, None], weight)
    partial = down_of(hidden, w_down, ep_count, tp_count)
    partial = partial.reshape(ep_count * tp_count, rows, width)
    return lax.psum_scatter(partial, ("ep", "tp"), scatter_dimension=0, tiled=False)


def per_device(
    layer_input,
    stream,
    expert_ids,
    kv_owner,
    attn_norm,
    moe_norm,
    k_norm,
    w_kv,
    router,
    w_gate,
    w_up,
    w_down,
):
    rows = layer_input.shape[0]
    tp_count = lax.axis_size("tp")
    pair = tp_count == 2
    columns = 2 * KVH * HD
    expert_count = router.shape[1]
    first = layer_input.astype(jnp.float32)
    second = stream.astype(jnp.float32)

    rows_out = gained(stream, moe_norm)

    logits = lax.dot_general(
        router, rows_out, (((0,), (1,)), ((), ())), preferred_element_type=jnp.float32
    )
    squares = jnp.stack([jnp.sum(first * first, 1), jnp.sum(second * second, 1)], 0)
    small = jnp.concatenate([squares, logits], 0)
    if pair:
        small = small + lax.ppermute(small, "tp", [(0, 1), (1, 0)])
    else:
        small = lax.psum(small, "tp")
    first_scale = lax.rsqrt(small[0] / D + EPS)
    second_scale = lax.rsqrt(small[1:2] / D + EPS)
    logits = small[2:] * second_scale
    expert_range = jnp.arange(expert_count, dtype=jnp.int32)
    chosen = jnp.any(expert_ids.T[None, :, :] == expert_range[:, None, None], 1)
    top = jnp.max(jnp.where(chosen, logits, -jnp.inf), 0, keepdims=True)
    weights = jnp.where(chosen, jnp.exp(jnp.where(chosen, logits - top, 0.0)), 0.0)
    weights = weights / jnp.sum(weights, 0, keepdims=True)
    fill = jnp.zeros((-(1 + expert_count) % 8, rows), jnp.float32)
    side = jnp.concatenate([second_scale, weights, fill], 0)

    attn_in = (first * attn_norm.astype(jnp.float32)).astype(jnp.bfloat16)
    kv = jnp.dot(attn_in, w_kv, preferred_element_type=jnp.float32) * first_scale[:, None]
    owner_cap = 2 * rows // tp_count
    owner = kv_owner[:, 0]
    owner_hot = (owner[:, None] == jnp.arange(tp_count, dtype=jnp.int32)[None, :]).astype(jnp.int32)
    owner_slot = jnp.sum(
        (jnp.cumsum(owner_hot, 0, dtype=jnp.int32) - owner_hot) * owner_hot, 1, dtype=jnp.int32
    )
    if pair:
        owner = jnp.where(owner == lax.axis_index("tp"), 0, 1)
    target = owner * owner_cap + owner_slot
    placing = target[None, :] == jnp.arange(tp_count * owner_cap, dtype=jnp.int32)[:, None]
    placed = jnp.dot(
        placing.astype(jnp.bfloat16), kv.astype(jnp.bfloat16), preferred_element_type=jnp.float32
    )
    placed = placed.astype(jnp.bfloat16).reshape(tp_count, owner_cap, columns)
    if pair:
        arrived = lax.ppermute(placed[1], "tp", [(0, 1), (1, 0)])
        heads = placed[0].astype(jnp.float32) + arrived.astype(jnp.float32)
    else:
        arrived = lax.all_to_all(placed, "tp", split_axis=0, concat_axis=0, tiled=True)
        heads = jnp.sum(arrived.astype(jnp.float32), 0)
    heads = heads.reshape(owner_cap, 2 * KVH, HD)
    keys = heads[:, :KVH]
    keys = keys * lax.rsqrt(jnp.mean(keys * keys, 2, keepdims=True) + EPS)
    keys = keys * k_norm.astype(jnp.float32)
    kv_cache = jnp.concatenate([keys, heads[:, KVH:]], 1).astype(jnp.bfloat16)
    kv_cache = kv_cache.reshape(1, 1, owner_cap, columns)

    experts = ring_experts if pair and lax.axis_size("ep") % 2 == 0 else plain_experts
    moe_out = experts(rows_out, side, w_gate, w_up, w_down)
    return (moe_out, kv_cache)


def solution(mesh):
    placed = (
        P(("group", "ep"), "tp"),
        P(("group", "ep"), "tp"),
        P(("group", "ep"), None),
        P(("group", "ep"), None),
        P("tp"),
        P("tp"),
        P(),
        P("tp", None),
        P("tp", None),
        P("ep", None, "tp"),
        P("ep", None, "tp"),
        P("ep", "tp", None),
    )
    return jax.shard_map(
        per_device,
        mesh=mesh,
        in_specs=placed,
        out_specs=(P(("group", "ep"), "tp"), P(("group", "ep"), "tp", None, None)),
        check_vma=False,
    )
```

time: 255 us -> 206 us (0.81)
  waiting for transfers between devices: 137 us -> 52.6 us
  Pallas kernels: 52.2 us -> 103 us
  blocking collectives: 27.1 us -> 0 us
  starting transfers between devices: 3.59 us -> 21.6 us
  between operations: 14.2 us -> 1.03 us
  other arithmetic: 5.8 us -> 17.1 us
  local copies, waits for them, and re-layouts: 9.51 us -> 5.13 us
    reduce_scatter x1 -> x0, waiting for transfers between devices: 84.1 us -> none  [per_device(): lax.psum_scatter(partial, ('ep', 'tp'), scatter_dimension=0, tiled=False)]
    ppermute x0 -> x32, waiting for transfers between devices: none -> 52.6 us  [the longest x3 19.4 us: ring_experts(): lane.append(along(lane[-1]))]
    pallas_call x2 -> x9, Pallas kernels: 52.2 us -> 103 us  [the longest x4 58 us: block_hidden(): pl.pallas_call(block_hidden_kernel, grid_spec=pltpu.PrefetchScalarGridSpe...]
    all_gather x1 -> x0, waiting for transfers between devices: 44.4 us -> none  [per_device(): gathered = lax.all_gather(rows_out, ('ep', 'tp'), axis=0, tiled=False)]
    ppermute x0 -> x32, starting transfers between devices: none -> 21.6 us  [the longest x3 4.92 us: ring_experts(): along(travelling)]
    all_gather x1 -> x0, blocking collectives: 17.5 us -> none  [per_device(): lax.all_gather(jnp.concatenate([second_scale, weights], 1), 'ep', axis=0,...]
    psum x1 -> x0, blocking collectives: 9.59 us -> none  [per_device(): small = lax.psum(jnp.concatenate([squares, partial_logits], 1), 'tp')]
    all_to_all x1 -> x0, waiting for transfers between devices: 8.67 us -> none  [per_device(): lax.all_to_all(placed, 'tp', split_axis=0, concat_axis=0, tiled=True)]
  transfers between devices with their start and end apart: 3 -> 32, of which waited for: 3 -> 7; matrix products, arithmetic and copies ran while one was open for 7% -> 10% of each run, Pallas kernels for 0% -> 49%
where the time goes in v2:
time: 206 us; the launch traced here: 205 us
  Pallas kernels  103 us (50%)
  waiting for transfers between devices  52.6 us (26%)
  starting transfers between devices  21.6 us (10%)
  other arithmetic  17.1 us (8%)
  local copies, waits for them, and re-layouts  5.13 us (2%)
  matrix products  4.56 us (2%)
    pallas_call x4, Pallas kernels, block_hidden(): pl.pallas_call(block_hidden_kernel, grid_spec=pltpu.PrefetchScalarGridSpe...  58 us
    pallas_call x4, Pallas kernels, block_down(): pl.pallas_call(block_down_kernel, grid_spec=pltpu.PrefetchScalarGridSpec(...  43.4 us
    ppermute x3, waiting for transfers between devices, ring_experts(): lane.append(along(lane[-1]))  19.4 us
    ppermute x3, waiting for transfers between devices, ring_experts(): along(travelling)  13.5 us
    ppermute x4, waiting for transfers between devices, ring_experts(): swapped = across(total(own[1], back[1]))  11.2 us
    convert_element_type x8, other arithmetic, total(): sum((term.astype(jnp.float32) for term in terms)).astype(jnp.bfloat16)  8.88 us
    ppermute x3, waiting for transfers between devices, ring_experts(): sides.append(along(sides[-1]))  8.54 us
    ppermute x3, starting transfers between devices, ring_experts(): along(travelling)  4.92 us
  transfers between devices with their start and end apart: 32, of which 7 were waited for; matrix products, arithmetic and copies ran while one was open for 10% of the time, Pallas kernels for 49%

profile of v2, /device:TPU:0, one launch (start us, length us, event | category | flops | bytes accessed | tf_op | source)
XLA Modules:
  0.0 205.4 jit_solution(13643807203176028612)
XLA Ops:
  0.6 1.3 broadcast_in_dim.33.gain_ref
  2.0 1.9 shard_map.131.own_ref
  3.9 3.0 %collective-permute-start = (bf16[128,2048]{1,0:T(8,128)(2,1)}, bf16[128,2048]{1,0:T(8,128)(2,1)S(1)}, u32[]{:S(2)}, u32[]{:S(2)}) collective-permute-start(bf16[128,2048]{1,0:T(8,128)(2,1)} %shard_map.131.own_ref), channel_id=1, source_target_pairs={{0,4},{2,6},{4,8},{6,10},{8,12},{10,14},{12,0},{14,2},{1,5},{3,7},... | collective-permute-start | bytes 1572872 | tf_op jit(solution)/shard_map/ppermute | solution.py:161
  6.9 1.2 multiply_reduce_fusion
  8.2 1.3 convolution_bitcast_fusion
  9.4 1.2 fusion.1
  10.7 1.6 collective-permute-start.4
  12.2 0.7 fusion.20
  13.2 0.8 select_reduce_fusion
  14.7 0.7 fusion.21
  15.4 5.7 %collective-permute-done.own_ref = bf16[128,2048]{1,0:T(8,128)(2,1)S(1)} collective-permute-done((bf16[128,2048]{1,0:T(8,128)(2,1)}, bf16[128,2048]{1,0:T(8,128)(2,1)S(1)}, u32[]{:S(2)}, u32[]{:S(2)}) %collective-permute-start) | collective-permute-done | bytes 524320 | tf_op jit(solution)/shard_map/ppermute | solution.py:161
  21.1 1.5 collective-permute-start.1
  23.2 13.7 %collective-permute-done.10.own_ref = bf16[128,2048]{1,0:T(8,128)(2,1)S(1)} collective-permute-done((bf16[128,2048]{1,0:T(8,128)(2,1)S(1)}, bf16[128,2048]{1,0:T(8,128)(2,1)S(1)}, u32[]{:S(2)}, u32[]{:S(2)}) %collective-permute-start.10) | collective-permute-done | bytes 524320 | tf_op jit(solution)/shard_map/ppermute | solution.py:161
  37.0 0.8 collective-permute-start.11
  38.4 0.7 convert_element_type.219
  39.8 3.3 %convolution_convert_fusion = bf16[256,1024]{1,0:T(8,128)(2,1)S(1)} fusion(bf16[2048,1024]{1,0:T(8,128)(2,1)} %param.19, bf16[128,2048]{1,0:T(8,128)(2,1)} %param.12, f32[2048]{0:T(1024)S(1)} %convert_element_type.219, f32[128]{0:T(128)S(1)} %get-tuple-element.18, s32[128]{0:T(128)S(1)} %fusion.25), kind=kOutput, calls=%fused_computation.2 | convolution fusion | flops 605323264 | bytes 5252096 | tf_op jit(solution)/shard_map/dot_general | solution.py:316
  43.2 8.5 %collective-permute-done.6.side_ref = f32[24,256]{1,0:T(8,128)S(1)} collective-permute-done((f32[24,256]{1,0:T(8,128)S(1)}, f32[24,256]{1,0:T(8,128)S(1)}, u32[]{:S(2)}, u32[]{:S(2)}) %collective-permute-start.6) | collective-permute-done | bytes 24608 | tf_op jit(solution)/shard_map/ppermute | solution.py:162
  51.7 1.0 collective-permute-start.31
  53.3 1.0 collective-permute-start.19
  54.3 14.5 %shard_map.132.h_ref = bf16[2,256,768]{2,1,0:T(8,128)(2,1)} custom-call(s32[2]{0:T(128)} %pad_add_fusion.where_ref, bf16[128,2048]{1,0:T(8,128)(2,1)} %copy-done.8, bf16[128,2048]{1,0:T(8,128)(2,1)} %copy-done.11, bf16[128,2048]{1,0:T(8,128)(2,1)} %collective-permute-done.2.sib_own_ref, bf16[128,2048]{1,0:T(8,128)(2,1)} %collective-permute-done.3.sib_other_ref, ...), custom_call_target="tpu_custom_call" | custom-call | flops 6442450944 | bytes 27262976 | tf_op jit(solution)/shard_map/pallas_call | solution.py:80
  68.8 10.8 %shard_map.133 = (bf16[2,128,2048]{2,1,0:T(8,128)(2,1)}, bf16[2,128,2048]{2,1,0:T(8,128)(2,1)}) custom-call(s32[2]{0:T(128)} %pad_add_fusion.where_ref, bf16[2,256,768]{2,1,0:T(8,128)(2,1)} %shard_map.132.h_ref, bf16[2,768,4096]{2,1,0:T(8,128)(2,1)} %w_ref.7), custom_call_target="tpu_custom_call" | custom-call | flops 3221225472 | bytes 14680064 | tf_op jit(solution)/shard_map/pallas_call | solution.py:120
  79.9 1.1 collective-permute-start.26
  81.9 14.5 %shard_map.134.h_ref = bf16[2,256,768]{2,1,0:T(8,128)(2,1)} custom-call(s32[2]{0:T(128)} %pad_add_fusion.where_ref, bf16[128,2048]{1,0:T(8,128)(2,1)} %copy-done.9, bf16[128,2048]{1,0:T(8,128)(2,1)} %copy-done.10, bf16[128,2048]{1,0:T(8,128)(2,1)} %copy-done.13, bf16[128,2048]{1,0:T(8,128)(2,1)} %copy-done.15, f32[24,256]{1,0:T(8,128)} %copy-done.20, ...), custom_call_target="tpu_custom_call" | custom-call | flops 6442450944 | bytes 27262976 | tf_op jit(solution)/shard_map/pallas_call | solution.py:80
  96.4 10.9 %shard_map.135 = (bf16[2,128,2048]{2,1,0:T(8,128)(2,1)}, bf16[2,128,2048]{2,1,0:T(8,128)(2,1)}) custom-call(s32[2]{0:T(128)} %pad_add_fusion.where_ref, bf16[2,256,768]{2,1,0:T(8,128)(2,1)} %shard_map.134.h_ref, bf16[2,768,4096]{2,1,0:T(8,128)(2,1)} %w_ref.7), custom_call_target="tpu_custom_call" | custom-call | flops 3221225472 | bytes 14680064 | tf_op jit(solution)/shard_map/pallas_call | solution.py:120
  107.5 0.9 fusion.10
  109.0 1.0 collective-permute-start.8
  110.1 0.8 copy-done.18
  110.9 14.5 %shard_map.136.h_ref = bf16[2,256,768]{2,1,0:T(8,128)(2,1)} custom-call(s32[2]{0:T(128)} %pad_add_fusion.where_ref, bf16[128,2048]{1,0:T(8,128)(2,1)} %copy-done.7, bf16[128,2048]{1,0:T(8,128)(2,1)} %copy-done.12, bf16[128,2048]{1,0:T(8,128)(2,1)} %copy-done.17, bf16[128,2048]{1,0:T(8,128)(2,1)} %copy-done.18, f32[24,256]{1,0:T(8,128)} %copy-done.22, ...), custom_call_target="tpu_custom_call" | custom-call | flops 6442450944 | bytes 27262976 | tf_op jit(solution)/shard_map/pallas_call | solution.py:80
  125.4 10.8 %shard_map.137 = (bf16[2,128,2048]{2,1,0:T(8,128)(2,1)}, bf16[2,128,2048]{2,1,0:T(8,128)(2,1)}) custom-call(s32[2]{0:T(128)} %pad_add_fusion.where_ref, bf16[2,256,768]{2,1,0:T(8,128)(2,1)} %shard_map.136.h_ref, bf16[2,768,4096]{2,1,0:T(8,128)(2,1)} %w_ref.7), custom_call_target="tpu_custom_call" | custom-call | flops 3221225472 | bytes 14680064 | tf_op jit(solution)/shard_map/pallas_call | solution.py:120
  136.3 0.9 fusion.11
  137.2 1.0 collective-permute-start.16
  138.2 1.0 fusion.9
  139.7 0.8 copy-done.14
  140.5 0.8 copy-done.16
  141.3 14.5 %shard_map.138.h_ref = bf16[2,256,768]{2,1,0:T(8,128)(2,1)} custom-call(s32[2]{0:T(128)} %pad_add_fusion.where_ref, bf16[128,2048]{1,0:T(8,128)(2,1)} %shard_map.131.own_ref, bf16[128,2048]{1,0:T(8,128)(2,1)} %collective-permute-done.26.other_ref, bf16[128,2048]{1,0:T(8,128)(2,1)} %copy-done.14, bf16[128,2048]{1,0:T(8,128)(2,1)} %copy-done.16, ...), custom_call_target="tpu_custom_call" | custom-call | flops 6442450944 | bytes 27262976 | tf_op jit(solution)/shard_map/pallas_call | solution.py:80
  155.8 10.9 %shard_map.139 = (bf16[2,128,2048]{2,1,0:T(8,128)(2,1)}, bf16[2,128,2048]{2,1,0:T(8,128)(2,1)}) custom-call(s32[2]{0:T(128)} %pad_add_fusion.where_ref, bf16[2,256,768]{2,1,0:T(8,128)(2,1)} %shard_map.138.h_ref, bf16[2,768,4096]{2,1,0:T(8,128)(2,1)} %w_ref.7), custom_call_target="tpu_custom_call" | custom-call | flops 3221225472 | bytes 14680064 | tf_op jit(solution)/shard_map/pallas_call | solution.py:120
  166.7 1.6 fusion.8
  168.3 4.3 %collective-permute-start.17 = (bf16[128,2048]{1,0:T(8,128)(2,1)S(1)}, bf16[128,2048]{1,0:T(8,128)(2,1)S(1)}, u32[]{:S(2)}, u32[]{:S(2)}) collective-permute-start(bf16[128,2048]{1,0:T(8,128)(2,1)S(1)} %fusion.8), channel_id=1, source_target_pairs={{0,4},{2,6},{4,8},{6,10},{8,12},{10,14},{12,0},{14,2},{1,5},{3,7},... | collective-permute-start | bytes 1572872 | tf_op jit(solution)/shard_map/ppermute | solution.py:175
  172.8 1.1 collective-permute-start.24
  174.2 0.9 fusion.13
  175.1 1.0 collective-permute-start.30
  176.1 8.3 %collective-permute-done.17 = bf16[128,2048]{1,0:T(8,128)(2,1)S(1)} collective-permute-done((bf16[128,2048]{1,0:T(8,128)(2,1)S(1)}, bf16[128,2048]{1,0:T(8,128)(2,1)S(1)}, u32[]{:S(2)}, u32[]{:S(2)}) %collective-permute-start.17) | collective-permute-done | bytes 524320 | tf_op jit(solution)/shard_map/ppermute | solution.py:175
  184.4 3.2 %collective-permute-done.24 = bf16[128,2048]{1,0:T(8,128)(2,1)S(1)} collective-permute-done((bf16[128,2048]{1,0:T(8,128)(2,1)S(1)}, bf16[128,2048]{1,0:T(8,128)(2,1)S(1)}, u32[]{:S(2)}, u32[]{:S(2)}) %collective-permute-start.24) | collective-permute-done | bytes 524320 | tf_op jit(solution)/shard_map/ppermute | solution.py:173
  187.6 1.1 fusion.6
  189.3 0.8 convert_element_type.226
  190.1 8.0 %collective-permute-done.30 = bf16[128,2048]{1,0:T(8,128)(2,1)S(1)} collective-permute-done((bf16[128,2048]{1,0:T(8,128)(2,1)}, bf16[128,2048]{1,0:T(8,128)(2,1)S(1)}, u32[]{:S(2)}, u32[]{:S(2)}) %collective-permute-start.30) | collective-permute-done | bytes 524320 | tf_op jit(solution)/shard_map/ppermute | solution.py:173
  198.1 5.2 %collective-permute-done.25 = bf16[128,2048]{1,0:T(8,128)(2,1)} collective-permute-done((bf16[128,2048]{1,0:T(8,128)(2,1)}, bf16[128,2048]{1,0:T(8,128)(2,1)}, u32[]{:S(2)}, u32[]{:S(2)}) %collective-permute-start.25) | collective-permute-done | bytes 524320 | tf_op jit(solution)/shard_map/ppermute | solution.py:175
  203.2 2.2 %fusion.4 = bf16[128,2048]{1,0:T(8,128)(2,1)} fusion(bf16[128,2048]{1,0:T(8,128)(2,1)S(1)} %collective-permute-done.30, bf16[128,2048]{1,0:T(8,128)(2,1)} %collective-permute-done.25, bf16[2,128,2048]{2,1,0:T(8,128)(2,1)S(1)} %collective-permute-done.29, bf16[2,128,2048]{2,1,0:T(8,128)(2,1)S(1)} %copy-done.5), kind=kLoop, calls=%fused_computation.10 | loop fusion | flops 2097152 | bytes 2621440 | tf_op jit(solution)/shard_map/convert_element_type | solution.py:145
  (110 shorter events, 6.8 us)
Async XLA Ops:
  0.6 7.5 %copy-start = (bf16[2048,16]{0,1:T(8,128)(2,1)S(1)}, bf16[2048,16]{0,1:T(8,128)(2,1)}, u32[]{:S(2)}) copy-start(bf16[2048,16]{0,1:T(8,128)(2,1)} %param.20) | copy-start | bytes 196612
  3.9 17.2 %collective-permute-start = (bf16[128,2048]{1,0:T(8,128)(2,1)}, bf16[128,2048]{1,0:T(8,128)(2,1)S(1)}, u32[]{:S(2)}, u32[]{:S(2)}) collective-permute-start(bf16[128,2048]{1,0:T(8,128)(2,1)} %shard_map.131.own_ref), channel_id=1, source_target_pairs={{0,4},{2,6},{4,8},{6,10},{8,12},{10,14},{12,0},{14,2},{1,5},{3,7},... | collective-permute-start | bytes 1572872 | tf_op jit(solution)/shard_map/ppermute | solution.py:161
  10.7 4.7 %collective-permute-start.4 = (f32[18,128]{1,0:T(8,128)S(1)}, f32[18,128]{1,0:T(8,128)S(1)}, u32[]{:S(2)}, u32[]{:S(2)}) collective-permute-start(f32[18,128]{1,0:T(8,128)S(1)} %pad_maximum_fusion.2), channel_id=1, source_target_pairs={{0,1},{1,0},{2,3},{3,2},{4,5},{5,4},{6,7},{7,6},{8,9},{9,8},{10,11... | collective-permute-start | bytes 27656 | tf_op jit(solution)/shard_map/ppermute | solution.py:290
  21.1 33.2 %copy-start.8 = (bf16[128,2048]{1,0:T(8,128)(2,1)}, bf16[128,2048]{1,0:T(8,128)(2,1)S(1)}, u32[]{:S(2)}) copy-start(bf16[128,2048]{1,0:T(8,128)(2,1)S(1)} %collective-permute-done.own_ref) | copy-start | bytes 1572868
  21.1 16.7 %collective-permute-start.1 = (bf16[128,2048]{1,0:T(8,128)(2,1)S(1)}, bf16[128,2048]{1,0:T(8,128)(2,1)S(1)}, u32[]{:S(2)}, u32[]{:S(2)}) collective-permute-start(bf16[128,2048]{1,0:T(8,128)(2,1)S(1)} %collective-permute-done.own_ref), channel_id=1, source_target_pairs={{0,1},{1,0},{2,3},{3,2},{4,5},{5,4},{6,7},{7,6},{8,9},{9,8},{10,11... | collective-permute-start | bytes 1572872 | tf_op jit(solution)/shard_map/ppermute | solution.py:163
  22.6 14.4 %collective-permute-start.10 = (bf16[128,2048]{1,0:T(8,128)(2,1)S(1)}, bf16[128,2048]{1,0:T(8,128)(2,1)S(1)}, u32[]{:S(2)}, u32[]{:S(2)}) collective-permute-start(bf16[128,2048]{1,0:T(8,128)(2,1)S(1)} %collective-permute-done.own_ref), channel_id=1, source_target_pairs={{0,4},{2,6},{4,8},{6,10},{8,12},{10,14},{12,0},{14,2},{1,5},{3,7},... | collective-permute-start | bytes 1572872 | tf_op jit(solution)/shard_map/ppermute | solution.py:161
  22.7 17.1 %collective-permute-start.5 = (f32[24,128]{1,0:T(8,128)S(1)}, f32[24,128]{1,0:T(8,128)S(1)}, u32[]{:S(2)}, u32[]{:S(2)}) collective-permute-start(f32[24,128]{1,0:T(8,128)S(1)} %pad_maximum_fusion.3), channel_id=1, source_target_pairs={{0,2},{2,0},{4,6},{6,4},{8,10},{10,8},{12,14},{14,12},{1,3},{3,1},... | collective-permute-start | bytes 36872 | tf_op jit(solution)/shard_map/ppermute | solution.py:159
  22.7 29.9 %collective-permute-start.2 = (bf16[128,2048]{1,0:T(8,128)(2,1)S(1)}, bf16[128,2048]{1,0:T(8,128)(2,1)}, u32[]{:S(2)}, u32[]{:S(2)}) collective-permute-start(bf16[128,2048]{1,0:T(8,128)(2,1)S(1)} %collective-permute-done.own_ref), channel_id=1, source_target_pairs={{0,2},{2,0},{4,6},{6,4},{8,10},{10,8},{12,14},{14,12},{1,3},{3,1},... | collective-permute-start | bytes 1572872 | tf_op jit(solution)/shard_map/ppermute | solution.py:166
  37.0 31.9 %copy-start.9 = (bf16[128,2048]{1,0:T(8,128)(2,1)}, bf16[128,2048]{1,0:T(8,128)(2,1)S(1)}, u32[]{:S(2)}) copy-start(bf16[128,2048]{1,0:T(8,128)(2,1)S(1)} %collective-permute-done.10.own_ref) | copy-start | bytes 1572868
  37.0 15.8 %collective-permute-start.11 = (bf16[128,2048]{1,0:T(8,128)(2,1)S(1)}, bf16[128,2048]{1,0:T(8,128)(2,1)S(1)}, u32[]{:S(2)}, u32[]{:S(2)}) collective-permute-start(bf16[128,2048]{1,0:T(8,128)(2,1)S(1)} %collective-permute-done.10.own_ref), channel_id=1, source_target_pairs={{0,1},{1,0},{2,3},{3,2},{4,5},{5,4},{6,7},{7,6},{8,9},{9,8},{10,11... | collective-permute-start | bytes 1572872 | tf_op jit(solution)/shard_map/ppermute | solution.py:163
  37.7 15.6 %collective-permute-start.18 = (bf16[128,2048]{1,0:T(8,128)(2,1)S(1)}, bf16[128,2048]{1,0:T(8,128)(2,1)S(1)}, u32[]{:S(2)}, u32[]{:S(2)}) collective-permute-start(bf16[128,2048]{1,0:T(8,128)(2,1)S(1)} %collective-permute-done.10.own_ref), channel_id=1, source_target_pairs={{0,4},{2,6},{4,8},{6,10},{8,12},{10,14},{12,0},{14,2},{1,5},{3,7},... | collective-permute-start | bytes 1572872 | tf_op jit(solution)/shard_map/ppermute | solution.py:161
  37.7 16.6 %copy-start.11 = (bf16[128,2048]{1,0:T(8,128)(2,1)}, bf16[128,2048]{1,0:T(8,128)(2,1)S(1)}, u32[]{:S(2)}) copy-start(bf16[128,2048]{1,0:T(8,128)(2,1)S(1)} %collective-permute-done.1.other_ref) | copy-start | bytes 1572868
  37.7 15.0 %collective-permute-start.3 = (bf16[128,2048]{1,0:T(8,128)(2,1)S(1)}, bf16[128,2048]{1,0:T(8,128)(2,1)}, u32[]{:S(2)}, u32[]{:S(2)}) collective-permute-start(bf16[128,2048]{1,0:T(8,128)(2,1)S(1)} %collective-permute-done.1.other_ref), channel_id=1, source_target_pairs={{0,2},{2,0},{4,6},{6,4},{8,10},{10,8},{12,14},{14,12},{1,3},{3,1},... | collective-permute-start | bytes 1572872 | tf_op jit(solution)/shard_map/ppermute | solution.py:166
  39.8 29.1 %copy-start.19 = (f32[24,256]{1,0:T(8,128)}, f32[24,256]{1,0:T(8,128)S(1)}, u32[]{:S(2)}) copy-start(f32[24,256]{1,0:T(8,128)S(1)} %pad_maximum_fusion.1.side_ref) | copy-start | bytes 73732
  39.8 11.9 %collective-permute-start.6 = (f32[24,256]{1,0:T(8,128)S(1)}, f32[24,256]{1,0:T(8,128)S(1)}, u32[]{:S(2)}, u32[]{:S(2)}) collective-permute-start(f32[24,256]{1,0:T(8,128)S(1)} %pad_maximum_fusion.1.side_ref), channel_id=1, source_target_pairs={{0,4},{2,6},{4,8},{6,10},{8,12},{10,14},{12,0},{14,2},{1,5},{3,7},... | collective-permute-start | bytes 73736 | tf_op jit(solution)/shard_map/ppermute | solution.py:162
  51.7 2.6 %copy-start.21 = (f32[24,256]{1,0:T(8,128)}, f32[24,256]{1,0:T(8,128)S(1)}, u32[]{:S(2)}) copy-start(f32[24,256]{1,0:T(8,128)S(1)} %collective-permute-done.6.side_ref) | copy-start | bytes 73732
  51.7 28.0 %collective-permute-start.31 = (bf16[128,1024]{1,0:T(8,128)(2,1)S(1)}, bf16[128,1024]{1,0:T(8,128)(2,1)S(1)}, u32[]{:S(2)}, u32[]{:S(2)}) collective-permute-start(bf16[128,1024]{1,0:T(8,128)(2,1)S(1)} %slice.107), channel_id=1, source_target_pairs={{0,1},{1,0},{2,3},{3,2},{4,5},{5,4},{6,7},{7,6},{8,9},{9,8},{10,11... | collective-permute-start | bytes 786440 | tf_op jit(solution)/shard_map/ppermute | solution.py:321
  52.7 27.2 %collective-permute-start.14 = (f32[24,256]{1,0:T(8,128)S(1)}, f32[24,256]{1,0:T(8,128)S(1)}, u32[]{:S(2)}, u32[]{:S(2)}) collective-permute-start(f32[24,256]{1,0:T(8,128)S(1)} %collective-permute-done.6.side_ref), channel_id=1, source_target_pairs={{0,4},{2,6},{4,8},{6,10},{8,12},{10,14},{12,0},{14,2},{1,5},{3,7},... | collective-permute-start | bytes 73736 | tf_op jit(solution)/shard_map/ppermute | solution.py:162
  52.7 28.3 %collective-permute-start.12 = (bf16[128,2048]{1,0:T(8,128)(2,1)S(1)}, bf16[128,2048]{1,0:T(8,128)(2,1)S(1)}, u32[]{:S(2)}, u32[]{:S(2)}) collective-permute-start(bf16[128,2048]{1,0:T(8,128)(2,1)S(1)} %collective-permute-done.10.own_ref), channel_id=1, source_target_pairs={{0,2},{2,0},{4,6},{6,4},{8,10},{10,8},{12,14},{14,12},{1,3},{3,1},... | collective-permute-start | bytes 1572872 | tf_op jit(solution)/shard_map/ppermute | solution.py:166
  52.8 16.0 %copy-start.10 = (bf16[128,2048]{1,0:T(8,128)(2,1)}, bf16[128,2048]{1,0:T(8,128)(2,1)S(1)}, u32[]{:S(2)}) copy-start(bf16[128,2048]{1,0:T(8,128)(2,1)S(1)} %collective-permute-done.11.other_ref) | copy-start | bytes 1572868
  52.8 28.2 %collective-permute-start.13 = (bf16[128,2048]{1,0:T(8,128)(2,1)S(1)}, bf16[128,2048]{1,0:T(8,128)(2,1)S(1)}, u32[]{:S(2)}, u32[]{:S(2)}) collective-permute-start(bf16[128,2048]{1,0:T(8,128)(2,1)S(1)} %collective-permute-done.11.other_ref), channel_id=1, source_target_pairs={{0,2},{2,0},{4,6},{6,4},{8,10},{10,8},{12,14},{14,12},{1,3},{3,1},... | collective-permute-start | bytes 1572872 | tf_op jit(solution)/shard_map/ppermute | solution.py:166
  53.3 27.7 %copy-start.7 = (bf16[128,2048]{1,0:T(8,128)(2,1)}, bf16[128,2048]{1,0:T(8,128)(2,1)S(1)}, u32[]{:S(2)}) copy-start(bf16[128,2048]{1,0:T(8,128)(2,1)S(1)} %collective-permute-done.18.own_ref) | copy-start | bytes 1572868
  53.3 28.0 %collective-permute-start.19 = (bf16[128,2048]{1,0:T(8,128)(2,1)S(1)}, bf16[128,2048]{1,0:T(8,128)(2,1)S(1)}, u32[]{:S(2)}, u32[]{:S(2)}) collective-permute-start(bf16[128,2048]{1,0:T(8,128)(2,1)S(1)} %collective-permute-done.18.own_ref), channel_id=1, source_target_pairs={{0,1},{1,0},{2,3},{3,2},{4,5},{5,4},{6,7},{7,6},{8,9},{9,8},{10,11... | collective-permute-start | bytes 1572872 | tf_op jit(solution)/shard_map/ppermute | solution.py:163
  68.8 11.1 %copy-start.2 = (bf16[128,2048]{1,0:T(8,128)(2,1)S(1)}, bf16[128,2048]{1,0:T(8,128)(2,1)}, u32[]{:S(2)}) copy-start(bf16[128,2048]{1,0:T(8,128)(2,1)} %shard_map.131.own_ref) | copy-start | bytes 1572868
  79.7 27.6 %collective-permute-start.7 = (bf16[2,128,2048]{2,1,0:T(8,128)(2,1)}, bf16[2,128,2048]{2,1,0:T(8,128)(2,1)S(1)}, u32[]{:S(2)}, u32[]{:S(2)}) collective-permute-start(bf16[2,128,2048]{2,1,0:T(8,128)(2,1)} %get-tuple-element.11), channel_id=1, source_target_pairs={{0,2},{2,0},{4,6},{6,4},{8,10},{10,8},{12,14},{14,12},{1,3},{3,1},... | collective-permute-start | bytes 3145736 | tf_op jit(solution)/shard_map/ppermute | solution.py:172
  79.9 1.7 copy-start.20
  79.9 28.9 %collective-permute-start.26 = (bf16[128,2048]{1,0:T(8,128)(2,1)S(1)}, bf16[128,2048]{1,0:T(8,128)(2,1)}, u32[]{:S(2)}, u32[]{:S(2)}) collective-permute-start(bf16[128,2048]{1,0:T(8,128)(2,1)S(1)} %copy-done.2), channel_id=1, source_target_pairs={{0,1},{1,0},{2,3},{3,2},{4,5},{5,4},{6,7},{7,6},{8,9},{9,8},{10,11... | collective-permute-start | bytes 1572872 | tf_op jit(solution)/shard_map/ppermute | solution.py:163
  81.0 27.5 %collective-permute-start.22 = (f32[24,256]{1,0:T(8,128)S(1)}, f32[24,256]{1,0:T(8,128)S(1)}, u32[]{:S(2)}, u32[]{:S(2)}) collective-permute-start(f32[24,256]{1,0:T(8,128)S(1)} %collective-permute-done.14.side_ref), channel_id=1, source_target_pairs={{0,4},{2,6},{4,8},{6,10},{8,12},{10,14},{12,0},{14,2},{1,5},{3,7},... | collective-permute-start | bytes 73736 | tf_op jit(solution)/shard_map/ppermute | solution.py:162
  81.0 28.0 %collective-permute-start.20 = (bf16[128,2048]{1,0:T(8,128)(2,1)S(1)}, bf16[128,2048]{1,0:T(8,128)(2,1)S(1)}, u32[]{:S(2)}, u32[]{:S(2)}) collective-permute-start(bf16[128,2048]{1,0:T(8,128)(2,1)S(1)} %collective-permute-done.18.own_ref), channel_id=1, source_target_pairs={{0,2},{2,0},{4,6},{6,4},{8,10},{10,8},{12,14},{14,12},{1,3},{3,1},... | collective-permute-start | bytes 1572872 | tf_op jit(solution)/shard_map/ppermute | solution.py:166
  81.3 15.1 %copy-start.12 = (bf16[128,2048]{1,0:T(8,128)(2,1)}, bf16[128,2048]{1,0:T(8,128)(2,1)S(1)}, u32[]{:S(2)}) copy-start(bf16[128,2048]{1,0:T(8,128)(2,1)S(1)} %collective-permute-done.19.other_ref) | copy-start | bytes 1572868
  81.3 28.7 %collective-permute-start.21 = (bf16[128,2048]{1,0:T(8,128)(2,1)S(1)}, bf16[128,2048]{1,0:T(8,128)(2,1)S(1)}, u32[]{:S(2)}, u32[]{:S(2)}) collective-permute-start(bf16[128,2048]{1,0:T(8,128)(2,1)S(1)} %collective-permute-done.19.other_ref), channel_id=1, source_target_pairs={{0,2},{2,0},{4,6},{6,4},{8,10},{10,8},{12,14},{14,12},{1,3},{3,1},... | collective-permute-start | bytes 1572872 | tf_op jit(solution)/shard_map/ppermute | solution.py:166
  96.4 11.1 %copy-start.6 = (bf16[2,128,2048]{2,1,0:T(8,128)(2,1)S(1)}, bf16[2,128,2048]{2,1,0:T(8,128)(2,1)}, u32[]{:S(2)}) copy-start(bf16[2,128,2048]{2,1,0:T(8,128)(2,1)} %get-tuple-element.10) | copy-start | bytes 3145732
  107.3 28.9 %collective-permute-start.15 = (bf16[2,128,2048]{2,1,0:T(8,128)(2,1)}, bf16[2,128,2048]{2,1,0:T(8,128)(2,1)S(1)}, u32[]{:S(2)}, u32[]{:S(2)}) collective-permute-start(bf16[2,128,2048]{2,1,0:T(8,128)(2,1)} %get-tuple-element.13), channel_id=1, source_target_pairs={{0,2},{2,0},{4,6},{6,4},{8,10},{10,8},{12,14},{14,12},{1,3},{3,1},... | collective-permute-start | bytes 3145736 | tf_op jit(solution)/shard_map/ppermute | solution.py:172
  108.5 31.2 %collective-permute-start.27 = (bf16[128,2048]{1,0:T(8,128)(2,1)S(1)}, bf16[128,2048]{1,0:T(8,128)(2,1)S(1)}, u32[]{:S(2)}, u32[]{:S(2)}) collective-permute-start(bf16[128,2048]{1,0:T(8,128)(2,1)S(1)} %copy-done.2), channel_id=1, source_target_pairs={{0,2},{2,0},{4,6},{6,4},{8,10},{10,8},{12,14},{14,12},{1,3},{3,1},... | collective-permute-start | bytes 1572872 | tf_op jit(solution)/shard_map/ppermute | solution.py:166
  108.8 30.9 %collective-permute-start.28 = (bf16[128,2048]{1,0:T(8,128)(2,1)}, bf16[128,2048]{1,0:T(8,128)(2,1)S(1)}, u32[]{:S(2)}, u32[]{:S(2)}) collective-permute-start(bf16[128,2048]{1,0:T(8,128)(2,1)} %collective-permute-done.26.other_ref), channel_id=1, source_target_pairs={{0,2},{2,0},{4,6},{6,4},{8,10},{10,8},{12,14},{14,12},{1,3},{3,1},... | collective-permute-start | bytes 1572872 | tf_op jit(solution)/shard_map/ppermute | solution.py:166
  109.0 29.2 %collective-permute-start.8 = (bf16[128,2048]{1,0:T(8,128)(2,1)}, bf16[128,2048]{1,0:T(8,128)(2,1)S(1)}, u32[]{:S(2)}, u32[]{:S(2)}) collective-permute-start(bf16[128,2048]{1,0:T(8,128)(2,1)} %fusion.10), channel_id=1, source_target_pairs={{0,1},{1,0},{2,3},{3,2},{4,5},{5,4},{6,7},{7,6},{8,9},{9,8},{10,11... | collective-permute-start | bytes 1572872 | tf_op jit(solution)/shard_map/ppermute | solution.py:173
  125.4 10.9 %copy-start.3 = (bf16[2,128,2048]{2,1,0:T(8,128)(2,1)S(1)}, bf16[2,128,2048]{2,1,0:T(8,128)(2,1)}, u32[]{:S(2)}) copy-start(bf16[2,128,2048]{2,1,0:T(8,128)(2,1)} %get-tuple-element.12) | copy-start | bytes 3145732
  136.2 36.5 %collective-permute-start.23 = (bf16[2,128,2048]{2,1,0:T(8,128)(2,1)}, bf16[2,128,2048]{2,1,0:T(8,128)(2,1)S(1)}, u32[]{:S(2)}, u32[]{:S(2)}) collective-permute-start(bf16[2,128,2048]{2,1,0:T(8,128)(2,1)} %get-tuple-element.15), channel_id=1, source_target_pairs={{0,2},{2,0},{4,6},{6,4},{8,10},{10,8},{12,14},{14,12},{1,3},{3,1},... | collective-permute-start | bytes 3145736 | tf_op jit(solution)/shard_map/ppermute | solution.py:172
  137.2 29.5 %collective-permute-start.16 = (bf16[128,2048]{1,0:T(8,128)(2,1)}, bf16[128,2048]{1,0:T(8,128)(2,1)}, u32[]{:S(2)}, u32[]{:S(2)}) collective-permute-start(bf16[128,2048]{1,0:T(8,128)(2,1)} %fusion.11), channel_id=1, source_target_pairs={{0,1},{1,0},{2,3},{3,2},{4,5},{5,4},{6,7},{7,6},{8,9},{9,8},{10,11... | collective-permute-start | bytes 1572872 | tf_op jit(solution)/shard_map/ppermute | solution.py:173
  139.3 27.4 %collective-permute-start.9 = (bf16[128,2048]{1,0:T(8,128)(2,1)}, bf16[128,2048]{1,0:T(8,128)(2,1)}, u32[]{:S(2)}, u32[]{:S(2)}) collective-permute-start(bf16[128,2048]{1,0:T(8,128)(2,1)} %fusion.9), channel_id=1, source_target_pairs={{0,4},{2,6},{4,8},{6,10},{8,12},{10,14},{12,0},{14,2},{1,5},{3,7},... | collective-permute-start | bytes 1572872 | tf_op jit(solution)/shard_map/ppermute | solution.py:175
  155.8 16.9 %copy-start.4 = (bf16[2,128,2048]{2,1,0:T(8,128)(2,1)S(1)}, bf16[2,128,2048]{2,1,0:T(8,128)(2,1)}, u32[]{:S(2)}) copy-start(bf16[2,128,2048]{2,1,0:T(8,128)(2,1)} %get-tuple-element.14) | copy-start | bytes 3145732
  166.7 7.5 %copy-start.5 = (bf16[2,128,2048]{2,1,0:T(8,128)(2,1)S(1)}, bf16[2,128,2048]{2,1,0:T(8,128)(2,1)}, u32[]{:S(2)}) copy-start(bf16[2,128,2048]{2,1,0:T(8,128)(2,1)} %get-tuple-element.16) | copy-start | bytes 3145732
  166.7 7.5 %collective-permute-start.29 = (bf16[2,128,2048]{2,1,0:T(8,128)(2,1)}, bf16[2,128,2048]{2,1,0:T(8,128)(2,1)S(1)}, u32[]{:S(2)}, u32[]{:S(2)}) collective-permute-start(bf16[2,128,2048]{2,1,0:T(8,128)(2,1)} %get-tuple-element.17), channel_id=1, source_target_pairs={{0,2},{2,0},{4,6},{6,4},{8,10},{10,8},{12,14},{14,12},{1,3},{3,1},... | collective-permute-start | bytes 3145736 | tf_op jit(solution)/shard_map/ppermute | solution.py:172
  168.3 16.1 %collective-permute-start.17 = (bf16[128,2048]{1,0:T(8,128)(2,1)S(1)}, bf16[128,2048]{1,0:T(8,128)(2,1)S(1)}, u32[]{:S(2)}, u32[]{:S(2)}) collective-permute-start(bf16[128,2048]{1,0:T(8,128)(2,1)S(1)} %fusion.8), channel_id=1, source_target_pairs={{0,4},{2,6},{4,8},{6,10},{8,12},{10,14},{12,0},{14,2},{1,5},{3,7},... | collective-permute-start | bytes 1572872 | tf_op jit(solution)/shard_map/ppermute | solution.py:175
  172.8 14.8 %collective-permute-start.24 = (bf16[128,2048]{1,0:T(8,128)(2,1)S(1)}, bf16[128,2048]{1,0:T(8,128)(2,1)S(1)}, u32[]{:S(2)}, u32[]{:S(2)}) collective-permute-start(bf16[128,2048]{1,0:T(8,128)(2,1)S(1)} %fusion.12), channel_id=1, source_target_pairs={{0,1},{1,0},{2,3},{3,2},{4,5},{5,4},{6,7},{7,6},{8,9},{9,8},{10,11... | collective-permute-start | bytes 1572872 | tf_op jit(solution)/shard_map/ppermute | solution.py:173
  174.2 31.3 %copy-start.1 = (bf16[2048,16]{0,1:T(8,128)(2,1)S(1)}, bf16[2048,16]{0,1:T(8,128)(2,1)}, u32[]{:S(2)}) copy-start(bf16[2048,16]{0,1:T(8,128)(2,1)} %param.20) | copy-start | bytes 196612
  175.1 23.0 %collective-permute-start.30 = (bf16[128,2048]{1,0:T(8,128)(2,1)}, bf16[128,2048]{1,0:T(8,128)(2,1)S(1)}, u32[]{:S(2)}, u32[]{:S(2)}) collective-permute-start(bf16[128,2048]{1,0:T(8,128)(2,1)} %fusion.13), channel_id=1, source_target_pairs={{0,1},{1,0},{2,3},{3,2},{4,5},{5,4},{6,7},{7,6},{8,9},{9,8},{10,11... | collective-permute-start | bytes 1572872 | tf_op jit(solution)/shard_map/ppermute | solution.py:173
  188.8 14.5 %collective-permute-start.25 = (bf16[128,2048]{1,0:T(8,128)(2,1)}, bf16[128,2048]{1,0:T(8,128)(2,1)}, u32[]{:S(2)}, u32[]{:S(2)}) collective-permute-start(bf16[128,2048]{1,0:T(8,128)(2,1)} %fusion.6), channel_id=1, source_target_pairs={{0,4},{2,6},{4,8},{6,10},{8,12},{10,14},{12,0},{14,2},{1,5},{3,7},... | collective-permute-start | bytes 1572872 | tf_op jit(solution)/shard_map/ppermute | solution.py:175
  (7 other events, 6.7 us)

commit v3 on v2

--- a/solution.py
+++ b/solution.py
@@ -15,6 +15,8 @@
 
 EPS = 1e-06
 VMEM_LIMIT = 56 * 1024 * 1024
+BLOCK_VMEM_LIMIT = 24 * 1024 * 1024
+MXU = 256
 
 
 def tile_of(size, most):
@@ -46,9 +48,30 @@
     )(x, gain[None])
 
 
+def paired_products(rows, steps):
+    def stage(index):
+        _, first_tile, second_tile = steps[index]
+        pltpu.matmul_push_rhs(first_tile(), index % 2, 0)
+        pltpu.matmul_push_rhs(second_tile(), index % 2, 1)
+
+    def run(first_acc, second_acc):
+        stage(0)
+        for index, (lhs, _, _) in enumerate(steps):
+            if index + 1 < len(steps):
+                stage(index + 1)
+            left = lhs()
+            pltpu.matmul_acc_lhs(first_acc, left, index % 2)
+            pltpu.matmul_acc_lhs(second_acc, left, index % 2)
+        return pltpu.matmul_pop(first_acc), pltpu.matmul_pop(second_acc)
+
+    return pl.run_scoped(
+        run, pltpu.ACC(0)((rows, MXU), jnp.float32), pltpu.ACC(1)((rows, MXU), jnp.float32)
+    )
+
+
 def block_hidden_kernel(
     where_ref, own_ref, other_ref, sib_own_ref, sib_other_ref, side_ref, wg_ref, wu_ref,
-    out_ref, x_ref, gates_ref,
+    _, out_ref, x_ref, gates_ref,
 ):
     rows, width = own_ref.shape
     expert = pl.program_id(0)
@@ -63,18 +86,21 @@
         x_ref[rows : 2 * rows, theirs] = sib_other_ref[...]
         gates_ref[...] = jnp.transpose(side_ref[...])
 
-    x = x_ref[...]
-    gate = jnp.dot(x, wg_ref[0], preferred_element_type=jnp.float32)
-    up = jnp.dot(x, wu_ref[0], preferred_element_type=jnp.float32)
+    def step(k):
+        depth = pl.ds(k * MXU, MXU)
+        return (lambda: x_ref[:, depth], lambda: wg_ref[0, depth], lambda: wu_ref[0, depth])
+
+    steps = [step(k) for k in range(2 * width // MXU)]
+    gate, up = paired_products(2 * rows, steps)
     side = gates_ref[...]
     weight = column_of(side, 1 + where_ref[1] + expert)
     out_ref[0] = silu_up(gate, up, column_of(side, 0), weight)
 
 
-def block_hidden(where, chunks, side, w_gate, w_up):
+def block_hidden(where, chunks, side, w_gate, w_up, after):
     rows, width = chunks[0].shape
     experts, depth, units = w_gate.shape
-    tile = tile_of(units, 256)
+    tile = MXU
     chunk_spec = pl.BlockSpec((rows, width), lambda e, f, s: (0, 0))
     weight_spec = pl.BlockSpec((1, depth, tile), lambda e, f, s: (e, 0, f))
     return pl.pallas_call(
@@ -83,7 +109,8 @@
             num_scalar_prefetch=1,
             grid=(experts, units // tile),
             in_specs=[chunk_spec] * 4
-            + [pl.BlockSpec(side.shape, lambda e, f, s: (0, 0)), weight_spec, weight_spec],
+            + [pl.BlockSpec(side.shape, lambda e, f, s: (0, 0)), weight_spec, weight_spec]
+            + [pl.BlockSpec(memory_space=pl.ANY)],
             out_specs=pl.BlockSpec((1, 2 * rows, tile), lambda e, f, s: (e, 0, f)),
             scratch_shapes=[
                 pltpu.VMEM((2 * rows, depth), jnp.bfloat16),
@@ -91,29 +118,38 @@
             ],
         ),
         out_shape=jax.ShapeDtypeStruct((experts, 2 * rows, units), jnp.bfloat16),
-        compiler_params=pltpu.CompilerParams(vmem_limit_bytes=VMEM_LIMIT),
+        compiler_params=pltpu.CompilerParams(vmem_limit_bytes=BLOCK_VMEM_LIMIT),
         cost_estimate=pl.CostEstimate(
             flops=8 * rows * depth * units * experts,
             bytes_accessed=4 * experts * depth * units + 4 * rows * depth,
             transcendentals=2 * rows * units * experts,
         ),
-    )(where, *chunks, side, w_gate, w_up)
-
-
-def block_down_kernel(where_ref, h_ref, w_ref, own_ref, sib_ref):
+    )(where, *chunks, side, w_gate, w_up, after)
+
+
+def block_down_kernel(where_ref, h_ref, w_ref, _, own_ref, sib_ref):
     rows = own_ref.shape[1]
-    y = None
-    for e in range(h_ref.shape[0]):
-        term = jnp.dot(h_ref[e], w_ref[e], preferred_element_type=jnp.float32)
-        y = term if y is None else y + term
-    own_ref[0] = y[:rows].astype(jnp.bfloat16)
-    sib_ref[0] = y[rows:].astype(jnp.bfloat16)
-
-
-def block_down(where, hidden, w_down):
+    experts, _, units = h_ref.shape
+
+    def step(e, k):
+        depth = pl.ds(k * MXU, MXU)
+        return (
+            lambda: h_ref[e, :, depth],
+            lambda: w_ref[e, depth, 0:MXU],
+            lambda: w_ref[e, depth, MXU : 2 * MXU],
+        )
+
+    steps = [step(e, k) for e in range(experts) for k in range(units // MXU)]
+    for half, y in enumerate(paired_products(2 * rows, steps)):
+        columns = slice(half * MXU, (half + 1) * MXU)
+        own_ref[0, :, columns] = y[:rows].astype(jnp.bfloat16)
+        sib_ref[0, :, columns] = y[rows:].astype(jnp.bfloat16)
+
+
+def block_down(where, hidden, w_down, after):
     experts, tokens, units = hidden.shape
     rows, width = tokens // 2, w_down.shape[2] // 2
-    tile = tile_of(width, 512)
+    tile = 2 * MXU
     tiles = width // tile
     out_spec = pl.BlockSpec((1, rows, tile), lambda h, n, s: (h, 0, n))
     out = jax.ShapeDtypeStruct((2, rows, width), jnp.bfloat16)
@@ -128,17 +164,18 @@
                     (experts, units, tile),
                     lambda h, n, s: (0, 0, (h + s[0] - 2 * h * s[0]) * tiles + n),
                 ),
+                pl.BlockSpec(memory_space=pl.ANY),
             ],
             out_specs=[out_spec, out_spec],
         ),
         out_shape=[out, out],
-        compiler_params=pltpu.CompilerParams(vmem_limit_bytes=VMEM_LIMIT),
+        compiler_params=pltpu.CompilerParams(vmem_limit_bytes=BLOCK_VMEM_LIMIT),
         cost_estimate=pl.CostEstimate(
             flops=4 * experts * tokens * units * width,
             bytes_accessed=4 * (experts * units + tokens) * width,
             transcendentals=0,
         ),
-    )(where, hidden, w_down)
+    )(where, hidden, w_down, after)
 
 
 def total(*terms):
@@ -161,14 +198,19 @@
         lane.append(along(lane[-1]))
         sides.append(along(sides[-1]))
     crossed = [across(chunk) for chunk in lane]
-    hidden = []
-    for s in range(chips):
+    hidden, after = [None] * chips, where
+
+    def up_of(s, after):
         chunks = (lane[s], crossed[s], beside(lane[s]), beside(crossed[s]))
-        hidden.append(block_hidden(where, chunks, sides[s], w_gate, w_up))
-
-    travelling = None
+        hidden[s] = block_hidden(where, chunks, sides[s], w_gate, w_up, after)
+        return hidden[s]
+
+    after, travelling = up_of(0, where), None
     for s in list(range(1, chips)) + [0]:
-        own, sib = block_down(where, hidden[s], w_down)
+        if s:
+            after = up_of(s, after)
+        own, sib = block_down(where, hidden[s], w_down, after)
+        after = own
         back = beside(sib)
         swapped = across(total(own[1], back[1]))
         terms = (own[0], back[0], swapped)
@@ -330,7 +372,9 @@
     kv_cache = jnp.concatenate([keys, heads[:, KVH:]], 1).astype(jnp.bfloat16)
     kv_cache = kv_cache.reshape(1, 1, owner_cap, columns)
 
-    experts = ring_experts if pair and lax.axis_size("ep") % 2 == 0 else plain_experts
+    tiled = w_gate.shape[2] % MXU == 0 and stream.shape[1] % (2 * MXU) == 0
+    ringed = pair and tiled and lax.axis_size("ep") % 2 == 0
+    experts = ring_experts if ringed else plain_experts
     moe_out = experts(rows_out, side, w_gate, w_up, w_down)
     return (moe_out, kv_cache)
 

time: 206 us -> 225 us (1.092)
  local copies, waits for them, and re-layouts: 5.13 us -> 54.7 us
  Pallas kernels: 103 us -> 74.4 us
  waiting for transfers between devices: 52.6 us -> 45.2 us
  other arithmetic: 17.1 us -> 19.5 us
  starting transfers between devices: 21.6 us -> 23.9 us
    unnamed x47 -> x79, local copies, waits for them, and re-layouts: 2.91 us -> 51.7 us
    pallas_call x4, Pallas kernels: 43.4 us -> 27.2 us  [block_down(): pl.pallas_call(block_down_kernel, grid_spec=pltpu.PrefetchScalarGridSpec(...]
    ppermute x3, waiting for transfers between devices: 19.4 us -> 4.03 us  [ring_experts(): lane.append(along(lane[-1]))]
    pallas_call x4, Pallas kernels: 58 us -> 45.3 us  [block_hidden(): pl.pallas_call(block_hidden_kernel, grid_spec=pltpu.PrefetchScalarGridSpe...]
    ppermute x1, waiting for transfers between devices: 0.01 us -> 3.97 us  [per_device(): small = small + lax.ppermute(small, 'tp', [(0, 1), (1, 0)])]
    ppermute x3, waiting for transfers between devices: 13.5 us -> 17.1 us  [ring_experts(): along(travelling)]
    ppermute x3, waiting for transfers between devices: 8.54 us -> 11 us  [ring_experts(): sides.append(along(sides[-1]))]
    ppermute x4, waiting for transfers between devices: 11.2 us -> 8.9 us  [ring_experts(): swapped = across(total(own[1], back[1]))]
  transfers between devices with their start and end apart: 32 -> 32, of which waited for: 7 -> 9; matrix products, arithmetic and copies ran while one was open for 10% -> 11% of each run, Pallas kernels for 49% -> 32%
where the time goes in v3:
time: 225 us; the launch traced here: 224 us
  Pallas kernels  74.4 us (33%)
  local copies, waits for them, and re-layouts  54.7 us (24%)
  waiting for transfers between devices  45.2 us (20%)
  starting transfers between devices  23.9 us (11%)
  other arithmetic  19.5 us (9%)
  matrix products  4.77 us (2%)
    unnamed x79, local copies, waits for them, and re-layouts  51.7 us
    pallas_call x4, Pallas kernels, block_hidden(): pl.pallas_call(block_hidden_kernel, grid_spec=pltpu.PrefetchScalarGridSpe...  45.3 us
    pallas_call x4, Pallas kernels, block_down(): pl.pallas_call(block_down_kernel, grid_spec=pltpu.PrefetchScalarGridSpec(...  27.2 us
    ppermute x3, waiting for transfers between devices, ring_experts(): along(travelling)  17.1 us
    ppermute x3, waiting for transfers between devices, ring_experts(): sides.append(along(sides[-1]))  11 us
    convert_element_type x8, other arithmetic, total(): sum((term.astype(jnp.float32) for term in terms)).astype(jnp.bfloat16)  10.8 us
    ppermute x4, waiting for transfers between devices, ring_experts(): swapped = across(total(own[1], back[1]))  8.9 us
    ppermute x3, starting transfers between devices, ring_experts(): along(travelling)  6.5 us
  transfers between devices with their start and end apart: 32, of which 9 were waited for; matrix products, arithmetic and copies ran while one was open for 11% of the time, Pallas kernels for 32%

profile of v3, /device:TPU:0, one launch (start us, length us, event | category | flops | bytes accessed | tf_op | source)
XLA Modules:
  0.0 223.6 jit_solution(9362820221714146830)
XLA Ops:
  0.6 1.3 broadcast_in_dim.33.gain_ref
  2.0 1.9 shard_map.131.own_ref
  3.9 2.9 %collective-permute-start.7 = (bf16[128,2048]{1,0:T(8,128)(2,1)}, bf16[128,2048]{1,0:T(8,128)(2,1)S(1)}, u32[]{:S(2)}, u32[]{:S(2)}) collective-permute-start(bf16[128,2048]{1,0:T(8,128)(2,1)} %shard_map.131.own_ref), channel_id=1, source_target_pairs={{0,1},{1,0},{2,3},{3,2},{4,5},{5,4},{6,7},{7,6},{8,9},{9,8},{10,11... | collective-permute-start | bytes 1572872 | tf_op jit(solution)/shard_map/ppermute | solution.py:200
  6.8 1.6 collective-permute-start
  8.4 1.2 multiply_reduce_fusion
  9.6 1.3 convolution_bitcast_fusion
  10.9 1.2 fusion.1
  15.3 4.0 %collective-permute-done.4 = f32[18,128]{1,0:T(8,128)S(1)} collective-permute-done((f32[18,128]{1,0:T(8,128)S(1)}, f32[18,128]{1,0:T(8,128)S(1)}, u32[]{:S(2)}, u32[]{:S(2)}) %collective-permute-start.4) | collective-permute-done | bytes 9248 | tf_op jit(solution)/shard_map/ppermute | solution.py:332
  19.3 4.0 %collective-permute-done.own_ref = bf16[128,2048]{1,0:T(8,128)(2,1)} collective-permute-done((bf16[128,2048]{1,0:T(8,128)(2,1)}, bf16[128,2048]{1,0:T(8,128)(2,1)}, u32[]{:S(2)}, u32[]{:S(2)}) %collective-permute-start) | collective-permute-done | bytes 524320 | tf_op jit(solution)/shard_map/ppermute | solution.py:198
  26.1 1.3 collective-permute-start.6
  28.9 11.0 %collective-permute-done.6.side_ref = f32[24,256]{1,0:T(8,128)S(1)} collective-permute-done((f32[24,256]{1,0:T(8,128)S(1)}, f32[24,256]{1,0:T(8,128)S(1)}, u32[]{:S(2)}, u32[]{:S(2)}) %collective-permute-start.6) | collective-permute-done | bytes 24608 | tf_op jit(solution)/shard_map/ppermute | solution.py:199
  40.7 1.4 collective-permute-start.14
  43.1 4.6 %copy-done.2 = bf16[2,4096,768]{2,1,0:T(8,128)(2,1)S(1)} copy-done((bf16[2,4096,768]{2,1,0:T(8,128)(2,1)S(1)}, bf16[2,4096,768]{2,1,0:T(8,128)(2,1)}, u32[]{:S(2)}) %copy-start.2) | copy-done | bytes 12582936
  47.7 4.6 %copy-done.5 = bf16[2,4096,768]{2,1,0:T(8,128)(2,1)S(1)} copy-done((bf16[2,4096,768]{2,1,0:T(8,128)(2,1)S(1)}, bf16[2,4096,768]{2,1,0:T(8,128)(2,1)}, u32[]{:S(2)}) %copy-start.5) | copy-done | bytes 12582936
  56.4 10.3 %shard_map.132._.h_ref = bf16[2,256,768]{2,1,0:T(8,128)(2,1)S(1)} custom-call(s32[2]{0:T(128)S(1)} %pad_add_fusion.where_ref._, bf16[128,2048]{1,0:T(8,128)(2,1)S(1)} %copy-done.15, bf16[128,2048]{1,0:T(8,128)(2,1)S(1)} %copy-done.24, bf16[128,2048]{1,0:T(8,128)(2,1)S(1)} %copy-done.26, bf16[128,2048]{1,0:T(8,128)(2,1)S(1)} %copy-done.28, ...), custom_call_target="tpu_custom_call" | custom-call | flops 6442450944 | bytes 27262976 | tf_op jit(solution)/shard_map/pallas_call | solution.py:106
  69.6 4.6 %copy-done.6 = bf16[2,4096,768]{2,1,0:T(8,128)(2,1)S(1)} copy-done((bf16[2,4096,768]{2,1,0:T(8,128)(2,1)S(1)}, bf16[2,4096,768]{2,1,0:T(8,128)(2,1)}, u32[]{:S(2)}) %copy-start.6) | copy-done | bytes 12582936
  74.1 1.1 copy-done.13
  76.3 11.4 %shard_map.133.h_ref._ = bf16[2,256,768]{2,1,0:T(8,128)(2,1)S(1)} custom-call(s32[2]{0:T(128)S(1)} %pad_add_fusion.where_ref._, bf16[128,2048]{1,0:T(8,128)(2,1)} %collective-permute-done.own_ref, bf16[128,2048]{1,0:T(8,128)(2,1)} %collective-permute-done.1.other_ref, bf16[128,2048]{1,0:T(8,128)(2,1)S(1)} %copy-done.22, ...), custom_call_target="tpu_custom_call" | custom-call | flops 6442450944 | bytes 27262976 | tf_op jit(solution)/shard_map/pallas_call | solution.py:106
  87.7 4.6 %copy-done.9 = bf16[2,768,4096]{2,1,0:T(8,128)(2,1)S(1)} copy-done((bf16[2,768,4096]{2,1,0:T(8,128)(2,1)S(1)}, bf16[2,768,4096]{2,1,0:T(8,128)(2,1)}, u32[]{:S(2)}) %copy-start.9) | copy-done | bytes 12582936
  92.3 7.1 %shard_map.134 = (bf16[2,128,2048]{2,1,0:T(8,128)(2,1)S(1)}, bf16[2,128,2048]{2,1,0:T(8,128)(2,1)}) custom-call(s32[2]{0:T(128)S(1)} %pad_add_fusion.where_ref._, bf16[2,256,768]{2,1,0:T(8,128)(2,1)S(1)} %shard_map.133.h_ref._, bf16[2,768,4096]{2,1,0:T(8,128)(2,1)S(1)} %copy-done.9, bf16[2,256,768]{2,1,0:T(8,128)(2,1)S(1)} %shard_map.133.h_ref._), custom_call_target="tpu_custom_call" | custom-call | flops 3221225472 | bytes 14680064 | tf_op jit(solution)/shard_map/pallas_call | solution.py:156
  99.4 3.5 %convolution_convert_fusion = bf16[256,1024]{1,0:T(8,128)(2,1)S(1)} fusion(bf16[2048,1024]{1,0:T(8,128)(2,1)} %param.19, bf16[128,2048]{1,0:T(8,128)(2,1)S(1)} %copy-done.29, f32[2048]{0:T(1024)S(1)} %convert_element_type.219, f32[128]{0:T(128)S(1)} %get-tuple-element.18, s32[128]{0:T(128)S(1)} %fusion.25), kind=kOutput, calls=%fused_computation.2 | convolution fusion | flops 605323264 | bytes 5252096 | tf_op jit(solution)/shard_map/dot_general | solution.py:358
  103.7 1.4 collective-permute-start.31
  106.4 4.6 %copy-done.4 = bf16[2,4096,768]{2,1,0:T(8,128)(2,1)S(1)} copy-done((bf16[2,4096,768]{2,1,0:T(8,128)(2,1)S(1)}, bf16[2,4096,768]{2,1,0:T(8,128)(2,1)}, u32[]{:S(2)}) %copy-start.4) | copy-done | bytes 12582936
  111.0 4.6 %copy-done.7 = bf16[2,4096,768]{2,1,0:T(8,128)(2,1)S(1)} copy-done((bf16[2,4096,768]{2,1,0:T(8,128)(2,1)S(1)}, bf16[2,4096,768]{2,1,0:T(8,128)(2,1)}, u32[]{:S(2)}) %copy-start.7) | copy-done | bytes 12582936
  115.6 12.0 %shard_map.135.h_ref._ = bf16[2,256,768]{2,1,0:T(8,128)(2,1)S(1)} custom-call(s32[2]{0:T(128)S(1)} %pad_add_fusion.where_ref._, bf16[128,2048]{1,0:T(8,128)(2,1)} %collective-permute-done.13.own_ref, bf16[128,2048]{1,0:T(8,128)(2,1)} %collective-permute-done.14.other_ref, bf16[128,2048]{1,0:T(8,128)(2,1)} %collective-permute-done.15.sib_own_ref, ...), custom_call_target="tpu_custom_call" | custom-call | flops 6442450944 | bytes 27262976 | tf_op jit(solution)/shard_map/pallas_call | solution.py:106
  127.6 4.6 %copy-done.10 = bf16[2,768,4096]{2,1,0:T(8,128)(2,1)S(1)} copy-done((bf16[2,768,4096]{2,1,0:T(8,128)(2,1)S(1)}, bf16[2,768,4096]{2,1,0:T(8,128)(2,1)}, u32[]{:S(2)}) %copy-start.10) | copy-done | bytes 12582936
  132.2 7.1 %shard_map.136 = (bf16[2,128,2048]{2,1,0:T(8,128)(2,1)S(1)}, bf16[2,128,2048]{2,1,0:T(8,128)(2,1)}) custom-call(s32[2]{0:T(128)S(1)} %pad_add_fusion.where_ref._, bf16[2,256,768]{2,1,0:T(8,128)(2,1)S(1)} %shard_map.135.h_ref._, bf16[2,768,4096]{2,1,0:T(8,128)(2,1)S(1)} %copy-done.10, bf16[2,256,768]{2,1,0:T(8,128)(2,1)S(1)} %shard_map.135.h_ref._), custom_call_target="tpu_custom_call" | custom-call | flops 3221225472 | bytes 14680064 | tf_op jit(solution)/shard_map/pallas_call | solution.py:156
  139.3 2.3 %fusion.10 = bf16[128,2048]{1,0:T(8,128)(2,1)} fusion(bf16[2,128,2048]{2,1,0:T(8,128)(2,1)} %collective-permute-done.10, bf16[2,128,2048]{2,1,0:T(8,128)(2,1)S(1)} %copy-done.19), kind=kLoop, calls=%fused_computation.27 | loop fusion | flops 1048576 | bytes 1572864 | tf_op jit(solution)/shard_map/convert_element_type | solution.py:182
  142.2 4.6 %copy-done.8 = bf16[2,4096,768]{2,1,0:T(8,128)(2,1)S(1)} copy-done((bf16[2,4096,768]{2,1,0:T(8,128)(2,1)S(1)}, bf16[2,4096,768]{2,1,0:T(8,128)(2,1)}, u32[]{:S(2)}) %copy-start.8) | copy-done | bytes 12582936
  146.8 11.6 %shard_map.137.h_ref._ = bf16[2,256,768]{2,1,0:T(8,128)(2,1)S(1)} custom-call(s32[2]{0:T(128)S(1)} %pad_add_fusion.where_ref._, bf16[128,2048]{1,0:T(8,128)(2,1)} %collective-permute-done.21.own_ref, bf16[128,2048]{1,0:T(8,128)(2,1)} %collective-permute-done.22.other_ref, bf16[128,2048]{1,0:T(8,128)(2,1)S(1)} %collective-permute-done.23.sib_own_ref, ...), custom_call_target="tpu_custom_call" | custom-call | flops 6442450944 | bytes 27262976 | tf_op jit(solution)/shard_map/pallas_call | solution.py:106
  158.4 4.6 %copy-done.11 = bf16[2,768,4096]{2,1,0:T(8,128)(2,1)S(1)} copy-done((bf16[2,768,4096]{2,1,0:T(8,128)(2,1)S(1)}, bf16[2,768,4096]{2,1,0:T(8,128)(2,1)}, u32[]{:S(2)}) %copy-start.11) | copy-done | bytes 12582936
  163.0 6.5 %shard_map.138 = (bf16[2,128,2048]{2,1,0:T(8,128)(2,1)S(1)}, bf16[2,128,2048]{2,1,0:T(8,128)(2,1)S(1)}) custom-call(s32[2]{0:T(128)S(1)} %pad_add_fusion.where_ref._, bf16[2,256,768]{2,1,0:T(8,128)(2,1)S(1)} %shard_map.137.h_ref._, bf16[2,768,4096]{2,1,0:T(8,128)(2,1)S(1)} %copy-done.11, bf16[2,256,768]{2,1,0:T(8,128)(2,1)S(1)} %shard_map.137.h_ref._), custom_call_target="tpu_custom_call" | custom-call | flops 3221225472 | bytes 14680064 | tf_op jit(solution)/shard_map/pallas_call | solution.py:156
  169.6 1.2 fusion.11
  170.9 1.6 collective-permute-start.19
  172.4 1.5 fusion.9
  173.9 4.0 %collective-permute-start.12 = (bf16[128,2048]{1,0:T(8,128)(2,1)S(1)}, bf16[128,2048]{1,0:T(8,128)(2,1)S(1)}, u32[]{:S(2)}, u32[]{:S(2)}) collective-permute-start(bf16[128,2048]{1,0:T(8,128)(2,1)S(1)} %fusion.9), channel_id=1, source_target_pairs={{0,4},{2,6},{4,8},{6,10},{8,12},{10,14},{12,0},{14,2},{1,5},{3,7},... | collective-permute-start | bytes 1572872 | tf_op jit(solution)/shard_map/ppermute | solution.py:217
  179.1 6.5 %shard_map.139 = (bf16[2,128,2048]{2,1,0:T(8,128)(2,1)S(1)}, bf16[2,128,2048]{2,1,0:T(8,128)(2,1)S(1)}) custom-call(s32[2]{0:T(128)S(1)} %pad_add_fusion.where_ref._, bf16[2,256,768]{2,1,0:T(8,128)(2,1)S(1)} %copy-done.14, bf16[2,768,4096]{2,1,0:T(8,128)(2,1)S(1)} %bitcast.57, bf16[2,128,2048]{2,1,0:T(8,128)(2,1)S(1)} %get-tuple-element.14._), custom_call_target="tpu_custom_call" | custom-call | flops 3221225472 | bytes 14680064 | tf_op jit(solution)/shard_map/pallas_call | solution.py:156
  185.7 4.0 %collective-permute-done.12 = bf16[128,2048]{1,0:T(8,128)(2,1)S(1)} collective-permute-done((bf16[128,2048]{1,0:T(8,128)(2,1)S(1)}, bf16[128,2048]{1,0:T(8,128)(2,1)S(1)}, u32[]{:S(2)}, u32[]{:S(2)}) %collective-permute-start.12) | collective-permute-done | bytes 524320 | tf_op jit(solution)/shard_map/ppermute | solution.py:217
  189.7 1.4 fusion.8
  191.1 2.2 collective-permute-start.20
  194.4 1.1 fusion.13
  195.5 1.4 collective-permute-start.30
  196.9 9.2 %collective-permute-done.20 = bf16[128,2048]{1,0:T(8,128)(2,1)S(1)} collective-permute-done((bf16[128,2048]{1,0:T(8,128)(2,1)S(1)}, bf16[128,2048]{1,0:T(8,128)(2,1)S(1)}, u32[]{:S(2)}, u32[]{:S(2)}) %collective-permute-start.20) | collective-permute-done | bytes 524320 | tf_op jit(solution)/shard_map/ppermute | solution.py:217
  206.1 2.3 %collective-permute-done.27 = bf16[128,2048]{1,0:T(8,128)(2,1)S(1)} collective-permute-done((bf16[128,2048]{1,0:T(8,128)(2,1)S(1)}, bf16[128,2048]{1,0:T(8,128)(2,1)S(1)}, u32[]{:S(2)}, u32[]{:S(2)}) %collective-permute-start.27) | collective-permute-done | bytes 524320 | tf_op jit(solution)/shard_map/ppermute | solution.py:215
  208.4 1.1 fusion.6
  211.0 6.6 %collective-permute-done.30 = bf16[128,2048]{1,0:T(8,128)(2,1)S(1)} collective-permute-done((bf16[128,2048]{1,0:T(8,128)(2,1)}, bf16[128,2048]{1,0:T(8,128)(2,1)S(1)}, u32[]{:S(2)}, u32[]{:S(2)}) %collective-permute-start.30) | collective-permute-done | bytes 524320 | tf_op jit(solution)/shard_map/ppermute | solution.py:215
  217.6 3.9 %collective-permute-done.28 = bf16[128,2048]{1,0:T(8,128)(2,1)S(1)} collective-permute-done((bf16[128,2048]{1,0:T(8,128)(2,1)}, bf16[128,2048]{1,0:T(8,128)(2,1)S(1)}, u32[]{:S(2)}, u32[]{:S(2)}) %collective-permute-start.28) | collective-permute-done | bytes 524320 | tf_op jit(solution)/shard_map/ppermute | solution.py:217
  221.5 2.2 fusion.4
  (144 shorter events, 23.9 us)
Async XLA Ops:
  0.6 9.0 %copy-start = (bf16[2048,16]{0,1:T(8,128)(2,1)S(1)}, bf16[2048,16]{0,1:T(8,128)(2,1)}, u32[]{:S(2)}) copy-start(bf16[2048,16]{0,1:T(8,128)(2,1)} %param.20) | copy-start | bytes 196612
  3.9 20.0 %collective-permute-start.7 = (bf16[128,2048]{1,0:T(8,128)(2,1)}, bf16[128,2048]{1,0:T(8,128)(2,1)S(1)}, u32[]{:S(2)}, u32[]{:S(2)}) collective-permute-start(bf16[128,2048]{1,0:T(8,128)(2,1)} %shard_map.131.own_ref), channel_id=1, source_target_pairs={{0,1},{1,0},{2,3},{3,2},{4,5},{5,4},{6,7},{7,6},{8,9},{9,8},{10,11... | collective-permute-start | bytes 1572872 | tf_op jit(solution)/shard_map/ppermute | solution.py:200
  6.8 33.0 %collective-permute-start.8 = (bf16[128,2048]{1,0:T(8,128)(2,1)}, bf16[128,2048]{1,0:T(8,128)(2,1)S(1)}, u32[]{:S(2)}, u32[]{:S(2)}) collective-permute-start(bf16[128,2048]{1,0:T(8,128)(2,1)} %shard_map.131.own_ref), channel_id=1, source_target_pairs={{0,2},{2,0},{4,6},{6,4},{8,10},{10,8},{12,14},{14,12},{1,3},{3,1},... | collective-permute-start | bytes 1572872 | tf_op jit(solution)/shard_map/ppermute | solution.py:204
  6.8 16.5 %collective-permute-start = (bf16[128,2048]{1,0:T(8,128)(2,1)}, bf16[128,2048]{1,0:T(8,128)(2,1)}, u32[]{:S(2)}, u32[]{:S(2)}) collective-permute-start(bf16[128,2048]{1,0:T(8,128)(2,1)} %shard_map.131.own_ref), channel_id=1, source_target_pairs={{0,4},{2,6},{4,8},{6,10},{8,12},{10,14},{12,0},{14,2},{1,5},{3,7},... | collective-permute-start | bytes 1572872 | tf_op jit(solution)/shard_map/ppermute | solution.py:198
  12.2 7.0 %collective-permute-start.4 = (f32[18,128]{1,0:T(8,128)S(1)}, f32[18,128]{1,0:T(8,128)S(1)}, u32[]{:S(2)}, u32[]{:S(2)}) collective-permute-start(f32[18,128]{1,0:T(8,128)S(1)} %pad_maximum_fusion.2), channel_id=1, source_target_pairs={{0,1},{1,0},{2,3},{3,2},{4,5},{5,4},{6,7},{7,6},{8,9},{9,8},{10,11... | collective-permute-start | bytes 27656 | tf_op jit(solution)/shard_map/ppermute | solution.py:332
  23.4 19.5 %collective-permute-start.1 = (bf16[128,2048]{1,0:T(8,128)(2,1)}, bf16[128,2048]{1,0:T(8,128)(2,1)}, u32[]{:S(2)}, u32[]{:S(2)}) collective-permute-start(bf16[128,2048]{1,0:T(8,128)(2,1)} %collective-permute-done.own_ref), channel_id=1, source_target_pairs={{0,1},{1,0},{2,3},{3,2},{4,5},{5,4},{6,7},{7,6},{8,9},{9,8},{10,11... | collective-permute-start | bytes 1572872 | tf_op jit(solution)/shard_map/ppermute | solution.py:200
  23.9 16.8 %collective-permute-start.13 = (bf16[128,2048]{1,0:T(8,128)(2,1)}, bf16[128,2048]{1,0:T(8,128)(2,1)}, u32[]{:S(2)}, u32[]{:S(2)}) collective-permute-start(bf16[128,2048]{1,0:T(8,128)(2,1)} %collective-permute-done.own_ref), channel_id=1, source_target_pairs={{0,4},{2,6},{4,8},{6,10},{8,12},{10,14},{12,0},{14,2},{1,5},{3,7},... | collective-permute-start | bytes 1572872 | tf_op jit(solution)/shard_map/ppermute | solution.py:198
  23.9 18.2 %collective-permute-start.9 = (bf16[128,2048]{1,0:T(8,128)(2,1)S(1)}, bf16[128,2048]{1,0:T(8,128)(2,1)S(1)}, u32[]{:S(2)}, u32[]{:S(2)}) collective-permute-start(bf16[128,2048]{1,0:T(8,128)(2,1)S(1)} %collective-permute-done.7.other_ref), channel_id=1, source_target_pairs={{0,2},{2,0},{4,6},{6,4},{8,10},{10,8},{12,14},{14,12},{1,3},{3,1},... | collective-permute-start | bytes 1572872 | tf_op jit(solution)/shard_map/ppermute | solution.py:204
  24.7 1.4 collective-permute-start.5
  26.1 13.7 %collective-permute-start.6 = (f32[24,256]{1,0:T(8,128)S(1)}, f32[24,256]{1,0:T(8,128)S(1)}, u32[]{:S(2)}, u32[]{:S(2)}) collective-permute-start(f32[24,256]{1,0:T(8,128)S(1)} %pad_maximum_fusion.1.side_ref), channel_id=1, source_target_pairs={{0,4},{2,6},{4,8},{6,10},{8,12},{10,14},{12,0},{14,2},{1,5},{3,7},... | collective-permute-start | bytes 73736 | tf_op jit(solution)/shard_map/ppermute | solution.py:199
  39.9 63.8 %collective-permute-start.17 = (f32[24,256]{1,0:T(8,128)S(1)}, f32[24,256]{1,0:T(8,128)S(1)}, u32[]{:S(2)}, u32[]{:S(2)}) collective-permute-start(f32[24,256]{1,0:T(8,128)S(1)} %collective-permute-done.6.side_ref), channel_id=1, source_target_pairs={{0,4},{2,6},{4,8},{6,10},{8,12},{10,14},{12,0},{14,2},{1,5},{3,7},... | collective-permute-start | bytes 73736 | tf_op jit(solution)/shard_map/ppermute | solution.py:199
  40.7 27.0 %collective-permute-start.2 = (bf16[128,2048]{1,0:T(8,128)(2,1)}, bf16[128,2048]{1,0:T(8,128)(2,1)S(1)}, u32[]{:S(2)}, u32[]{:S(2)}) collective-permute-start(bf16[128,2048]{1,0:T(8,128)(2,1)} %collective-permute-done.own_ref), channel_id=1, source_target_pairs={{0,2},{2,0},{4,6},{6,4},{8,10},{10,8},{12,14},{14,12},{1,3},{3,1},... | collective-permute-start | bytes 1572872 | tf_op jit(solution)/shard_map/ppermute | solution.py:204
  40.7 28.0 %collective-permute-start.14 = (bf16[128,2048]{1,0:T(8,128)(2,1)}, bf16[128,2048]{1,0:T(8,128)(2,1)}, u32[]{:S(2)}, u32[]{:S(2)}) collective-permute-start(bf16[128,2048]{1,0:T(8,128)(2,1)} %collective-permute-done.13.own_ref), channel_id=1, source_target_pairs={{0,1},{1,0},{2,3},{3,2},{4,5},{5,4},{6,7},{7,6},{8,9},{9,8},{10,11... | collective-permute-start | bytes 1572872 | tf_op jit(solution)/shard_map/ppermute | solution.py:200
  42.9 26.1 %collective-permute-start.21 = (bf16[128,2048]{1,0:T(8,128)(2,1)}, bf16[128,2048]{1,0:T(8,128)(2,1)}, u32[]{:S(2)}, u32[]{:S(2)}) collective-permute-start(bf16[128,2048]{1,0:T(8,128)(2,1)} %collective-permute-done.13.own_ref), channel_id=1, source_target_pairs={{0,4},{2,6},{4,8},{6,10},{8,12},{10,14},{12,0},{14,2},{1,5},{3,7},... | collective-permute-start | bytes 1572872 | tf_op jit(solution)/shard_map/ppermute | solution.py:198
  42.9 26.7 %collective-permute-start.3 = (bf16[128,2048]{1,0:T(8,128)(2,1)}, bf16[128,2048]{1,0:T(8,128)(2,1)}, u32[]{:S(2)}, u32[]{:S(2)}) collective-permute-start(bf16[128,2048]{1,0:T(8,128)(2,1)} %collective-permute-done.1.other_ref), channel_id=1, source_target_pairs={{0,2},{2,0},{4,6},{6,4},{8,10},{10,8},{12,14},{14,12},{1,3},{3,1},... | collective-permute-start | bytes 1572872 | tf_op jit(solution)/shard_map/ppermute | solution.py:204
  56.4 13.1 %copy-start.3 = (bf16[2,4096,768]{2,1,0:T(8,128)(2,1)S(1)}, bf16[2,4096,768]{2,1,0:T(8,128)(2,1)}, u32[]{:S(2)}) copy-start(bf16[2,4096,768]{2,1,0:T(8,128)(2,1)} %wg_ref.7) | copy-start | bytes 37748740
  68.4 36.7 %collective-permute-start.15 = (bf16[128,2048]{1,0:T(8,128)(2,1)}, bf16[128,2048]{1,0:T(8,128)(2,1)}, u32[]{:S(2)}, u32[]{:S(2)}) collective-permute-start(bf16[128,2048]{1,0:T(8,128)(2,1)} %collective-permute-done.13.own_ref), channel_id=1, source_target_pairs={{0,2},{2,0},{4,6},{6,4},{8,10},{10,8},{12,14},{14,12},{1,3},{3,1},... | collective-permute-start | bytes 1572872 | tf_op jit(solution)/shard_map/ppermute | solution.py:204
  68.7 37.2 %collective-permute-start.16 = (bf16[128,2048]{1,0:T(8,128)(2,1)}, bf16[128,2048]{1,0:T(8,128)(2,1)}, u32[]{:S(2)}, u32[]{:S(2)}) collective-permute-start(bf16[128,2048]{1,0:T(8,128)(2,1)} %collective-permute-done.14.other_ref), channel_id=1, source_target_pairs={{0,2},{2,0},{4,6},{6,4},{8,10},{10,8},{12,14},{14,12},{1,3},{3,1},... | collective-permute-start | bytes 1572872 | tf_op jit(solution)/shard_map/ppermute | solution.py:204
  68.9 37.0 %collective-permute-start.22 = (bf16[128,2048]{1,0:T(8,128)(2,1)}, bf16[128,2048]{1,0:T(8,128)(2,1)}, u32[]{:S(2)}, u32[]{:S(2)}) collective-permute-start(bf16[128,2048]{1,0:T(8,128)(2,1)} %collective-permute-done.21.own_ref), channel_id=1, source_target_pairs={{0,1},{1,0},{2,3},{3,2},{4,5},{5,4},{6,7},{7,6},{8,9},{9,8},{10,11... | collective-permute-start | bytes 1572872 | tf_op jit(solution)/shard_map/ppermute | solution.py:200
  99.4 39.9 %collective-permute-start.10 = (bf16[2,128,2048]{2,1,0:T(8,128)(2,1)}, bf16[2,128,2048]{2,1,0:T(8,128)(2,1)}, u32[]{:S(2)}, u32[]{:S(2)}) collective-permute-start(bf16[2,128,2048]{2,1,0:T(8,128)(2,1)} %get-tuple-element.11), channel_id=1, source_target_pairs={{0,2},{2,0},{4,6},{6,4},{8,10},{10,8},{12,14},{14,12},{1,3},{3,1},... | collective-permute-start | bytes 3145736 | tf_op jit(solution)/shard_map/ppermute | solution.py:214
  103.7 74.2 %collective-permute-start.31 = (bf16[128,1024]{1,0:T(8,128)(2,1)}, bf16[128,1024]{1,0:T(8,128)(2,1)}, u32[]{:S(2)}, u32[]{:S(2)}) collective-permute-start(bf16[128,1024]{1,0:T(8,128)(2,1)} %slice.107), channel_id=1, source_target_pairs={{0,1},{1,0},{2,3},{3,2},{4,5},{5,4},{6,7},{7,6},{8,9},{9,8},{10,11... | collective-permute-start | bytes 786440 | tf_op jit(solution)/shard_map/ppermute | solution.py:363
  105.1 36.5 %collective-permute-start.25 = (f32[24,256]{1,0:T(8,128)S(1)}, f32[24,256]{1,0:T(8,128)S(1)}, u32[]{:S(2)}, u32[]{:S(2)}) collective-permute-start(f32[24,256]{1,0:T(8,128)S(1)} %collective-permute-done.17.side_ref), channel_id=1, source_target_pairs={{0,4},{2,6},{4,8},{6,10},{8,12},{10,14},{12,0},{14,2},{1,5},{3,7},... | collective-permute-start | bytes 73736 | tf_op jit(solution)/shard_map/ppermute | solution.py:199
  105.9 36.2 %collective-permute-start.23 = (bf16[128,2048]{1,0:T(8,128)(2,1)}, bf16[128,2048]{1,0:T(8,128)(2,1)S(1)}, u32[]{:S(2)}, u32[]{:S(2)}) collective-permute-start(bf16[128,2048]{1,0:T(8,128)(2,1)} %collective-permute-done.21.own_ref), channel_id=1, source_target_pairs={{0,2},{2,0},{4,6},{6,4},{8,10},{10,8},{12,14},{14,12},{1,3},{3,1},... | collective-permute-start | bytes 1572872 | tf_op jit(solution)/shard_map/ppermute | solution.py:204
  105.9 36.2 %collective-permute-start.24 = (bf16[128,2048]{1,0:T(8,128)(2,1)}, bf16[128,2048]{1,0:T(8,128)(2,1)S(1)}, u32[]{:S(2)}, u32[]{:S(2)}) collective-permute-start(bf16[128,2048]{1,0:T(8,128)(2,1)} %collective-permute-done.22.other_ref), channel_id=1, source_target_pairs={{0,2},{2,0},{4,6},{6,4},{8,10},{10,8},{12,14},{14,12},{1,3},{3,1},... | collective-permute-start | bytes 1572872 | tf_op jit(solution)/shard_map/ppermute | solution.py:204
  115.6 26.6 %slice-start = ((s8[12582912]{0:T(1024)(128)(4,1)}), s8[4194304]{0:T(1024)(128)(4,1)S(1)}, s32[]{:S(2)}) async-start(s8[12582912]{0:T(1024)(128)(4,1)} %bitcast.54), calls=%async_computation | async-start | bytes 8388608
  115.6 26.6 %slice-start.1 = ((s8[12582912]{0:T(1024)(128)(4,1)}), s8[4194304]{0:T(1024)(128)(4,1)S(1)}, s32[]{:S(2)}) async-start(s8[12582912]{0:T(1024)(128)(4,1)} %bitcast.54), calls=%async_computation.1 | async-start | bytes 8388608
  132.2 7.2 %copy-start.19 = (bf16[2,128,2048]{2,1,0:T(8,128)(2,1)S(1)}, bf16[2,128,2048]{2,1,0:T(8,128)(2,1)}, u32[]{:S(2)}) copy-start(bf16[2,128,2048]{2,1,0:T(8,128)(2,1)} %copy-done.18) | copy-start | bytes 3145732
  132.2 10.0 %slice-start.2 = ((s8[12582912]{0:T(1024)(128)(4,1)}), s8[4194304]{0:T(1024)(128)(4,1)S(1)}, s32[]{:S(2)}) async-start(s8[12582912]{0:T(1024)(128)(4,1)} %bitcast.54), calls=%async_computation.2 | async-start | bytes 8388608
  139.3 30.4 %copy-start.16 = (bf16[2,128,2048]{2,1,0:T(8,128)(2,1)}, bf16[2,128,2048]{2,1,0:T(8,128)(2,1)S(1)}, u32[]{:S(2)}) copy-start(bf16[2,128,2048]{2,1,0:T(8,128)(2,1)S(1)} %get-tuple-element.12._) | copy-start | bytes 3145732
  139.3 30.3 %collective-permute-start.18 = (bf16[2,128,2048]{2,1,0:T(8,128)(2,1)}, bf16[2,128,2048]{2,1,0:T(8,128)(2,1)}, u32[]{:S(2)}, u32[]{:S(2)}) collective-permute-start(bf16[2,128,2048]{2,1,0:T(8,128)(2,1)} %get-tuple-element.13), channel_id=1, source_target_pairs={{0,2},{2,0},{4,6},{6,4},{8,10},{10,8},{12,14},{14,12},{1,3},{3,1},... | collective-permute-start | bytes 3145736 | tf_op jit(solution)/shard_map/ppermute | solution.py:214
  141.6 30.8 %collective-permute-start.11 = (bf16[128,2048]{1,0:T(8,128)(2,1)}, bf16[128,2048]{1,0:T(8,128)(2,1)}, u32[]{:S(2)}, u32[]{:S(2)}) collective-permute-start(bf16[128,2048]{1,0:T(8,128)(2,1)} %fusion.10), channel_id=1, source_target_pairs={{0,1},{1,0},{2,3},{3,2},{4,5},{5,4},{6,7},{7,6},{8,9},{9,8},{10,11... | collective-permute-start | bytes 1572872 | tf_op jit(solution)/shard_map/ppermute | solution.py:215
  146.8 32.2 %slice-start.3 = ((s8[12582912]{0:T(1024)(128)(4,1)}), s8[4194304]{0:T(1024)(128)(4,1)S(1)}, s32[]{:S(2)}) async-start(s8[12582912]{0:T(1024)(128)(4,1)} %bitcast.56), calls=%async_computation.3 | async-start | bytes 8388608
  146.8 32.2 %slice-start.4 = ((s8[12582912]{0:T(1024)(128)(4,1)}), s8[4194304]{0:T(1024)(128)(4,1)S(1)}, s32[]{:S(2)}) async-start(s8[12582912]{0:T(1024)(128)(4,1)} %bitcast.56), calls=%async_computation.4 | async-start | bytes 8388608
  163.0 9.4 %copy-start.20 = (bf16[2,128,2048]{2,1,0:T(8,128)(2,1)S(1)}, bf16[2,128,2048]{2,1,0:T(8,128)(2,1)}, u32[]{:S(2)}) copy-start(bf16[2,128,2048]{2,1,0:T(8,128)(2,1)} %copy-done.18) | copy-start | bytes 3145732
  163.0 14.9 %copy-start.31 = (bf16[256,1024]{1,0:T(8,128)(2,1)S(1)}, bf16[256,1024]{1,0:T(8,128)(2,1)}, u32[]{:S(2)}) copy-start(bf16[256,1024]{1,0:T(8,128)(2,1)} %copy-done.30) | copy-start | bytes 1572868
  163.0 16.0 %slice-start.5 = ((s8[12582912]{0:T(1024)(128)(4,1)}), s8[4194304]{0:T(1024)(128)(4,1)S(1)}, s32[]{:S(2)}) async-start(s8[12582912]{0:T(1024)(128)(4,1)} %bitcast.56), calls=%async_computation.5 | async-start | bytes 8388608
  169.5 9.5 %copy-start.14 = (bf16[2,256,768]{2,1,0:T(8,128)(2,1)S(1)}, bf16[2,256,768]{2,1,0:T(8,128)(2,1)}, u32[]{:S(2)}) copy-start(bf16[2,256,768]{2,1,0:T(8,128)(2,1)} %copy-done.12) | copy-start | bytes 2359300
  169.5 23.8 %collective-permute-start.26 = (bf16[2,128,2048]{2,1,0:T(8,128)(2,1)S(1)}, bf16[2,128,2048]{2,1,0:T(8,128)(2,1)S(1)}, u32[]{:S(2)}, u32[]{:S(2)}) collective-permute-start(bf16[2,128,2048]{2,1,0:T(8,128)(2,1)S(1)} %get-tuple-element.15), channel_id=1, source_target_pairs={{0,2},{2,0},{4,6},{6,4},{8,10},{10,8},{12,14},{14,12},{1,3},{3,1},... | collective-permute-start | bytes 3145736 | tf_op jit(solution)/shard_map/ppermute | solution.py:214
  170.9 14.8 %collective-permute-start.19 = (bf16[128,2048]{1,0:T(8,128)(2,1)S(1)}, bf16[128,2048]{1,0:T(8,128)(2,1)S(1)}, u32[]{:S(2)}, u32[]{:S(2)}) collective-permute-start(bf16[128,2048]{1,0:T(8,128)(2,1)S(1)} %fusion.11), channel_id=1, source_target_pairs={{0,1},{1,0},{2,3},{3,2},{4,5},{5,4},{6,7},{7,6},{8,9},{9,8},{10,11... | collective-permute-start | bytes 1572872 | tf_op jit(solution)/shard_map/ppermute | solution.py:215
  173.9 15.8 %collective-permute-start.12 = (bf16[128,2048]{1,0:T(8,128)(2,1)S(1)}, bf16[128,2048]{1,0:T(8,128)(2,1)S(1)}, u32[]{:S(2)}, u32[]{:S(2)}) collective-permute-start(bf16[128,2048]{1,0:T(8,128)(2,1)S(1)} %fusion.9), channel_id=1, source_target_pairs={{0,4},{2,6},{4,8},{6,10},{8,12},{10,14},{12,0},{14,2},{1,5},{3,7},... | collective-permute-start | bytes 1572872 | tf_op jit(solution)/shard_map/ppermute | solution.py:217
  179.1 10.7 %copy-start.17 = (bf16[2,128,2048]{2,1,0:T(8,128)(2,1)S(1)}, bf16[2,128,2048]{2,1,0:T(8,128)(2,1)}, u32[]{:S(2)}) copy-start(bf16[2,128,2048]{2,1,0:T(8,128)(2,1)} %copy-done.16) | copy-start | bytes 3145732
  185.6 8.8 %collective-permute-start.29 = (bf16[2,128,2048]{2,1,0:T(8,128)(2,1)S(1)}, bf16[2,128,2048]{2,1,0:T(8,128)(2,1)S(1)}, u32[]{:S(2)}, u32[]{:S(2)}) collective-permute-start(bf16[2,128,2048]{2,1,0:T(8,128)(2,1)S(1)} %get-tuple-element.17), channel_id=1, source_target_pairs={{0,2},{2,0},{4,6},{6,4},{8,10},{10,8},{12,14},{14,12},{1,3},{3,1},... | collective-permute-start | bytes 3145736 | tf_op jit(solution)/shard_map/ppermute | solution.py:214
  191.1 15.0 %collective-permute-start.20 = (bf16[128,2048]{1,0:T(8,128)(2,1)S(1)}, bf16[128,2048]{1,0:T(8,128)(2,1)S(1)}, u32[]{:S(2)}, u32[]{:S(2)}) collective-permute-start(bf16[128,2048]{1,0:T(8,128)(2,1)S(1)} %fusion.8), channel_id=1, source_target_pairs={{0,4},{2,6},{4,8},{6,10},{8,12},{10,14},{12,0},{14,2},{1,5},{3,7},... | collective-permute-start | bytes 1572872 | tf_op jit(solution)/shard_map/ppermute | solution.py:217
  193.4 14.9 %collective-permute-start.27 = (bf16[128,2048]{1,0:T(8,128)(2,1)S(1)}, bf16[128,2048]{1,0:T(8,128)(2,1)S(1)}, u32[]{:S(2)}, u32[]{:S(2)}) collective-permute-start(bf16[128,2048]{1,0:T(8,128)(2,1)S(1)} %fusion.12), channel_id=1, source_target_pairs={{0,1},{1,0},{2,3},{3,2},{4,5},{5,4},{6,7},{7,6},{8,9},{9,8},{10,11... | collective-permute-start | bytes 1572872 | tf_op jit(solution)/shard_map/ppermute | solution.py:215
  194.4 15.6 %copy-start.32 = (bf16[2,128,2048]{2,1,0:T(8,128)(2,1)}, bf16[2,128,2048]{2,1,0:T(8,128)(2,1)S(1)}, u32[]{:S(2)}) copy-start(bf16[2,128,2048]{2,1,0:T(8,128)(2,1)S(1)} %collective-permute-done.29) | copy-start | bytes 3145732
  194.4 29.2 %copy-start.1 = (bf16[2048,16]{0,1:T(8,128)(2,1)S(1)}, bf16[2048,16]{0,1:T(8,128)(2,1)}, u32[]{:S(2)}) copy-start(bf16[2048,16]{0,1:T(8,128)(2,1)} %param.20) | copy-start | bytes 196612
  195.5 22.1 %collective-permute-start.30 = (bf16[128,2048]{1,0:T(8,128)(2,1)}, bf16[128,2048]{1,0:T(8,128)(2,1)S(1)}, u32[]{:S(2)}, u32[]{:S(2)}) collective-permute-start(bf16[128,2048]{1,0:T(8,128)(2,1)} %fusion.13), channel_id=1, source_target_pairs={{0,1},{1,0},{2,3},{3,2},{4,5},{5,4},{6,7},{7,6},{8,9},{9,8},{10,11... | collective-permute-start | bytes 1572872 | tf_op jit(solution)/shard_map/ppermute | solution.py:215
  209.5 12.0 %collective-permute-start.28 = (bf16[128,2048]{1,0:T(8,128)(2,1)}, bf16[128,2048]{1,0:T(8,128)(2,1)S(1)}, u32[]{:S(2)}, u32[]{:S(2)}) collective-permute-start(bf16[128,2048]{1,0:T(8,128)(2,1)} %fusion.6), channel_id=1, source_target_pairs={{0,4},{2,6},{4,8},{6,10},{8,12},{10,14},{12,0},{14,2},{1,5},{3,7},... | collective-permute-start | bytes 1572872 | tf_op jit(solution)/shard_map/ppermute | solution.py:217
  (23 other events, 69.3 us)

commit v4 on v3

--- a/solution.py
+++ b/solution.py
@@ -15,7 +15,7 @@
 
 EPS = 1e-06
 VMEM_LIMIT = 56 * 1024 * 1024
-BLOCK_VMEM_LIMIT = 24 * 1024 * 1024
+BLOCK_VMEM_LIMIT = 8 * 1024 * 1024
 MXU = 256
 
 
@@ -69,59 +69,82 @@
     )
 
 
+def load_kernel(source_ref, held_ref, sem):
+    copies = [
+        pltpu.make_async_copy(source_ref.at[e], held_ref.at[e], sem.at[e])
+        for e in range(source_ref.shape[0])
+    ]
+    for copy in copies:
+        copy.start()
+    for copy in copies:
+        copy.wait()
+
+
+def loaded(w, after):
+    return pl.pallas_call(
+        lambda source_ref, _, held_ref, sem: load_kernel(source_ref, held_ref, sem),
+        in_specs=[pl.BlockSpec(memory_space=pl.ANY)] * 2,
+        out_specs=pl.BlockSpec(memory_space=pltpu.VMEM),
+        out_shape=pltpu.VMEM(w.shape, w.dtype),
+        scratch_shapes=[pltpu.SemaphoreType.DMA((w.shape[0],))],
+        compiler_params=pltpu.CompilerParams(vmem_limit_bytes=1024 * 1024),
+        cost_estimate=pl.CostEstimate(flops=0, bytes_accessed=2 * w.size, transcendentals=0),
+    )(pltpu.with_memory_space_constraint(w, pltpu.HBM), after)
+
+
 def block_hidden_kernel(
     where_ref, own_ref, other_ref, sib_own_ref, sib_other_ref, side_ref, wg_ref, wu_ref,
-    _, out_ref, x_ref, gates_ref,
+    _, out_ref, x_ref,
 ):
     rows, width = own_ref.shape
-    expert = pl.program_id(0)
-
-    @pl.when((expert == 0) & (pl.program_id(1) == 0))
-    def _():
-        mine = pl.ds(pl.multiple_of(where_ref[0] * width, width), width)
-        theirs = pl.ds(pl.multiple_of((1 - where_ref[0]) * width, width), width)
-        x_ref[0:rows, mine] = own_ref[...]
-        x_ref[0:rows, theirs] = other_ref[...]
-        x_ref[rows : 2 * rows, mine] = sib_own_ref[...]
-        x_ref[rows : 2 * rows, theirs] = sib_other_ref[...]
-        gates_ref[...] = jnp.transpose(side_ref[...])
-
-    def step(k):
-        depth = pl.ds(k * MXU, MXU)
-        return (lambda: x_ref[:, depth], lambda: wg_ref[0, depth], lambda: wu_ref[0, depth])
-
-    steps = [step(k) for k in range(2 * width // MXU)]
-    gate, up = paired_products(2 * rows, steps)
-    side = gates_ref[...]
-    weight = column_of(side, 1 + where_ref[1] + expert)
-    out_ref[0] = silu_up(gate, up, column_of(side, 0), weight)
+    experts, depth, units = wg_ref.shape
+    mine = pl.ds(pl.multiple_of(where_ref[0] * width, width), width)
+    theirs = pl.ds(pl.multiple_of((1 - where_ref[0]) * width, width), width)
+    x_ref[0:rows, mine] = own_ref[...]
+    x_ref[0:rows, theirs] = other_ref[...]
+    x_ref[rows : 2 * rows, mine] = sib_own_ref[...]
+    x_ref[rows : 2 * rows, theirs] = sib_other_ref[...]
+    side = jnp.transpose(side_ref[...])
+    scale = column_of(side, 0)
+    for e in range(experts):
+        weight = column_of(side, 1 + where_ref[1] + e)
+
+        @pl.loop(0, units // MXU)
+        def _(tile):
+            columns = pl.ds(pl.multiple_of(tile * MXU, MXU), MXU)
+
+            def step(k):
+                part = pl.ds(k * MXU, MXU)
+                return (
+                    lambda: x_ref[:, part],
+                    lambda: wg_ref[e, part, columns],
+                    lambda: wu_ref[e, part, columns],
+                )
+
+            steps = [step(k) for k in range(depth // MXU)]
+            gate, up = paired_products(2 * rows, steps)
+            out_ref[e, :, columns] = silu_up(gate, up, scale, weight)
+
+
+def in_vmem(count):
+    return [pl.BlockSpec(memory_space=pltpu.VMEM)] * count
 
 
 def block_hidden(where, chunks, side, w_gate, w_up, after):
-    rows, width = chunks[0].shape
+    rows, _ = chunks[0].shape
     experts, depth, units = w_gate.shape
-    tile = MXU
-    chunk_spec = pl.BlockSpec((rows, width), lambda e, f, s: (0, 0))
-    weight_spec = pl.BlockSpec((1, depth, tile), lambda e, f, s: (e, 0, f))
     return pl.pallas_call(
         block_hidden_kernel,
-        grid_spec=pltpu.PrefetchScalarGridSpec(
-            num_scalar_prefetch=1,
-            grid=(experts, units // tile),
-            in_specs=[chunk_spec] * 4
-            + [pl.BlockSpec(side.shape, lambda e, f, s: (0, 0)), weight_spec, weight_spec]
-            + [pl.BlockSpec(memory_space=pl.ANY)],
-            out_specs=pl.BlockSpec((1, 2 * rows, tile), lambda e, f, s: (e, 0, f)),
-            scratch_shapes=[
-                pltpu.VMEM((2 * rows, depth), jnp.bfloat16),
-                pltpu.VMEM((2 * rows, side.shape[0]), jnp.float32),
-            ],
-        ),
+        in_specs=[pl.BlockSpec(memory_space=pltpu.SMEM)]
+        + in_vmem(7)
+        + [pl.BlockSpec(memory_space=pl.ANY)],
+        out_specs=pl.BlockSpec(memory_space=pltpu.VMEM),
+        scratch_shapes=[pltpu.VMEM((2 * rows, depth), jnp.bfloat16)],
         out_shape=jax.ShapeDtypeStruct((experts, 2 * rows, units), jnp.bfloat16),
         compiler_params=pltpu.CompilerParams(vmem_limit_bytes=BLOCK_VMEM_LIMIT),
         cost_estimate=pl.CostEstimate(
             flops=8 * rows * depth * units * experts,
-            bytes_accessed=4 * experts * depth * units + 4 * rows * depth,
+            bytes_accessed=4 * rows * depth,
             transcendentals=2 * rows * units * experts,
         ),
     )(where, *chunks, side, w_gate, w_up, after)
@@ -175,7 +198,7 @@
             bytes_accessed=4 * (experts * units + tokens) * width,
             transcendentals=0,
         ),
-    )(where, hidden, w_down, after)
+    )(where, hidden, pltpu.with_memory_space_constraint(w_down, pltpu.HBM), after)
 
 
 def total(*terms):
@@ -192,6 +215,7 @@
     across = functools.partial(lax.ppermute, axis_name="tp", perm=[(0, 1), (1, 0)])
     where = jnp.stack([lax.axis_index("tp"), lax.axis_index("ep") * w_gate.shape[0]])
     where = where.astype(jnp.int32)
+    w_gate, w_up = [loaded(w, where) for w in (w_gate, w_up)]
 
     lane, sides = [rows_out], [jnp.concatenate([side, beside(side)], 1)]
     for _ in range(chips - 1):

time: 225 us -> 190 us (0.84)
  local copies, waits for them, and re-layouts: 54.7 us -> 15.9 us
  Pallas kernels: 74.4 us -> 92.2 us
  other arithmetic: 19.5 us -> 12.2 us
  waiting for transfers between devices: 45.2 us -> 40.4 us
    unnamed x79 -> x37, local copies, waits for them, and re-layouts: 51.7 us -> 12.7 us
    pallas_call x4, Pallas kernels: 27.2 us -> 39.4 us  [block_down(): pl.pallas_call(block_down_kernel, grid_spec=pltpu.PrefetchScalarGridSpec(...]
    ppermute x3, waiting for transfers between devices: 11 us -> 0.01 us  [ring_experts(): sides.append(along(sides[-1]))]
    ppermute x3, starting transfers between devices: 6.5 us -> 0.74 us  [ring_experts(): along(travelling)]
    pallas_call x4 -> x6, Pallas kernels: 45.3 us -> 50.8 us  [the longest x4 37 us: block_hidden(): pl.pallas_call(block_hidden_kernel, in_specs=[pl.BlockSpec(memory_space=p...]
    convert_element_type x8, other arithmetic: 10.8 us -> 5.81 us  [total(): sum((term.astype(jnp.float32) for term in terms)).astype(jnp.bfloat16)]
    ppermute x3, waiting for transfers between devices: 17.1 us -> 21.2 us  [ring_experts(): along(travelling)]
  transfers between devices with their start and end apart: 32 -> 32, of which waited for: 9 -> 10; matrix products, arithmetic and copies ran while one was open for 11% -> 9% of each run, Pallas kernels for 32% -> 48%
where the time goes in v4:
time: 190 us; the launch traced here: 189 us
  Pallas kernels  92.2 us (49%)
  waiting for transfers between devices  40.4 us (21%)
  starting transfers between devices  21.9 us (12%)
  local copies, waits for them, and re-layouts  15.9 us (8%)
  other arithmetic  12.2 us (6%)
  matrix products  5.36 us (3%)
    pallas_call x4, Pallas kernels, block_down(): pl.pallas_call(block_down_kernel, grid_spec=pltpu.PrefetchScalarGridSpec(...  39.4 us
    pallas_call x4, Pallas kernels, block_hidden(): pl.pallas_call(block_hidden_kernel, in_specs=[pl.BlockSpec(memory_space=p...  37 us
    ppermute x3, waiting for transfers between devices, ring_experts(): along(travelling)  21.2 us
    pallas_call x2, Pallas kernels, loaded(): pl.pallas_call(lambda source_ref, _, held_ref, sem: load_kernel(source_re...  13.8 us
    unnamed x37, local copies, waits for them, and re-layouts  12.7 us
    ppermute x4, waiting for transfers between devices, ring_experts(): swapped = across(total(own[1], back[1]))  8.95 us
    convert_element_type x8, other arithmetic, total(): sum((term.astype(jnp.float32) for term in terms)).astype(jnp.bfloat16)  5.81 us
    ppermute x3, waiting for transfers between devices, ring_experts(): lane.append(along(lane[-1]))  5.53 us
  transfers between devices with their start and end apart: 32, of which 10 were waited for; matrix products, arithmetic and copies ran while one was open for 9% of the time, Pallas kernels for 48%

profile of v4, /device:TPU:0, one launch (start us, length us, event | category | flops | bytes accessed | tf_op | source)
XLA Modules:
  0.0 189.1 jit_solution(14080064215564212806)
XLA Ops:
  0.6 1.3 broadcast_in_dim.33.gain_ref
  2.0 1.9 %shard_map.131.own_ref = bf16[128,2048]{1,0:T(8,128)(2,1)} custom-call(bf16[128,2048]{1,0:T(8,128)(2,1)} %x_ref.1, bf16[1,2048]{1,0:T(2,128)(2,1)} %broadcast_in_dim.33.gain_ref), custom_call_target="tpu_custom_call" | custom-call | tf_op jit(solution)/shard_map/pallas_call | solution.py:46
  3.9 2.9 %collective-permute-start.7 = (bf16[128,2048]{1,0:T(8,128)(2,1)}, bf16[128,2048]{1,0:T(8,128)(2,1)S(1)}, u32[]{:S(2)}, u32[]{:S(2)}) collective-permute-start(bf16[128,2048]{1,0:T(8,128)(2,1)} %shard_map.131.own_ref), channel_id=1, source_target_pairs={{0,1},{1,0},{2,3},{3,2},{4,5},{5,4},{6,7},{7,6},{8,9},{9,8},{10,11... | collective-permute-start | bytes 1572872 | tf_op jit(solution)/shard_map/ppermute | solution.py:224
  6.8 1.6 collective-permute-start
  8.4 1.2 multiply_reduce_fusion
  9.6 1.3 convolution_bitcast_fusion
  10.9 1.2 fusion.1
  12.8 0.7 fusion.20
  13.7 0.8 select_reduce_fusion
  14.5 0.7 fusion.21
  15.3 4.0 %collective-permute-done.4 = f32[18,128]{1,0:T(8,128)S(1)} collective-permute-done((f32[18,128]{1,0:T(8,128)S(1)}, f32[18,128]{1,0:T(8,128)S(1)}, u32[]{:S(2)}, u32[]{:S(2)}) %collective-permute-start.4) | collective-permute-done | bytes 9248 | tf_op jit(solution)/shard_map/ppermute | solution.py:356
  19.3 3.9 %collective-permute-done.own_ref = bf16[128,2048]{1,0:T(8,128)(2,1)S(1)} collective-permute-done((bf16[128,2048]{1,0:T(8,128)(2,1)}, bf16[128,2048]{1,0:T(8,128)(2,1)S(1)}, u32[]{:S(2)}, u32[]{:S(2)}) %collective-permute-start) | collective-permute-done | bytes 524320 | tf_op jit(solution)/shard_map/ppermute | solution.py:222
  24.4 0.7 fusion.25
  25.1 0.7 collective-permute-done.5
  25.8 1.3 collective-permute-start.6
  27.1 4.6 %shard_map.132.wg_ref = bf16[2,4096,768]{2,1,0:T(8,128)(2,1)S(1)} custom-call(bf16[2,4096,768]{2,1,0:T(8,128)(2,1)} %source_ref.2, s32[2]{0:T(128)S(1)} %pad_add_fusion._.where_ref), custom_call_target="tpu_custom_call" | custom-call | bytes 12582912 | tf_op jit(solution)/shard_map/pallas_call | solution.py:84
  31.8 9.2 %shard_map.133.wu_ref = bf16[2,4096,768]{2,1,0:T(8,128)(2,1)S(1)} custom-call(bf16[2,4096,768]{2,1,0:T(8,128)(2,1)} %source_ref.3, s32[2]{0:T(128)S(1)} %pad_add_fusion._.where_ref), custom_call_target="tpu_custom_call" | custom-call | bytes 12582912 | tf_op jit(solution)/shard_map/pallas_call | solution.py:84
  41.1 1.6 collective-permute-start.17
  42.7 1.3 copy-done.9
  44.1 1.5 collective-permute-start.14
  45.6 2.1 %collective-permute-start.21 = (bf16[128,2048]{1,0:T(8,128)(2,1)S(1)}, bf16[128,2048]{1,0:T(8,128)(2,1)S(1)}, u32[]{:S(2)}, u32[]{:S(2)}) collective-permute-start(bf16[128,2048]{1,0:T(8,128)(2,1)S(1)} %collective-permute-done.13.own_ref), channel_id=1, source_target_pairs={{0,4},{2,6},{4,8},{6,10},{8,12},{10,14},{12,0},{14,2},{1,5},{3,7},... | collective-permute-start | bytes 1572872 | tf_op jit(solution)/shard_map/ppermute | solution.py:222
  47.7 1.0 copy-done.8
  48.8 1.0 copy-done.10
  49.8 9.3 %shard_map.134._.h_ref = bf16[2,256,768]{2,1,0:T(8,128)(2,1)S(1)} custom-call(s32[2]{0:T(128)S(1)} %pad_add_fusion._.where_ref, bf16[128,2048]{1,0:T(8,128)(2,1)S(1)} %copy-done.6, bf16[128,2048]{1,0:T(8,128)(2,1)S(1)} %copy-done.8, bf16[128,2048]{1,0:T(8,128)(2,1)S(1)} %copy-done.10, bf16[128,2048]{1,0:T(8,128)(2,1)} %collective-permute-done.9.sib_other_ref, ...), custom_call_target="tpu_custom_call" | custom-call | flops 6442450944 | bytes 2097152 | tf_op jit(solution)/shard_map/pallas_call | solution.py:136
  59.8 1.6 collective-permute-done.21.own_ref
  62.0 8.8 %shard_map.135.h_ref._ = bf16[2,256,768]{2,1,0:T(8,128)(2,1)S(1)} custom-call(s32[2]{0:T(128)S(1)} %pad_add_fusion._.where_ref, bf16[128,2048]{1,0:T(8,128)(2,1)S(1)} %collective-permute-done.own_ref, bf16[128,2048]{1,0:T(8,128)(2,1)S(1)} %collective-permute-done.1.other_ref, bf16[128,2048]{1,0:T(8,128)(2,1)S(1)} %collective-permute-done.2.sib_own_ref, ...), custom_call_target="tpu_custom_call" | custom-call | flops 6442450944 | bytes 2097152 | tf_op jit(solution)/shard_map/pallas_call | solution.py:136
  70.8 10.3 %shard_map.136 = (bf16[2,128,2048]{2,1,0:T(8,128)(2,1)S(1)}, bf16[2,128,2048]{2,1,0:T(8,128)(2,1)}) custom-call(s32[2]{0:T(128)S(1)} %pad_add_fusion._.where_ref, bf16[2,256,768]{2,1,0:T(8,128)(2,1)S(1)} %shard_map.135.h_ref._, bf16[2,768,4096]{2,1,0:T(8,128)(2,1)} %w_ref.7, bf16[2,256,768]{2,1,0:T(8,128)(2,1)S(1)} %shard_map.135.h_ref._), custom_call_target="tpu_custom_call" | custom-call | flops 3221225472 | bytes 14680064 | tf_op jit(solution)/shard_map/pallas_call | solution.py:179
  81.1 4.1 %convolution_convert_fusion = bf16[256,1024]{1,0:T(8,128)(2,1)} fusion(bf16[2048,1024]{1,0:T(8,128)(2,1)} %param.19, bf16[128,2048]{1,0:T(8,128)(2,1)} %param.12, f32[2048]{0:T(1024)S(1)} %convert_element_type.219, f32[128]{0:T(128)S(1)} %get-tuple-element.18, s32[128]{0:T(128)S(1)} %fusion.25), kind=kOutput, calls=%fused_computation.2 | convolution fusion | flops 605323264 | bytes 5252096 | tf_op jit(solution)/shard_map/dot_general | solution.py:382
  85.2 1.0 slice.107
  86.2 1.6 collective-permute-start.31
  88.6 4.6 %copy-done.3 = bf16[2,4096,768]{2,1,0:T(8,128)(2,1)S(1)} copy-done((bf16[2,4096,768]{2,1,0:T(8,128)(2,1)S(1)}, bf16[2,4096,768]{2,1,0:T(8,128)(2,1)}, u32[]{:S(2)}) %copy-start.3) | copy-done | bytes 12582936
  93.2 4.6 %copy-done.5 = bf16[2,4096,768]{2,1,0:T(8,128)(2,1)S(1)} copy-done((bf16[2,4096,768]{2,1,0:T(8,128)(2,1)S(1)}, bf16[2,4096,768]{2,1,0:T(8,128)(2,1)}, u32[]{:S(2)}) %copy-start.5) | copy-done | bytes 12582936
  97.8 9.6 %shard_map.137.h_ref._ = bf16[2,256,768]{2,1,0:T(8,128)(2,1)S(1)} custom-call(s32[2]{0:T(128)S(1)} %pad_add_fusion._.where_ref, bf16[128,2048]{1,0:T(8,128)(2,1)S(1)} %collective-permute-done.13.own_ref, bf16[128,2048]{1,0:T(8,128)(2,1)S(1)} %collective-permute-done.14.other_ref, bf16[128,2048]{1,0:T(8,128)(2,1)} %collective-permute-done.15.sib_own_ref, ...), custom_call_target="tpu_custom_call" | custom-call | flops 6442450944 | bytes 2097152 | tf_op jit(solution)/shard_map/pallas_call | solution.py:136
  107.4 9.9 %shard_map.138 = (bf16[2,128,2048]{2,1,0:T(8,128)(2,1)S(1)}, bf16[2,128,2048]{2,1,0:T(8,128)(2,1)S(1)}) custom-call(s32[2]{0:T(128)S(1)} %pad_add_fusion._.where_ref, bf16[2,256,768]{2,1,0:T(8,128)(2,1)S(1)} %shard_map.137.h_ref._, bf16[2,768,4096]{2,1,0:T(8,128)(2,1)} %w_ref.7, bf16[2,256,768]{2,1,0:T(8,128)(2,1)S(1)} %shard_map.137.h_ref._), custom_call_target="tpu_custom_call" | custom-call | flops 3221225472 | bytes 14680064 | tf_op jit(solution)/shard_map/pallas_call | solution.py:179
  117.4 1.2 fusion.10
  119.2 9.3 %shard_map.139.h_ref._ = bf16[2,256,768]{2,1,0:T(8,128)(2,1)S(1)} custom-call(s32[2]{0:T(128)S(1)} %pad_add_fusion._.where_ref, bf16[128,2048]{1,0:T(8,128)(2,1)S(1)} %collective-permute-done.21.own_ref, bf16[128,2048]{1,0:T(8,128)(2,1)} %collective-permute-done.22.other_ref, bf16[128,2048]{1,0:T(8,128)(2,1)S(1)} %collective-permute-done.23.sib_own_ref, ...), custom_call_target="tpu_custom_call" | custom-call | flops 6442450944 | bytes 2097152 | tf_op jit(solution)/shard_map/pallas_call | solution.py:136
  128.5 9.6 %shard_map.140 = (bf16[2,128,2048]{2,1,0:T(8,128)(2,1)S(1)}, bf16[2,128,2048]{2,1,0:T(8,128)(2,1)S(1)}) custom-call(s32[2]{0:T(128)S(1)} %pad_add_fusion._.where_ref, bf16[2,256,768]{2,1,0:T(8,128)(2,1)S(1)} %shard_map.139.h_ref._, bf16[2,768,4096]{2,1,0:T(8,128)(2,1)} %w_ref.7, bf16[2,256,768]{2,1,0:T(8,128)(2,1)S(1)} %shard_map.139.h_ref._), custom_call_target="tpu_custom_call" | custom-call | flops 3221225472 | bytes 14680064 | tf_op jit(solution)/shard_map/pallas_call | solution.py:179
  138.5 1.6 collective-permute-start.19
  140.1 1.3 fusion.9
  141.9 9.6 %shard_map.141 = (bf16[2,128,2048]{2,1,0:T(8,128)(2,1)S(1)}, bf16[2,128,2048]{2,1,0:T(8,128)(2,1)S(1)}) custom-call(s32[2]{0:T(128)S(1)} %pad_add_fusion._.where_ref, bf16[2,256,768]{2,1,0:T(8,128)(2,1)S(1)} %shard_map.134._.h_ref, bf16[2,768,4096]{2,1,0:T(8,128)(2,1)} %w_ref.7, bf16[2,128,2048]{2,1,0:T(8,128)(2,1)S(1)} %get-tuple-element.14._), custom_call_target="tpu_custom_call" | custom-call | flops 3221225472 | bytes 14680064 | tf_op jit(solution)/shard_map/pallas_call | solution.py:179
  151.6 1.2 collective-permute-done.19
  152.7 4.4 %collective-permute-done.12 = bf16[128,2048]{1,0:T(8,128)(2,1)S(1)} collective-permute-done((bf16[128,2048]{1,0:T(8,128)(2,1)S(1)}, bf16[128,2048]{1,0:T(8,128)(2,1)S(1)}, u32[]{:S(2)}, u32[]{:S(2)}) %collective-permute-start.12) | collective-permute-done | bytes 524320 | tf_op jit(solution)/shard_map/ppermute | solution.py:241
  158.7 1.6 collective-permute-start.30
  160.3 12.1 %collective-permute-done.20 = bf16[128,2048]{1,0:T(8,128)(2,1)S(1)} collective-permute-done((bf16[128,2048]{1,0:T(8,128)(2,1)S(1)}, bf16[128,2048]{1,0:T(8,128)(2,1)S(1)}, u32[]{:S(2)}, u32[]{:S(2)}) %collective-permute-start.20) | collective-permute-done | bytes 524320 | tf_op jit(solution)/shard_map/ppermute | solution.py:241
  173.7 0.8 convert_element_type.226
  174.5 7.5 %collective-permute-done.30 = bf16[128,2048]{1,0:T(8,128)(2,1)S(1)} collective-permute-done((bf16[128,2048]{1,0:T(8,128)(2,1)S(1)}, bf16[128,2048]{1,0:T(8,128)(2,1)S(1)}, u32[]{:S(2)}, u32[]{:S(2)}) %collective-permute-start.30) | collective-permute-done | bytes 524320 | tf_op jit(solution)/shard_map/ppermute | solution.py:239
  182.0 4.8 %collective-permute-done.28 = bf16[128,2048]{1,0:T(8,128)(2,1)} collective-permute-done((bf16[128,2048]{1,0:T(8,128)(2,1)S(1)}, bf16[128,2048]{1,0:T(8,128)(2,1)}, u32[]{:S(2)}, u32[]{:S(2)}) %collective-permute-start.28) | collective-permute-done | bytes 524320 | tf_op jit(solution)/shard_map/ppermute | solution.py:241
  186.8 2.3 %fusion.4 = bf16[128,2048]{1,0:T(8,128)(2,1)} fusion(bf16[128,2048]{1,0:T(8,128)(2,1)S(1)} %collective-permute-done.30, bf16[128,2048]{1,0:T(8,128)(2,1)} %collective-permute-done.28, bf16[2,128,2048]{2,1,0:T(8,128)(2,1)} %copy-done.12, bf16[2,128,2048]{2,1,0:T(8,128)(2,1)S(1)} %get-tuple-element.16), kind=kLoop, calls=%fused_computation.10 | loop fusion | flops 2097152 | bytes 2621440 | tf_op jit(solution)/shard_map/convert_element_type | solution.py:205
  (103 shorter events, 8.7 us)
Async XLA Ops:
  0.6 9.0 %copy-start = (bf16[2048,16]{0,1:T(8,128)(2,1)S(1)}, bf16[2048,16]{0,1:T(8,128)(2,1)}, u32[]{:S(2)}) copy-start(bf16[2048,16]{0,1:T(8,128)(2,1)} %param.20) | copy-start | bytes 196612
  3.9 19.9 %collective-permute-start.7 = (bf16[128,2048]{1,0:T(8,128)(2,1)}, bf16[128,2048]{1,0:T(8,128)(2,1)S(1)}, u32[]{:S(2)}, u32[]{:S(2)}) collective-permute-start(bf16[128,2048]{1,0:T(8,128)(2,1)} %shard_map.131.own_ref), channel_id=1, source_target_pairs={{0,1},{1,0},{2,3},{3,2},{4,5},{5,4},{6,7},{7,6},{8,9},{9,8},{10,11... | collective-permute-start | bytes 1572872 | tf_op jit(solution)/shard_map/ppermute | solution.py:224
  6.8 35.9 %collective-permute-start.8 = (bf16[128,2048]{1,0:T(8,128)(2,1)}, bf16[128,2048]{1,0:T(8,128)(2,1)S(1)}, u32[]{:S(2)}, u32[]{:S(2)}) collective-permute-start(bf16[128,2048]{1,0:T(8,128)(2,1)} %shard_map.131.own_ref), channel_id=1, source_target_pairs={{0,2},{2,0},{4,6},{6,4},{8,10},{10,8},{12,14},{14,12},{1,3},{3,1},... | collective-permute-start | bytes 1572872 | tf_op jit(solution)/shard_map/ppermute | solution.py:228
  6.8 16.4 %collective-permute-start = (bf16[128,2048]{1,0:T(8,128)(2,1)}, bf16[128,2048]{1,0:T(8,128)(2,1)S(1)}, u32[]{:S(2)}, u32[]{:S(2)}) collective-permute-start(bf16[128,2048]{1,0:T(8,128)(2,1)} %shard_map.131.own_ref), channel_id=1, source_target_pairs={{0,4},{2,6},{4,8},{6,10},{8,12},{10,14},{12,0},{14,2},{1,5},{3,7},... | collective-permute-start | bytes 1572872 | tf_op jit(solution)/shard_map/ppermute | solution.py:222
  12.2 7.0 %collective-permute-start.4 = (f32[18,128]{1,0:T(8,128)S(1)}, f32[18,128]{1,0:T(8,128)S(1)}, u32[]{:S(2)}, u32[]{:S(2)}) collective-permute-start(f32[18,128]{1,0:T(8,128)S(1)} %pad_maximum_fusion.2), channel_id=1, source_target_pairs={{0,1},{1,0},{2,3},{3,2},{4,5},{5,4},{6,7},{7,6},{8,9},{9,8},{10,11... | collective-permute-start | bytes 27656 | tf_op jit(solution)/shard_map/ppermute | solution.py:356
  23.2 24.5 %collective-permute-start.1 = (bf16[128,2048]{1,0:T(8,128)(2,1)S(1)}, bf16[128,2048]{1,0:T(8,128)(2,1)S(1)}, u32[]{:S(2)}, u32[]{:S(2)}) collective-permute-start(bf16[128,2048]{1,0:T(8,128)(2,1)S(1)} %collective-permute-done.own_ref), channel_id=1, source_target_pairs={{0,1},{1,0},{2,3},{3,2},{4,5},{5,4},{6,7},{7,6},{8,9},{9,8},{10,11... | collective-permute-start | bytes 1572872 | tf_op jit(solution)/shard_map/ppermute | solution.py:224
  23.8 20.3 %collective-permute-start.13 = (bf16[128,2048]{1,0:T(8,128)(2,1)S(1)}, bf16[128,2048]{1,0:T(8,128)(2,1)S(1)}, u32[]{:S(2)}, u32[]{:S(2)}) collective-permute-start(bf16[128,2048]{1,0:T(8,128)(2,1)S(1)} %collective-permute-done.own_ref), channel_id=1, source_target_pairs={{0,4},{2,6},{4,8},{6,10},{8,12},{10,14},{12,0},{14,2},{1,5},{3,7},... | collective-permute-start | bytes 1572872 | tf_op jit(solution)/shard_map/ppermute | solution.py:222
  23.8 8.0 %copy-start.7 = (bf16[128,2048]{1,0:T(8,128)(2,1)}, bf16[128,2048]{1,0:T(8,128)(2,1)S(1)}, u32[]{:S(2)}) copy-start(bf16[128,2048]{1,0:T(8,128)(2,1)S(1)} %collective-permute-done.7.other_ref) | copy-start | bytes 1572868
  23.8 21.8 %collective-permute-start.9 = (bf16[128,2048]{1,0:T(8,128)(2,1)S(1)}, bf16[128,2048]{1,0:T(8,128)(2,1)}, u32[]{:S(2)}, u32[]{:S(2)}) collective-permute-start(bf16[128,2048]{1,0:T(8,128)(2,1)S(1)} %collective-permute-done.7.other_ref), channel_id=1, source_target_pairs={{0,2},{2,0},{4,6},{6,4},{8,10},{10,8},{12,14},{14,12},{1,3},{3,1},... | collective-permute-start | bytes 1572872 | tf_op jit(solution)/shard_map/ppermute | solution.py:228
  23.9 1.9 collective-permute-start.5
  25.8 15.3 %collective-permute-start.6 = (f32[24,256]{1,0:T(8,128)S(1)}, f32[24,256]{1,0:T(8,128)S(1)}, u32[]{:S(2)}, u32[]{:S(2)}) collective-permute-start(f32[24,256]{1,0:T(8,128)S(1)} %pad_maximum_fusion.1.side_ref), channel_id=1, source_target_pairs={{0,4},{2,6},{4,8},{6,10},{8,12},{10,14},{12,0},{14,2},{1,5},{3,7},... | collective-permute-start | bytes 73736 | tf_op jit(solution)/shard_map/ppermute | solution.py:223
  31.8 30.2 %copy-start.2 = (bf16[2,4096,768]{2,1,0:T(8,128)(2,1)}, bf16[2,4096,768]{2,1,0:T(8,128)(2,1)S(1)}, u32[]{:S(2)}) copy-start(bf16[2,4096,768]{2,1,0:T(8,128)(2,1)S(1)} %shard_map.132.wg_ref) | copy-start | bytes 37748740
  31.8 9.2 %copy-start.13 = (bf16[2048]{0:T(1024)(128)(2,1)S(1)}, bf16[2048]{0:T(1024)(128)(2,1)}, u32[]{:S(2)}) copy-start(bf16[2048]{0:T(1024)(128)(2,1)} %param.16) | copy-start | bytes 12292
  31.8 9.2 %copy-start.14 = (bf16[128]{0:T(256)(128)(2,1)S(1)}, bf16[128]{0:T(256)(128)(2,1)}, u32[]{:S(2)}) copy-start(bf16[128]{0:T(256)(128)(2,1)} %param.18) | copy-start | bytes 772
  31.8 15.9 %copy-start.6 = (bf16[128,2048]{1,0:T(8,128)(2,1)S(1)}, bf16[128,2048]{1,0:T(8,128)(2,1)}, u32[]{:S(2)}) copy-start(bf16[128,2048]{1,0:T(8,128)(2,1)} %shard_map.131.own_ref) | copy-start | bytes 1572868
  41.0 20.9 %copy-start.4 = (bf16[2,4096,768]{2,1,0:T(8,128)(2,1)}, bf16[2,4096,768]{2,1,0:T(8,128)(2,1)S(1)}, u32[]{:S(2)}) copy-start(bf16[2,4096,768]{2,1,0:T(8,128)(2,1)S(1)} %shard_map.133.wu_ref) | copy-start | bytes 37748740
  41.1 45.1 %collective-permute-start.17 = (f32[24,256]{1,0:T(8,128)S(1)}, f32[24,256]{1,0:T(8,128)S(1)}, u32[]{:S(2)}, u32[]{:S(2)}) collective-permute-start(f32[24,256]{1,0:T(8,128)S(1)} %collective-permute-done.6.side_ref), channel_id=1, source_target_pairs={{0,4},{2,6},{4,8},{6,10},{8,12},{10,14},{12,0},{14,2},{1,5},{3,7},... | collective-permute-start | bytes 73736 | tf_op jit(solution)/shard_map/ppermute | solution.py:223
  42.7 1.3 copy-start.9
  44.1 15.1 %collective-permute-start.2 = (bf16[128,2048]{1,0:T(8,128)(2,1)S(1)}, bf16[128,2048]{1,0:T(8,128)(2,1)S(1)}, u32[]{:S(2)}, u32[]{:S(2)}) collective-permute-start(bf16[128,2048]{1,0:T(8,128)(2,1)S(1)} %collective-permute-done.own_ref), channel_id=1, source_target_pairs={{0,2},{2,0},{4,6},{6,4},{8,10},{10,8},{12,14},{14,12},{1,3},{3,1},... | collective-permute-start | bytes 1572872 | tf_op jit(solution)/shard_map/ppermute | solution.py:228
  44.1 15.7 %collective-permute-start.14 = (bf16[128,2048]{1,0:T(8,128)(2,1)S(1)}, bf16[128,2048]{1,0:T(8,128)(2,1)S(1)}, u32[]{:S(2)}, u32[]{:S(2)}) collective-permute-start(bf16[128,2048]{1,0:T(8,128)(2,1)S(1)} %collective-permute-done.13.own_ref), channel_id=1, source_target_pairs={{0,1},{1,0},{2,3},{3,2},{4,5},{5,4},{6,7},{7,6},{8,9},{9,8},{10,11... | collective-permute-start | bytes 1572872 | tf_op jit(solution)/shard_map/ppermute | solution.py:224
  45.6 15.9 %collective-permute-start.21 = (bf16[128,2048]{1,0:T(8,128)(2,1)S(1)}, bf16[128,2048]{1,0:T(8,128)(2,1)S(1)}, u32[]{:S(2)}, u32[]{:S(2)}) collective-permute-start(bf16[128,2048]{1,0:T(8,128)(2,1)S(1)} %collective-permute-done.13.own_ref), channel_id=1, source_target_pairs={{0,4},{2,6},{4,8},{6,10},{8,12},{10,14},{12,0},{14,2},{1,5},{3,7},... | collective-permute-start | bytes 1572872 | tf_op jit(solution)/shard_map/ppermute | solution.py:222
  47.7 14.2 %collective-permute-start.3 = (bf16[128,2048]{1,0:T(8,128)(2,1)S(1)}, bf16[128,2048]{1,0:T(8,128)(2,1)S(1)}, u32[]{:S(2)}, u32[]{:S(2)}) collective-permute-start(bf16[128,2048]{1,0:T(8,128)(2,1)S(1)} %collective-permute-done.1.other_ref), channel_id=1, source_target_pairs={{0,2},{2,0},{4,6},{6,4},{8,10},{10,8},{12,14},{14,12},{1,3},{3,1},... | collective-permute-start | bytes 1572872 | tf_op jit(solution)/shard_map/ppermute | solution.py:228
  59.1 28.6 %collective-permute-start.15 = (bf16[128,2048]{1,0:T(8,128)(2,1)S(1)}, bf16[128,2048]{1,0:T(8,128)(2,1)}, u32[]{:S(2)}, u32[]{:S(2)}) collective-permute-start(bf16[128,2048]{1,0:T(8,128)(2,1)S(1)} %collective-permute-done.13.own_ref), channel_id=1, source_target_pairs={{0,2},{2,0},{4,6},{6,4},{8,10},{10,8},{12,14},{14,12},{1,3},{3,1},... | collective-permute-start | bytes 1572872 | tf_op jit(solution)/shard_map/ppermute | solution.py:228
  59.7 28.4 %collective-permute-start.16 = (bf16[128,2048]{1,0:T(8,128)(2,1)S(1)}, bf16[128,2048]{1,0:T(8,128)(2,1)}, u32[]{:S(2)}, u32[]{:S(2)}) collective-permute-start(bf16[128,2048]{1,0:T(8,128)(2,1)S(1)} %collective-permute-done.14.other_ref), channel_id=1, source_target_pairs={{0,2},{2,0},{4,6},{6,4},{8,10},{10,8},{12,14},{14,12},{1,3},{3,1},... | collective-permute-start | bytes 1572872 | tf_op jit(solution)/shard_map/ppermute | solution.py:228
  61.4 26.7 %collective-permute-start.22 = (bf16[128,2048]{1,0:T(8,128)(2,1)S(1)}, bf16[128,2048]{1,0:T(8,128)(2,1)}, u32[]{:S(2)}, u32[]{:S(2)}) collective-permute-start(bf16[128,2048]{1,0:T(8,128)(2,1)S(1)} %collective-permute-done.21.own_ref), channel_id=1, source_target_pairs={{0,1},{1,0},{2,3},{3,2},{4,5},{5,4},{6,7},{7,6},{8,9},{9,8},{10,11... | collective-permute-start | bytes 1572872 | tf_op jit(solution)/shard_map/ppermute | solution.py:224
  81.1 36.2 %collective-permute-start.10 = (bf16[2,128,2048]{2,1,0:T(8,128)(2,1)}, bf16[2,128,2048]{2,1,0:T(8,128)(2,1)}, u32[]{:S(2)}, u32[]{:S(2)}) collective-permute-start(bf16[2,128,2048]{2,1,0:T(8,128)(2,1)} %get-tuple-element.11), channel_id=1, source_target_pairs={{0,2},{2,0},{4,6},{6,4},{8,10},{10,8},{12,14},{14,12},{1,3},{3,1},... | collective-permute-start | bytes 3145736 | tf_op jit(solution)/shard_map/ppermute | solution.py:238
  86.2 55.5 %collective-permute-start.31 = (bf16[128,1024]{1,0:T(8,128)(2,1)S(1)}, bf16[128,1024]{1,0:T(8,128)(2,1)S(1)}, u32[]{:S(2)}, u32[]{:S(2)}) collective-permute-start(bf16[128,1024]{1,0:T(8,128)(2,1)S(1)} %slice.107), channel_id=1, source_target_pairs={{0,1},{1,0},{2,3},{3,2},{4,5},{5,4},{6,7},{7,6},{8,9},{9,8},{10,11... | collective-permute-start | bytes 786440 | tf_op jit(solution)/shard_map/ppermute | solution.py:387
  87.7 30.8 %collective-permute-start.25 = (f32[24,256]{1,0:T(8,128)S(1)}, f32[24,256]{1,0:T(8,128)S(1)}, u32[]{:S(2)}, u32[]{:S(2)}) collective-permute-start(f32[24,256]{1,0:T(8,128)S(1)} %collective-permute-done.17.side_ref), channel_id=1, source_target_pairs={{0,4},{2,6},{4,8},{6,10},{8,12},{10,14},{12,0},{14,2},{1,5},{3,7},... | collective-permute-start | bytes 73736 | tf_op jit(solution)/shard_map/ppermute | solution.py:223
  88.1 31.1 %collective-permute-start.23 = (bf16[128,2048]{1,0:T(8,128)(2,1)S(1)}, bf16[128,2048]{1,0:T(8,128)(2,1)S(1)}, u32[]{:S(2)}, u32[]{:S(2)}) collective-permute-start(bf16[128,2048]{1,0:T(8,128)(2,1)S(1)} %collective-permute-done.21.own_ref), channel_id=1, source_target_pairs={{0,2},{2,0},{4,6},{6,4},{8,10},{10,8},{12,14},{14,12},{1,3},{3,1},... | collective-permute-start | bytes 1572872 | tf_op jit(solution)/shard_map/ppermute | solution.py:228
  88.1 31.1 %collective-permute-start.24 = (bf16[128,2048]{1,0:T(8,128)(2,1)}, bf16[128,2048]{1,0:T(8,128)(2,1)S(1)}, u32[]{:S(2)}, u32[]{:S(2)}) collective-permute-start(bf16[128,2048]{1,0:T(8,128)(2,1)} %collective-permute-done.22.other_ref), channel_id=1, source_target_pairs={{0,2},{2,0},{4,6},{6,4},{8,10},{10,8},{12,14},{14,12},{1,3},{3,1},... | collective-permute-start | bytes 1572872 | tf_op jit(solution)/shard_map/ppermute | solution.py:228
  88.6 4.6 %copy-start.3 = (bf16[2,4096,768]{2,1,0:T(8,128)(2,1)S(1)}, bf16[2,4096,768]{2,1,0:T(8,128)(2,1)}, u32[]{:S(2)}) copy-start(bf16[2,4096,768]{2,1,0:T(8,128)(2,1)} %copy-done.2) | copy-start | bytes 37748740
  93.2 4.6 %copy-start.5 = (bf16[2,4096,768]{2,1,0:T(8,128)(2,1)S(1)}, bf16[2,4096,768]{2,1,0:T(8,128)(2,1)}, u32[]{:S(2)}) copy-start(bf16[2,4096,768]{2,1,0:T(8,128)(2,1)} %copy-done.4) | copy-start | bytes 37748740
  97.8 21.4 %slice-start = ((s8[12582912]{0:T(1024)(128)(4,1)}), s8[4194304]{0:T(1024)(128)(4,1)S(1)}, s32[]{:S(2)}) async-start(s8[12582912]{0:T(1024)(128)(4,1)} %bitcast.54), calls=%async_computation | async-start | bytes 8388608
  97.8 21.4 %slice-start.1 = ((s8[12582912]{0:T(1024)(128)(4,1)}), s8[4194304]{0:T(1024)(128)(4,1)S(1)}, s32[]{:S(2)}) async-start(s8[12582912]{0:T(1024)(128)(4,1)} %bitcast.54), calls=%async_computation.1 | async-start | bytes 8388608
  107.4 11.8 %slice-start.2 = ((s8[12582912]{0:T(1024)(128)(4,1)}), s8[4194304]{0:T(1024)(128)(4,1)S(1)}, s32[]{:S(2)}) async-start(s8[12582912]{0:T(1024)(128)(4,1)} %bitcast.54), calls=%async_computation.2 | async-start | bytes 8388608
  117.3 21.1 %collective-permute-start.18 = (bf16[2,128,2048]{2,1,0:T(8,128)(2,1)S(1)}, bf16[2,128,2048]{2,1,0:T(8,128)(2,1)S(1)}, u32[]{:S(2)}, u32[]{:S(2)}) collective-permute-start(bf16[2,128,2048]{2,1,0:T(8,128)(2,1)S(1)} %get-tuple-element.13), channel_id=1, source_target_pairs={{0,2},{2,0},{4,6},{6,4},{8,10},{10,8},{12,14},{14,12},{1,3},{3,1},... | collective-permute-start | bytes 3145736 | tf_op jit(solution)/shard_map/ppermute | solution.py:238
  118.6 21.5 %collective-permute-start.11 = (bf16[128,2048]{1,0:T(8,128)(2,1)S(1)}, bf16[128,2048]{1,0:T(8,128)(2,1)S(1)}, u32[]{:S(2)}, u32[]{:S(2)}) collective-permute-start(bf16[128,2048]{1,0:T(8,128)(2,1)S(1)} %fusion.10), channel_id=1, source_target_pairs={{0,1},{1,0},{2,3},{3,2},{4,5},{5,4},{6,7},{7,6},{8,9},{9,8},{10,11... | collective-permute-start | bytes 1572872 | tf_op jit(solution)/shard_map/ppermute | solution.py:239
  128.5 13.2 %copy-start.11 = (bf16[256,1024]{1,0:T(8,128)(2,1)S(1)}, bf16[256,1024]{1,0:T(8,128)(2,1)}, u32[]{:S(2)}) copy-start(bf16[256,1024]{1,0:T(8,128)(2,1)} %convolution_convert_fusion) | copy-start | bytes 1572868
  138.1 19.4 %collective-permute-start.26 = (bf16[2,128,2048]{2,1,0:T(8,128)(2,1)S(1)}, bf16[2,128,2048]{2,1,0:T(8,128)(2,1)S(1)}, u32[]{:S(2)}, u32[]{:S(2)}) collective-permute-start(bf16[2,128,2048]{2,1,0:T(8,128)(2,1)S(1)} %get-tuple-element.15), channel_id=1, source_target_pairs={{0,2},{2,0},{4,6},{6,4},{8,10},{10,8},{12,14},{14,12},{1,3},{3,1},... | collective-permute-start | bytes 3145736 | tf_op jit(solution)/shard_map/ppermute | solution.py:238
  138.5 14.2 %collective-permute-start.19 = (bf16[128,2048]{1,0:T(8,128)(2,1)S(1)}, bf16[128,2048]{1,0:T(8,128)(2,1)S(1)}, u32[]{:S(2)}, u32[]{:S(2)}) collective-permute-start(bf16[128,2048]{1,0:T(8,128)(2,1)S(1)} %fusion.11), channel_id=1, source_target_pairs={{0,1},{1,0},{2,3},{3,2},{4,5},{5,4},{6,7},{7,6},{8,9},{9,8},{10,11... | collective-permute-start | bytes 1572872 | tf_op jit(solution)/shard_map/ppermute | solution.py:239
  141.4 15.7 %collective-permute-start.12 = (bf16[128,2048]{1,0:T(8,128)(2,1)S(1)}, bf16[128,2048]{1,0:T(8,128)(2,1)S(1)}, u32[]{:S(2)}, u32[]{:S(2)}) collective-permute-start(bf16[128,2048]{1,0:T(8,128)(2,1)S(1)} %fusion.9), channel_id=1, source_target_pairs={{0,4},{2,6},{4,8},{6,10},{8,12},{10,14},{12,0},{14,2},{1,5},{3,7},... | collective-permute-start | bytes 1572872 | tf_op jit(solution)/shard_map/ppermute | solution.py:241
  141.9 47.2 %copy-start.1 = (bf16[2048,16]{0,1:T(8,128)(2,1)S(1)}, bf16[2048,16]{0,1:T(8,128)(2,1)}, u32[]{:S(2)}) copy-start(bf16[2048,16]{0,1:T(8,128)(2,1)} %param.20) | copy-start | bytes 196612
  151.5 7.0 %collective-permute-start.29 = (bf16[2,128,2048]{2,1,0:T(8,128)(2,1)S(1)}, bf16[2,128,2048]{2,1,0:T(8,128)(2,1)S(1)}, u32[]{:S(2)}, u32[]{:S(2)}) collective-permute-start(bf16[2,128,2048]{2,1,0:T(8,128)(2,1)S(1)} %get-tuple-element.17), channel_id=1, source_target_pairs={{0,2},{2,0},{4,6},{6,4},{8,10},{10,8},{12,14},{14,12},{1,3},{3,1},... | collective-permute-start | bytes 3145736 | tf_op jit(solution)/shard_map/ppermute | solution.py:238
  157.5 14.9 %collective-permute-start.20 = (bf16[128,2048]{1,0:T(8,128)(2,1)S(1)}, bf16[128,2048]{1,0:T(8,128)(2,1)S(1)}, u32[]{:S(2)}, u32[]{:S(2)}) collective-permute-start(bf16[128,2048]{1,0:T(8,128)(2,1)S(1)} %fusion.8), channel_id=1, source_target_pairs={{0,4},{2,6},{4,8},{6,10},{8,12},{10,14},{12,0},{14,2},{1,5},{3,7},... | collective-permute-start | bytes 1572872 | tf_op jit(solution)/shard_map/ppermute | solution.py:241
  157.7 14.9 %collective-permute-start.27 = (bf16[128,2048]{1,0:T(8,128)(2,1)S(1)}, bf16[128,2048]{1,0:T(8,128)(2,1)S(1)}, u32[]{:S(2)}, u32[]{:S(2)}) collective-permute-start(bf16[128,2048]{1,0:T(8,128)(2,1)S(1)} %fusion.12), channel_id=1, source_target_pairs={{0,1},{1,0},{2,3},{3,2},{4,5},{5,4},{6,7},{7,6},{8,9},{9,8},{10,11... | collective-permute-start | bytes 1572872 | tf_op jit(solution)/shard_map/ppermute | solution.py:239
  158.5 15.0 %copy-start.12 = (bf16[2,128,2048]{2,1,0:T(8,128)(2,1)}, bf16[2,128,2048]{2,1,0:T(8,128)(2,1)S(1)}, u32[]{:S(2)}) copy-start(bf16[2,128,2048]{2,1,0:T(8,128)(2,1)S(1)} %collective-permute-done.29) | copy-start | bytes 3145732
  158.7 23.3 %collective-permute-start.30 = (bf16[128,2048]{1,0:T(8,128)(2,1)S(1)}, bf16[128,2048]{1,0:T(8,128)(2,1)S(1)}, u32[]{:S(2)}, u32[]{:S(2)}) collective-permute-start(bf16[128,2048]{1,0:T(8,128)(2,1)S(1)} %fusion.13), channel_id=1, source_target_pairs={{0,1},{1,0},{2,3},{3,2},{4,5},{5,4},{6,7},{7,6},{8,9},{9,8},{10,11... | collective-permute-start | bytes 1572872 | tf_op jit(solution)/shard_map/ppermute | solution.py:239
  172.9 13.9 %collective-permute-start.28 = (bf16[128,2048]{1,0:T(8,128)(2,1)S(1)}, bf16[128,2048]{1,0:T(8,128)(2,1)}, u32[]{:S(2)}, u32[]{:S(2)}) collective-permute-start(bf16[128,2048]{1,0:T(8,128)(2,1)S(1)} %fusion.6), channel_id=1, source_target_pairs={{0,4},{2,6},{4,8},{6,10},{8,12},{10,14},{12,0},{14,2},{1,5},{3,7},... | collective-permute-start | bytes 1572872 | tf_op jit(solution)/shard_map/ppermute | solution.py:241
  (2 other events, 2.1 us)

commit v5 on v4

--- a/solution.py
+++ b/solution.py
@@ -15,7 +15,6 @@
 
 EPS = 1e-06
 VMEM_LIMIT = 56 * 1024 * 1024
-BLOCK_VMEM_LIMIT = 8 * 1024 * 1024
 MXU = 256
 
 
@@ -37,15 +36,130 @@
     return jnp.sum(jnp.where(lane == index, side, 0.0), 1, keepdims=True)
 
 
-def gained_kernel(x_ref, gain_ref, out_ref):
+def in_vmem(count):
+    return [pl.BlockSpec(memory_space=pltpu.VMEM)] * count
+
+
+def whole_call(body, outs, operands, after=None, kinds=None, scratch=(), limit=6, cost=None):
+    kinds = kinds or [pltpu.VMEM] * len(operands)
+    count = len(operands)
+
+    token = jax.ShapeDtypeStruct((8, 128), jnp.float32)
+
+    def with_token(*refs):
+        inputs, rest = refs[:count], refs[count + 1 :]
+        results, spare = rest[: len(outs)], rest[len(outs) + 1 :]
+        rest[len(outs)][...] = jnp.zeros((8, 128), jnp.float32)
+        body(*inputs, *results, *spare)
+
+    if after is None:
+        after = jnp.zeros((8, 128), jnp.float32)
+    return pl.pallas_call(
+        with_token,
+        in_specs=[pl.BlockSpec(memory_space=kind) for kind in kinds]
+        + [pl.BlockSpec(memory_space=pl.ANY)],
+        out_specs=in_vmem(len(outs) + 1),
+        out_shape=[*outs, token],
+        scratch_shapes=scratch,
+        compiler_params=pltpu.CompilerParams(vmem_limit_bytes=limit * 1024 * 1024),
+        cost_estimate=cost,
+    )(*operands, after)
+
+
+def opening_kernel(x_ref, gain_ref, out_ref):
     gained = x_ref[...].astype(jnp.float32) * gain_ref[...].astype(jnp.float32)
     out_ref[...] = gained.astype(jnp.bfloat16)
 
 
-def gained(x, gain):
+def stats_kernel(first_ref, second_ref, rows_ref, router_ref, gain_ref, w_ref, small_ref, kv_ref):
+    first = first_ref[...].astype(jnp.float32)
+    second = second_ref[...].astype(jnp.float32)
+    tokens = first.shape[0]
+    squares = [jnp.sum(x * x, 1, keepdims=True) for x in (first, second)]
+    logits = jnp.dot(rows_ref[...], router_ref[...], preferred_element_type=jnp.float32)
+    fill = jnp.zeros((tokens, 128 - 2 - logits.shape[1]), jnp.float32)
+    small = jnp.concatenate([squares[0], squares[1], logits, fill], 1)
+    small_ref[...] = jnp.transpose(small)[: small_ref.shape[0]]
+    attn_in = (first * gain_ref[...].astype(jnp.float32)).astype(jnp.bfloat16)
+    kv_ref[...] = jnp.dot(attn_in, w_ref[...], preferred_element_type=jnp.float32)
+
+
+def sides_kernel(where_ref, mine_ref, other_ref, ids_ref, owner_ref, kv_ref, side_ref, kept_ref, sent_ref):
+    small = mine_ref[...] + other_ref[...]
+    tokens = small.shape[1]
+    fill = jnp.zeros((128 - small.shape[0], tokens), jnp.float32)
+    sums = jnp.transpose(jnp.concatenate([small, fill], 0))
+    lane = lax.broadcasted_iota(jnp.int32, (tokens, 128), 1)
+    first_scale = lax.rsqrt(sums[:, 0:1] / D + EPS)
+    second_scale = lax.rsqrt(sums[:, 1:2] / D + EPS)
+    logits = sums * second_scale
+    ids = ids_ref[...]
+    chosen = lane == ids[:, 0:1] + 2
+    for k in range(1, ids.shape[1]):
+        chosen = chosen | (lane == ids[:, k : k + 1] + 2)
+    top = jnp.max(jnp.where(chosen, logits, -jnp.inf), 1, keepdims=True)
+    weights = jnp.where(chosen, jnp.exp(jnp.where(chosen, logits - top, 0.0)), 0.0)
+    weights = weights / jnp.sum(weights, 1, keepdims=True)
+    side = jnp.where(lane == 1, second_scale, weights)
+    side_ref[...] = jnp.transpose(side)[: side_ref.shape[0]]
+
+    theirs = jnp.where(owner_ref[...] == where_ref[0], 0, 1)
+    hot = (lane == theirs).astype(jnp.float32)
+    row = lax.broadcasted_iota(jnp.int32, (tokens, tokens), 0)
+    column = lax.broadcasted_iota(jnp.int32, (tokens, tokens), 1)
+    before = (column < row).astype(jnp.bfloat16)
+    earlier = jnp.dot(before, hot.astype(jnp.bfloat16), preferred_element_type=jnp.float32)
+    slot = jnp.sum(earlier * hot, 1, keepdims=True).astype(jnp.int32)
+    kv = (kv_ref[...] * first_scale).astype(jnp.bfloat16)
+    for side_of, out_ref in enumerate((kept_ref, sent_ref)):
+        placing = jnp.where((slot == column) & (theirs == side_of), 1.0, 0.0)
+        placing = jnp.transpose(placing).astype(jnp.bfloat16)
+        out = jnp.dot(placing, kv, preferred_element_type=jnp.float32)
+        out_ref[...] = out.astype(jnp.bfloat16)
+
+
+def cache_kernel(kept_ref, arrived_ref, gain_ref, out_ref):
+    gain = gain_ref[...].astype(jnp.float32)
+    for head in range(2 * KVH):
+        columns = slice(head * HD, (head + 1) * HD)
+        x = kept_ref[:, columns].astype(jnp.float32) + arrived_ref[:, columns].astype(jnp.float32)
+        if head < KVH:
+            x = x * lax.rsqrt(jnp.mean(x * x, 1, keepdims=True) + EPS) * gain
+        out_ref[:, columns] = x.astype(jnp.bfloat16)
+
+
+def joined_kernel(first_ref, second_ref, out_ref):
+    tokens = first_ref.shape[1]
+    out_ref[:, :tokens] = first_ref[...]
+    out_ref[:, tokens:] = second_ref[...]
+
+
+def tied(arrays, after):
+    count = len(arrays)
+    anywhere = pl.BlockSpec(memory_space=pl.ANY)
+
+    def kernel(*refs):
+        refs[-1][...] = jnp.zeros((8, 128), jnp.float32)
+
+    shapes = [jax.ShapeDtypeStruct(x.shape, x.dtype) for x in arrays]
     return pl.pallas_call(
-        gained_kernel, out_shape=jax.ShapeDtypeStruct(x.shape, jnp.bfloat16)
-    )(x, gain[None])
+        kernel,
+        in_specs=[anywhere] * (count + 1),
+        out_specs=[anywhere] * count + in_vmem(1),
+        out_shape=[*shapes, jax.ShapeDtypeStruct((8, 128), jnp.float32)],
+        input_output_aliases={n: n for n in range(count)},
+    )(*arrays, after)
+
+
+def sum_kernel(part, count, *refs):
+    terms = [ref[part] if len(ref.shape) == 3 else ref[...] for ref in refs[:count]]
+    refs[count][...] = total(*terms)
+
+
+def summed(part, terms, after):
+    out = jax.ShapeDtypeStruct(terms[-1].shape[-2:], jnp.bfloat16)
+    body = functools.partial(sum_kernel, part, len(terms))
+    return whole_call(body, [out], terms, after)
 
 
 def paired_products(rows, steps):
@@ -81,20 +195,21 @@
 
 
 def loaded(w, after):
-    return pl.pallas_call(
-        lambda source_ref, _, held_ref, sem: load_kernel(source_ref, held_ref, sem),
-        in_specs=[pl.BlockSpec(memory_space=pl.ANY)] * 2,
-        out_specs=pl.BlockSpec(memory_space=pltpu.VMEM),
-        out_shape=pltpu.VMEM(w.shape, w.dtype),
-        scratch_shapes=[pltpu.SemaphoreType.DMA((w.shape[0],))],
-        compiler_params=pltpu.CompilerParams(vmem_limit_bytes=1024 * 1024),
-        cost_estimate=pl.CostEstimate(flops=0, bytes_accessed=2 * w.size, transcendentals=0),
-    )(pltpu.with_memory_space_constraint(w, pltpu.HBM), after)
+    return whole_call(
+        load_kernel,
+        [pltpu.VMEM(w.shape, w.dtype)],
+        [pltpu.with_memory_space_constraint(w, pltpu.HBM)],
+        after,
+        kinds=[pl.ANY],
+        scratch=[pltpu.SemaphoreType.DMA((w.shape[0],))],
+        limit=1,
+        cost=pl.CostEstimate(flops=0, bytes_accessed=2 * w.size, transcendentals=0),
+    )
 
 
 def block_hidden_kernel(
     where_ref, own_ref, other_ref, sib_own_ref, sib_other_ref, side_ref, wg_ref, wu_ref,
-    _, out_ref, x_ref,
+    out_ref, x_ref,
 ):
     rows, width = own_ref.shape
     experts, depth, units = wg_ref.shape
@@ -105,13 +220,13 @@
     x_ref[rows : 2 * rows, mine] = sib_own_ref[...]
     x_ref[rows : 2 * rows, theirs] = sib_other_ref[...]
     side = jnp.transpose(side_ref[...])
-    scale = column_of(side, 0)
-    for e in range(experts):
-        weight = column_of(side, 1 + where_ref[1] + e)
-
-        @pl.loop(0, units // MXU)
-        def _(tile):
-            columns = pl.ds(pl.multiple_of(tile * MXU, MXU), MXU)
+    scale = column_of(side, 1)
+
+    @pl.loop(0, experts)
+    def _(e):
+        weight = column_of(side, 2 + where_ref[1] + e)
+        for tile in range(units // MXU):
+            columns = pl.ds(tile * MXU, MXU)
 
             def step(k):
                 part = pl.ds(k * MXU, MXU)
@@ -126,86 +241,102 @@
             out_ref[e, :, columns] = silu_up(gate, up, scale, weight)
 
 
-def in_vmem(count):
-    return [pl.BlockSpec(memory_space=pltpu.VMEM)] * count
-
-
 def block_hidden(where, chunks, side, w_gate, w_up, after):
     rows, _ = chunks[0].shape
     experts, depth, units = w_gate.shape
-    return pl.pallas_call(
+    return whole_call(
         block_hidden_kernel,
-        in_specs=[pl.BlockSpec(memory_space=pltpu.SMEM)]
-        + in_vmem(7)
-        + [pl.BlockSpec(memory_space=pl.ANY)],
-        out_specs=pl.BlockSpec(memory_space=pltpu.VMEM),
-        scratch_shapes=[pltpu.VMEM((2 * rows, depth), jnp.bfloat16)],
-        out_shape=jax.ShapeDtypeStruct((experts, 2 * rows, units), jnp.bfloat16),
-        compiler_params=pltpu.CompilerParams(vmem_limit_bytes=BLOCK_VMEM_LIMIT),
-        cost_estimate=pl.CostEstimate(
+        [jax.ShapeDtypeStruct((experts, 2 * rows, units), jnp.bfloat16)],
+        [where, *chunks, side, w_gate, w_up],
+        after,
+        kinds=[pltpu.SMEM] + [pltpu.VMEM] * 7,
+        scratch=[pltpu.VMEM((2 * rows, depth), jnp.bfloat16)],
+        cost=pl.CostEstimate(
             flops=8 * rows * depth * units * experts,
             bytes_accessed=4 * rows * depth,
             transcendentals=2 * rows * units * experts,
         ),
-    )(where, *chunks, side, w_gate, w_up, after)
-
-
-def block_down_kernel(where_ref, h_ref, w_ref, _, own_ref, sib_ref):
-    rows = own_ref.shape[1]
+    )
+
+
+def block_down_kernel(where_ref, h_ref, w_ref, own_ref, sib_ref, held_ref, sem):
+    _, rows, width = own_ref.shape
     experts, _, units = h_ref.shape
-
-    def step(e, k):
-        depth = pl.ds(k * MXU, MXU)
-        return (
-            lambda: h_ref[e, :, depth],
-            lambda: w_ref[e, depth, 0:MXU],
-            lambda: w_ref[e, depth, MXU : 2 * MXU],
+    slots, tile = held_ref.shape[0], held_ref.shape[3]
+    tiles = width // tile
+
+    def fetch(n):
+        half, part = n // tiles, n % tiles
+        first = (half + where_ref[0] - 2 * half * where_ref[0]) * width
+        columns = pl.ds(pl.multiple_of(first + part * tile, tile), tile)
+        return pltpu.make_async_copy(
+            w_ref.at[:, :, columns], held_ref.at[n % slots], sem.at[n % slots]
         )
 
-    steps = [step(e, k) for e in range(experts) for k in range(units // MXU)]
-    for half, y in enumerate(paired_products(2 * rows, steps)):
-        columns = slice(half * MXU, (half + 1) * MXU)
-        own_ref[0, :, columns] = y[:rows].astype(jnp.bfloat16)
-        sib_ref[0, :, columns] = y[rows:].astype(jnp.bfloat16)
+    for n in range(slots - 1):
+        fetch(n).start()
+    for n in range(2 * tiles):
+        if n + slots - 1 < 2 * tiles:
+            fetch(n + slots - 1).start()
+        fetch(n).wait()
+
+        def step(e, k):
+            part = pl.ds(k * MXU, MXU)
+            return (
+                lambda: h_ref[e, :, part],
+                lambda: held_ref[n % slots, e, part, 0:MXU],
+                lambda: held_ref[n % slots, e, part, MXU : 2 * MXU],
+            )
+
+        steps = [step(e, k) for e in range(experts) for k in range(units // MXU)]
+        for m, y in enumerate(paired_products(2 * rows, steps)):
+            columns = pl.ds((n % tiles) * tile + m * MXU, MXU)
+            own_ref[n // tiles, :, columns] = y[:rows].astype(jnp.bfloat16)
+            sib_ref[n // tiles, :, columns] = y[rows:].astype(jnp.bfloat16)
 
 
 def block_down(where, hidden, w_down, after):
     experts, tokens, units = hidden.shape
     rows, width = tokens // 2, w_down.shape[2] // 2
-    tile = 2 * MXU
-    tiles = width // tile
-    out_spec = pl.BlockSpec((1, rows, tile), lambda h, n, s: (h, 0, n))
     out = jax.ShapeDtypeStruct((2, rows, width), jnp.bfloat16)
-    return pl.pallas_call(
+    slots = 4
+    return whole_call(
         block_down_kernel,
-        grid_spec=pltpu.PrefetchScalarGridSpec(
-            num_scalar_prefetch=1,
-            grid=(2, tiles),
-            in_specs=[
-                pl.BlockSpec((experts, tokens, units), lambda h, n, s: (0, 0, 0)),
-                pl.BlockSpec(
-                    (experts, units, tile),
-                    lambda h, n, s: (0, 0, (h + s[0] - 2 * h * s[0]) * tiles + n),
-                ),
-                pl.BlockSpec(memory_space=pl.ANY),
-            ],
-            out_specs=[out_spec, out_spec],
-        ),
-        out_shape=[out, out],
-        compiler_params=pltpu.CompilerParams(vmem_limit_bytes=BLOCK_VMEM_LIMIT),
-        cost_estimate=pl.CostEstimate(
+        [out, out],
+        [where, hidden, pltpu.with_memory_space_constraint(w_down, pltpu.HBM)],
+        after,
+        kinds=[pltpu.SMEM, pltpu.VMEM, pl.ANY],
+        scratch=[
+            pltpu.VMEM((slots, experts, units, 2 * MXU), jnp.bfloat16),
+            pltpu.SemaphoreType.DMA((slots,)),
+        ],
+        limit=10,
+        cost=pl.CostEstimate(
             flops=4 * experts * tokens * units * width,
             bytes_accessed=4 * (experts * units + tokens) * width,
             transcendentals=0,
         ),
-    )(where, hidden, pltpu.with_memory_space_constraint(w_down, pltpu.HBM), after)
+    )
 
 
 def total(*terms):
     return sum(term.astype(jnp.float32) for term in terms).astype(jnp.bfloat16)
 
 
-def ring_experts(rows_out, side, w_gate, w_up, w_down):
+def ring_device(
+    layer_input,
+    stream,
+    expert_ids,
+    kv_owner,
+    attn_norm,
+    moe_norm,
+    k_norm,
+    w_kv,
+    router,
+    w_gate,
+    w_up,
+    w_down,
+):
     ep_count = lax.axis_size("ep")
     chips = ep_count // 2
     forward = [(d, (d + 2) % ep_count) for d in range(ep_count)]
@@ -215,31 +346,88 @@
     across = functools.partial(lax.ppermute, axis_name="tp", perm=[(0, 1), (1, 0)])
     where = jnp.stack([lax.axis_index("tp"), lax.axis_index("ep") * w_gate.shape[0]])
     where = where.astype(jnp.int32)
-    w_gate, w_up = [loaded(w, where) for w in (w_gate, w_up)]
-
-    lane, sides = [rows_out], [jnp.concatenate([side, beside(side)], 1)]
+    rows = stream.shape[0]
+    side_rows = -(-(2 + router.shape[1]) // 8) * 8
+    columns = w_kv.shape[1]
+    row_shape = jax.ShapeDtypeStruct(stream.shape, jnp.bfloat16)
+    small_shape = jax.ShapeDtypeStruct((side_rows, rows), jnp.float32)
+    kv_shape = jax.ShapeDtypeStruct((rows, columns), jnp.float32)
+    pair_shape = jax.ShapeDtypeStruct((side_rows, 2 * rows), jnp.float32)
+    placed_shape = jax.ShapeDtypeStruct((rows, columns), jnp.bfloat16)
+
+    rows_out, token = whole_call(opening_kernel, [row_shape], [stream, moe_norm[None]])
+    lane, crossed = [rows_out, along(rows_out)], [across(rows_out)]
+
+    operands = [layer_input, stream, rows_out, router, attn_norm[None], w_kv]
+    small, kv, token = whole_call(
+        stats_kernel, [small_shape, kv_shape], operands, token, limit=16
+    )
+    small_other = across(small)
+    gate_held, token = loaded(w_gate, token)
+    up_held, token = loaded(w_up, token)
+    lane[1], crossed[0], token = tied([lane[1], crossed[0]], token)
+    for _ in range(chips - 2):
+        lane.append(along(lane[-1]))
+    for s in range(1, chips):
+        crossed.append(across(lane[s]))
+
+    operands = [where, small, small_other, expert_ids, kv_owner, kv]
+    side, kept, sent, token = whole_call(
+        sides_kernel,
+        [small_shape, placed_shape, placed_shape],
+        operands,
+        token,
+        kinds=[pltpu.SMEM] + [pltpu.VMEM] * 5,
+    )
+    arrived = across(sent)
+    side, token = whole_call(joined_kernel, [pair_shape], [side, beside(side)], token)
+    sides = [side]
     for _ in range(chips - 1):
-        lane.append(along(lane[-1]))
         sides.append(along(sides[-1]))
-    crossed = [across(chunk) for chunk in lane]
-    hidden, after = [None] * chips, where
-
-    def up_of(s, after):
+
+    hidden, own, back, swapped = [[None] * chips for _ in range(4)]
+
+    def up(s, after):
         chunks = (lane[s], crossed[s], beside(lane[s]), beside(crossed[s]))
-        hidden[s] = block_hidden(where, chunks, sides[s], w_gate, w_up, after)
-        return hidden[s]
-
-    after, travelling = up_of(0, where), None
-    for s in list(range(1, chips)) + [0]:
-        if s:
-            after = up_of(s, after)
-        own, sib = block_down(where, hidden[s], w_down, after)
-        after = own
-        back = beside(sib)
-        swapped = across(total(own[1], back[1]))
-        terms = (own[0], back[0], swapped)
-        travelling = total(*terms) if travelling is None else total(along(travelling), *terms)
-    return travelling
+        hidden[s], after = block_hidden(where, chunks, sides[s], gate_held, up_held, after)
+        return after
+
+    def down(s, after):
+        own[s], sib, after = block_down(where, hidden[s], w_down, after)
+        back[s] = beside(sib)
+        return after
+
+    def swap(s, after):
+        sent, after = summed(1, [own[s], back[s]], after)
+        swapped[s] = across(sent)
+        return after
+
+    def gather(s, travelling, after):
+        terms = [own[s], back[s], swapped[s]] + travelling
+        return summed(0, terms, after)
+
+    token = up(0, token)
+    token = up(1, token)
+    token = down(1, token)
+    kv_cache, token = whole_call(
+        cache_kernel, [placed_shape], [kept, arrived, k_norm[None]], token
+    )
+    token = swap(1, token)
+    travelling = []
+    for s in range(1, chips - 1):
+        token = up(s + 1, token) if s == 1 else token
+        token = down(s + 1, token) if s == 1 else token
+        passed, token = gather(s, travelling, token)
+        travelling = [along(passed)]
+        token = swap(s + 1, token)
+        if s == 1:
+            token = up(3, token)
+            token = down(3, token)
+    token = down(0, token)
+    token = swap(0, token)
+    passed, token = gather(chips - 1, travelling, token)
+    moe_out, token = gather(0, [along(passed)], token)
+    return moe_out, kv_cache.reshape(1, 1, rows, columns)
 
 
 def hidden_kernel(x_ref, wg_ref, wu_ref, scale_ref, weight_ref, out_ref):
@@ -339,23 +527,25 @@
 ):
     rows = layer_input.shape[0]
     tp_count = lax.axis_size("tp")
-    pair = tp_count == 2
+    tiled = w_gate.shape[2] % MXU == 0 and stream.shape[1] % (2 * MXU) == 0
+    if tp_count == 2 and tiled and rows == 128 and lax.axis_size("ep") == 8:
+        return ring_device(
+            layer_input, stream, expert_ids, kv_owner, attn_norm, moe_norm, k_norm, w_kv, router,
+            w_gate, w_up, w_down,
+        )
     columns = 2 * KVH * HD
     expert_count = router.shape[1]
     first = layer_input.astype(jnp.float32)
     second = stream.astype(jnp.float32)
 
-    rows_out = gained(stream, moe_norm)
+    rows_out = (second * moe_norm.astype(jnp.float32)).astype(jnp.bfloat16)
 
     logits = lax.dot_general(
         router, rows_out, (((0,), (1,)), ((), ())), preferred_element_type=jnp.float32
     )
     squares = jnp.stack([jnp.sum(first * first, 1), jnp.sum(second * second, 1)], 0)
     small = jnp.concatenate([squares, logits], 0)
-    if pair:
-        small = small + lax.ppermute(small, "tp", [(0, 1), (1, 0)])
-    else:
-        small = lax.psum(small, "tp")
+    small = lax.psum(small, "tp")
     first_scale = lax.rsqrt(small[0] / D + EPS)
     second_scale = lax.rsqrt(small[1:2] / D + EPS)
     logits = small[2:] * second_scale
@@ -375,20 +565,14 @@
     owner_slot = jnp.sum(
         (jnp.cumsum(owner_hot, 0, dtype=jnp.int32) - owner_hot) * owner_hot, 1, dtype=jnp.int32
     )
-    if pair:
-        owner = jnp.where(owner == lax.axis_index("tp"), 0, 1)
     target = owner * owner_cap + owner_slot
     placing = target[None, :] == jnp.arange(tp_count * owner_cap, dtype=jnp.int32)[:, None]
     placed = jnp.dot(
         placing.astype(jnp.bfloat16), kv.astype(jnp.bfloat16), preferred_element_type=jnp.float32
     )
     placed = placed.astype(jnp.bfloat16).reshape(tp_count, owner_cap, columns)
-    if pair:
-        arrived = lax.ppermute(placed[1], "tp", [(0, 1), (1, 0)])
-        heads = placed[0].astype(jnp.float32) + arrived.astype(jnp.float32)
-    else:
-        arrived = lax.all_to_all(placed, "tp", split_axis=0, concat_axis=0, tiled=True)
-        heads = jnp.sum(arrived.astype(jnp.float32), 0)
+    arrived = lax.all_to_all(placed, "tp", split_axis=0, concat_axis=0, tiled=True)
+    heads = jnp.sum(arrived.astype(jnp.float32), 0)
     heads = heads.reshape(owner_cap, 2 * KVH, HD)
     keys = heads[:, :KVH]
     keys = keys * lax.rsqrt(jnp.mean(keys * keys, 2, keepdims=True) + EPS)
@@ -396,10 +580,7 @@
     kv_cache = jnp.concatenate([keys, heads[:, KVH:]], 1).astype(jnp.bfloat16)
     kv_cache = kv_cache.reshape(1, 1, owner_cap, columns)
 
-    tiled = w_gate.shape[2] % MXU == 0 and stream.shape[1] % (2 * MXU) == 0
-    ringed = pair and tiled and lax.axis_size("ep") % 2 == 0
-    experts = ring_experts if ringed else plain_experts
-    moe_out = experts(rows_out, side, w_gate, w_up, w_down)
+    moe_out = plain_experts(rows_out, side, w_gate, w_up, w_down)
     return (moe_out, kv_cache)
 
 

time: 190 us -> 226 us (1.19)
  waiting for transfers between devices: 40.4 us -> 98.8 us
  Pallas kernels: 92.2 us -> 74.8 us
  local copies, waits for them, and re-layouts: 15.9 us -> 29.7 us
  other arithmetic: 12.2 us -> 0.07 us
  matrix products: 5.36 us -> 0 us
    ppermute x32, waiting for transfers between devices: 40.4 us -> 98.8 us  [the longest x2 27.1 us: ring_device(): travelling = [along(passed)]]
    pallas_call x11 -> x24, Pallas kernels: 92.2 us -> 74.8 us  [the longest x23 74.2 us: whole_call(): pl.pallas_call(with_token, in_specs=[pl.BlockSpec(memory_space=kind) for...]
    unnamed x37 -> x41, local copies, waits for them, and re-layouts: 12.7 us -> 28.3 us
    convert_element_type x11 -> x0, other arithmetic: 6.55 us -> none  [the longest x8 5.81 us: total(): sum((term.astype(jnp.float32) for term in terms)).astype(jnp.bfloat16)]
    dot_general x2 -> x0, matrix products: 5.36 us -> none  [the longest x1 4.08 us: per_device(): jnp.dot(placing.astype(jnp.bfloat16), kv.astype(jnp.bfloat16), preferred_...]
    reduce_sum x5 -> x0, other arithmetic: 3.53 us -> none  [the longest x1 1.25 us: per_device(): jnp.sum(first * first, 1)]
  transfers between devices with their start and end apart: 32 -> 32, of which waited for: 10 -> 10; matrix products, arithmetic and copies ran while one was open for 9% -> 1% of each run, Pallas kernels for 48% -> 23%
where the time goes in v5:
time: 226 us
  waiting for transfers between devices  98.8 us (44%)
  Pallas kernels  74.8 us (33%)
  local copies, waits for them, and re-layouts  29.7 us (13%)
  starting transfers between devices  21.5 us (10%)
    pallas_call x23, Pallas kernels, whole_call(): pl.pallas_call(with_token, in_specs=[pl.BlockSpec(memory_space=kind) for...  74.2 us
    unnamed x41, local copies, waits for them, and re-layouts  28.3 us
    ppermute x2, waiting for transfers between devices, ring_device(): travelling = [along(passed)]  27.1 us
    ppermute x3, waiting for transfers between devices, ring_device(): crossed.append(across(lane[s]))  26.1 us
    ppermute x1, waiting for transfers between devices, ring_device(): moe_out, token = gather(0, [along(passed)], token)  14.2 us
    ppermute x1, waiting for transfers between devices, ring_device(): small_other = across(small)  12.3 us
    ppermute x4, waiting for transfers between devices, swap(): swapped[s] = across(sent)  9.19 us
    ppermute x1, waiting for transfers between devices, ring_device(): arrived = across(sent)  8.1 us
  transfers between devices with their start and end apart: 32, of which 10 were waited for; matrix products, arithmetic and copies ran while one was open for 1% of the time, Pallas kernels for 23%

profile of v5, /device:TPU:0, one launch (start us, length us, event | category | flops | bytes accessed | tf_op | source)
XLA Modules:
  0.0 225.9 jit_solution(14427243173077060464)
XLA Ops:
  0.6 0.7 broadcast_in_dim.12.refs_1_
  1.3 1.0 copy-done.11
  2.5 3.1 %collective-permute-start = (bf16[128,2048]{1,0:T(8,128)(2,1)S(1)}, bf16[128,2048]{1,0:T(8,128)(2,1)S(1)}, u32[]{:S(2)}, u32[]{:S(2)}) collective-permute-start(bf16[128,2048]{1,0:T(8,128)(2,1)S(1)} %get-tuple-element.57.refs_2_.refs_1_), channel_id=1, source_target_pairs={{0,4},{2,6},{4,8},{6,10},{8,12},{10,14},{12,0},{14,2},{1,5},{3,7},... | collective-permute-start | bytes 1572872 | tf_op jit(solution)/shard_map/ppermute | solution.py:359
  5.5 1.5 collective-permute-start.1
  7.0 1.1 copy.16.refs_3_
  8.2 0.7 broadcast_in_dim.14.refs_4_
  8.9 2.2 copy-done.6
  11.0 1.0 copy-done.12
  12.1 1.0 copy-done.13
  13.1 1.1 shard_map.132
  14.2 4.6 %shard_map.133 = (bf16[2,4096,768]{2,1,0:T(8,128)(2,1)S(1)}, f32[8,128]{1,0:T(8,128)S(1)}) custom-call(bf16[2,4096,768]{2,1,0:T(8,128)(2,1)} %refs_0_.6, f32[8,128]{1,0:T(8,128)S(1)} %get-tuple-element.59.refs_1_), custom_call_target="tpu_custom_call" | custom-call | bytes 12582912 | tf_op jit(solution)/shard_map/pallas_call | solution.py:57
  18.9 4.6 %copy-done = bf16[2,4096,768]{2,1,0:T(8,128)(2,1)} copy-done((bf16[2,4096,768]{2,1,0:T(8,128)(2,1)}, bf16[2,4096,768]{2,1,0:T(8,128)(2,1)S(1)}, u32[]{:S(2)}) %copy-start) | copy-done | bytes 12582936
  23.4 4.6 %shard_map.134 = (bf16[2,4096,768]{2,1,0:T(8,128)(2,1)S(1)}, f32[8,128]{1,0:T(8,128)S(1)}) custom-call(bf16[2,4096,768]{2,1,0:T(8,128)(2,1)} %refs_0_.7, f32[8,128]{1,0:T(8,128)S(1)} %get-tuple-element.60.refs_1_), custom_call_target="tpu_custom_call" | custom-call | bytes 12582912 | tf_op jit(solution)/shard_map/pallas_call | solution.py:57
  28.1 4.6 %copy-done.3 = bf16[2,4096,768]{2,1,0:T(8,128)(2,1)} copy-done((bf16[2,4096,768]{2,1,0:T(8,128)(2,1)}, bf16[2,4096,768]{2,1,0:T(8,128)(2,1)S(1)}, u32[]{:S(2)}) %copy-start.3) | copy-done | bytes 12582936
  33.3 0.8 copy-done.7
  34.2 0.6 shard_map.135
  35.6 1.5 collective-permute-start.4
  37.4 12.3 %collective-permute-done.4.refs_2_ = f32[24,128]{1,0:T(8,128)S(1)} collective-permute-done((f32[24,128]{1,0:T(8,128)S(1)}, f32[24,128]{1,0:T(8,128)S(1)}, u32[]{:S(2)}, u32[]{:S(2)}) %collective-permute-start.4) | collective-permute-done | bytes 12320 | tf_op jit(solution)/shard_map/ppermute | solution.py:365
  49.6 0.7 copy-done.14
  50.3 1.4 shard_map.136
  52.3 0.7 collective-permute-done.5.refs_1_
  52.9 1.6 collective-permute-start.6
  54.5 1.6 collective-permute-start.11
  56.1 4.6 %copy-done.1 = bf16[2,4096,768]{2,1,0:T(8,128)(2,1)S(1)} copy-done((bf16[2,4096,768]{2,1,0:T(8,128)(2,1)S(1)}, bf16[2,4096,768]{2,1,0:T(8,128)(2,1)}, u32[]{:S(2)}) %copy-start.1) | copy-done | bytes 12582936
  60.7 4.6 %copy-done.4 = bf16[2,4096,768]{2,1,0:T(8,128)(2,1)S(1)} copy-done((bf16[2,4096,768]{2,1,0:T(8,128)(2,1)S(1)}, bf16[2,4096,768]{2,1,0:T(8,128)(2,1)}, u32[]{:S(2)}) %copy-start.4) | copy-done | bytes 12582936
  65.2 1.0 copy-done.10
  66.3 8.1 %shard_map.138 = (bf16[2,256,768]{2,1,0:T(8,128)(2,1)S(1)}, f32[8,128]{1,0:T(8,128)S(1)}) custom-call(s32[2]{0:T(128)S(1)} %pad_add_fusion.refs_0_, bf16[128,2048]{1,0:T(8,128)(2,1)S(1)} %get-tuple-element.57.refs_2_.refs_1_, bf16[128,2048]{1,0:T(8,128)(2,1)S(1)} %copy-done.10, bf16[128,2048]{1,0:T(8,128)(2,1)S(1)} %collective-permute-done.2.refs_3_, ...), custom_call_target="tpu_custom_call" | custom-call | flops 6442450944 | bytes 2097152 | tf_op jit(solution)/shard_map/pallas_call | solution.py:57
  74.6 8.2 %shard_map.139 = (bf16[2,256,768]{2,1,0:T(8,128)(2,1)S(1)}, f32[8,128]{1,0:T(8,128)S(1)}) custom-call(s32[2]{0:T(128)S(1)} %pad_add_fusion.refs_0_, bf16[128,2048]{1,0:T(8,128)(2,1)S(1)} %copy-done.8, bf16[128,2048]{1,0:T(8,128)(2,1)S(1)} %collective-permute-done.17.refs_2_, bf16[128,2048]{1,0:T(8,128)(2,1)S(1)} %collective-permute-done.18.refs_3_, ...), custom_call_target="tpu_custom_call" | custom-call | flops 6442450944 | bytes 2097152 | tf_op jit(solution)/shard_map/pallas_call | solution.py:57
  82.8 6.6 %shard_map.140 = (bf16[2,128,2048]{2,1,0:T(8,128)(2,1)S(1)}, bf16[2,128,2048]{2,1,0:T(8,128)(2,1)S(1)}, f32[8,128]{1,0:T(8,128)S(1)}) custom-call(s32[2]{0:T(128)S(1)} %pad_add_fusion.refs_0_, bf16[2,256,768]{2,1,0:T(8,128)(2,1)S(1)} %get-tuple-element.75.refs_1_, bf16[2,768,4096]{2,1,0:T(8,128)(2,1)} %refs_2_.7, f32[8,128]{1,0:T(8,128)S(1)} %get-tuple-element.76.refs_3_), custom_call_target="tpu_custom_call" | custom-call | flops 3221225472 | bytes 14680064 | tf_op jit(solution)/shard_map/pallas_call | solution.py:57
  90.5 13.4 %collective-permute-done.14.refs_2_ = bf16[128,2048]{1,0:T(8,128)(2,1)S(1)} collective-permute-done((bf16[128,2048]{1,0:T(8,128)(2,1)S(1)}, bf16[128,2048]{1,0:T(8,128)(2,1)S(1)}, u32[]{:S(2)}, u32[]{:S(2)}) %collective-permute-start.14) | collective-permute-done | bytes 524320 | tf_op jit(solution)/shard_map/ppermute | solution.py:372
  104.5 8.1 %collective-permute-done.21.refs_1_ = bf16[128,1024]{1,0:T(8,128)(2,1)S(1)} collective-permute-done((bf16[128,1024]{1,0:T(8,128)(2,1)S(1)}, bf16[128,1024]{1,0:T(8,128)(2,1)S(1)}, u32[]{:S(2)}, u32[]{:S(2)}) %collective-permute-start.21) | collective-permute-done | bytes 262176 | tf_op jit(solution)/shard_map/ppermute | solution.py:382
  112.9 0.9 shard_map.141
  113.9 8.2 %shard_map.143 = (bf16[2,256,768]{2,1,0:T(8,128)(2,1)S(1)}, f32[8,128]{1,0:T(8,128)S(1)}) custom-call(s32[2]{0:T(128)S(1)} %pad_add_fusion.refs_0_, bf16[128,2048]{1,0:T(8,128)(2,1)S(1)} %collective-permute-done.6.refs_1_, bf16[128,2048]{1,0:T(8,128)(2,1)S(1)} %collective-permute-done.14.refs_2_, bf16[128,2048]{1,0:T(8,128)(2,1)S(1)} %collective-permute-done.15.refs_3_, ...), custom_call_target="tpu_custom_call" | custom-call | flops 6442450944 | bytes 2097152 | tf_op jit(solution)/shard_map/pallas_call | solution.py:57
  122.1 6.6 %shard_map.144 = (bf16[2,128,2048]{2,1,0:T(8,128)(2,1)S(1)}, bf16[2,128,2048]{2,1,0:T(8,128)(2,1)S(1)}, f32[8,128]{1,0:T(8,128)S(1)}) custom-call(s32[2]{0:T(128)S(1)} %pad_add_fusion.refs_0_, bf16[2,256,768]{2,1,0:T(8,128)(2,1)S(1)} %get-tuple-element.84.refs_1_, bf16[2,768,4096]{2,1,0:T(8,128)(2,1)} %refs_2_.7, f32[8,128]{1,0:T(8,128)S(1)} %get-tuple-element.85.refs_3_), custom_call_target="tpu_custom_call" | custom-call | flops 3221225472 | bytes 14680064 | tf_op jit(solution)/shard_map/pallas_call | solution.py:57
  129.3 1.6 collective-permute-start.23
  131.0 12.7 %collective-permute-done.8.refs_2_ = bf16[128,2048]{1,0:T(8,128)(2,1)S(1)} collective-permute-done((bf16[128,2048]{1,0:T(8,128)(2,1)S(1)}, bf16[128,2048]{1,0:T(8,128)(2,1)S(1)}, u32[]{:S(2)}, u32[]{:S(2)}) %collective-permute-start.8) | collective-permute-done | bytes 524320 | tf_op jit(solution)/shard_map/ppermute | solution.py:372
  143.7 1.6 collective-permute-start.13
  145.2 9.2 %collective-permute-done.23.refs_2_ = bf16[128,2048]{1,0:T(8,128)(2,1)S(1)} collective-permute-done((bf16[128,2048]{1,0:T(8,128)(2,1)S(1)}, bf16[128,2048]{1,0:T(8,128)(2,1)S(1)}, u32[]{:S(2)}, u32[]{:S(2)}) %collective-permute-start.23) | collective-permute-done | bytes 524320 | tf_op jit(solution)/shard_map/ppermute | solution.py:402
  154.8 8.2 %shard_map.147 = (bf16[2,256,768]{2,1,0:T(8,128)(2,1)S(1)}, f32[8,128]{1,0:T(8,128)S(1)}) custom-call(s32[2]{0:T(128)S(1)} %pad_add_fusion.refs_0_, bf16[128,2048]{1,0:T(8,128)(2,1)S(1)} %collective-permute-done.7.refs_1_, bf16[128,2048]{1,0:T(8,128)(2,1)S(1)} %collective-permute-done.8.refs_2_, bf16[128,2048]{1,0:T(8,128)(2,1)S(1)} %collective-permute-done.9.refs_3_, ...), custom_call_target="tpu_custom_call" | custom-call | flops 6442450944 | bytes 2097152 | tf_op jit(solution)/shard_map/pallas_call | solution.py:57
  163.0 6.6 %shard_map.148 = (bf16[2,128,2048]{2,1,0:T(8,128)(2,1)S(1)}, bf16[2,128,2048]{2,1,0:T(8,128)(2,1)S(1)}, f32[8,128]{1,0:T(8,128)S(1)}) custom-call(s32[2]{0:T(128)S(1)} %pad_add_fusion.refs_0_, bf16[2,256,768]{2,1,0:T(8,128)(2,1)S(1)} %get-tuple-element.92.refs_1_, bf16[2,768,4096]{2,1,0:T(8,128)(2,1)} %refs_2_.7, f32[8,128]{1,0:T(8,128)S(1)} %get-tuple-element.93.refs_3_), custom_call_target="tpu_custom_call" | custom-call | flops 3221225472 | bytes 14680064 | tf_op jit(solution)/shard_map/pallas_call | solution.py:57
  169.7 1.9 collective-permute-start.26
  172.1 13.8 %collective-permute-done.26.refs_3_ = bf16[128,2048]{1,0:T(8,128)(2,1)S(1)} collective-permute-done((bf16[128,2048]{1,0:T(8,128)(2,1)S(1)}, bf16[128,2048]{1,0:T(8,128)(2,1)S(1)}, u32[]{:S(2)}, u32[]{:S(2)}) %collective-permute-start.26) | collective-permute-done | bytes 524320 | tf_op jit(solution)/shard_map/ppermute | solution.py:421
  186.4 6.6 %shard_map.151 = (bf16[2,128,2048]{2,1,0:T(8,128)(2,1)S(1)}, bf16[2,128,2048]{2,1,0:T(8,128)(2,1)S(1)}, f32[8,128]{1,0:T(8,128)S(1)}) custom-call(s32[2]{0:T(128)S(1)} %pad_add_fusion.refs_0_, bf16[2,256,768]{2,1,0:T(8,128)(2,1)S(1)} %get-tuple-element.72.refs_1_, bf16[2,768,4096]{2,1,0:T(8,128)(2,1)} %refs_2_.7, f32[8,128]{1,0:T(8,128)S(1)} %get-tuple-element.100.refs_3_), custom_call_target="tpu_custom_call" | custom-call | flops 3221225472 | bytes 14680064 | tf_op jit(solution)/shard_map/pallas_call | solution.py:57
  193.1 1.1 collective-permute-start.30
  194.7 1.1 collective-permute-done.27.refs_1_
  195.9 13.4 %collective-permute-done.30.refs_3_ = bf16[128,2048]{1,0:T(8,128)(2,1)S(1)} collective-permute-done((bf16[128,2048]{1,0:T(8,128)(2,1)S(1)}, bf16[128,2048]{1,0:T(8,128)(2,1)S(1)}, u32[]{:S(2)}, u32[]{:S(2)}) %collective-permute-start.30) | collective-permute-done | bytes 524320 | tf_op jit(solution)/shard_map/ppermute | solution.py:421
  210.6 14.2 %collective-permute-done.31.refs_3_ = bf16[128,2048]{1,0:T(8,128)(2,1)S(1)} collective-permute-done((bf16[128,2048]{1,0:T(8,128)(2,1)S(1)}, bf16[128,2048]{1,0:T(8,128)(2,1)S(1)}, u32[]{:S(2)}, u32[]{:S(2)}) %collective-permute-start.31) | collective-permute-done | bytes 524320 | tf_op jit(solution)/shard_map/ppermute | solution.py:429
  224.8 1.1 shard_map.154
  (85 shorter events, 8.7 us)
Async XLA Ops:
  1.3 1.0 copy-start.11
  2.5 30.8 %collective-permute-start = (bf16[128,2048]{1,0:T(8,128)(2,1)S(1)}, bf16[128,2048]{1,0:T(8,128)(2,1)S(1)}, u32[]{:S(2)}, u32[]{:S(2)}) collective-permute-start(bf16[128,2048]{1,0:T(8,128)(2,1)S(1)} %get-tuple-element.57.refs_2_.refs_1_), channel_id=1, source_target_pairs={{0,4},{2,6},{4,8},{6,10},{8,12},{10,14},{12,0},{14,2},{1,5},{3,7},... | collective-permute-start | bytes 1572872 | tf_op jit(solution)/shard_map/ppermute | solution.py:359
  5.5 27.7 %collective-permute-start.1 = (bf16[128,2048]{1,0:T(8,128)(2,1)S(1)}, bf16[128,2048]{1,0:T(8,128)(2,1)S(1)}, u32[]{:S(2)}, u32[]{:S(2)}) collective-permute-start(bf16[128,2048]{1,0:T(8,128)(2,1)S(1)} %get-tuple-element.57.refs_2_.refs_1_), channel_id=1, source_target_pairs={{0,1},{1,0},{2,3},{3,2},{4,5},{5,4},{6,7},{7,6},{8,9},{9,8},{10,11... | collective-permute-start | bytes 1572872 | tf_op jit(solution)/shard_map/ppermute | solution.py:359
  7.0 47.5 %collective-permute-start.2 = (bf16[128,2048]{1,0:T(8,128)(2,1)S(1)}, bf16[128,2048]{1,0:T(8,128)(2,1)S(1)}, u32[]{:S(2)}, u32[]{:S(2)}) collective-permute-start(bf16[128,2048]{1,0:T(8,128)(2,1)S(1)} %get-tuple-element.57.refs_2_.refs_1_), channel_id=1, source_target_pairs={{0,2},{2,0},{4,6},{6,4},{8,10},{10,8},{12,14},{14,12},{1,3},{3,1},... | collective-permute-start | bytes 1572872 | tf_op jit(solution)/shard_map/ppermute | solution.py:391
  8.9 2.2 copy-start.6
  11.0 1.0 copy-start.12
  12.1 1.0 copy-start.13
  14.2 23.0 %copy-start.17 = (s32[128,8]{0,1:T(8,128)S(1)}, s32[128,8]{0,1:T(8,128)}, u32[]{:S(2)}) copy-start(s32[128,8]{0,1:T(8,128)} %param.14) | copy-start | bytes 12292
  14.2 23.0 %copy-start.18 = (s32[128,1]{0,1:T(1,128)S(1)}, s32[128,1]{0,1:T(1,128)}, u32[]{:S(2)}) copy-start(s32[128,1]{0,1:T(1,128)} %param.15) | copy-start | bytes 1540
  18.9 4.6 %copy-start = (bf16[2,4096,768]{2,1,0:T(8,128)(2,1)}, bf16[2,4096,768]{2,1,0:T(8,128)(2,1)S(1)}, u32[]{:S(2)}) copy-start(bf16[2,4096,768]{2,1,0:T(8,128)(2,1)S(1)} %get-tuple-element.69.refs_6_) | copy-start | bytes 37748740
  28.1 4.6 %copy-start.3 = (bf16[2,4096,768]{2,1,0:T(8,128)(2,1)}, bf16[2,4096,768]{2,1,0:T(8,128)(2,1)S(1)}, u32[]{:S(2)}) copy-start(bf16[2,4096,768]{2,1,0:T(8,128)(2,1)S(1)} %get-tuple-element.70.refs_7_) | copy-start | bytes 37748740
  33.3 1.0 copy-start.9
  34.8 21.3 %collective-permute-start.17 = (bf16[128,2048]{1,0:T(8,128)(2,1)}, bf16[128,2048]{1,0:T(8,128)(2,1)S(1)}, u32[]{:S(2)}, u32[]{:S(2)}) collective-permute-start(bf16[128,2048]{1,0:T(8,128)(2,1)} %get-tuple-element.73.refs_1_), channel_id=1, source_target_pairs={{0,1},{1,0},{2,3},{3,2},{4,5},{5,4},{6,7},{7,6},{8,9},{9,8},{10,11... | collective-permute-start | bytes 1572872 | tf_op jit(solution)/shard_map/ppermute | solution.py:372
  35.4 20.7 %collective-permute-start.3 = (bf16[128,2048]{1,0:T(8,128)(2,1)}, bf16[128,2048]{1,0:T(8,128)(2,1)S(1)}, u32[]{:S(2)}, u32[]{:S(2)}) collective-permute-start(bf16[128,2048]{1,0:T(8,128)(2,1)} %get-tuple-element.62.refs_2_), channel_id=1, source_target_pairs={{0,2},{2,0},{4,6},{6,4},{8,10},{10,8},{12,14},{14,12},{1,3},{3,1},... | collective-permute-start | bytes 1572872 | tf_op jit(solution)/shard_map/ppermute | solution.py:391
  35.6 14.0 %collective-permute-start.4 = (f32[24,128]{1,0:T(8,128)S(1)}, f32[24,128]{1,0:T(8,128)S(1)}, u32[]{:S(2)}, u32[]{:S(2)}) collective-permute-start(f32[24,128]{1,0:T(8,128)S(1)} %get-tuple-element.63.refs_1_), channel_id=1, source_target_pairs={{0,1},{1,0},{2,3},{3,2},{4,5},{5,4},{6,7},{7,6},{8,9},{9,8},{10,11... | collective-permute-start | bytes 36872 | tf_op jit(solution)/shard_map/ppermute | solution.py:365
  51.7 1.2 collective-permute-start.5
  51.8 22.6 %collective-permute-start.18 = (bf16[128,2048]{1,0:T(8,128)(2,1)}, bf16[128,2048]{1,0:T(8,128)(2,1)S(1)}, u32[]{:S(2)}, u32[]{:S(2)}) collective-permute-start(bf16[128,2048]{1,0:T(8,128)(2,1)} %get-tuple-element.73.refs_1_), channel_id=1, source_target_pairs={{0,2},{2,0},{4,6},{6,4},{8,10},{10,8},{12,14},{14,12},{1,3},{3,1},... | collective-permute-start | bytes 1572872 | tf_op jit(solution)/shard_map/ppermute | solution.py:391
  52.9 37.1 %collective-permute-start.6 = (bf16[128,2048]{1,0:T(8,128)(2,1)}, bf16[128,2048]{1,0:T(8,128)(2,1)S(1)}, u32[]{:S(2)}, u32[]{:S(2)}) collective-permute-start(bf16[128,2048]{1,0:T(8,128)(2,1)} %get-tuple-element.73.refs_1_), channel_id=1, source_target_pairs={{0,4},{2,6},{4,8},{6,10},{8,12},{10,14},{12,0},{14,2},{1,5},{3,7},... | collective-permute-start | bytes 1572872 | tf_op jit(solution)/shard_map/ppermute | solution.py:370
  54.5 19.9 %collective-permute-start.11 = (f32[24,256]{1,0:T(8,128)S(1)}, f32[24,256]{1,0:T(8,128)S(1)}, u32[]{:S(2)}, u32[]{:S(2)}) collective-permute-start(f32[24,256]{1,0:T(8,128)S(1)} %get-tuple-element.68.refs_5_), channel_id=1, source_target_pairs={{0,4},{2,6},{4,8},{6,10},{8,12},{10,14},{12,0},{14,2},{1,5},{3,7},... | collective-permute-start | bytes 73736 | tf_op jit(solution)/shard_map/ppermute | solution.py:386
  56.1 18.3 %collective-permute-start.19 = (bf16[128,2048]{1,0:T(8,128)(2,1)S(1)}, bf16[128,2048]{1,0:T(8,128)(2,1)S(1)}, u32[]{:S(2)}, u32[]{:S(2)}) collective-permute-start(bf16[128,2048]{1,0:T(8,128)(2,1)S(1)} %collective-permute-done.17.refs_2_), channel_id=1, source_target_pairs={{0,2},{2,0},{4,6},{6,4},{8,10},{10,8},{12,14},{14,12},{1,3},{3,1},... | collective-permute-start | bytes 1572872 | tf_op jit(solution)/shard_map/ppermute | solution.py:391
  56.1 4.6 %copy-start.1 = (bf16[2,4096,768]{2,1,0:T(8,128)(2,1)S(1)}, bf16[2,4096,768]{2,1,0:T(8,128)(2,1)}, u32[]{:S(2)}) copy-start(bf16[2,4096,768]{2,1,0:T(8,128)(2,1)} %copy-done) | copy-start | bytes 37748740
  60.7 4.6 %copy-start.4 = (bf16[2,4096,768]{2,1,0:T(8,128)(2,1)S(1)}, bf16[2,4096,768]{2,1,0:T(8,128)(2,1)}, u32[]{:S(2)}) copy-start(bf16[2,4096,768]{2,1,0:T(8,128)(2,1)} %copy-done.3) | copy-start | bytes 37748740
  65.2 1.0 copy-start.10
  66.3 8.1 %copy-start.2 = (bf16[2,4096,768]{2,1,0:T(8,128)(2,1)S(1)}, bf16[2,4096,768]{2,1,0:T(8,128)(2,1)}, u32[]{:S(2)}) copy-start(bf16[2,4096,768]{2,1,0:T(8,128)(2,1)} %copy-done) | copy-start | bytes 37748740
  66.3 8.2 %copy-start.5 = (bf16[2,4096,768]{2,1,0:T(8,128)(2,1)S(1)}, bf16[2,4096,768]{2,1,0:T(8,128)(2,1)}, u32[]{:S(2)}) copy-start(bf16[2,4096,768]{2,1,0:T(8,128)(2,1)} %copy-done.3) | copy-start | bytes 37748740
  66.3 8.3 %copy-start.8 = (bf16[128,2048]{1,0:T(8,128)(2,1)S(1)}, bf16[128,2048]{1,0:T(8,128)(2,1)}, u32[]{:S(2)}) copy-start(bf16[128,2048]{1,0:T(8,128)(2,1)} %get-tuple-element.73.refs_1_) | copy-start | bytes 1572868
  82.7 30.1 %copy-start.16 = (bf16[128]{0:T(256)(128)(2,1)S(1)}, bf16[128]{0:T(256)(128)(2,1)}, u32[]{:S(2)}) copy-start(bf16[128]{0:T(256)(128)(2,1)} %param.18) | copy-start | bytes 772
  89.4 24.3 %collective-permute-start.20 = (bf16[2,128,2048]{2,1,0:T(8,128)(2,1)S(1)}, bf16[2,128,2048]{2,1,0:T(8,128)(2,1)S(1)}, u32[]{:S(2)}, u32[]{:S(2)}) collective-permute-start(bf16[2,128,2048]{2,1,0:T(8,128)(2,1)S(1)} %get-tuple-element.78), channel_id=1, source_target_pairs={{0,2},{2,0},{4,6},{6,4},{8,10},{10,8},{12,14},{14,12},{1,3},{3,1},... | collective-permute-start | bytes 3145736 | tf_op jit(solution)/shard_map/ppermute | solution.py:397
  90.0 13.9 %collective-permute-start.14 = (bf16[128,2048]{1,0:T(8,128)(2,1)S(1)}, bf16[128,2048]{1,0:T(8,128)(2,1)S(1)}, u32[]{:S(2)}, u32[]{:S(2)}) collective-permute-start(bf16[128,2048]{1,0:T(8,128)(2,1)S(1)} %collective-permute-done.6.refs_1_), channel_id=1, source_target_pairs={{0,1},{1,0},{2,3},{3,2},{4,5},{5,4},{6,7},{7,6},{8,9},{9,8},{10,11... | collective-permute-start | bytes 1572872 | tf_op jit(solution)/shard_map/ppermute | solution.py:372
  90.5 23.4 %collective-permute-start.15 = (bf16[128,2048]{1,0:T(8,128)(2,1)S(1)}, bf16[128,2048]{1,0:T(8,128)(2,1)S(1)}, u32[]{:S(2)}, u32[]{:S(2)}) collective-permute-start(bf16[128,2048]{1,0:T(8,128)(2,1)S(1)} %collective-permute-done.6.refs_1_), channel_id=1, source_target_pairs={{0,2},{2,0},{4,6},{6,4},{8,10},{10,8},{12,14},{14,12},{1,3},{3,1},... | collective-permute-start | bytes 1572872 | tf_op jit(solution)/shard_map/ppermute | solution.py:391
  103.9 10.0 %collective-permute-start.16 = (bf16[128,2048]{1,0:T(8,128)(2,1)S(1)}, bf16[128,2048]{1,0:T(8,128)(2,1)S(1)}, u32[]{:S(2)}, u32[]{:S(2)}) collective-permute-start(bf16[128,2048]{1,0:T(8,128)(2,1)S(1)} %collective-permute-done.14.refs_2_), channel_id=1, source_target_pairs={{0,2},{2,0},{4,6},{6,4},{8,10},{10,8},{12,14},{14,12},{1,3},{3,1},... | collective-permute-start | bytes 1572872 | tf_op jit(solution)/shard_map/ppermute | solution.py:391
  103.9 8.7 %collective-permute-start.21 = (bf16[128,1024]{1,0:T(8,128)(2,1)S(1)}, bf16[128,1024]{1,0:T(8,128)(2,1)S(1)}, u32[]{:S(2)}, u32[]{:S(2)}) collective-permute-start(bf16[128,1024]{1,0:T(8,128)(2,1)S(1)} %get-tuple-element.80), channel_id=1, source_target_pairs={{0,1},{1,0},{2,3},{3,2},{4,5},{5,4},{6,7},{7,6},{8,9},{9,8},{10,11... | collective-permute-start | bytes 786440 | tf_op jit(solution)/shard_map/ppermute | solution.py:382
  104.5 9.4 %collective-permute-start.12 = (f32[24,256]{1,0:T(8,128)S(1)}, f32[24,256]{1,0:T(8,128)S(1)}, u32[]{:S(2)}, u32[]{:S(2)}) collective-permute-start(f32[24,256]{1,0:T(8,128)S(1)} %collective-permute-done.11.refs_5_), channel_id=1, source_target_pairs={{0,4},{2,6},{4,8},{6,10},{8,12},{10,14},{12,0},{14,2},{1,5},{3,7},... | collective-permute-start | bytes 73736 | tf_op jit(solution)/shard_map/ppermute | solution.py:386
  112.6 16.2 %collective-permute-start.7 = (bf16[128,2048]{1,0:T(8,128)(2,1)S(1)}, bf16[128,2048]{1,0:T(8,128)(2,1)S(1)}, u32[]{:S(2)}, u32[]{:S(2)}) collective-permute-start(bf16[128,2048]{1,0:T(8,128)(2,1)S(1)} %collective-permute-done.6.refs_1_), channel_id=1, source_target_pairs={{0,4},{2,6},{4,8},{6,10},{8,12},{10,14},{12,0},{14,2},{1,5},{3,7},... | collective-permute-start | bytes 1572872 | tf_op jit(solution)/shard_map/ppermute | solution.py:370
  128.8 25.9 %collective-permute-start.22 = (bf16[2,128,2048]{2,1,0:T(8,128)(2,1)S(1)}, bf16[2,128,2048]{2,1,0:T(8,128)(2,1)S(1)}, u32[]{:S(2)}, u32[]{:S(2)}) collective-permute-start(bf16[2,128,2048]{2,1,0:T(8,128)(2,1)S(1)} %get-tuple-element.87), channel_id=1, source_target_pairs={{0,2},{2,0},{4,6},{6,4},{8,10},{10,8},{12,14},{14,12},{1,3},{3,1},... | collective-permute-start | bytes 3145736 | tf_op jit(solution)/shard_map/ppermute | solution.py:397
  128.9 14.8 %collective-permute-start.8 = (bf16[128,2048]{1,0:T(8,128)(2,1)S(1)}, bf16[128,2048]{1,0:T(8,128)(2,1)S(1)}, u32[]{:S(2)}, u32[]{:S(2)}) collective-permute-start(bf16[128,2048]{1,0:T(8,128)(2,1)S(1)} %collective-permute-done.7.refs_1_), channel_id=1, source_target_pairs={{0,1},{1,0},{2,3},{3,2},{4,5},{5,4},{6,7},{7,6},{8,9},{9,8},{10,11... | collective-permute-start | bytes 1572872 | tf_op jit(solution)/shard_map/ppermute | solution.py:372
  129.3 25.1 %collective-permute-start.23 = (bf16[128,2048]{1,0:T(8,128)(2,1)S(1)}, bf16[128,2048]{1,0:T(8,128)(2,1)S(1)}, u32[]{:S(2)}, u32[]{:S(2)}) collective-permute-start(bf16[128,2048]{1,0:T(8,128)(2,1)S(1)} %get-tuple-element.88), channel_id=1, source_target_pairs={{0,1},{1,0},{2,3},{3,2},{4,5},{5,4},{6,7},{7,6},{8,9},{9,8},{10,11... | collective-permute-start | bytes 1572872 | tf_op jit(solution)/shard_map/ppermute | solution.py:402
  131.0 23.8 %collective-permute-start.9 = (bf16[128,2048]{1,0:T(8,128)(2,1)S(1)}, bf16[128,2048]{1,0:T(8,128)(2,1)S(1)}, u32[]{:S(2)}, u32[]{:S(2)}) collective-permute-start(bf16[128,2048]{1,0:T(8,128)(2,1)S(1)} %collective-permute-done.7.refs_1_), channel_id=1, source_target_pairs={{0,2},{2,0},{4,6},{6,4},{8,10},{10,8},{12,14},{14,12},{1,3},{3,1},... | collective-permute-start | bytes 1572872 | tf_op jit(solution)/shard_map/ppermute | solution.py:391
  143.7 11.1 %collective-permute-start.10 = (bf16[128,2048]{1,0:T(8,128)(2,1)S(1)}, bf16[128,2048]{1,0:T(8,128)(2,1)S(1)}, u32[]{:S(2)}, u32[]{:S(2)}) collective-permute-start(bf16[128,2048]{1,0:T(8,128)(2,1)S(1)} %collective-permute-done.8.refs_2_), channel_id=1, source_target_pairs={{0,2},{2,0},{4,6},{6,4},{8,10},{10,8},{12,14},{14,12},{1,3},{3,1},... | collective-permute-start | bytes 1572872 | tf_op jit(solution)/shard_map/ppermute | solution.py:391
  143.7 11.1 %collective-permute-start.13 = (f32[24,256]{1,0:T(8,128)S(1)}, f32[24,256]{1,0:T(8,128)S(1)}, u32[]{:S(2)}, u32[]{:S(2)}) collective-permute-start(f32[24,256]{1,0:T(8,128)S(1)} %collective-permute-done.12.refs_5_), channel_id=1, source_target_pairs={{0,4},{2,6},{4,8},{6,10},{8,12},{10,14},{12,0},{14,2},{1,5},{3,7},... | collective-permute-start | bytes 73736 | tf_op jit(solution)/shard_map/ppermute | solution.py:386
  169.7 16.6 %collective-permute-start.24 = (bf16[2,128,2048]{2,1,0:T(8,128)(2,1)S(1)}, bf16[2,128,2048]{2,1,0:T(8,128)(2,1)S(1)}, u32[]{:S(2)}, u32[]{:S(2)}) collective-permute-start(bf16[2,128,2048]{2,1,0:T(8,128)(2,1)S(1)} %get-tuple-element.95), channel_id=1, source_target_pairs={{0,2},{2,0},{4,6},{6,4},{8,10},{10,8},{12,14},{14,12},{1,3},{3,1},... | collective-permute-start | bytes 3145736 | tf_op jit(solution)/shard_map/ppermute | solution.py:397
  169.7 16.2 %collective-permute-start.26 = (bf16[128,2048]{1,0:T(8,128)(2,1)S(1)}, bf16[128,2048]{1,0:T(8,128)(2,1)S(1)}, u32[]{:S(2)}, u32[]{:S(2)}) collective-permute-start(bf16[128,2048]{1,0:T(8,128)(2,1)S(1)} %get-tuple-element.97), channel_id=1, source_target_pairs={{0,4},{2,6},{4,8},{6,10},{8,12},{10,14},{12,0},{14,2},{1,5},{3,7},... | collective-permute-start | bytes 1572872 | tf_op jit(solution)/shard_map/ppermute | solution.py:421
  171.6 14.3 %collective-permute-start.25 = (bf16[128,2048]{1,0:T(8,128)(2,1)S(1)}, bf16[128,2048]{1,0:T(8,128)(2,1)S(1)}, u32[]{:S(2)}, u32[]{:S(2)}) collective-permute-start(bf16[128,2048]{1,0:T(8,128)(2,1)S(1)} %get-tuple-element.96), channel_id=1, source_target_pairs={{0,1},{1,0},{2,3},{3,2},{4,5},{5,4},{6,7},{7,6},{8,9},{9,8},{10,11... | collective-permute-start | bytes 1572872 | tf_op jit(solution)/shard_map/ppermute | solution.py:402
  193.0 2.7 %collective-permute-start.27 = (bf16[2,128,2048]{2,1,0:T(8,128)(2,1)S(1)}, bf16[2,128,2048]{2,1,0:T(8,128)(2,1)S(1)}, u32[]{:S(2)}, u32[]{:S(2)}) collective-permute-start(bf16[2,128,2048]{2,1,0:T(8,128)(2,1)S(1)} %get-tuple-element.102), channel_id=1, source_target_pairs={{0,2},{2,0},{4,6},{6,4},{8,10},{10,8},{12,14},{14,12},{1,3},{3,1},... | collective-permute-start | bytes 3145736 | tf_op jit(solution)/shard_map/ppermute | solution.py:397
  193.1 16.1 %collective-permute-start.30 = (bf16[128,2048]{1,0:T(8,128)(2,1)S(1)}, bf16[128,2048]{1,0:T(8,128)(2,1)S(1)}, u32[]{:S(2)}, u32[]{:S(2)}) collective-permute-start(bf16[128,2048]{1,0:T(8,128)(2,1)S(1)} %get-tuple-element.106), channel_id=1, source_target_pairs={{0,4},{2,6},{4,8},{6,10},{8,12},{10,14},{12,0},{14,2},{1,5},{3,7},... | collective-permute-start | bytes 1572872 | tf_op jit(solution)/shard_map/ppermute | solution.py:421
  194.2 15.1 %collective-permute-start.29 = (bf16[128,2048]{1,0:T(8,128)(2,1)S(1)}, bf16[128,2048]{1,0:T(8,128)(2,1)S(1)}, u32[]{:S(2)}, u32[]{:S(2)}) collective-permute-start(bf16[128,2048]{1,0:T(8,128)(2,1)S(1)} %get-tuple-element.105), channel_id=1, source_target_pairs={{0,1},{1,0},{2,3},{3,2},{4,5},{5,4},{6,7},{7,6},{8,9},{9,8},{10,11... | collective-permute-start | bytes 1572872 | tf_op jit(solution)/shard_map/ppermute | solution.py:402
  209.5 15.3 %collective-permute-start.31 = (bf16[128,2048]{1,0:T(8,128)(2,1)S(1)}, bf16[128,2048]{1,0:T(8,128)(2,1)S(1)}, u32[]{:S(2)}, u32[]{:S(2)}) collective-permute-start(bf16[128,2048]{1,0:T(8,128)(2,1)S(1)} %get-tuple-element.108), channel_id=1, source_target_pairs={{0,4},{2,6},{4,8},{6,10},{8,12},{10,14},{12,0},{14,2},{1,5},{3,7},... | collective-permute-start | bytes 1572872 | tf_op jit(solution)/shard_map/ppermute | solution.py:429
  210.0 14.8 %collective-permute-start.28 = (bf16[128,2048]{1,0:T(8,128)(2,1)S(1)}, bf16[128,2048]{1,0:T(8,128)(2,1)S(1)}, u32[]{:S(2)}, u32[]{:S(2)}) collective-permute-start(bf16[128,2048]{1,0:T(8,128)(2,1)S(1)} %get-tuple-element.104), channel_id=1, source_target_pairs={{0,1},{1,0},{2,3},{3,2},{4,5},{5,4},{6,7},{7,6},{8,9},{9,8},{10,11... | collective-permute-start | bytes 1572872 | tf_op jit(solution)/shard_map/ppermute | solution.py:402
  (3 other events, 2.1 us)

commit v6 on v5

--- a/solution.py
+++ b/solution.py
@@ -18,6 +18,14 @@
 MXU = 256
 
 
+def weight_work(rows, *weights):
+    size = sum(w.size for w in weights)
+    return pl.CostEstimate(flops=2 * rows * size, bytes_accessed=2 * size, transcendentals=0)
+
+
+BRIEF = pl.CostEstimate(flops=1, bytes_accessed=1, transcendentals=0)
+
+
 def tile_of(size, most):
     for candidate in range(most, 127, -128):
         if size % candidate == 0:
@@ -40,7 +48,7 @@
     return [pl.BlockSpec(memory_space=pltpu.VMEM)] * count
 
 
-def whole_call(body, outs, operands, after=None, kinds=None, scratch=(), limit=6, cost=None):
+def whole_call(body, outs, operands, after=None, kinds=None, scratch=(), limit=6, work=BRIEF):
     kinds = kinds or [pltpu.VMEM] * len(operands)
     count = len(operands)
 
@@ -62,7 +70,7 @@
         out_shape=[*outs, token],
         scratch_shapes=scratch,
         compiler_params=pltpu.CompilerParams(vmem_limit_bytes=limit * 1024 * 1024),
-        cost_estimate=cost,
+        cost_estimate=work,
     )(*operands, after)
 
 
@@ -71,26 +79,23 @@
     out_ref[...] = gained.astype(jnp.bfloat16)
 
 
-def stats_kernel(first_ref, second_ref, rows_ref, router_ref, gain_ref, w_ref, small_ref, kv_ref):
+def stats_kernel(first_ref, second_ref, rows_ref, router_ref, small_ref):
     first = first_ref[...].astype(jnp.float32)
     second = second_ref[...].astype(jnp.float32)
-    tokens = first.shape[0]
     squares = [jnp.sum(x * x, 1, keepdims=True) for x in (first, second)]
     logits = jnp.dot(rows_ref[...], router_ref[...], preferred_element_type=jnp.float32)
-    fill = jnp.zeros((tokens, 128 - 2 - logits.shape[1]), jnp.float32)
+    fill = jnp.zeros((first.shape[0], 128 - 2 - logits.shape[1]), jnp.float32)
     small = jnp.concatenate([squares[0], squares[1], logits, fill], 1)
     small_ref[...] = jnp.transpose(small)[: small_ref.shape[0]]
-    attn_in = (first * gain_ref[...].astype(jnp.float32)).astype(jnp.bfloat16)
-    kv_ref[...] = jnp.dot(attn_in, w_ref[...], preferred_element_type=jnp.float32)
-
-
-def sides_kernel(where_ref, mine_ref, other_ref, ids_ref, owner_ref, kv_ref, side_ref, kept_ref, sent_ref):
+
+
+def sides_kernel(mine_ref, other_ref, ids_ref, side_ref, scale_ref):
     small = mine_ref[...] + other_ref[...]
     tokens = small.shape[1]
     fill = jnp.zeros((128 - small.shape[0], tokens), jnp.float32)
     sums = jnp.transpose(jnp.concatenate([small, fill], 0))
     lane = lax.broadcasted_iota(jnp.int32, (tokens, 128), 1)
-    first_scale = lax.rsqrt(sums[:, 0:1] / D + EPS)
+    scale_ref[...] = jnp.broadcast_to(lax.rsqrt(sums[:, 0:1] / D + EPS), scale_ref.shape)
     second_scale = lax.rsqrt(sums[:, 1:2] / D + EPS)
     logits = sums * second_scale
     ids = ids_ref[...]
@@ -103,6 +108,13 @@
     side = jnp.where(lane == 1, second_scale, weights)
     side_ref[...] = jnp.transpose(side)[: side_ref.shape[0]]
 
+
+def rows_kernel(where_ref, first_ref, gain_ref, w_ref, scale_ref, owner_ref, kept_ref, sent_ref):
+    tokens = first_ref.shape[0]
+    attn_in = first_ref[...].astype(jnp.float32) * gain_ref[...].astype(jnp.float32)
+    kv = jnp.dot(attn_in.astype(jnp.bfloat16), w_ref[...], preferred_element_type=jnp.float32)
+    kv = (kv * scale_ref[:, 0:1]).astype(jnp.bfloat16)
+    lane = lax.broadcasted_iota(jnp.int32, (tokens, 128), 1)
     theirs = jnp.where(owner_ref[...] == where_ref[0], 0, 1)
     hot = (lane == theirs).astype(jnp.float32)
     row = lax.broadcasted_iota(jnp.int32, (tokens, tokens), 0)
@@ -110,9 +122,8 @@
     before = (column < row).astype(jnp.bfloat16)
     earlier = jnp.dot(before, hot.astype(jnp.bfloat16), preferred_element_type=jnp.float32)
     slot = jnp.sum(earlier * hot, 1, keepdims=True).astype(jnp.int32)
-    kv = (kv_ref[...] * first_scale).astype(jnp.bfloat16)
-    for side_of, out_ref in enumerate((kept_ref, sent_ref)):
-        placing = jnp.where((slot == column) & (theirs == side_of), 1.0, 0.0)
+    for side, out_ref in enumerate((kept_ref, sent_ref)):
+        placing = jnp.where((slot == column) & (theirs == side), 1.0, 0.0)
         placing = jnp.transpose(placing).astype(jnp.bfloat16)
         out = jnp.dot(placing, kv, preferred_element_type=jnp.float32)
         out_ref[...] = out.astype(jnp.bfloat16)
@@ -148,6 +159,7 @@
         out_specs=[anywhere] * count + in_vmem(1),
         out_shape=[*shapes, jax.ShapeDtypeStruct((8, 128), jnp.float32)],
         input_output_aliases={n: n for n in range(count)},
+        cost_estimate=BRIEF,
     )(*arrays, after)
 
 
@@ -203,7 +215,7 @@
         kinds=[pl.ANY],
         scratch=[pltpu.SemaphoreType.DMA((w.shape[0],))],
         limit=1,
-        cost=pl.CostEstimate(flops=0, bytes_accessed=2 * w.size, transcendentals=0),
+        work=weight_work(1, w),
     )
 
 
@@ -251,11 +263,7 @@
         after,
         kinds=[pltpu.SMEM] + [pltpu.VMEM] * 7,
         scratch=[pltpu.VMEM((2 * rows, depth), jnp.bfloat16)],
-        cost=pl.CostEstimate(
-            flops=8 * rows * depth * units * experts,
-            bytes_accessed=4 * rows * depth,
-            transcendentals=2 * rows * units * experts,
-        ),
+        work=weight_work(2 * rows, w_gate, w_up),
     )
 
 
@@ -311,11 +319,7 @@
             pltpu.SemaphoreType.DMA((slots,)),
         ],
         limit=10,
-        cost=pl.CostEstimate(
-            flops=4 * experts * tokens * units * width,
-            bytes_accessed=4 * (experts * units + tokens) * width,
-            transcendentals=0,
-        ),
+        work=weight_work(tokens, w_down),
     )
 
 
@@ -351,36 +355,34 @@
     columns = w_kv.shape[1]
     row_shape = jax.ShapeDtypeStruct(stream.shape, jnp.bfloat16)
     small_shape = jax.ShapeDtypeStruct((side_rows, rows), jnp.float32)
-    kv_shape = jax.ShapeDtypeStruct((rows, columns), jnp.float32)
+    scale_shape = jax.ShapeDtypeStruct((rows, 128), jnp.float32)
     pair_shape = jax.ShapeDtypeStruct((side_rows, 2 * rows), jnp.float32)
     placed_shape = jax.ShapeDtypeStruct((rows, columns), jnp.bfloat16)
 
+    layer_input, stream, w_kv = [
+        pltpu.with_memory_space_constraint(x, pltpu.HBM) for x in (layer_input, stream, w_kv)
+    ]
+
     rows_out, token = whole_call(opening_kernel, [row_shape], [stream, moe_norm[None]])
     lane, crossed = [rows_out, along(rows_out)], [across(rows_out)]
-
-    operands = [layer_input, stream, rows_out, router, attn_norm[None], w_kv]
-    small, kv, token = whole_call(
-        stats_kernel, [small_shape, kv_shape], operands, token, limit=16
+    where, expert_ids, kv_owner, attn_gain, key_gain, token = tied(
+        [where, expert_ids, kv_owner, attn_norm[None], k_norm[None]], token
+    )
+
+    small, token = whole_call(
+        stats_kernel, [small_shape], [layer_input, stream, rows_out, router], token
     )
     small_other = across(small)
     gate_held, token = loaded(w_gate, token)
+    lane[1], crossed[0], small_other, token = tied([lane[1], crossed[0], small_other], token)
+    lane.append(along(lane[1]))
+    crossed.append(across(lane[1]))
+    side, scale, token = whole_call(
+        sides_kernel, [small_shape, scale_shape], [small, small_other, expert_ids], token
+    )
+    side_other = beside(side)
     up_held, token = loaded(w_up, token)
-    lane[1], crossed[0], token = tied([lane[1], crossed[0]], token)
-    for _ in range(chips - 2):
-        lane.append(along(lane[-1]))
-    for s in range(1, chips):
-        crossed.append(across(lane[s]))
-
-    operands = [where, small, small_other, expert_ids, kv_owner, kv]
-    side, kept, sent, token = whole_call(
-        sides_kernel,
-        [small_shape, placed_shape, placed_shape],
-        operands,
-        token,
-        kinds=[pltpu.SMEM] + [pltpu.VMEM] * 5,
-    )
-    arrived = across(sent)
-    side, token = whole_call(joined_kernel, [pair_shape], [side, beside(side)], token)
+    side, token = whole_call(joined_kernel, [pair_shape], [side, side_other], token)
     sides = [side]
     for _ in range(chips - 1):
         sides.append(along(sides[-1]))
@@ -393,9 +395,13 @@
         return after
 
     def down(s, after):
-        own[s], sib, after = block_down(where, hidden[s], w_down, after)
-        back[s] = beside(sib)
+        own[s], back[s], after = block_down(where, hidden[s], w_down, after)
         return after
+
+    def exchange(s, arrays, after):
+        *arrays, sent, after = tied([*arrays, back[s]], after)
+        back[s] = beside(sent)
+        return *arrays, after
 
     def swap(s, after):
         sent, after = summed(1, [own[s], back[s]], after)
@@ -407,26 +413,41 @@
         return summed(0, terms, after)
 
     token = up(0, token)
+    kept, sent, token = whole_call(
+        rows_kernel,
+        [placed_shape, placed_shape],
+        [where, layer_input, attn_gain, w_kv, scale, kv_owner],
+        token,
+        kinds=[pltpu.SMEM] + [pltpu.VMEM] * 5,
+        limit=10,
+    )
+    lane[2], crossed[1], token = tied([lane[2], crossed[1]], token)
+    lane.append(along(lane[2]))
+    crossed.append(across(lane[2]))
     token = up(1, token)
     token = down(1, token)
-    kv_cache, token = whole_call(
-        cache_kernel, [placed_shape], [kept, arrived, k_norm[None]], token
-    )
+    lane[3], crossed[2], token = exchange(1, [lane[3], crossed[2]], token)
+    crossed.append(across(lane[3]))
     token = swap(1, token)
-    travelling = []
-    for s in range(1, chips - 1):
-        token = up(s + 1, token) if s == 1 else token
-        token = down(s + 1, token) if s == 1 else token
-        passed, token = gather(s, travelling, token)
-        travelling = [along(passed)]
-        token = swap(s + 1, token)
-        if s == 1:
-            token = up(3, token)
-            token = down(3, token)
+    token = up(2, token)
+    token = down(2, token)
+    passed, token = gather(1, [], token)
+    travelling = [along(passed)]
+    crossed[3], token = exchange(2, [crossed[3]], token)
+    token = swap(2, token)
+    token = up(3, token)
+    token = down(3, token)
+    passed, token = gather(2, travelling, token)
+    travelling = [along(passed)]
+    arrived, token = exchange(3, [across(sent)], token)
+    token = swap(3, token)
     token = down(0, token)
+    passed, token = gather(3, travelling, token)
+    travelling = [along(passed)]
+    (token,) = exchange(0, [], token)
     token = swap(0, token)
-    passed, token = gather(chips - 1, travelling, token)
-    moe_out, token = gather(0, [along(passed)], token)
+    kv_cache, token = whole_call(cache_kernel, [placed_shape], [kept, arrived, key_gain], token)
+    moe_out, token = gather(0, travelling, token)
     return moe_out, kv_cache.reshape(1, 1, rows, columns)
 
 

time: 226 us -> 199 us (0.88)
  waiting for transfers between devices: 98.8 us -> 32.5 us
  local copies, waits for them, and re-layouts: 29.7 us -> 63.7 us
  Pallas kernels: 74.8 us -> 82.6 us
  starting transfers between devices: 21.5 us -> 17.9 us
    ppermute x12 -> x11, waiting for transfers between devices: 50.1 us -> 10.9 us  [the longest x4 10.9 us: exchange(): back[s] = beside(sent)]
    unnamed x41 -> x118, local copies, waits for them, and re-layouts: 28.3 us -> 61.7 us
    ppermute x2 -> x3, waiting for transfers between devices: 27.1 us -> 12.4 us  [ring_device(): travelling = [along(passed)]]
    ppermute x1, waiting for transfers between devices: 12.3 us -> 0.01 us  [ring_device(): small_other = across(small)]
    ppermute x4, waiting for transfers between devices: 9.19 us -> 2.92 us  [swap(): swapped[s] = across(sent)]
    ppermute x3, waiting for transfers between devices: 0.01 us -> 6.24 us  [ring_device(): sides.append(along(sides[-1]))]
    pallas_call x23 -> x24, Pallas kernels: 74.2 us -> 78.5 us  [whole_call(): pl.pallas_call(with_token, in_specs=[pl.BlockSpec(memory_space=kind) for...]
    pallas_call x1 -> x7, Pallas kernels: 0.59 us -> 4.12 us  [tied(): pl.pallas_call(kernel, in_specs=[anywhere] * (count + 1), out_specs=[anyw...]
  transfers between devices with their start and end apart: 32 -> 32, of which waited for: 10 -> 11; matrix products, arithmetic and copies ran while one was open for 1% -> 3% of each run, Pallas kernels for 23% -> 39%
where the time goes in v6:
time: 199 us; the launch traced here: 198 us
  Pallas kernels  82.6 us (42%)
  local copies, waits for them, and re-layouts  63.7 us (32%)
  waiting for transfers between devices  32.5 us (16%)
  starting transfers between devices  17.9 us (9%)
    pallas_call x24, Pallas kernels, whole_call(): pl.pallas_call(with_token, in_specs=[pl.BlockSpec(memory_space=kind) for...  78.5 us
    unnamed x118, local copies, waits for them, and re-layouts  61.7 us
    ppermute x3, waiting for transfers between devices, ring_device(): travelling = [along(passed)]  12.4 us
    ppermute x4, waiting for transfers between devices, exchange(): back[s] = beside(sent)  10.9 us
    ppermute x3, waiting for transfers between devices, ring_device(): sides.append(along(sides[-1]))  6.24 us
    ppermute x2, starting transfers between devices, ring_device(): lane, crossed = ([rows_out, along(rows_out)], [across(rows_out)])  4.51 us
    ppermute x4, starting transfers between devices, swap(): swapped[s] = across(sent)  4.25 us
    pallas_call x7, Pallas kernels, tied(): pl.pallas_call(kernel, in_specs=[anywhere] * (count + 1), out_specs=[anyw...  4.12 us
  transfers between devices with their start and end apart: 32, of which 11 were waited for; matrix products, arithmetic and copies ran while one was open for 3% of the time, Pallas kernels for 39%

profile of v6, /device:TPU:0, one launch (start us, length us, event | category | flops | bytes accessed | tf_op | source)
XLA Modules:
  0.0 198.4 jit_solution(4032270874297237536)
XLA Ops:
  0.6 1.1 copy.54
  2.5 1.1 shard_map.131
  4.2 3.0 %collective-permute-start = (bf16[128,2048]{1,0:T(8,128)(2,1)S(1)}, bf16[128,2048]{1,0:T(8,128)(2,1)S(1)}, u32[]{:S(2)}, u32[]{:S(2)}) collective-permute-start(bf16[128,2048]{1,0:T(8,128)(2,1)S(1)} %get-tuple-element.82.refs_2_.refs_1_), channel_id=1, source_target_pairs={{0,4},{2,6},{4,8},{6,10},{8,12},{10,14},{12,0},{14,2},{1,5},{3,7},... | collective-permute-start | bytes 1572872 | tf_op jit(solution)/shard_map/ppermute | solution.py:367
  7.2 1.5 collective-permute-start.1
  8.7 1.4 copy.32.refs_1_
  10.1 1.4 copy.33.refs_2_
  11.5 1.3 broadcast_in_dim.12.refs_3_
  14.0 1.1 copy.34.refs_3_
  15.8 1.7 shard_map.133
  18.1 4.6 %shard_map.134 = (bf16[2,4096,768]{2,1,0:T(8,128)(2,1)S(1)}, f32[8,128]{1,0:T(8,128)S(1)}) custom-call(bf16[2,4096,768]{2,1,0:T(8,128)(2,1)} %refs_0_.6, f32[8,128]{1,0:T(8,128)S(1)} %get-tuple-element.85.refs_1_), custom_call_target="tpu_custom_call" | custom-call | flops 12582912 | bytes 12582912 | tf_op jit(solution)/shard_map/pallas_call | solution.py:65
  22.7 4.6 %copy-done = bf16[2,4096,768]{2,1,0:T(8,128)(2,1)} copy-done((bf16[2,4096,768]{2,1,0:T(8,128)(2,1)}, bf16[2,4096,768]{2,1,0:T(8,128)(2,1)S(1)}, u32[]{:S(2)}) %copy-start) | copy-done | bytes 12582936
  32.5 1.6 collective-permute-start.6
  34.1 1.5 collective-permute-start.7
  35.6 4.6 %shard_map.137 = (bf16[2,4096,768]{2,1,0:T(8,128)(2,1)S(1)}, f32[8,128]{1,0:T(8,128)S(1)}) custom-call(bf16[2,4096,768]{2,1,0:T(8,128)(2,1)} %refs_0_.7, f32[8,128]{1,0:T(8,128)S(1)} %get-tuple-element.92.refs_1_), custom_call_target="tpu_custom_call" | custom-call | flops 12582912 | bytes 12582912 | tf_op jit(solution)/shard_map/pallas_call | solution.py:65
  40.4 1.4 copy-done.14
  41.9 8.1 %shard_map.139 = (bf16[2,256,768]{2,1,0:T(8,128)(2,1)S(1)}, f32[8,128]{1,0:T(8,128)S(1)}) custom-call(s32[2]{0:T(128)S(1)} %copy-done.36, bf16[128,2048]{1,0:T(8,128)(2,1)S(1)} %get-tuple-element.82.refs_2_.refs_1_, bf16[128,2048]{1,0:T(8,128)(2,1)S(1)} %copy-done.14, bf16[128,2048]{1,0:T(8,128)(2,1)S(1)} %collective-permute-done.3.refs_3_, ...), custom_call_target="tpu_custom_call" | custom-call | flops 6442450944 | bytes 25165824 | tf_op jit(solution)/shard_map/pallas_call | solution.py:65
  50.0 3.8 %shard_map.140 = (bf16[128,1024]{1,0:T(8,128)(2,1)S(1)}, bf16[128,1024]{1,0:T(8,128)(2,1)S(1)}, f32[8,128]{1,0:T(8,128)S(1)}) custom-call(s32[2]{0:T(128)S(1)} %copy-done.36, bf16[128,2048]{1,0:T(8,128)(2,1)} %refs_1_.4, bf16[1,2048]{1,0:T(2,128)(2,1)S(1)} %copy-done.35, bf16[2048,1024]{1,0:T(8,128)(2,1)} %refs_3_.2, ...), custom_call_target="tpu_custom_call" | custom-call | flops 1 | bytes 1 | tf_op jit(solution)/shard_map/pallas_call | solution.py:65
  57.7 1.6 collective-permute-start.12
  59.9 3.4 %collective-permute-done.12.refs_5_ = f32[24,256]{1,0:T(8,128)S(1)} collective-permute-done((f32[24,256]{1,0:T(8,128)S(1)}, f32[24,256]{1,0:T(8,128)S(1)}, u32[]{:S(2)}, u32[]{:S(2)}) %collective-permute-start.12) | collective-permute-done | bytes 24608 | tf_op jit(solution)/shard_map/ppermute | solution.py:388
  63.4 4.6 %copy-done.2 = bf16[2,4096,768]{2,1,0:T(8,128)(2,1)S(1)} copy-done((bf16[2,4096,768]{2,1,0:T(8,128)(2,1)S(1)}, bf16[2,4096,768]{2,1,0:T(8,128)(2,1)}, u32[]{:S(2)}) %copy-start.2) | copy-done | bytes 12582936
  67.9 4.6 %copy-done.6 = bf16[2,4096,768]{2,1,0:T(8,128)(2,1)S(1)} copy-done((bf16[2,4096,768]{2,1,0:T(8,128)(2,1)S(1)}, bf16[2,4096,768]{2,1,0:T(8,128)(2,1)}, u32[]{:S(2)}) %copy-start.6) | copy-done | bytes 12582936
  72.5 1.0 copy-done.18
  74.2 8.1 %shard_map.142 = (bf16[2,256,768]{2,1,0:T(8,128)(2,1)S(1)}, f32[8,128]{1,0:T(8,128)S(1)}) custom-call(s32[2]{0:T(128)S(1)} %copy-done.36, bf16[128,2048]{1,0:T(8,128)(2,1)S(1)} %copy-done.12, bf16[128,2048]{1,0:T(8,128)(2,1)S(1)} %copy-done.18, bf16[128,2048]{1,0:T(8,128)(2,1)S(1)} %collective-permute-done.10.refs_3_, ...), custom_call_target="tpu_custom_call" | custom-call | flops 6442450944 | bytes 25165824 | tf_op jit(solution)/shard_map/pallas_call | solution.py:65
  82.3 6.6 %shard_map.143 = (bf16[2,128,2048]{2,1,0:T(8,128)(2,1)S(1)}, bf16[2,128,2048]{2,1,0:T(8,128)(2,1)S(1)}, f32[8,128]{1,0:T(8,128)S(1)}) custom-call(s32[2]{0:T(128)S(1)} %copy-done.36, bf16[2,256,768]{2,1,0:T(8,128)(2,1)S(1)} %get-tuple-element.108.refs_1_, bf16[2,768,4096]{2,1,0:T(8,128)(2,1)} %refs_2_.8, f32[8,128]{1,0:T(8,128)S(1)} %get-tuple-element.109.refs_3_), custom_call_target="tpu_custom_call" | custom-call | flops 3221225472 | bytes 12582912 | tf_op jit(solution)/shard_map/pallas_call | solution.py:65
  93.2 2.6 %collective-permute-done.17.refs_1_ = bf16[2,128,2048]{2,1,0:T(8,128)(2,1)S(1)} collective-permute-done((bf16[2,128,2048]{2,1,0:T(8,128)(2,1)}, bf16[2,128,2048]{2,1,0:T(8,128)(2,1)S(1)}, u32[]{:S(2)}, u32[]{:S(2)}) %collective-permute-start.17) | collective-permute-done | bytes 1048608 | tf_op jit(solution)/shard_map/ppermute | solution.py:403
  97.2 1.1 collective-permute-done.16.refs_5_
  98.3 4.6 %copy-done.3 = bf16[2,4096,768]{2,1,0:T(8,128)(2,1)S(1)} copy-done((bf16[2,4096,768]{2,1,0:T(8,128)(2,1)S(1)}, bf16[2,4096,768]{2,1,0:T(8,128)(2,1)}, u32[]{:S(2)}) %copy-start.3) | copy-done | bytes 12582936
  102.9 4.6 %copy-done.7 = bf16[2,4096,768]{2,1,0:T(8,128)(2,1)S(1)} copy-done((bf16[2,4096,768]{2,1,0:T(8,128)(2,1)S(1)}, bf16[2,4096,768]{2,1,0:T(8,128)(2,1)}, u32[]{:S(2)}) %copy-start.7) | copy-done | bytes 12582936
  107.4 1.0 copy-done.22
  108.5 8.1 %shard_map.146 = (bf16[2,256,768]{2,1,0:T(8,128)(2,1)S(1)}, f32[8,128]{1,0:T(8,128)S(1)}) custom-call(s32[2]{0:T(128)S(1)} %copy-done.36, bf16[128,2048]{1,0:T(8,128)(2,1)S(1)} %copy-done.16, bf16[128,2048]{1,0:T(8,128)(2,1)S(1)} %copy-done.22, bf16[128,2048]{1,0:T(8,128)(2,1)S(1)} %collective-permute-done.14.refs_3_, ...), custom_call_target="tpu_custom_call" | custom-call | flops 6442450944 | bytes 25165824 | tf_op jit(solution)/shard_map/pallas_call | solution.py:65
  116.6 6.6 %shard_map.147 = (bf16[2,128,2048]{2,1,0:T(8,128)(2,1)S(1)}, bf16[2,128,2048]{2,1,0:T(8,128)(2,1)S(1)}, f32[8,128]{1,0:T(8,128)S(1)}) custom-call(s32[2]{0:T(128)S(1)} %copy-done.36, bf16[2,256,768]{2,1,0:T(8,128)(2,1)S(1)} %get-tuple-element.118.refs_1_, bf16[2,768,4096]{2,1,0:T(8,128)(2,1)} %refs_2_.8, f32[8,128]{1,0:T(8,128)S(1)} %get-tuple-element.119.refs_3_), custom_call_target="tpu_custom_call" | custom-call | flops 3221225472 | bytes 12582912 | tf_op jit(solution)/shard_map/pallas_call | solution.py:65
  126.9 2.6 %collective-permute-done.22.refs_1_ = bf16[2,128,2048]{2,1,0:T(8,128)(2,1)S(1)} collective-permute-done((bf16[2,128,2048]{2,1,0:T(8,128)(2,1)}, bf16[2,128,2048]{2,1,0:T(8,128)(2,1)S(1)}, u32[]{:S(2)}, u32[]{:S(2)}) %collective-permute-start.22) | collective-permute-done | bytes 1048608 | tf_op jit(solution)/shard_map/ppermute | solution.py:403
  130.2 1.7 collective-permute-done.21.refs_5_
  132.5 4.6 %copy-done.4 = bf16[2,4096,768]{2,1,0:T(8,128)(2,1)S(1)} copy-done((bf16[2,4096,768]{2,1,0:T(8,128)(2,1)S(1)}, bf16[2,4096,768]{2,1,0:T(8,128)(2,1)}, u32[]{:S(2)}) %copy-start.4) | copy-done | bytes 12582936
  137.1 4.6 %copy-done.8 = bf16[2,4096,768]{2,1,0:T(8,128)(2,1)S(1)} copy-done((bf16[2,4096,768]{2,1,0:T(8,128)(2,1)S(1)}, bf16[2,4096,768]{2,1,0:T(8,128)(2,1)}, u32[]{:S(2)}) %copy-start.8) | copy-done | bytes 12582936
  142.7 8.1 %shard_map.151 = (bf16[2,256,768]{2,1,0:T(8,128)(2,1)S(1)}, f32[8,128]{1,0:T(8,128)S(1)}) custom-call(s32[2]{0:T(128)S(1)} %copy-done.36, bf16[128,2048]{1,0:T(8,128)(2,1)S(1)} %copy-done.20, bf16[128,2048]{1,0:T(8,128)(2,1)S(1)} %copy-done.10, bf16[128,2048]{1,0:T(8,128)(2,1)S(1)} %collective-permute-done.19.refs_3_, ...), custom_call_target="tpu_custom_call" | custom-call | flops 6442450944 | bytes 25165824 | tf_op jit(solution)/shard_map/pallas_call | solution.py:65
  150.8 6.6 %shard_map.152 = (bf16[2,128,2048]{2,1,0:T(8,128)(2,1)S(1)}, bf16[2,128,2048]{2,1,0:T(8,128)(2,1)S(1)}, f32[8,128]{1,0:T(8,128)S(1)}) custom-call(s32[2]{0:T(128)S(1)} %copy-done.36, bf16[2,256,768]{2,1,0:T(8,128)(2,1)S(1)} %get-tuple-element.129.refs_1_, bf16[2,768,4096]{2,1,0:T(8,128)(2,1)} %refs_2_.8, f32[8,128]{1,0:T(8,128)S(1)} %get-tuple-element.130.refs_3_), custom_call_target="tpu_custom_call" | custom-call | flops 3221225472 | bytes 12582912 | tf_op jit(solution)/shard_map/pallas_call | solution.py:65
  160.5 2.9 %collective-permute-done.26.refs_1_ = bf16[2,128,2048]{2,1,0:T(8,128)(2,1)S(1)} collective-permute-done((bf16[2,128,2048]{2,1,0:T(8,128)(2,1)}, bf16[2,128,2048]{2,1,0:T(8,128)(2,1)S(1)}, u32[]{:S(2)}, u32[]{:S(2)}) %collective-permute-start.26) | collective-permute-done | bytes 1048608 | tf_op jit(solution)/shard_map/ppermute | solution.py:403
  164.1 1.6 collective-permute-start.27
  165.7 1.1 copy-done.30
  166.8 6.6 %shard_map.156 = (bf16[2,128,2048]{2,1,0:T(8,128)(2,1)S(1)}, bf16[2,128,2048]{2,1,0:T(8,128)(2,1)S(1)}, f32[8,128]{1,0:T(8,128)S(1)}) custom-call(s32[2]{0:T(128)S(1)} %copy-done.36, bf16[2,256,768]{2,1,0:T(8,128)(2,1)S(1)} %copy-done.30, bf16[2,768,4096]{2,1,0:T(8,128)(2,1)} %refs_2_.8, f32[8,128]{1,0:T(8,128)S(1)} %get-tuple-element.140.refs_3_), custom_call_target="tpu_custom_call" | custom-call | flops 3221225472 | bytes 12582912 | tf_op jit(solution)/shard_map/pallas_call | solution.py:65
  173.5 3.3 %collective-permute-done.28.refs_3_ = bf16[128,2048]{1,0:T(8,128)(2,1)S(1)} collective-permute-done((bf16[128,2048]{1,0:T(8,128)(2,1)}, bf16[128,2048]{1,0:T(8,128)(2,1)S(1)}, u32[]{:S(2)}, u32[]{:S(2)}) %collective-permute-start.28) | collective-permute-done | bytes 524320 | tf_op jit(solution)/shard_map/ppermute | solution.py:441
  176.8 1.4 collective-permute-done.27.refs_2_
  179.6 2.9 %collective-permute-done.29.refs_1_ = bf16[2,128,2048]{2,1,0:T(8,128)(2,1)S(1)} collective-permute-done((bf16[2,128,2048]{2,1,0:T(8,128)(2,1)}, bf16[2,128,2048]{2,1,0:T(8,128)(2,1)S(1)}, u32[]{:S(2)}, u32[]{:S(2)}) %collective-permute-start.29) | collective-permute-done | bytes 1048608 | tf_op jit(solution)/shard_map/ppermute | solution.py:403
  183.3 1.6 collective-permute-start.30
  186.7 9.1 %collective-permute-done.31.refs_3_ = bf16[128,2048]{1,0:T(8,128)(2,1)S(1)} collective-permute-done((bf16[128,2048]{1,0:T(8,128)(2,1)S(1)}, bf16[128,2048]{1,0:T(8,128)(2,1)S(1)}, u32[]{:S(2)}, u32[]{:S(2)}) %collective-permute-start.31) | collective-permute-done | bytes 524320 | tf_op jit(solution)/shard_map/ppermute | solution.py:446
  195.8 1.6 collective-permute-done.30.refs_2_
  197.3 1.1 shard_map.161
  (169 shorter events, 33.7 us)
Async XLA Ops:
  4.2 23.7 %collective-permute-start = (bf16[128,2048]{1,0:T(8,128)(2,1)S(1)}, bf16[128,2048]{1,0:T(8,128)(2,1)S(1)}, u32[]{:S(2)}, u32[]{:S(2)}) collective-permute-start(bf16[128,2048]{1,0:T(8,128)(2,1)S(1)} %get-tuple-element.82.refs_2_.refs_1_), channel_id=1, source_target_pairs={{0,4},{2,6},{4,8},{6,10},{8,12},{10,14},{12,0},{14,2},{1,5},{3,7},... | collective-permute-start | bytes 1572872 | tf_op jit(solution)/shard_map/ppermute | solution.py:367
  7.2 20.7 %collective-permute-start.1 = (bf16[128,2048]{1,0:T(8,128)(2,1)S(1)}, bf16[128,2048]{1,0:T(8,128)(2,1)S(1)}, u32[]{:S(2)}, u32[]{:S(2)}) collective-permute-start(bf16[128,2048]{1,0:T(8,128)(2,1)S(1)} %get-tuple-element.82.refs_2_.refs_1_), channel_id=1, source_target_pairs={{0,1},{1,0},{2,3},{3,2},{4,5},{5,4},{6,7},{7,6},{8,9},{9,8},{10,11... | collective-permute-start | bytes 1572872 | tf_op jit(solution)/shard_map/ppermute | solution.py:367
  14.0 16.0 %copy-start.32 = (s32[128,8]{1,0:T(8,128)S(1)}, s32[128,8]{1,0:T(8,128)}, u32[]{:S(2)}) copy-start(s32[128,8]{1,0:T(8,128)} %get-tuple-element.89.refs_2_) | copy-start | bytes 12292
  17.5 10.4 %collective-permute-start.2 = (f32[24,128]{1,0:T(8,128)S(1)}, f32[24,128]{1,0:T(8,128)S(1)}, u32[]{:S(2)}, u32[]{:S(2)}) collective-permute-start(f32[24,128]{1,0:T(8,128)S(1)} %get-tuple-element.84.refs_0_), channel_id=1, source_target_pairs={{0,1},{1,0},{2,3},{3,2},{4,5},{5,4},{6,7},{7,6},{8,9},{9,8},{10,11... | collective-permute-start | bytes 36872 | tf_op jit(solution)/shard_map/ppermute | solution.py:375
  18.1 22.3 %collective-permute-start.3 = (bf16[128,2048]{1,0:T(8,128)(2,1)S(1)}, bf16[128,2048]{1,0:T(8,128)(2,1)S(1)}, u32[]{:S(2)}, u32[]{:S(2)}) collective-permute-start(bf16[128,2048]{1,0:T(8,128)(2,1)S(1)} %get-tuple-element.82.refs_2_.refs_1_), channel_id=1, source_target_pairs={{0,2},{2,0},{4,6},{6,4},{8,10},{10,8},{12,14},{14,12},{1,3},{3,1},... | collective-permute-start | bytes 1572872 | tf_op jit(solution)/shard_map/ppermute | solution.py:393
  18.1 22.3 %copy-start.36 = (s32[2]{0:T(128)S(1)}, s32[2]{0:T(128)}, u32[]{:S(2)}) copy-start(s32[2]{0:T(128)} %get-tuple-element.81.refs_0_) | copy-start | bytes 28
  29.5 10.9 %copy-start.1 = (bf16[2,4096,768]{2,1,0:T(8,128)(2,1)S(1)}, bf16[2,4096,768]{2,1,0:T(8,128)(2,1)}, u32[]{:S(2)}) copy-start(bf16[2,4096,768]{2,1,0:T(8,128)(2,1)} %copy-done) | copy-start | bytes 37748740
  29.5 10.9 %collective-permute-start.4 = (bf16[128,2048]{1,0:T(8,128)(2,1)}, bf16[128,2048]{1,0:T(8,128)(2,1)S(1)}, u32[]{:S(2)}, u32[]{:S(2)}) collective-permute-start(bf16[128,2048]{1,0:T(8,128)(2,1)} %get-tuple-element.87.refs_2_), channel_id=1, source_target_pairs={{0,2},{2,0},{4,6},{6,4},{8,10},{10,8},{12,14},{14,12},{1,3},{3,1},... | collective-permute-start | bytes 1572872 | tf_op jit(solution)/shard_map/ppermute | solution.py:393
  32.5 7.8 %collective-permute-start.5 = (f32[24,128]{1,0:T(8,128)S(1)}, f32[24,128]{1,0:T(8,128)S(1)}, u32[]{:S(2)}, u32[]{:S(2)}) collective-permute-start(f32[24,128]{1,0:T(8,128)S(1)} %get-tuple-element.91.refs_0_), channel_id=1, source_target_pairs={{0,2},{2,0},{4,6},{6,4},{8,10},{10,8},{12,14},{14,12},{1,3},{3,1},... | collective-permute-start | bytes 36872 | tf_op jit(solution)/shard_map/ppermute | solution.py:383
  32.5 22.6 %collective-permute-start.6 = (bf16[128,2048]{1,0:T(8,128)(2,1)}, bf16[128,2048]{1,0:T(8,128)(2,1)S(1)}, u32[]{:S(2)}, u32[]{:S(2)}) collective-permute-start(bf16[128,2048]{1,0:T(8,128)(2,1)} %get-tuple-element.99.refs_1_), channel_id=1, source_target_pairs={{0,4},{2,6},{4,8},{6,10},{8,12},{10,14},{12,0},{14,2},{1,5},{3,7},... | collective-permute-start | bytes 1572872 | tf_op jit(solution)/shard_map/ppermute | solution.py:378
  34.1 21.0 %collective-permute-start.7 = (bf16[128,2048]{1,0:T(8,128)(2,1)}, bf16[128,2048]{1,0:T(8,128)(2,1)S(1)}, u32[]{:S(2)}, u32[]{:S(2)}) collective-permute-start(bf16[128,2048]{1,0:T(8,128)(2,1)} %get-tuple-element.99.refs_1_), channel_id=1, source_target_pairs={{0,1},{1,0},{2,3},{3,2},{4,5},{5,4},{6,7},{7,6},{8,9},{9,8},{10,11... | collective-permute-start | bytes 1572872 | tf_op jit(solution)/shard_map/ppermute | solution.py:379
  40.3 9.7 %copy-start.5 = (bf16[2,4096,768]{2,1,0:T(8,128)(2,1)}, bf16[2,4096,768]{2,1,0:T(8,128)(2,1)S(1)}, u32[]{:S(2)}) copy-start(bf16[2,4096,768]{2,1,0:T(8,128)(2,1)S(1)} %get-tuple-element.96.refs_7_) | copy-start | bytes 37748740
  40.3 23.1 %collective-permute-start.10 = (bf16[128,2048]{1,0:T(8,128)(2,1)}, bf16[128,2048]{1,0:T(8,128)(2,1)S(1)}, u32[]{:S(2)}, u32[]{:S(2)}) collective-permute-start(bf16[128,2048]{1,0:T(8,128)(2,1)} %get-tuple-element.99.refs_1_), channel_id=1, source_target_pairs={{0,2},{2,0},{4,6},{6,4},{8,10},{10,8},{12,14},{14,12},{1,3},{3,1},... | collective-permute-start | bytes 1572872 | tf_op jit(solution)/shard_map/ppermute | solution.py:393
  41.9 8.1 %copy-start.31 = (s32[128,1]{1,0:T(8,128)S(1)}, s32[128,1]{1,0:T(8,128)}, u32[]{:S(2)}) copy-start(s32[128,1]{1,0:T(8,128)} %get-tuple-element.102.refs_5_) | copy-start | bytes 1540
  41.9 8.1 %copy-start.35 = (bf16[1,2048]{1,0:T(2,128)(2,1)S(1)}, bf16[1,2048]{1,0:T(2,128)(2,1)}, u32[]{:S(2)}) copy-start(bf16[1,2048]{1,0:T(2,128)(2,1)} %get-tuple-element.100.refs_2_) | copy-start | bytes 12292
  41.9 21.5 %copy-start.12 = (bf16[128,2048]{1,0:T(8,128)(2,1)S(1)}, bf16[128,2048]{1,0:T(8,128)(2,1)}, u32[]{:S(2)}) copy-start(bf16[128,2048]{1,0:T(8,128)(2,1)} %get-tuple-element.99.refs_1_) | copy-start | bytes 1572868
  50.0 5.2 %copy-start.29 = (bf16[2,256,768]{2,1,0:T(8,128)(2,1)}, bf16[2,256,768]{2,1,0:T(8,128)(2,1)S(1)}, u32[]{:S(2)}) copy-start(bf16[2,256,768]{2,1,0:T(8,128)(2,1)S(1)} %get-tuple-element.98.refs_1_) | copy-start | bytes 2359300
  57.3 6.1 %collective-permute-start.11 = (bf16[128,2048]{1,0:T(8,128)(2,1)}, bf16[128,2048]{1,0:T(8,128)(2,1)S(1)}, u32[]{:S(2)}, u32[]{:S(2)}) collective-permute-start(bf16[128,2048]{1,0:T(8,128)(2,1)} %get-tuple-element.106.refs_2_), channel_id=1, source_target_pairs={{0,2},{2,0},{4,6},{6,4},{8,10},{10,8},{12,14},{14,12},{1,3},{3,1},... | collective-permute-start | bytes 1572872 | tf_op jit(solution)/shard_map/ppermute | solution.py:393
  57.7 5.6 %collective-permute-start.12 = (f32[24,256]{1,0:T(8,128)S(1)}, f32[24,256]{1,0:T(8,128)S(1)}, u32[]{:S(2)}, u32[]{:S(2)}) collective-permute-start(f32[24,256]{1,0:T(8,128)S(1)} %get-tuple-element.94.refs_5_), channel_id=1, source_target_pairs={{0,4},{2,6},{4,8},{6,10},{8,12},{10,14},{12,0},{14,2},{1,5},{3,7},... | collective-permute-start | bytes 73736 | tf_op jit(solution)/shard_map/ppermute | solution.py:388
  59.3 31.2 %collective-permute-start.8 = (bf16[128,2048]{1,0:T(8,128)(2,1)}, bf16[128,2048]{1,0:T(8,128)(2,1)S(1)}, u32[]{:S(2)}, u32[]{:S(2)}) collective-permute-start(bf16[128,2048]{1,0:T(8,128)(2,1)} %get-tuple-element.105.refs_1_), channel_id=1, source_target_pairs={{0,4},{2,6},{4,8},{6,10},{8,12},{10,14},{12,0},{14,2},{1,5},{3,7},... | collective-permute-start | bytes 1572872 | tf_op jit(solution)/shard_map/ppermute | solution.py:425
  59.5 31.0 %collective-permute-start.9 = (bf16[128,2048]{1,0:T(8,128)(2,1)}, bf16[128,2048]{1,0:T(8,128)(2,1)S(1)}, u32[]{:S(2)}, u32[]{:S(2)}) collective-permute-start(bf16[128,2048]{1,0:T(8,128)(2,1)} %get-tuple-element.105.refs_1_), channel_id=1, source_target_pairs={{0,1},{1,0},{2,3},{3,2},{4,5},{5,4},{6,7},{7,6},{8,9},{9,8},{10,11... | collective-permute-start | bytes 1572872 | tf_op jit(solution)/shard_map/ppermute | solution.py:426
  63.4 4.6 %copy-start.2 = (bf16[2,4096,768]{2,1,0:T(8,128)(2,1)S(1)}, bf16[2,4096,768]{2,1,0:T(8,128)(2,1)}, u32[]{:S(2)}) copy-start(bf16[2,4096,768]{2,1,0:T(8,128)(2,1)} %copy-done) | copy-start | bytes 37748740
  82.3 9.8 %copy-start.16 = (bf16[128,2048]{1,0:T(8,128)(2,1)S(1)}, bf16[128,2048]{1,0:T(8,128)(2,1)}, u32[]{:S(2)}) copy-start(bf16[128,2048]{1,0:T(8,128)(2,1)} %get-tuple-element.105.refs_1_) | copy-start | bytes 1572868
  92.1 3.6 %collective-permute-start.17 = (bf16[2,128,2048]{2,1,0:T(8,128)(2,1)}, bf16[2,128,2048]{2,1,0:T(8,128)(2,1)S(1)}, u32[]{:S(2)}, u32[]{:S(2)}) collective-permute-start(bf16[2,128,2048]{2,1,0:T(8,128)(2,1)} %get-tuple-element.115), channel_id=1, source_target_pairs={{0,2},{2,0},{4,6},{6,4},{8,10},{10,8},{12,14},{14,12},{1,3},{3,1},... | collective-permute-start | bytes 3145736 | tf_op jit(solution)/shard_map/ppermute | solution.py:403
  92.1 6.1 %collective-permute-start.14 = (bf16[128,2048]{1,0:T(8,128)(2,1)S(1)}, bf16[128,2048]{1,0:T(8,128)(2,1)S(1)}, u32[]{:S(2)}, u32[]{:S(2)}) collective-permute-start(bf16[128,2048]{1,0:T(8,128)(2,1)S(1)} %copy-done.16), channel_id=1, source_target_pairs={{0,2},{2,0},{4,6},{6,4},{8,10},{10,8},{12,14},{14,12},{1,3},{3,1},... | collective-permute-start | bytes 1572872 | tf_op jit(solution)/shard_map/ppermute | solution.py:393
  92.6 5.6 %collective-permute-start.15 = (bf16[128,2048]{1,0:T(8,128)(2,1)}, bf16[128,2048]{1,0:T(8,128)(2,1)S(1)}, u32[]{:S(2)}, u32[]{:S(2)}) collective-permute-start(bf16[128,2048]{1,0:T(8,128)(2,1)} %get-tuple-element.113.refs_2_), channel_id=1, source_target_pairs={{0,2},{2,0},{4,6},{6,4},{8,10},{10,8},{12,14},{14,12},{1,3},{3,1},... | collective-permute-start | bytes 1572872 | tf_op jit(solution)/shard_map/ppermute | solution.py:393
  92.6 5.6 %collective-permute-start.16 = (f32[24,256]{1,0:T(8,128)S(1)}, f32[24,256]{1,0:T(8,128)S(1)}, u32[]{:S(2)}, u32[]{:S(2)}) collective-permute-start(f32[24,256]{1,0:T(8,128)S(1)} %collective-permute-done.12.refs_5_), channel_id=1, source_target_pairs={{0,4},{2,6},{4,8},{6,10},{8,12},{10,14},{12,0},{14,2},{1,5},{3,7},... | collective-permute-start | bytes 73736 | tf_op jit(solution)/shard_map/ppermute | solution.py:388
  92.7 31.5 %collective-permute-start.13 = (bf16[128,2048]{1,0:T(8,128)(2,1)}, bf16[128,2048]{1,0:T(8,128)(2,1)S(1)}, u32[]{:S(2)}, u32[]{:S(2)}) collective-permute-start(bf16[128,2048]{1,0:T(8,128)(2,1)} %get-tuple-element.112.refs_1_), channel_id=1, source_target_pairs={{0,1},{1,0},{2,3},{3,2},{4,5},{5,4},{6,7},{7,6},{8,9},{9,8},{10,11... | collective-permute-start | bytes 1572872 | tf_op jit(solution)/shard_map/ppermute | solution.py:430
  96.6 26.7 %collective-permute-start.18 = (bf16[128,2048]{1,0:T(8,128)(2,1)S(1)}, bf16[128,2048]{1,0:T(8,128)(2,1)S(1)}, u32[]{:S(2)}, u32[]{:S(2)}) collective-permute-start(bf16[128,2048]{1,0:T(8,128)(2,1)S(1)} %get-tuple-element.121), channel_id=1, source_target_pairs={{0,1},{1,0},{2,3},{3,2},{4,5},{5,4},{6,7},{7,6},{8,9},{9,8},{10,11... | collective-permute-start | bytes 1572872 | tf_op jit(solution)/shard_map/ppermute | solution.py:408
  98.3 4.6 %copy-start.3 = (bf16[2,4096,768]{2,1,0:T(8,128)(2,1)S(1)}, bf16[2,4096,768]{2,1,0:T(8,128)(2,1)}, u32[]{:S(2)}) copy-start(bf16[2,4096,768]{2,1,0:T(8,128)(2,1)} %copy-done) | copy-start | bytes 37748740
  116.6 9.3 %copy-start.20 = (bf16[128,2048]{1,0:T(8,128)(2,1)S(1)}, bf16[128,2048]{1,0:T(8,128)(2,1)}, u32[]{:S(2)}) copy-start(bf16[128,2048]{1,0:T(8,128)(2,1)} %get-tuple-element.112.refs_1_) | copy-start | bytes 1572868
  125.8 3.6 %collective-permute-start.22 = (bf16[2,128,2048]{2,1,0:T(8,128)(2,1)}, bf16[2,128,2048]{2,1,0:T(8,128)(2,1)S(1)}, u32[]{:S(2)}, u32[]{:S(2)}) collective-permute-start(bf16[2,128,2048]{2,1,0:T(8,128)(2,1)} %get-tuple-element.126), channel_id=1, source_target_pairs={{0,2},{2,0},{4,6},{6,4},{8,10},{10,8},{12,14},{14,12},{1,3},{3,1},... | collective-permute-start | bytes 3145736 | tf_op jit(solution)/shard_map/ppermute | solution.py:403
  125.8 6.7 %collective-permute-start.19 = (bf16[128,2048]{1,0:T(8,128)(2,1)S(1)}, bf16[128,2048]{1,0:T(8,128)(2,1)S(1)}, u32[]{:S(2)}, u32[]{:S(2)}) collective-permute-start(bf16[128,2048]{1,0:T(8,128)(2,1)S(1)} %copy-done.20), channel_id=1, source_target_pairs={{0,2},{2,0},{4,6},{6,4},{8,10},{10,8},{12,14},{14,12},{1,3},{3,1},... | collective-permute-start | bytes 1572872 | tf_op jit(solution)/shard_map/ppermute | solution.py:393
  126.3 6.2 %collective-permute-start.20 = (bf16[128,2048]{1,0:T(8,128)(2,1)}, bf16[128,2048]{1,0:T(8,128)(2,1)S(1)}, u32[]{:S(2)}, u32[]{:S(2)}) collective-permute-start(bf16[128,2048]{1,0:T(8,128)(2,1)} %get-tuple-element.124.refs_2_), channel_id=1, source_target_pairs={{0,2},{2,0},{4,6},{6,4},{8,10},{10,8},{12,14},{14,12},{1,3},{3,1},... | collective-permute-start | bytes 1572872 | tf_op jit(solution)/shard_map/ppermute | solution.py:393
  126.3 5.6 %collective-permute-start.21 = (f32[24,256]{1,0:T(8,128)S(1)}, f32[24,256]{1,0:T(8,128)S(1)}, u32[]{:S(2)}, u32[]{:S(2)}) collective-permute-start(f32[24,256]{1,0:T(8,128)S(1)} %collective-permute-done.16.refs_5_), channel_id=1, source_target_pairs={{0,4},{2,6},{4,8},{6,10},{8,12},{10,14},{12,0},{14,2},{1,5},{3,7},... | collective-permute-start | bytes 73736 | tf_op jit(solution)/shard_map/ppermute | solution.py:388
  126.3 32.9 %collective-permute-start.23 = (bf16[128,1024]{1,0:T(8,128)(2,1)}, bf16[128,1024]{1,0:T(8,128)(2,1)S(1)}, u32[]{:S(2)}, u32[]{:S(2)}) collective-permute-start(bf16[128,1024]{1,0:T(8,128)(2,1)} %copy-done.56), channel_id=1, source_target_pairs={{0,1},{1,0},{2,3},{3,2},{4,5},{5,4},{6,7},{7,6},{8,9},{9,8},{10,11... | collective-permute-start | bytes 786440 | tf_op jit(solution)/shard_map/ppermute | solution.py:442
  129.4 28.0 %collective-permute-start.25 = (bf16[128,2048]{1,0:T(8,128)(2,1)}, bf16[128,2048]{1,0:T(8,128)(2,1)S(1)}, u32[]{:S(2)}, u32[]{:S(2)}) collective-permute-start(bf16[128,2048]{1,0:T(8,128)(2,1)} %copy-done.54), channel_id=1, source_target_pairs={{0,4},{2,6},{4,8},{6,10},{8,12},{10,14},{12,0},{14,2},{1,5},{3,7},... | collective-permute-start | bytes 1572872 | tf_op jit(solution)/shard_map/ppermute | solution.py:435
  131.9 25.5 %collective-permute-start.24 = (bf16[128,2048]{1,0:T(8,128)(2,1)S(1)}, bf16[128,2048]{1,0:T(8,128)(2,1)S(1)}, u32[]{:S(2)}, u32[]{:S(2)}) collective-permute-start(bf16[128,2048]{1,0:T(8,128)(2,1)S(1)} %get-tuple-element.134), channel_id=1, source_target_pairs={{0,1},{1,0},{2,3},{3,2},{4,5},{5,4},{6,7},{7,6},{8,9},{9,8},{10,11... | collective-permute-start | bytes 1572872 | tf_op jit(solution)/shard_map/ppermute | solution.py:408
  132.5 4.6 %copy-start.4 = (bf16[2,4096,768]{2,1,0:T(8,128)(2,1)S(1)}, bf16[2,4096,768]{2,1,0:T(8,128)(2,1)}, u32[]{:S(2)}) copy-start(bf16[2,4096,768]{2,1,0:T(8,128)(2,1)} %copy-done) | copy-start | bytes 37748740
  157.5 27.4 %copy-start.53 = (bf16[1,128]{1,0:T(2,128)(2,1)S(1)}, bf16[1,128]{1,0:T(2,128)(2,1)}, u32[]{:S(2)}) copy-start(bf16[1,128]{1,0:T(2,128)(2,1)} %get-tuple-element.153.refs_2_) | copy-start | bytes 772
  160.5 24.4 %copy-start.24 = (bf16[128,1024]{1,0:T(8,128)(2,1)S(1)}, bf16[128,1024]{1,0:T(8,128)(2,1)}, u32[]{:S(2)}) copy-start(bf16[128,1024]{1,0:T(8,128)(2,1)} %get-tuple-element.152.refs_1_) | copy-start | bytes 786436
  160.5 2.9 %collective-permute-start.26 = (bf16[2,128,2048]{2,1,0:T(8,128)(2,1)}, bf16[2,128,2048]{2,1,0:T(8,128)(2,1)S(1)}, u32[]{:S(2)}, u32[]{:S(2)}) collective-permute-start(bf16[2,128,2048]{2,1,0:T(8,128)(2,1)} %get-tuple-element.138), channel_id=1, source_target_pairs={{0,2},{2,0},{4,6},{6,4},{8,10},{10,8},{12,14},{14,12},{1,3},{3,1},... | collective-permute-start | bytes 3145736 | tf_op jit(solution)/shard_map/ppermute | solution.py:403
  160.5 16.3 %collective-permute-start.28 = (bf16[128,2048]{1,0:T(8,128)(2,1)}, bf16[128,2048]{1,0:T(8,128)(2,1)S(1)}, u32[]{:S(2)}, u32[]{:S(2)}) collective-permute-start(bf16[128,2048]{1,0:T(8,128)(2,1)} %copy-done.55), channel_id=1, source_target_pairs={{0,4},{2,6},{4,8},{6,10},{8,12},{10,14},{12,0},{14,2},{1,5},{3,7},... | collective-permute-start | bytes 1572872 | tf_op jit(solution)/shard_map/ppermute | solution.py:441
  164.1 14.0 %collective-permute-start.27 = (bf16[128,2048]{1,0:T(8,128)(2,1)S(1)}, bf16[128,2048]{1,0:T(8,128)(2,1)S(1)}, u32[]{:S(2)}, u32[]{:S(2)}) collective-permute-start(bf16[128,2048]{1,0:T(8,128)(2,1)S(1)} %get-tuple-element.143), channel_id=1, source_target_pairs={{0,1},{1,0},{2,3},{3,2},{4,5},{5,4},{6,7},{7,6},{8,9},{9,8},{10,11... | collective-permute-start | bytes 1572872 | tf_op jit(solution)/shard_map/ppermute | solution.py:408
  173.5 5.0 %copy-start.27 = (bf16[2,128,2048]{2,1,0:T(8,128)(2,1)}, bf16[2,128,2048]{2,1,0:T(8,128)(2,1)S(1)}, u32[]{:S(2)}) copy-start(bf16[2,128,2048]{2,1,0:T(8,128)(2,1)S(1)} %get-tuple-element.142.refs_0_) | copy-start | bytes 3145732
  179.6 2.9 %collective-permute-start.29 = (bf16[2,128,2048]{2,1,0:T(8,128)(2,1)}, bf16[2,128,2048]{2,1,0:T(8,128)(2,1)S(1)}, u32[]{:S(2)}, u32[]{:S(2)}) collective-permute-start(bf16[2,128,2048]{2,1,0:T(8,128)(2,1)} %get-tuple-element.147), channel_id=1, source_target_pairs={{0,2},{2,0},{4,6},{6,4},{8,10},{10,8},{12,14},{14,12},{1,3},{3,1},... | collective-permute-start | bytes 3145736 | tf_op jit(solution)/shard_map/ppermute | solution.py:403
  179.6 16.1 %collective-permute-start.31 = (bf16[128,2048]{1,0:T(8,128)(2,1)S(1)}, bf16[128,2048]{1,0:T(8,128)(2,1)S(1)}, u32[]{:S(2)}, u32[]{:S(2)}) collective-permute-start(bf16[128,2048]{1,0:T(8,128)(2,1)S(1)} %get-tuple-element.150), channel_id=1, source_target_pairs={{0,4},{2,6},{4,8},{6,10},{8,12},{10,14},{12,0},{14,2},{1,5},{3,7},... | collective-permute-start | bytes 1572872 | tf_op jit(solution)/shard_map/ppermute | solution.py:446
  183.3 14.0 %collective-permute-start.30 = (bf16[128,2048]{1,0:T(8,128)(2,1)S(1)}, bf16[128,2048]{1,0:T(8,128)(2,1)S(1)}, u32[]{:S(2)}, u32[]{:S(2)}) collective-permute-start(bf16[128,2048]{1,0:T(8,128)(2,1)S(1)} %get-tuple-element.149), channel_id=1, source_target_pairs={{0,1},{1,0},{2,3},{3,2},{4,5},{5,4},{6,7},{7,6},{8,9},{9,8},{10,11... | collective-permute-start | bytes 1572872 | tf_op jit(solution)/shard_map/ppermute | solution.py:408
  (41 other events, 49.6 us)

commit v7 on v6

--- a/solution.py
+++ b/solution.py
@@ -16,6 +16,7 @@
 EPS = 1e-06
 VMEM_LIMIT = 56 * 1024 * 1024
 MXU = 256
+SIDE = 8
 
 
 def weight_work(rows, *weights):
@@ -53,84 +54,88 @@
     count = len(operands)
 
     token = jax.ShapeDtypeStruct((8, 128), jnp.float32)
+    afters = [] if after is None else [after]
 
     def with_token(*refs):
-        inputs, rest = refs[:count], refs[count + 1 :]
+        inputs, rest = refs[:count], refs[count + len(afters) :]
         results, spare = rest[: len(outs)], rest[len(outs) + 1 :]
         rest[len(outs)][...] = jnp.zeros((8, 128), jnp.float32)
         body(*inputs, *results, *spare)
 
-    if after is None:
-        after = jnp.zeros((8, 128), jnp.float32)
     return pl.pallas_call(
         with_token,
         in_specs=[pl.BlockSpec(memory_space=kind) for kind in kinds]
-        + [pl.BlockSpec(memory_space=pl.ANY)],
+        + [pl.BlockSpec(memory_space=pl.ANY)] * len(afters),
         out_specs=in_vmem(len(outs) + 1),
         out_shape=[*outs, token],
         scratch_shapes=scratch,
         compiler_params=pltpu.CompilerParams(vmem_limit_bytes=limit * 1024 * 1024),
         cost_estimate=work,
-    )(*operands, after)
+    )(*operands, *afters)
+
+
+def row_of(gain_ref):
+    return gain_ref[...].astype(jnp.float32).reshape(1, -1)
 
 
 def opening_kernel(x_ref, gain_ref, out_ref):
-    gained = x_ref[...].astype(jnp.float32) * gain_ref[...].astype(jnp.float32)
-    out_ref[...] = gained.astype(jnp.bfloat16)
+    out_ref[...] = (x_ref[...].astype(jnp.float32) * row_of(gain_ref)).astype(jnp.bfloat16)
 
 
 def stats_kernel(first_ref, second_ref, rows_ref, router_ref, small_ref):
-    first = first_ref[...].astype(jnp.float32)
-    second = second_ref[...].astype(jnp.float32)
-    squares = [jnp.sum(x * x, 1, keepdims=True) for x in (first, second)]
-    logits = jnp.dot(rows_ref[...], router_ref[...], preferred_element_type=jnp.float32)
-    fill = jnp.zeros((first.shape[0], 128 - 2 - logits.shape[1]), jnp.float32)
-    small = jnp.concatenate([squares[0], squares[1], logits, fill], 1)
-    small_ref[...] = jnp.transpose(small)[: small_ref.shape[0]]
-
-
-def sides_kernel(mine_ref, other_ref, ids_ref, side_ref, scale_ref):
+    tokens = first_ref.shape[0]
+    squares = []
+    for ref in (first_ref, second_ref):
+        x = ref[...].astype(jnp.float32)
+        squares.append(jnp.sum(x * x, 1, keepdims=True))
+    squares = jnp.concatenate(squares + [jnp.zeros((tokens, 126), jnp.float32)], 1)
+    small_ref[0:SIDE] = jnp.transpose(squares)[0:SIDE]
+    small_ref[SIDE:] = lax.dot_general(
+        router_ref[...],
+        rows_ref[...],
+        (((1,), (1,)), ((), ())),
+        preferred_element_type=jnp.float32,
+    )
+
+
+def sides_kernel(mine_ref, other_ref, ids_ref, side_ref):
     small = mine_ref[...] + other_ref[...]
-    tokens = small.shape[1]
-    fill = jnp.zeros((128 - small.shape[0], tokens), jnp.float32)
-    sums = jnp.transpose(jnp.concatenate([small, fill], 0))
-    lane = lax.broadcasted_iota(jnp.int32, (tokens, 128), 1)
-    scale_ref[...] = jnp.broadcast_to(lax.rsqrt(sums[:, 0:1] / D + EPS), scale_ref.shape)
-    second_scale = lax.rsqrt(sums[:, 1:2] / D + EPS)
-    logits = sums * second_scale
+    scales = lax.rsqrt(small[0:SIDE] / D + EPS)
+    logits = small[SIDE:] * scales[1:2]
+    expert = lax.broadcasted_iota(jnp.int32, logits.shape, 0)
     ids = ids_ref[...]
-    chosen = lane == ids[:, 0:1] + 2
-    for k in range(1, ids.shape[1]):
-        chosen = chosen | (lane == ids[:, k : k + 1] + 2)
-    top = jnp.max(jnp.where(chosen, logits, -jnp.inf), 1, keepdims=True)
+    chosen = expert == ids[0:1]
+    for k in range(1, ids.shape[0]):
+        chosen = chosen | (expert == ids[k : k + 1])
+    top = jnp.max(jnp.where(chosen, logits, -jnp.inf), 0, keepdims=True)
     weights = jnp.where(chosen, jnp.exp(jnp.where(chosen, logits - top, 0.0)), 0.0)
-    weights = weights / jnp.sum(weights, 1, keepdims=True)
-    side = jnp.where(lane == 1, second_scale, weights)
-    side_ref[...] = jnp.transpose(side)[: side_ref.shape[0]]
-
-
-def rows_kernel(where_ref, first_ref, gain_ref, w_ref, scale_ref, owner_ref, kept_ref, sent_ref):
+    side_ref[0:SIDE] = scales
+    side_ref[SIDE:] = weights / jnp.sum(weights, 0, keepdims=True)
+
+
+def rows_kernel(first_ref, gain_ref, w_ref, side_ref, owner_ref, kept_ref, sent_ref):
     tokens = first_ref.shape[0]
-    attn_in = first_ref[...].astype(jnp.float32) * gain_ref[...].astype(jnp.float32)
-    kv = jnp.dot(attn_in.astype(jnp.bfloat16), w_ref[...], preferred_element_type=jnp.float32)
-    kv = (kv * scale_ref[:, 0:1]).astype(jnp.bfloat16)
-    lane = lax.broadcasted_iota(jnp.int32, (tokens, 128), 1)
-    theirs = jnp.where(owner_ref[...] == where_ref[0], 0, 1)
-    hot = (lane == theirs).astype(jnp.float32)
+    attn_in = (first_ref[...].astype(jnp.float32) * row_of(gain_ref)).astype(jnp.bfloat16)
+    kv = jnp.dot(attn_in, w_ref[...], preferred_element_type=jnp.float32)
+    fill = jnp.zeros((tokens - SIDE, tokens), jnp.float32)
+    scales = jnp.transpose(jnp.concatenate([side_ref[0:SIDE], fill], 0))
+    kv = (kv * scales[:, 0:1]).astype(jnp.bfloat16)
+    theirs = jnp.where(owner_ref[...] == lax.axis_index("tp"), 0, 1)
+    hot = lax.broadcasted_iota(jnp.int32, (SIDE, tokens), 0) == theirs
+    hot = jnp.where(hot, 1.0, 0.0)
     row = lax.broadcasted_iota(jnp.int32, (tokens, tokens), 0)
     column = lax.broadcasted_iota(jnp.int32, (tokens, tokens), 1)
-    before = (column < row).astype(jnp.bfloat16)
-    earlier = jnp.dot(before, hot.astype(jnp.bfloat16), preferred_element_type=jnp.float32)
-    slot = jnp.sum(earlier * hot, 1, keepdims=True).astype(jnp.int32)
+    before = jnp.where(row < column, 1.0, 0.0).astype(jnp.bfloat16)
+    earlier = jnp.dot(hot.astype(jnp.bfloat16), before, preferred_element_type=jnp.float32)
+    slot = jnp.sum(earlier * hot, 0, keepdims=True).astype(jnp.int32)
     for side, out_ref in enumerate((kept_ref, sent_ref)):
-        placing = jnp.where((slot == column) & (theirs == side), 1.0, 0.0)
-        placing = jnp.transpose(placing).astype(jnp.bfloat16)
+        placing = jnp.where((slot == row) & (theirs == side), 1.0, 0.0).astype(jnp.bfloat16)
         out = jnp.dot(placing, kv, preferred_element_type=jnp.float32)
         out_ref[...] = out.astype(jnp.bfloat16)
 
 
 def cache_kernel(kept_ref, arrived_ref, gain_ref, out_ref):
-    gain = gain_ref[...].astype(jnp.float32)
+    gain = row_of(gain_ref)
     for head in range(2 * KVH):
         columns = slice(head * HD, (head + 1) * HD)
         x = kept_ref[:, columns].astype(jnp.float32) + arrived_ref[:, columns].astype(jnp.float32)
@@ -159,19 +164,19 @@
         out_specs=[anywhere] * count + in_vmem(1),
         out_shape=[*shapes, jax.ShapeDtypeStruct((8, 128), jnp.float32)],
         input_output_aliases={n: n for n in range(count)},
+        compiler_params=pltpu.CompilerParams(vmem_limit_bytes=1024 * 1024),
         cost_estimate=BRIEF,
     )(*arrays, after)
 
 
-def sum_kernel(part, count, *refs):
-    terms = [ref[part] if len(ref.shape) == 3 else ref[...] for ref in refs[:count]]
-    refs[count][...] = total(*terms)
-
-
-def summed(part, terms, after):
-    out = jax.ShapeDtypeStruct(terms[-1].shape[-2:], jnp.bfloat16)
-    body = functools.partial(sum_kernel, part, len(terms))
-    return whole_call(body, [out], terms, after)
+def sum_kernel(*refs):
+    refs[-1][...] = total(*[ref[...] for ref in refs[:-1]])
+
+
+def summed(terms, after):
+    return whole_call(
+        sum_kernel, [jax.ShapeDtypeStruct(terms[0].shape, jnp.bfloat16)], terms, after, limit=4
+    )
 
 
 def paired_products(rows, steps):
@@ -220,13 +225,14 @@
 
 
 def block_hidden_kernel(
-    where_ref, own_ref, other_ref, sib_own_ref, sib_other_ref, side_ref, wg_ref, wu_ref,
-    out_ref, x_ref,
+    own_ref, other_ref, sib_own_ref, sib_other_ref, side_ref, wg_ref, wu_ref, out_ref, x_ref
 ):
     rows, width = own_ref.shape
     experts, depth, units = wg_ref.shape
-    mine = pl.ds(pl.multiple_of(where_ref[0] * width, width), width)
-    theirs = pl.ds(pl.multiple_of((1 - where_ref[0]) * width, width), width)
+    half = lax.axis_index("tp")
+    first_expert = SIDE + lax.axis_index("ep") * experts
+    mine = pl.ds(pl.multiple_of(half * width, width), width)
+    theirs = pl.ds(pl.multiple_of((1 - half) * width, width), width)
     x_ref[0:rows, mine] = own_ref[...]
     x_ref[0:rows, theirs] = other_ref[...]
     x_ref[rows : 2 * rows, mine] = sib_own_ref[...]
@@ -236,7 +242,7 @@
 
     @pl.loop(0, experts)
     def _(e):
-        weight = column_of(side, 2 + where_ref[1] + e)
+        weight = column_of(side, first_expert + e)
         for tile in range(units // MXU):
             columns = pl.ds(tile * MXU, MXU)
 
@@ -253,73 +259,54 @@
             out_ref[e, :, columns] = silu_up(gate, up, scale, weight)
 
 
-def block_hidden(where, chunks, side, w_gate, w_up, after):
+def block_hidden(chunks, side, w_gate, w_up, after):
     rows, _ = chunks[0].shape
     experts, depth, units = w_gate.shape
     return whole_call(
         block_hidden_kernel,
         [jax.ShapeDtypeStruct((experts, 2 * rows, units), jnp.bfloat16)],
-        [where, *chunks, side, w_gate, w_up],
+        [*chunks, side, w_gate, w_up],
         after,
-        kinds=[pltpu.SMEM] + [pltpu.VMEM] * 7,
         scratch=[pltpu.VMEM((2 * rows, depth), jnp.bfloat16)],
         work=weight_work(2 * rows, w_gate, w_up),
     )
 
 
-def block_down_kernel(where_ref, h_ref, w_ref, own_ref, sib_ref, held_ref, sem):
-    _, rows, width = own_ref.shape
+def block_down_kernel(half, h_ref, w_ref, own_ref, sib_ref):
+    rows, width = own_ref.shape
     experts, _, units = h_ref.shape
-    slots, tile = held_ref.shape[0], held_ref.shape[3]
-    tiles = width // tile
-
-    def fetch(n):
-        half, part = n // tiles, n % tiles
-        first = (half + where_ref[0] - 2 * half * where_ref[0]) * width
-        columns = pl.ds(pl.multiple_of(first + part * tile, tile), tile)
-        return pltpu.make_async_copy(
-            w_ref.at[:, :, columns], held_ref.at[n % slots], sem.at[n % slots]
-        )
-
-    for n in range(slots - 1):
-        fetch(n).start()
-    for n in range(2 * tiles):
-        if n + slots - 1 < 2 * tiles:
-            fetch(n + slots - 1).start()
-        fetch(n).wait()
+    here = lax.axis_index("tp")
+    first = (here + half - 2 * half * here) * width
+
+    @pl.loop(0, width // (2 * MXU))
+    def _(tile):
+        start = pl.multiple_of(tile * (2 * MXU), 2 * MXU)
 
         def step(e, k):
             part = pl.ds(k * MXU, MXU)
+            at = [pl.ds(pl.multiple_of(first + start + MXU * n, MXU), MXU) for n in (0, 1)]
             return (
                 lambda: h_ref[e, :, part],
-                lambda: held_ref[n % slots, e, part, 0:MXU],
-                lambda: held_ref[n % slots, e, part, MXU : 2 * MXU],
+                lambda: w_ref[e, part, at[0]],
+                lambda: w_ref[e, part, at[1]],
             )
 
         steps = [step(e, k) for e in range(experts) for k in range(units // MXU)]
-        for m, y in enumerate(paired_products(2 * rows, steps)):
-            columns = pl.ds((n % tiles) * tile + m * MXU, MXU)
-            own_ref[n // tiles, :, columns] = y[:rows].astype(jnp.bfloat16)
-            sib_ref[n // tiles, :, columns] = y[rows:].astype(jnp.bfloat16)
-
-
-def block_down(where, hidden, w_down, after):
-    experts, tokens, units = hidden.shape
-    rows, width = tokens // 2, w_down.shape[2] // 2
-    out = jax.ShapeDtypeStruct((2, rows, width), jnp.bfloat16)
-    slots = 4
+        for n, y in enumerate(paired_products(2 * rows, steps)):
+            columns = pl.ds(pl.multiple_of(start + n * MXU, MXU), MXU)
+            own_ref[:, columns] = y[:rows].astype(jnp.bfloat16)
+            sib_ref[:, columns] = y[rows:].astype(jnp.bfloat16)
+
+
+def block_down(half, hidden, w_down, after):
+    _, tokens, _ = hidden.shape
+    out = jax.ShapeDtypeStruct((tokens // 2, w_down.shape[2] // 2), jnp.bfloat16)
     return whole_call(
-        block_down_kernel,
+        functools.partial(block_down_kernel, half),
         [out, out],
-        [where, hidden, pltpu.with_memory_space_constraint(w_down, pltpu.HBM)],
+        [hidden, w_down],
         after,
-        kinds=[pltpu.SMEM, pltpu.VMEM, pl.ANY],
-        scratch=[
-            pltpu.VMEM((slots, experts, units, 2 * MXU), jnp.bfloat16),
-            pltpu.SemaphoreType.DMA((slots,)),
-        ],
-        limit=10,
-        work=weight_work(tokens, w_down),
+        work=weight_work(tokens // 2, w_down),
     )
 
 
@@ -348,42 +335,36 @@
     along = functools.partial(lax.ppermute, axis_name="ep", perm=forward)
     beside = functools.partial(lax.ppermute, axis_name="ep", perm=siblings)
     across = functools.partial(lax.ppermute, axis_name="tp", perm=[(0, 1), (1, 0)])
-    where = jnp.stack([lax.axis_index("tp"), lax.axis_index("ep") * w_gate.shape[0]])
-    where = where.astype(jnp.int32)
     rows = stream.shape[0]
-    side_rows = -(-(2 + router.shape[1]) // 8) * 8
     columns = w_kv.shape[1]
+    side_rows = SIDE + router.shape[1]
     row_shape = jax.ShapeDtypeStruct(stream.shape, jnp.bfloat16)
     small_shape = jax.ShapeDtypeStruct((side_rows, rows), jnp.float32)
-    scale_shape = jax.ShapeDtypeStruct((rows, 128), jnp.float32)
     pair_shape = jax.ShapeDtypeStruct((side_rows, 2 * rows), jnp.float32)
     placed_shape = jax.ShapeDtypeStruct((rows, columns), jnp.bfloat16)
-
     layer_input, stream, w_kv = [
         pltpu.with_memory_space_constraint(x, pltpu.HBM) for x in (layer_input, stream, w_kv)
     ]
 
-    rows_out, token = whole_call(opening_kernel, [row_shape], [stream, moe_norm[None]])
+    rows_out, token = whole_call(opening_kernel, [row_shape], [stream, moe_norm])
     lane, crossed = [rows_out, along(rows_out)], [across(rows_out)]
-    where, expert_ids, kv_owner, attn_gain, key_gain, token = tied(
-        [where, expert_ids, kv_owner, attn_norm[None], k_norm[None]], token
-    )
 
     small, token = whole_call(
-        stats_kernel, [small_shape], [layer_input, stream, rows_out, router], token
+        stats_kernel, [small_shape], [layer_input, stream, rows_out, router.T], token
     )
     small_other = across(small)
     gate_held, token = loaded(w_gate, token)
+    up_held, token = loaded(w_up, token)
     lane[1], crossed[0], small_other, token = tied([lane[1], crossed[0], small_other], token)
     lane.append(along(lane[1]))
     crossed.append(across(lane[1]))
-    side, scale, token = whole_call(
-        sides_kernel, [small_shape, scale_shape], [small, small_other, expert_ids], token
+    side, token = whole_call(
+        sides_kernel, [small_shape], [small, small_other, expert_ids.T], token
     )
     side_other = beside(side)
-    up_held, token = loaded(w_up, token)
-    side, token = whole_call(joined_kernel, [pair_shape], [side, side_other], token)
-    sides = [side]
+    down_held, token = loaded(w_down, token)
+    pair, token = whole_call(joined_kernel, [pair_shape], [side, side_other], token)
+    sides = [pair]
     for _ in range(chips - 1):
         sides.append(along(sides[-1]))
 
@@ -391,63 +372,54 @@
 
     def up(s, after):
         chunks = (lane[s], crossed[s], beside(lane[s]), beside(crossed[s]))
-        hidden[s], after = block_hidden(where, chunks, sides[s], gate_held, up_held, after)
+        hidden[s], after = block_hidden(chunks, sides[s], gate_held, up_held, after)
         return after
 
-    def down(s, after):
-        own[s], back[s], after = block_down(where, hidden[s], w_down, after)
+    def down(s, arrays, after, meanwhile=lambda after: after):
+        kept, sent, after = block_down(1, hidden[s], down_held, after)
+        *arrays, sent, after = tied([*arrays, sent], after)
+        own[s], back[s], after = block_down(0, hidden[s], down_held, after)
+        after = meanwhile(after)
+        passed, after = summed([kept, beside(sent)], after)
+        swapped[s] = across(passed)
+        return *arrays, after
+
+    def exchange(s, after):
+        sent, after = tied([back[s]], after)
+        back[s] = beside(sent)
         return after
 
-    def exchange(s, arrays, after):
-        *arrays, sent, after = tied([*arrays, back[s]], after)
-        back[s] = beside(sent)
-        return *arrays, after
-
-    def swap(s, after):
-        sent, after = summed(1, [own[s], back[s]], after)
-        swapped[s] = across(sent)
+    def gather(s, after):
+        passed, after = summed([own[s], back[s], swapped[s]] + travelling, after)
+        travelling[:] = [along(passed)]
         return after
 
-    def gather(s, travelling, after):
-        terms = [own[s], back[s], swapped[s]] + travelling
-        return summed(0, terms, after)
-
+    travelling = []
     token = up(0, token)
+    lane[2], crossed[1], token = tied([lane[2], crossed[1]], token)
+    lane.append(along(lane[2]))
+    crossed.append(across(lane[2]))
     kept, sent, token = whole_call(
         rows_kernel,
         [placed_shape, placed_shape],
-        [where, layer_input, attn_gain, w_kv, scale, kv_owner],
+        [layer_input, attn_norm, w_kv, side, kv_owner.T],
         token,
-        kinds=[pltpu.SMEM] + [pltpu.VMEM] * 5,
         limit=10,
     )
-    lane[2], crossed[1], token = tied([lane[2], crossed[1]], token)
-    lane.append(along(lane[2]))
-    crossed.append(across(lane[2]))
     token = up(1, token)
-    token = down(1, token)
-    lane[3], crossed[2], token = exchange(1, [lane[3], crossed[2]], token)
+    lane[3], crossed[2], token = down(1, [lane[3], crossed[2]], token)
     crossed.append(across(lane[3]))
-    token = swap(1, token)
+    token = exchange(1, token)
     token = up(2, token)
-    token = down(2, token)
-    passed, token = gather(1, [], token)
-    travelling = [along(passed)]
-    crossed[3], token = exchange(2, [crossed[3]], token)
-    token = swap(2, token)
+    crossed[3], token = down(2, [crossed[3]], token, functools.partial(gather, 1))
+    token = exchange(2, token)
     token = up(3, token)
-    token = down(3, token)
-    passed, token = gather(2, travelling, token)
-    travelling = [along(passed)]
-    arrived, token = exchange(3, [across(sent)], token)
-    token = swap(3, token)
-    token = down(0, token)
-    passed, token = gather(3, travelling, token)
-    travelling = [along(passed)]
-    (token,) = exchange(0, [], token)
-    token = swap(0, token)
-    kv_cache, token = whole_call(cache_kernel, [placed_shape], [kept, arrived, key_gain], token)
-    moe_out, token = gather(0, travelling, token)
+    arrived, token = down(3, [across(sent)], token, functools.partial(gather, 2))
+    token = exchange(3, token)
+    kv_cache, token = whole_call(cache_kernel, [placed_shape], [kept, arrived, k_norm], token)
+    (token,) = down(0, [], token, functools.partial(gather, 3))
+    token = exchange(0, token)
+    moe_out, _ = summed([own[0], back[0], swapped[0], *travelling], token)
     return moe_out, kv_cache.reshape(1, 1, rows, columns)
 
 

time: 199 us -> 141 us (0.71)
  local copies, waits for them, and re-layouts: 63.7 us -> 6.14 us
  Pallas kernels: 82.6 us -> 73.4 us
  starting transfers between devices: 17.9 us -> 26.1 us
    unnamed x118 -> x22, local copies, waits for them, and re-layouts: 61.7 us -> 6.14 us
    ppermute x8 -> x12, waiting for transfers between devices: 15.3 us -> 29.8 us  [the longest x4 24.7 us: down(): swapped[s] = across(passed)]
    ppermute x4, waiting for transfers between devices: 10.9 us -> 0.24 us  [exchange(): back[s] = beside(sent)]
    pallas_call x24 -> x29, Pallas kernels: 78.5 us -> 73.3 us  [whole_call(): pl.pallas_call(with_token, in_specs=[pl.BlockSpec(memory_space=kind) for...]
    pallas_call x7 -> x10, Pallas kernels: 4.12 us -> 0.02 us  [tied(): pl.pallas_call(kernel, in_specs=[anywhere] * (count + 1), out_specs=[anyw...]
    ppermute x3, waiting for transfers between devices: 6.24 us -> 2.25 us  [ring_device(): sides.append(along(sides[-1]))]
    ppermute x8 -> x12, starting transfers between devices: 4.79 us -> 7.61 us  [the longest x4 4.2 us: down(): swapped[s] = across(passed)]
  transfers between devices with their start and end apart: 32 -> 36, of which waited for: 11 -> 10; matrix products, arithmetic and copies ran while one was open for 3% -> 0% of each run, Pallas kernels for 39% -> 50%
where the time goes in v7:
time: 141 us
  Pallas kernels  73.4 us (52%)
  waiting for transfers between devices  33.9 us (24%)
  starting transfers between devices  26.1 us (19%)
  local copies, waits for them, and re-layouts  6.14 us (4%)
    pallas_call x29, Pallas kernels, whole_call(): pl.pallas_call(with_token, in_specs=[pl.BlockSpec(memory_space=kind) for...  73.3 us
    ppermute x4, waiting for transfers between devices, down(): swapped[s] = across(passed)  24.7 us
    unnamed x22, local copies, waits for them, and re-layouts  6.14 us
    ppermute x3, waiting for transfers between devices, gather(): travelling[:] = [along(passed)]  5.06 us
    ppermute x2, starting transfers between devices, ring_device(): lane, crossed = ([rows_out, along(rows_out)], [across(rows_out)])  4.57 us
    ppermute x4, starting transfers between devices, down(): swapped[s] = across(passed)  4.2 us
    ppermute x3, starting transfers between devices, ring_device(): sides.append(along(sides[-1]))  3.25 us
    ppermute x3, starting transfers between devices, gather(): travelling[:] = [along(passed)]  2.84 us
  transfers between devices with their start and end apart: 36, of which 10 were waited for; matrix products, arithmetic and copies ran while one was open for 0% of the time, Pallas kernels for 50%

profile of v7, /device:TPU:0, one launch (start us, length us, event | category | flops | bytes accessed | tf_op | source)
XLA Modules:
  0.0 140.6 jit_solution(10609183618941484584)
XLA Ops:
  0.6 0.7 copy-done.3
  1.3 1.1 shard_map.131
  2.5 3.1 %collective-permute-start = (bf16[128,2048]{1,0:T(8,128)(2,1)S(1)}, bf16[128,2048]{1,0:T(8,128)(2,1)S(1)}, u32[]{:S(2)}, u32[]{:S(2)}) collective-permute-start(bf16[128,2048]{1,0:T(8,128)(2,1)S(1)} %get-tuple-element.95.refs_2_.refs_0_), channel_id=1, source_target_pairs={{0,4},{2,6},{4,8},{6,10},{8,12},{10,14},{12,0},{14,2},{1,5},{3,7},... | collective-permute-start | bytes 1572872 | tf_op jit(solution)/shard_map/ppermute | solution.py:350
  5.5 1.5 %collective-permute-start.1 = (bf16[128,2048]{1,0:T(8,128)(2,1)S(1)}, bf16[128,2048]{1,0:T(8,128)(2,1)S(1)}, u32[]{:S(2)}, u32[]{:S(2)}) collective-permute-start(bf16[128,2048]{1,0:T(8,128)(2,1)S(1)} %get-tuple-element.95.refs_2_.refs_0_), channel_id=1, source_target_pairs={{0,1},{1,0},{2,3},{3,2},{4,5},{5,4},{6,7},{7,6},{8,9},{9,8},{10,11... | collective-permute-start | bytes 1572872 | tf_op jit(solution)/shard_map/ppermute | solution.py:350
  7.0 0.8 copy-done.2
  7.9 1.5 %shard_map.132 = (f32[24,128]{1,0:T(8,128)S(1)}, f32[8,128]{1,0:T(8,128)S(1)}) custom-call(bf16[128,2048]{1,0:T(8,128)(2,1)} %refs_0_.11, bf16[128,2048]{1,0:T(8,128)(2,1)} %refs_1_.4, bf16[128,2048]{1,0:T(8,128)(2,1)S(1)} %get-tuple-element.95.refs_2_.refs_0_, bf16[16,2048]{1,0:T(8,128)(2,1)S(1)} %bitcast.6, f32[8,128]{1,0:T(8,128)S(1)} %get-tuple-element.96.refs_4_), custom_call_target="tpu_custom_call" | custom-call | flops 1 | bytes 1 | tf_op jit(solution)/shard_map/pallas_call | solution.py:65
  9.4 0.6 collective-permute-start.2
  10.0 4.6 %shard_map.133 = (bf16[2,4096,768]{2,1,0:T(8,128)(2,1)S(1)}, f32[8,128]{1,0:T(8,128)S(1)}) custom-call(bf16[2,4096,768]{2,1,0:T(8,128)(2,1)} %refs_0_.8, f32[8,128]{1,0:T(8,128)S(1)} %get-tuple-element.98.refs_1_), custom_call_target="tpu_custom_call" | custom-call | flops 12582912 | bytes 12582912 | tf_op jit(solution)/shard_map/pallas_call | solution.py:65
  14.6 4.6 %shard_map.134 = (bf16[2,4096,768]{2,1,0:T(8,128)(2,1)S(1)}, f32[8,128]{1,0:T(8,128)S(1)}) custom-call(bf16[2,4096,768]{2,1,0:T(8,128)(2,1)} %refs_0_.9, f32[8,128]{1,0:T(8,128)S(1)} %get-tuple-element.99.refs_1_), custom_call_target="tpu_custom_call" | custom-call | flops 12582912 | bytes 12582912 | tf_op jit(solution)/shard_map/pallas_call | solution.py:65
  20.1 1.5 %collective-permute-start.6 = (bf16[128,2048]{1,0:T(8,128)(2,1)S(1)}, bf16[128,2048]{1,0:T(8,128)(2,1)S(1)}, u32[]{:S(2)}, u32[]{:S(2)}) collective-permute-start(bf16[128,2048]{1,0:T(8,128)(2,1)S(1)} %get-tuple-element.113.refs_0_), channel_id=1, source_target_pairs={{0,4},{2,6},{4,8},{6,10},{8,12},{10,14},{12,0},{14,2},{1,5},{3,7},... | collective-permute-start | bytes 1572872 | tf_op jit(solution)/shard_map/ppermute | solution.py:359
  21.6 1.5 %collective-permute-start.7 = (bf16[128,2048]{1,0:T(8,128)(2,1)S(1)}, bf16[128,2048]{1,0:T(8,128)(2,1)S(1)}, u32[]{:S(2)}, u32[]{:S(2)}) collective-permute-start(bf16[128,2048]{1,0:T(8,128)(2,1)S(1)} %get-tuple-element.113.refs_0_), channel_id=1, source_target_pairs={{0,1},{1,0},{2,3},{3,2},{4,5},{5,4},{6,7},{7,6},{8,9},{9,8},{10,11... | collective-permute-start | bytes 1572872 | tf_op jit(solution)/shard_map/ppermute | solution.py:360
  23.1 4.9 %shard_map.137 = (bf16[2,768,4096]{2,1,0:T(8,128)(2,1)S(1)}, f32[8,128]{1,0:T(8,128)S(1)}) custom-call(bf16[2,768,4096]{2,1,0:T(8,128)(2,1)} %refs_0_.10, f32[8,128]{1,0:T(8,128)S(1)} %get-tuple-element.105.refs_1_), custom_call_target="tpu_custom_call" | custom-call | flops 12582912 | bytes 12582912 | tf_op jit(solution)/shard_map/pallas_call | solution.py:65
  28.1 0.6 collective-permute-start.11
  28.8 7.7 %shard_map.139 = (bf16[2,256,768]{2,1,0:T(8,128)(2,1)S(1)}, f32[8,128]{1,0:T(8,128)S(1)}) custom-call(bf16[128,2048]{1,0:T(8,128)(2,1)S(1)} %get-tuple-element.95.refs_2_.refs_0_, bf16[128,2048]{1,0:T(8,128)(2,1)S(1)} %get-tuple-element.101.refs_1_, bf16[128,2048]{1,0:T(8,128)(2,1)S(1)} %collective-permute-done.3.refs_2_, ...), custom_call_target="tpu_custom_call" | custom-call | flops 6442450944 | bytes 25165824 | tf_op jit(solution)/shard_map/pallas_call | solution.py:65
  36.6 1.6 %collective-permute-start.13 = (f32[24,256]{1,0:T(8,128)S(1)}, f32[24,256]{1,0:T(8,128)S(1)}, u32[]{:S(2)}, u32[]{:S(2)}) collective-permute-start(f32[24,256]{1,0:T(8,128)S(1)} %get-tuple-element.107.refs_4_), channel_id=1, source_target_pairs={{0,4},{2,6},{4,8},{6,10},{8,12},{10,14},{12,0},{14,2},{1,5},{3,7},... | collective-permute-start | bytes 73736 | tf_op jit(solution)/shard_map/ppermute | solution.py:369
  38.2 1.6 %collective-permute-start.10 = (bf16[128,2048]{1,0:T(8,128)(2,1)S(1)}, bf16[128,2048]{1,0:T(8,128)(2,1)S(1)}, u32[]{:S(2)}, u32[]{:S(2)}) collective-permute-start(bf16[128,2048]{1,0:T(8,128)(2,1)S(1)} %get-tuple-element.118.refs_0_), channel_id=1, source_target_pairs={{0,1},{1,0},{2,3},{3,2},{4,5},{5,4},{6,7},{7,6},{8,9},{9,8},{10,11... | collective-permute-start | bytes 1572872 | tf_op jit(solution)/shard_map/ppermute | solution.py:401
  39.8 1.7 %collective-permute-start.9 = (bf16[128,2048]{1,0:T(8,128)(2,1)S(1)}, bf16[128,2048]{1,0:T(8,128)(2,1)S(1)}, u32[]{:S(2)}, u32[]{:S(2)}) collective-permute-start(bf16[128,2048]{1,0:T(8,128)(2,1)S(1)} %get-tuple-element.118.refs_0_), channel_id=1, source_target_pairs={{0,4},{2,6},{4,8},{6,10},{8,12},{10,14},{12,0},{14,2},{1,5},{3,7},... | collective-permute-start | bytes 1572872 | tf_op jit(solution)/shard_map/ppermute | solution.py:400
  41.4 3.4 %shard_map.141 = (bf16[128,1024]{1,0:T(8,128)(2,1)S(1)}, bf16[128,1024]{1,0:T(8,128)(2,1)S(1)}, f32[8,128]{1,0:T(8,128)S(1)}) custom-call(bf16[128,2048]{1,0:T(8,128)(2,1)} %refs_0_.11, bf16[2048]{0:T(1024)(128)(2,1)S(1)} %copy-done.5, bf16[2048,1024]{1,0:T(8,128)(2,1)} %refs_2_.2, f32[24,128]{1,0:T(8,128)S(1)} %get-tuple-element.104.refs_0_.refs_3_, ...), custom_call_target="tpu_custom_call" | custom-call | flops 1 | bytes 1 | tf_op jit(solution)/shard_map/pallas_call | solution.py:65
  44.9 7.7 %shard_map.142 = (bf16[2,256,768]{2,1,0:T(8,128)(2,1)S(1)}, f32[8,128]{1,0:T(8,128)S(1)}) custom-call(bf16[128,2048]{1,0:T(8,128)(2,1)S(1)} %get-tuple-element.113.refs_0_, bf16[128,2048]{1,0:T(8,128)(2,1)S(1)} %get-tuple-element.119.refs_1_, bf16[128,2048]{1,0:T(8,128)(2,1)S(1)} %collective-permute-done.11.refs_2_, ...), custom_call_target="tpu_custom_call" | custom-call | flops 6442450944 | bytes 25165824 | tf_op jit(solution)/shard_map/pallas_call | solution.py:65
  52.5 2.4 %shard_map.143 = (bf16[128,2048]{1,0:T(8,128)(2,1)S(1)}, bf16[128,2048]{1,0:T(8,128)(2,1)S(1)}, f32[8,128]{1,0:T(8,128)S(1)}) custom-call(bf16[2,256,768]{2,1,0:T(8,128)(2,1)S(1)} %get-tuple-element.121.refs_0_, bf16[2,768,4096]{2,1,0:T(8,128)(2,1)S(1)} %get-tuple-element.112.refs_1_, f32[8,128]{1,0:T(8,128)S(1)} %get-tuple-element.122.refs_2_), custom_call_target="tpu_custom_call" | custom-call | flops 1610612736 | bytes 12582912 | tf_op jit(solution)/shard_map/pallas_call | solution.py:65
  55.3 0.5 collective-permute-start.15
  55.8 2.4 %shard_map.145 = (bf16[128,2048]{1,0:T(8,128)(2,1)S(1)}, bf16[128,2048]{1,0:T(8,128)(2,1)S(1)}, f32[8,128]{1,0:T(8,128)S(1)}) custom-call(bf16[2,256,768]{2,1,0:T(8,128)(2,1)S(1)} %get-tuple-element.121.refs_0_, bf16[2,768,4096]{2,1,0:T(8,128)(2,1)S(1)} %get-tuple-element.112.refs_1_, f32[8,128]{1,0:T(8,128)S(1)} %get-tuple-element.127.refs_2_), custom_call_target="tpu_custom_call" | custom-call | flops 1610612736 | bytes 12582912 | tf_op jit(solution)/shard_map/pallas_call | solution.py:65
  58.2 0.5 collective-permute-start.14
  59.2 2.2 %collective-permute-done.17.refs_4_ = f32[24,256]{1,0:T(8,128)S(1)} collective-permute-done((f32[24,256]{1,0:T(8,128)S(1)}, f32[24,256]{1,0:T(8,128)S(1)}, u32[]{:S(2)}, u32[]{:S(2)}) %collective-permute-start.17) | collective-permute-done | bytes 24608 | tf_op jit(solution)/shard_map/ppermute | solution.py:369
  61.9 7.5 %shard_map.148 = (bf16[2,256,768]{2,1,0:T(8,128)(2,1)S(1)}, f32[8,128]{1,0:T(8,128)S(1)}) custom-call(bf16[128,2048]{1,0:T(8,128)(2,1)S(1)} %get-tuple-element.118.refs_0_, bf16[128,2048]{1,0:T(8,128)(2,1)S(1)} %get-tuple-element.126.refs_1_, bf16[128,2048]{1,0:T(8,128)(2,1)S(1)} %collective-permute-done.15.refs_2_, ...), custom_call_target="tpu_custom_call" | custom-call | flops 6442450944 | bytes 25165824 | tf_op jit(solution)/shard_map/pallas_call | solution.py:65
  69.4 2.4 %shard_map.149 = (bf16[128,2048]{1,0:T(8,128)(2,1)S(1)}, bf16[128,2048]{1,0:T(8,128)(2,1)S(1)}, f32[8,128]{1,0:T(8,128)S(1)}) custom-call(bf16[2,256,768]{2,1,0:T(8,128)(2,1)S(1)} %get-tuple-element.134.refs_0_, bf16[2,768,4096]{2,1,0:T(8,128)(2,1)S(1)} %get-tuple-element.112.refs_1_, f32[8,128]{1,0:T(8,128)S(1)} %get-tuple-element.135.refs_2_), custom_call_target="tpu_custom_call" | custom-call | flops 1610612736 | bytes 12582912 | tf_op jit(solution)/shard_map/pallas_call | solution.py:65
  71.9 1.1 collective-permute-done.14.refs_0_
  73.0 0.5 collective-permute-start.19
  73.5 1.6 %collective-permute-start.21 = (f32[24,256]{1,0:T(8,128)S(1)}, f32[24,256]{1,0:T(8,128)S(1)}, u32[]{:S(2)}, u32[]{:S(2)}) collective-permute-start(f32[24,256]{1,0:T(8,128)S(1)} %collective-permute-done.17.refs_4_), channel_id=1, source_target_pairs={{0,4},{2,6},{4,8},{6,10},{8,12},{10,14},{12,0},{14,2},{1,5},{3,7},... | collective-permute-start | bytes 73736 | tf_op jit(solution)/shard_map/ppermute | solution.py:369
  75.2 2.4 %shard_map.151 = (bf16[128,2048]{1,0:T(8,128)(2,1)S(1)}, bf16[128,2048]{1,0:T(8,128)(2,1)S(1)}, f32[8,128]{1,0:T(8,128)S(1)}) custom-call(bf16[2,256,768]{2,1,0:T(8,128)(2,1)S(1)} %get-tuple-element.134.refs_0_, bf16[2,768,4096]{2,1,0:T(8,128)(2,1)S(1)} %get-tuple-element.112.refs_1_, f32[8,128]{1,0:T(8,128)S(1)} %get-tuple-element.139.refs_2_), custom_call_target="tpu_custom_call" | custom-call | flops 1610612736 | bytes 12582912 | tf_op jit(solution)/shard_map/pallas_call | solution.py:65
  77.6 6.2 %collective-permute-done.24.refs_2_ = bf16[128,2048]{1,0:T(8,128)(2,1)S(1)} collective-permute-done((bf16[128,2048]{1,0:T(8,128)(2,1)S(1)}, bf16[128,2048]{1,0:T(8,128)(2,1)S(1)}, u32[]{:S(2)}, u32[]{:S(2)}) %collective-permute-start.24) | collective-permute-done | bytes 524320 | tf_op jit(solution)/shard_map/ppermute | solution.py:384
  84.7 1.7 %collective-permute-start.27 = (bf16[128,2048]{1,0:T(8,128)(2,1)S(1)}, bf16[128,2048]{1,0:T(8,128)(2,1)S(1)}, u32[]{:S(2)}, u32[]{:S(2)}) collective-permute-start(bf16[128,2048]{1,0:T(8,128)(2,1)S(1)} %get-tuple-element.161), channel_id=1, source_target_pairs={{0,1},{1,0},{2,3},{3,2},{4,5},{5,4},{6,7},{7,6},{8,9},{9,8},{10,11... | collective-permute-start | bytes 1572872 | tf_op jit(solution)/shard_map/ppermute | solution.py:384
  86.4 1.3 collective-permute-start.28
  87.7 4.6 %copy-done.1 = bf16[2,4096,768]{2,1,0:T(8,128)(2,1)S(1)} copy-done((bf16[2,4096,768]{2,1,0:T(8,128)(2,1)S(1)}, bf16[2,4096,768]{2,1,0:T(8,128)(2,1)}, u32[]{:S(2)}) %copy-start.1) | copy-done | bytes 12582936
  92.2 7.5 %shard_map.155 = (bf16[2,256,768]{2,1,0:T(8,128)(2,1)S(1)}, f32[8,128]{1,0:T(8,128)S(1)}) custom-call(bf16[128,2048]{1,0:T(8,128)(2,1)S(1)} %get-tuple-element.125.refs_0_, bf16[128,2048]{1,0:T(8,128)(2,1)S(1)} %get-tuple-element.138.refs_1_, bf16[128,2048]{1,0:T(8,128)(2,1)S(1)} %collective-permute-done.19.refs_2_, ...), custom_call_target="tpu_custom_call" | custom-call | flops 6442450944 | bytes 25165824 | tf_op jit(solution)/shard_map/pallas_call | solution.py:65
  99.8 2.4 %shard_map.156 = (bf16[128,2048]{1,0:T(8,128)(2,1)S(1)}, bf16[128,2048]{1,0:T(8,128)(2,1)S(1)}, f32[8,128]{1,0:T(8,128)S(1)}) custom-call(bf16[2,256,768]{2,1,0:T(8,128)(2,1)S(1)} %get-tuple-element.150.refs_0_, bf16[2,768,4096]{2,1,0:T(8,128)(2,1)S(1)} %get-tuple-element.112.refs_1_, f32[8,128]{1,0:T(8,128)S(1)} %get-tuple-element.151.refs_2_), custom_call_target="tpu_custom_call" | custom-call | flops 1610612736 | bytes 12582912 | tf_op jit(solution)/shard_map/pallas_call | solution.py:65
  102.3 2.4 %shard_map.158 = (bf16[128,2048]{1,0:T(8,128)(2,1)S(1)}, bf16[128,2048]{1,0:T(8,128)(2,1)S(1)}, f32[8,128]{1,0:T(8,128)S(1)}) custom-call(bf16[2,256,768]{2,1,0:T(8,128)(2,1)S(1)} %get-tuple-element.150.refs_0_, bf16[2,768,4096]{2,1,0:T(8,128)(2,1)S(1)} %get-tuple-element.112.refs_1_, f32[8,128]{1,0:T(8,128)S(1)} %get-tuple-element.155.refs_2_), custom_call_target="tpu_custom_call" | custom-call | flops 1610612736 | bytes 12582912 | tf_op jit(solution)/shard_map/pallas_call | solution.py:65
  105.2 0.5 collective-permute-start.30
  106.2 1.6 %collective-permute-start.32 = (bf16[128,2048]{1,0:T(8,128)(2,1)S(1)}, bf16[128,2048]{1,0:T(8,128)(2,1)S(1)}, u32[]{:S(2)}, u32[]{:S(2)}) collective-permute-start(bf16[128,2048]{1,0:T(8,128)(2,1)S(1)} %get-tuple-element.178), channel_id=1, source_target_pairs={{0,4},{2,6},{4,8},{6,10},{8,12},{10,14},{12,0},{14,2},{1,5},{3,7},... | collective-permute-start | bytes 1572872 | tf_op jit(solution)/shard_map/ppermute | solution.py:394
  107.8 0.9 shard_map.162
  108.7 2.4 %shard_map.163 = (bf16[128,2048]{1,0:T(8,128)(2,1)S(1)}, bf16[128,2048]{1,0:T(8,128)(2,1)S(1)}, f32[8,128]{1,0:T(8,128)S(1)}) custom-call(bf16[2,256,768]{2,1,0:T(8,128)(2,1)S(1)} %get-tuple-element.111.refs_0_, bf16[2,768,4096]{2,1,0:T(8,128)(2,1)S(1)} %get-tuple-element.112.refs_1_, f32[8,128]{1,0:T(8,128)S(1)} %get-tuple-element.167.refs_2_), custom_call_target="tpu_custom_call" | custom-call | flops 1610612736 | bytes 12582912 | tf_op jit(solution)/shard_map/pallas_call | solution.py:65
  111.2 2.4 %shard_map.165 = (bf16[128,2048]{1,0:T(8,128)(2,1)S(1)}, bf16[128,2048]{1,0:T(8,128)(2,1)S(1)}, f32[8,128]{1,0:T(8,128)S(1)}) custom-call(bf16[2,256,768]{2,1,0:T(8,128)(2,1)S(1)} %get-tuple-element.111.refs_0_, bf16[2,768,4096]{2,1,0:T(8,128)(2,1)S(1)} %get-tuple-element.112.refs_1_, f32[8,128]{1,0:T(8,128)S(1)} %get-tuple-element.170.refs_2_), custom_call_target="tpu_custom_call" | custom-call | flops 1610612736 | bytes 12582912 | tf_op jit(solution)/shard_map/pallas_call | solution.py:65
  113.7 6.0 %collective-permute-done.31.refs_2_ = bf16[128,2048]{1,0:T(8,128)(2,1)S(1)} collective-permute-done((bf16[128,2048]{1,0:T(8,128)(2,1)S(1)}, bf16[128,2048]{1,0:T(8,128)(2,1)S(1)}, u32[]{:S(2)}, u32[]{:S(2)}) %collective-permute-start.31) | collective-permute-done | bytes 524320 | tf_op jit(solution)/shard_map/ppermute | solution.py:384
  119.7 1.9 %collective-permute-done.32.refs_3_ = bf16[128,2048]{1,0:T(8,128)(2,1)S(1)} collective-permute-done((bf16[128,2048]{1,0:T(8,128)(2,1)S(1)}, bf16[128,2048]{1,0:T(8,128)(2,1)S(1)}, u32[]{:S(2)}, u32[]{:S(2)}) %collective-permute-start.32) | collective-permute-done | bytes 524320 | tf_op jit(solution)/shard_map/ppermute | solution.py:394
  122.1 1.7 %collective-permute-start.34 = (bf16[128,2048]{1,0:T(8,128)(2,1)S(1)}, bf16[128,2048]{1,0:T(8,128)(2,1)S(1)}, u32[]{:S(2)}, u32[]{:S(2)}) collective-permute-start(bf16[128,2048]{1,0:T(8,128)(2,1)S(1)} %get-tuple-element.183), channel_id=1, source_target_pairs={{0,1},{1,0},{2,3},{3,2},{4,5},{5,4},{6,7},{7,6},{8,9},{9,8},{10,11... | collective-permute-start | bytes 1572872 | tf_op jit(solution)/shard_map/ppermute | solution.py:384
  124.0 12.4 %collective-permute-done.34.refs_2_ = bf16[128,2048]{1,0:T(8,128)(2,1)S(1)} collective-permute-done((bf16[128,2048]{1,0:T(8,128)(2,1)S(1)}, bf16[128,2048]{1,0:T(8,128)(2,1)S(1)}, u32[]{:S(2)}, u32[]{:S(2)}) %collective-permute-start.34) | collective-permute-done | bytes 524320 | tf_op jit(solution)/shard_map/ppermute | solution.py:384
  136.5 3.1 %collective-permute-done.35.refs_3_ = bf16[128,2048]{1,0:T(8,128)(2,1)S(1)} collective-permute-done((bf16[128,2048]{1,0:T(8,128)(2,1)S(1)}, bf16[128,2048]{1,0:T(8,128)(2,1)S(1)}, u32[]{:S(2)}, u32[]{:S(2)}) %collective-permute-start.35) | collective-permute-done | bytes 524320 | tf_op jit(solution)/shard_map/ppermute | solution.py:394
  139.6 1.1 shard_map.169
  (86 shorter events, 4.7 us)
Async XLA Ops:
  0.6 0.7 copy-start.3
  2.5 17.0 %collective-permute-start = (bf16[128,2048]{1,0:T(8,128)(2,1)S(1)}, bf16[128,2048]{1,0:T(8,128)(2,1)S(1)}, u32[]{:S(2)}, u32[]{:S(2)}) collective-permute-start(bf16[128,2048]{1,0:T(8,128)(2,1)S(1)} %get-tuple-element.95.refs_2_.refs_0_), channel_id=1, source_target_pairs={{0,4},{2,6},{4,8},{6,10},{8,12},{10,14},{12,0},{14,2},{1,5},{3,7},... | collective-permute-start | bytes 1572872 | tf_op jit(solution)/shard_map/ppermute | solution.py:350
  5.5 14.0 %collective-permute-start.1 = (bf16[128,2048]{1,0:T(8,128)(2,1)S(1)}, bf16[128,2048]{1,0:T(8,128)(2,1)S(1)}, u32[]{:S(2)}, u32[]{:S(2)}) collective-permute-start(bf16[128,2048]{1,0:T(8,128)(2,1)S(1)} %get-tuple-element.95.refs_2_.refs_0_), channel_id=1, source_target_pairs={{0,1},{1,0},{2,3},{3,2},{4,5},{5,4},{6,7},{7,6},{8,9},{9,8},{10,11... | collective-permute-start | bytes 1572872 | tf_op jit(solution)/shard_map/ppermute | solution.py:350
  7.0 0.8 copy-start.2
  9.4 9.9 %collective-permute-start.2 = (f32[24,128]{1,0:T(8,128)S(1)}, f32[24,128]{1,0:T(8,128)S(1)}, u32[]{:S(2)}, u32[]{:S(2)}) collective-permute-start(f32[24,128]{1,0:T(8,128)S(1)} %get-tuple-element.97.refs_0_), channel_id=1, source_target_pairs={{0,1},{1,0},{2,3},{3,2},{4,5},{5,4},{6,7},{7,6},{8,9},{9,8},{10,11... | collective-permute-start | bytes 36872 | tf_op jit(solution)/shard_map/ppermute | solution.py:355
  10.0 18.7 %collective-permute-start.3 = (bf16[128,2048]{1,0:T(8,128)(2,1)S(1)}, bf16[128,2048]{1,0:T(8,128)(2,1)S(1)}, u32[]{:S(2)}, u32[]{:S(2)}) collective-permute-start(bf16[128,2048]{1,0:T(8,128)(2,1)S(1)} %get-tuple-element.95.refs_2_.refs_0_), channel_id=1, source_target_pairs={{0,2},{2,0},{4,6},{6,4},{8,10},{10,8},{12,14},{14,12},{1,3},{3,1},... | collective-permute-start | bytes 1572872 | tf_op jit(solution)/shard_map/ppermute | solution.py:374
  10.0 9.9 %copy-start.4 = (s32[128,8]{0,1:T(8,128)S(1)}, s32[128,8]{0,1:T(8,128)}, u32[]{:S(2)}) copy-start(s32[128,8]{0,1:T(8,128)} %param.14) | copy-start | bytes 12292
  19.3 25.6 %copy-start = (bf16[2,4096,768]{2,1,0:T(8,128)(2,1)}, bf16[2,4096,768]{2,1,0:T(8,128)(2,1)S(1)}, u32[]{:S(2)}) copy-start(bf16[2,4096,768]{2,1,0:T(8,128)(2,1)S(1)} %get-tuple-element.109.refs_6_) | copy-start | bytes 37748740
  19.5 9.2 %collective-permute-start.4 = (bf16[128,2048]{1,0:T(8,128)(2,1)S(1)}, bf16[128,2048]{1,0:T(8,128)(2,1)S(1)}, u32[]{:S(2)}, u32[]{:S(2)}) collective-permute-start(bf16[128,2048]{1,0:T(8,128)(2,1)S(1)} %get-tuple-element.101.refs_1_), channel_id=1, source_target_pairs={{0,2},{2,0},{4,6},{6,4},{8,10},{10,8},{12,14},{14,12},{1,3},{3,1},... | collective-permute-start | bytes 1572872 | tf_op jit(solution)/shard_map/ppermute | solution.py:374
  19.9 8.2 %collective-permute-start.5 = (f32[24,128]{1,0:T(8,128)S(1)}, f32[24,128]{1,0:T(8,128)S(1)}, u32[]{:S(2)}, u32[]{:S(2)}) collective-permute-start(f32[24,128]{1,0:T(8,128)S(1)} %get-tuple-element.104.refs_0_.refs_3_), channel_id=1, source_target_pairs={{0,2},{2,0},{4,6},{6,4},{8,10},{10,8},{12,14},{14,12},{1,3},{3,1},... | collective-permute-start | bytes 36872 | tf_op jit(solution)/shard_map/ppermute | solution.py:364
  20.1 16.3 %collective-permute-start.6 = (bf16[128,2048]{1,0:T(8,128)(2,1)S(1)}, bf16[128,2048]{1,0:T(8,128)(2,1)S(1)}, u32[]{:S(2)}, u32[]{:S(2)}) collective-permute-start(bf16[128,2048]{1,0:T(8,128)(2,1)S(1)} %get-tuple-element.113.refs_0_), channel_id=1, source_target_pairs={{0,4},{2,6},{4,8},{6,10},{8,12},{10,14},{12,0},{14,2},{1,5},{3,7},... | collective-permute-start | bytes 1572872 | tf_op jit(solution)/shard_map/ppermute | solution.py:359
  21.6 14.8 %collective-permute-start.7 = (bf16[128,2048]{1,0:T(8,128)(2,1)S(1)}, bf16[128,2048]{1,0:T(8,128)(2,1)S(1)}, u32[]{:S(2)}, u32[]{:S(2)}) collective-permute-start(bf16[128,2048]{1,0:T(8,128)(2,1)S(1)} %get-tuple-element.113.refs_0_), channel_id=1, source_target_pairs={{0,1},{1,0},{2,3},{3,2},{4,5},{5,4},{6,7},{7,6},{8,9},{9,8},{10,11... | collective-permute-start | bytes 1572872 | tf_op jit(solution)/shard_map/ppermute | solution.py:360
  28.1 16.7 %collective-permute-start.11 = (bf16[128,2048]{1,0:T(8,128)(2,1)S(1)}, bf16[128,2048]{1,0:T(8,128)(2,1)S(1)}, u32[]{:S(2)}, u32[]{:S(2)}) collective-permute-start(bf16[128,2048]{1,0:T(8,128)(2,1)S(1)} %get-tuple-element.113.refs_0_), channel_id=1, source_target_pairs={{0,2},{2,0},{4,6},{6,4},{8,10},{10,8},{12,14},{14,12},{1,3},{3,1},... | collective-permute-start | bytes 1572872 | tf_op jit(solution)/shard_map/ppermute | solution.py:374
  28.7 12.7 %copy-start.5 = (bf16[2048]{0:T(1024)(128)(2,1)S(1)}, bf16[2048]{0:T(1024)(128)(2,1)}, u32[]{:S(2)}) copy-start(bf16[2048]{0:T(1024)(128)(2,1)} %refs_1_.5) | copy-start | bytes 12292
  28.7 12.7 %copy-start.6 = (s32[128,1]{0,1:T(1,128)S(1)}, s32[128,1]{0,1:T(1,128)}, u32[]{:S(2)}) copy-start(s32[128,1]{0,1:T(1,128)} %param.15) | copy-start | bytes 1540
  36.5 8.4 %collective-permute-start.12 = (bf16[128,2048]{1,0:T(8,128)(2,1)S(1)}, bf16[128,2048]{1,0:T(8,128)(2,1)S(1)}, u32[]{:S(2)}, u32[]{:S(2)}) collective-permute-start(bf16[128,2048]{1,0:T(8,128)(2,1)S(1)} %get-tuple-element.119.refs_1_), channel_id=1, source_target_pairs={{0,2},{2,0},{4,6},{6,4},{8,10},{10,8},{12,14},{14,12},{1,3},{3,1},... | collective-permute-start | bytes 1572872 | tf_op jit(solution)/shard_map/ppermute | solution.py:374
  36.6 8.3 %collective-permute-start.13 = (f32[24,256]{1,0:T(8,128)S(1)}, f32[24,256]{1,0:T(8,128)S(1)}, u32[]{:S(2)}, u32[]{:S(2)}) collective-permute-start(f32[24,256]{1,0:T(8,128)S(1)} %get-tuple-element.107.refs_4_), channel_id=1, source_target_pairs={{0,4},{2,6},{4,8},{6,10},{8,12},{10,14},{12,0},{14,2},{1,5},{3,7},... | collective-permute-start | bytes 73736 | tf_op jit(solution)/shard_map/ppermute | solution.py:369
  38.2 16.8 %collective-permute-start.10 = (bf16[128,2048]{1,0:T(8,128)(2,1)S(1)}, bf16[128,2048]{1,0:T(8,128)(2,1)S(1)}, u32[]{:S(2)}, u32[]{:S(2)}) collective-permute-start(bf16[128,2048]{1,0:T(8,128)(2,1)S(1)} %get-tuple-element.118.refs_0_), channel_id=1, source_target_pairs={{0,1},{1,0},{2,3},{3,2},{4,5},{5,4},{6,7},{7,6},{8,9},{9,8},{10,11... | collective-permute-start | bytes 1572872 | tf_op jit(solution)/shard_map/ppermute | solution.py:401
  39.8 15.5 %collective-permute-start.9 = (bf16[128,2048]{1,0:T(8,128)(2,1)S(1)}, bf16[128,2048]{1,0:T(8,128)(2,1)S(1)}, u32[]{:S(2)}, u32[]{:S(2)}) collective-permute-start(bf16[128,2048]{1,0:T(8,128)(2,1)S(1)} %get-tuple-element.118.refs_0_), channel_id=1, source_target_pairs={{0,4},{2,6},{4,8},{6,10},{8,12},{10,14},{12,0},{14,2},{1,5},{3,7},... | collective-permute-start | bytes 1572872 | tf_op jit(solution)/shard_map/ppermute | solution.py:400
  52.5 9.3 %slice-start = ((s8[12582912]{0:T(1024)(128)(4,1)}), s8[4194304]{0:T(1024)(128)(4,1)S(1)}, s32[]{:S(2)}) async-start(s8[12582912]{0:T(1024)(128)(4,1)} %bitcast.4), calls=%async_computation | async-start | bytes 8388608
  52.5 9.3 %slice-start.1 = ((s8[12582912]{0:T(1024)(128)(4,1)}), s8[4194304]{0:T(1024)(128)(4,1)S(1)}, s32[]{:S(2)}) async-start(s8[12582912]{0:T(1024)(128)(4,1)} %bitcast.4), calls=%async_computation.1 | async-start | bytes 8388608
  55.3 3.5 %collective-permute-start.18 = (bf16[128,2048]{1,0:T(8,128)(2,1)S(1)}, bf16[128,2048]{1,0:T(8,128)(2,1)S(1)}, u32[]{:S(2)}, u32[]{:S(2)}) collective-permute-start(bf16[128,2048]{1,0:T(8,128)(2,1)S(1)} %get-tuple-element.130), channel_id=1, source_target_pairs={{0,2},{2,0},{4,6},{6,4},{8,10},{10,8},{12,14},{14,12},{1,3},{3,1},... | collective-permute-start | bytes 1572872 | tf_op jit(solution)/shard_map/ppermute | solution.py:383
  55.3 6.6 %collective-permute-start.15 = (bf16[128,2048]{1,0:T(8,128)(2,1)S(1)}, bf16[128,2048]{1,0:T(8,128)(2,1)S(1)}, u32[]{:S(2)}, u32[]{:S(2)}) collective-permute-start(bf16[128,2048]{1,0:T(8,128)(2,1)S(1)} %get-tuple-element.118.refs_0_), channel_id=1, source_target_pairs={{0,2},{2,0},{4,6},{6,4},{8,10},{10,8},{12,14},{14,12},{1,3},{3,1},... | collective-permute-start | bytes 1572872 | tf_op jit(solution)/shard_map/ppermute | solution.py:374
  55.8 6.1 %collective-permute-start.16 = (bf16[128,2048]{1,0:T(8,128)(2,1)S(1)}, bf16[128,2048]{1,0:T(8,128)(2,1)S(1)}, u32[]{:S(2)}, u32[]{:S(2)}) collective-permute-start(bf16[128,2048]{1,0:T(8,128)(2,1)S(1)} %get-tuple-element.126.refs_1_), channel_id=1, source_target_pairs={{0,2},{2,0},{4,6},{6,4},{8,10},{10,8},{12,14},{14,12},{1,3},{3,1},... | collective-permute-start | bytes 1572872 | tf_op jit(solution)/shard_map/ppermute | solution.py:374
  55.8 5.6 %collective-permute-start.17 = (f32[24,256]{1,0:T(8,128)S(1)}, f32[24,256]{1,0:T(8,128)S(1)}, u32[]{:S(2)}, u32[]{:S(2)}) collective-permute-start(f32[24,256]{1,0:T(8,128)S(1)} %collective-permute-done.13.refs_4_), channel_id=1, source_target_pairs={{0,4},{2,6},{4,8},{6,10},{8,12},{10,14},{12,0},{14,2},{1,5},{3,7},... | collective-permute-start | bytes 73736 | tf_op jit(solution)/shard_map/ppermute | solution.py:369
  55.8 6.1 %slice-start.2 = ((s8[12582912]{0:T(1024)(128)(4,1)}), s8[4194304]{0:T(1024)(128)(4,1)S(1)}, s32[]{:S(2)}) async-start(s8[12582912]{0:T(1024)(128)(4,1)} %bitcast.4), calls=%async_computation.2 | async-start | bytes 8388608
  58.2 14.8 %collective-permute-start.14 = (bf16[128,2048]{1,0:T(8,128)(2,1)S(1)}, bf16[128,2048]{1,0:T(8,128)(2,1)S(1)}, u32[]{:S(2)}, u32[]{:S(2)}) collective-permute-start(bf16[128,2048]{1,0:T(8,128)(2,1)S(1)} %get-tuple-element.125.refs_0_), channel_id=1, source_target_pairs={{0,1},{1,0},{2,3},{3,2},{4,5},{5,4},{6,7},{7,6},{8,9},{9,8},{10,11... | collective-permute-start | bytes 1572872 | tf_op jit(solution)/shard_map/ppermute | solution.py:411
  58.9 14.7 %collective-permute-start.23 = (bf16[128,2048]{1,0:T(8,128)(2,1)S(1)}, bf16[128,2048]{1,0:T(8,128)(2,1)S(1)}, u32[]{:S(2)}, u32[]{:S(2)}) collective-permute-start(bf16[128,2048]{1,0:T(8,128)(2,1)S(1)} %get-tuple-element.144), channel_id=1, source_target_pairs={{0,2},{2,0},{4,6},{6,4},{8,10},{10,8},{12,14},{14,12},{1,3},{3,1},... | collective-permute-start | bytes 1572872 | tf_op jit(solution)/shard_map/ppermute | solution.py:389
  61.4 22.5 %collective-permute-start.24 = (bf16[128,2048]{1,0:T(8,128)(2,1)S(1)}, bf16[128,2048]{1,0:T(8,128)(2,1)S(1)}, u32[]{:S(2)}, u32[]{:S(2)}) collective-permute-start(bf16[128,2048]{1,0:T(8,128)(2,1)S(1)} %get-tuple-element.145), channel_id=1, source_target_pairs={{0,1},{1,0},{2,3},{3,2},{4,5},{5,4},{6,7},{7,6},{8,9},{9,8},{10,11... | collective-permute-start | bytes 1572872 | tf_op jit(solution)/shard_map/ppermute | solution.py:384
  73.0 11.5 %collective-permute-start.22 = (bf16[128,2048]{1,0:T(8,128)(2,1)S(1)}, bf16[128,2048]{1,0:T(8,128)(2,1)S(1)}, u32[]{:S(2)}, u32[]{:S(2)}) collective-permute-start(bf16[128,2048]{1,0:T(8,128)(2,1)S(1)} %get-tuple-element.142), channel_id=1, source_target_pairs={{0,2},{2,0},{4,6},{6,4},{8,10},{10,8},{12,14},{14,12},{1,3},{3,1},... | collective-permute-start | bytes 1572872 | tf_op jit(solution)/shard_map/ppermute | solution.py:383
  73.0 13.4 %collective-permute-start.19 = (bf16[128,2048]{1,0:T(8,128)(2,1)S(1)}, bf16[128,2048]{1,0:T(8,128)(2,1)S(1)}, u32[]{:S(2)}, u32[]{:S(2)}) collective-permute-start(bf16[128,2048]{1,0:T(8,128)(2,1)S(1)} %get-tuple-element.125.refs_0_), channel_id=1, source_target_pairs={{0,2},{2,0},{4,6},{6,4},{8,10},{10,8},{12,14},{14,12},{1,3},{3,1},... | collective-permute-start | bytes 1572872 | tf_op jit(solution)/shard_map/ppermute | solution.py:374
  73.5 14.1 %collective-permute-start.20 = (bf16[128,2048]{1,0:T(8,128)(2,1)S(1)}, bf16[128,2048]{1,0:T(8,128)(2,1)S(1)}, u32[]{:S(2)}, u32[]{:S(2)}) collective-permute-start(bf16[128,2048]{1,0:T(8,128)(2,1)S(1)} %get-tuple-element.138.refs_1_), channel_id=1, source_target_pairs={{0,2},{2,0},{4,6},{6,4},{8,10},{10,8},{12,14},{14,12},{1,3},{3,1},... | collective-permute-start | bytes 1572872 | tf_op jit(solution)/shard_map/ppermute | solution.py:374
  73.5 11.2 %collective-permute-start.21 = (f32[24,256]{1,0:T(8,128)S(1)}, f32[24,256]{1,0:T(8,128)S(1)}, u32[]{:S(2)}, u32[]{:S(2)}) collective-permute-start(f32[24,256]{1,0:T(8,128)S(1)} %collective-permute-done.17.refs_4_), channel_id=1, source_target_pairs={{0,4},{2,6},{4,8},{6,10},{8,12},{10,14},{12,0},{14,2},{1,5},{3,7},... | collective-permute-start | bytes 73736 | tf_op jit(solution)/shard_map/ppermute | solution.py:369
  83.9 18.3 %collective-permute-start.8 = (bf16[128,1024]{1,0:T(8,128)(2,1)S(1)}, bf16[128,1024]{1,0:T(8,128)(2,1)S(1)}, u32[]{:S(2)}, u32[]{:S(2)}) collective-permute-start(bf16[128,1024]{1,0:T(8,128)(2,1)S(1)} %get-tuple-element.117), channel_id=1, source_target_pairs={{0,1},{1,0},{2,3},{3,2},{4,5},{5,4},{6,7},{7,6},{8,9},{9,8},{10,11... | collective-permute-start | bytes 786440 | tf_op jit(solution)/shard_map/ppermute | solution.py:417
  84.6 20.1 %collective-permute-start.26 = (bf16[128,2048]{1,0:T(8,128)(2,1)S(1)}, bf16[128,2048]{1,0:T(8,128)(2,1)S(1)}, u32[]{:S(2)}, u32[]{:S(2)}) collective-permute-start(bf16[128,2048]{1,0:T(8,128)(2,1)S(1)} %get-tuple-element.160), channel_id=1, source_target_pairs={{0,2},{2,0},{4,6},{6,4},{8,10},{10,8},{12,14},{14,12},{1,3},{3,1},... | collective-permute-start | bytes 1572872 | tf_op jit(solution)/shard_map/ppermute | solution.py:389
  84.7 20.0 %collective-permute-start.27 = (bf16[128,2048]{1,0:T(8,128)(2,1)S(1)}, bf16[128,2048]{1,0:T(8,128)(2,1)S(1)}, u32[]{:S(2)}, u32[]{:S(2)}) collective-permute-start(bf16[128,2048]{1,0:T(8,128)(2,1)S(1)} %get-tuple-element.161), channel_id=1, source_target_pairs={{0,1},{1,0},{2,3},{3,2},{4,5},{5,4},{6,7},{7,6},{8,9},{9,8},{10,11... | collective-permute-start | bytes 1572872 | tf_op jit(solution)/shard_map/ppermute | solution.py:384
  86.4 18.4 %collective-permute-start.28 = (bf16[128,2048]{1,0:T(8,128)(2,1)S(1)}, bf16[128,2048]{1,0:T(8,128)(2,1)S(1)}, u32[]{:S(2)}, u32[]{:S(2)}) collective-permute-start(bf16[128,2048]{1,0:T(8,128)(2,1)S(1)} %get-tuple-element.162), channel_id=1, source_target_pairs={{0,4},{2,6},{4,8},{6,10},{8,12},{10,14},{12,0},{14,2},{1,5},{3,7},... | collective-permute-start | bytes 1572872 | tf_op jit(solution)/shard_map/ppermute | solution.py:394
  87.6 4.6 %copy-start.1 = (bf16[2,4096,768]{2,1,0:T(8,128)(2,1)S(1)}, bf16[2,4096,768]{2,1,0:T(8,128)(2,1)}, u32[]{:S(2)}) copy-start(bf16[2,4096,768]{2,1,0:T(8,128)(2,1)} %copy-done) | copy-start | bytes 37748740
  99.8 8.0 %copy-start.7 = (bf16[128]{0:T(256)(128)(2,1)S(1)}, bf16[128]{0:T(256)(128)(2,1)}, u32[]{:S(2)}) copy-start(bf16[128]{0:T(256)(128)(2,1)} %refs_2_.3) | copy-start | bytes 772
  102.2 2.9 %collective-permute-start.25 = (bf16[128,2048]{1,0:T(8,128)(2,1)S(1)}, bf16[128,2048]{1,0:T(8,128)(2,1)S(1)}, u32[]{:S(2)}, u32[]{:S(2)}) collective-permute-start(bf16[128,2048]{1,0:T(8,128)(2,1)S(1)} %get-tuple-element.158), channel_id=1, source_target_pairs={{0,2},{2,0},{4,6},{6,4},{8,10},{10,8},{12,14},{14,12},{1,3},{3,1},... | collective-permute-start | bytes 1572872 | tf_op jit(solution)/shard_map/ppermute | solution.py:383
  105.2 8.4 %collective-permute-start.30 = (bf16[128,2048]{1,0:T(8,128)(2,1)S(1)}, bf16[128,2048]{1,0:T(8,128)(2,1)S(1)}, u32[]{:S(2)}, u32[]{:S(2)}) collective-permute-start(bf16[128,2048]{1,0:T(8,128)(2,1)S(1)} %get-tuple-element.176), channel_id=1, source_target_pairs={{0,2},{2,0},{4,6},{6,4},{8,10},{10,8},{12,14},{14,12},{1,3},{3,1},... | collective-permute-start | bytes 1572872 | tf_op jit(solution)/shard_map/ppermute | solution.py:389
  105.8 13.9 %collective-permute-start.31 = (bf16[128,2048]{1,0:T(8,128)(2,1)S(1)}, bf16[128,2048]{1,0:T(8,128)(2,1)S(1)}, u32[]{:S(2)}, u32[]{:S(2)}) collective-permute-start(bf16[128,2048]{1,0:T(8,128)(2,1)S(1)} %get-tuple-element.177), channel_id=1, source_target_pairs={{0,1},{1,0},{2,3},{3,2},{4,5},{5,4},{6,7},{7,6},{8,9},{9,8},{10,11... | collective-permute-start | bytes 1572872 | tf_op jit(solution)/shard_map/ppermute | solution.py:384
  106.2 15.4 %collective-permute-start.32 = (bf16[128,2048]{1,0:T(8,128)(2,1)S(1)}, bf16[128,2048]{1,0:T(8,128)(2,1)S(1)}, u32[]{:S(2)}, u32[]{:S(2)}) collective-permute-start(bf16[128,2048]{1,0:T(8,128)(2,1)S(1)} %get-tuple-element.178), channel_id=1, source_target_pairs={{0,4},{2,6},{4,8},{6,10},{8,12},{10,14},{12,0},{14,2},{1,5},{3,7},... | collective-permute-start | bytes 1572872 | tf_op jit(solution)/shard_map/ppermute | solution.py:394
  111.1 10.8 %collective-permute-start.29 = (bf16[128,2048]{1,0:T(8,128)(2,1)S(1)}, bf16[128,2048]{1,0:T(8,128)(2,1)S(1)}, u32[]{:S(2)}, u32[]{:S(2)}) collective-permute-start(bf16[128,2048]{1,0:T(8,128)(2,1)S(1)} %get-tuple-element.174), channel_id=1, source_target_pairs={{0,2},{2,0},{4,6},{6,4},{8,10},{10,8},{12,14},{14,12},{1,3},{3,1},... | collective-permute-start | bytes 1572872 | tf_op jit(solution)/shard_map/ppermute | solution.py:383
  122.0 2.0 %collective-permute-start.33 = (bf16[128,2048]{1,0:T(8,128)(2,1)S(1)}, bf16[128,2048]{1,0:T(8,128)(2,1)S(1)}, u32[]{:S(2)}, u32[]{:S(2)}) collective-permute-start(bf16[128,2048]{1,0:T(8,128)(2,1)S(1)} %get-tuple-element.182), channel_id=1, source_target_pairs={{0,2},{2,0},{4,6},{6,4},{8,10},{10,8},{12,14},{14,12},{1,3},{3,1},... | collective-permute-start | bytes 1572872 | tf_op jit(solution)/shard_map/ppermute | solution.py:389
  122.1 14.3 %collective-permute-start.34 = (bf16[128,2048]{1,0:T(8,128)(2,1)S(1)}, bf16[128,2048]{1,0:T(8,128)(2,1)S(1)}, u32[]{:S(2)}, u32[]{:S(2)}) collective-permute-start(bf16[128,2048]{1,0:T(8,128)(2,1)S(1)} %get-tuple-element.183), channel_id=1, source_target_pairs={{0,1},{1,0},{2,3},{3,2},{4,5},{5,4},{6,7},{7,6},{8,9},{9,8},{10,11... | collective-permute-start | bytes 1572872 | tf_op jit(solution)/shard_map/ppermute | solution.py:384
  123.8 15.8 %collective-permute-start.35 = (bf16[128,2048]{1,0:T(8,128)(2,1)S(1)}, bf16[128,2048]{1,0:T(8,128)(2,1)S(1)}, u32[]{:S(2)}, u32[]{:S(2)}) collective-permute-start(bf16[128,2048]{1,0:T(8,128)(2,1)S(1)} %get-tuple-element.184), channel_id=1, source_target_pairs={{0,4},{2,6},{4,8},{6,10},{8,12},{10,14},{12,0},{14,2},{1,5},{3,7},... | collective-permute-start | bytes 1572872 | tf_op jit(solution)/shard_map/ppermute | solution.py:394

commit v8 on v7

--- a/solution.py
+++ b/solution.py
@@ -49,7 +49,7 @@
     return [pl.BlockSpec(memory_space=pltpu.VMEM)] * count
 
 
-def whole_call(body, outs, operands, after=None, kinds=None, scratch=(), limit=6, work=BRIEF):
+def whole_call(body, outs, operands, after=None, kinds=None, scratch=(), limit=2, work=BRIEF):
     kinds = kinds or [pltpu.VMEM] * len(operands)
     count = len(operands)
 
@@ -72,6 +72,13 @@
         compiler_params=pltpu.CompilerParams(vmem_limit_bytes=limit * 1024 * 1024),
         cost_estimate=work,
     )(*operands, *afters)
+
+
+def copies_of(source_ref, held_ref, sem):
+    return [
+        pltpu.make_async_copy(source_ref.at[e], held_ref.at[e], sem.at[e])
+        for e in range(source_ref.shape[0])
+    ]
 
 
 def row_of(gain_ref):
@@ -113,8 +120,13 @@
     side_ref[SIDE:] = weights / jnp.sum(weights, 0, keepdims=True)
 
 
-def rows_kernel(first_ref, gain_ref, w_ref, side_ref, owner_ref, kept_ref, sent_ref):
+def rows_kernel(
+    first_ref, gain_ref, w_ref, side_ref, owner_ref, source_ref, kept_ref, sent_ref, held_ref, sem
+):
     tokens = first_ref.shape[0]
+    copies = copies_of(source_ref, held_ref, sem)
+    for copy in copies:
+        copy.start()
     attn_in = (first_ref[...].astype(jnp.float32) * row_of(gain_ref)).astype(jnp.bfloat16)
     kv = jnp.dot(attn_in, w_ref[...], preferred_element_type=jnp.float32)
     fill = jnp.zeros((tokens - SIDE, tokens), jnp.float32)
@@ -132,6 +144,8 @@
         placing = jnp.where((slot == row) & (theirs == side), 1.0, 0.0).astype(jnp.bfloat16)
         out = jnp.dot(placing, kv, preferred_element_type=jnp.float32)
         out_ref[...] = out.astype(jnp.bfloat16)
+    for copy in copies:
+        copy.wait()
 
 
 def cache_kernel(kept_ref, arrived_ref, gain_ref, out_ref):
@@ -169,42 +183,60 @@
     )(*arrays, after)
 
 
-def sum_kernel(*refs):
-    refs[-1][...] = total(*[ref[...] for ref in refs[:-1]])
-
-
-def summed(terms, after):
-    return whole_call(
-        sum_kernel, [jax.ShapeDtypeStruct(terms[0].shape, jnp.bfloat16)], terms, after, limit=4
-    )
-
-
-def paired_products(rows, steps):
+def sum_kernel(first, *refs):
+    *terms, out_ref = refs
+    rows = out_ref.shape[0]
+    at = [pl.ds(first if ref.shape[0] > rows else 0, rows) for ref in terms]
+    out_ref[...] = total(*[ref[part] for ref, part in zip(terms, at)])
+
+
+def summed(terms, after, first=0, rows=None, work=BRIEF):
+    rows = rows or terms[0].shape[0]
+    out = jax.ShapeDtypeStruct((rows, terms[0].shape[1]), jnp.bfloat16)
+    return whole_call(functools.partial(sum_kernel, first), [out], terms, after, work=work)
+
+
+def final_kernel(*refs):
+    *terms, out_ref = refs
+    rows = out_ref.shape[0] // 2
+    for n in range(2):
+        part = pl.ds(n * rows, rows)
+        whole = [ref[part] for ref in terms if ref.shape[0] > rows]
+        halves = [ref[...] for ref in terms if ref.shape[0] == rows][n::2]
+        out_ref[part] = total(*whole, *halves)
+
+
+def paired_products(rows, tiles):
+    flat = [(t, k) for t, (steps, _) in enumerate(tiles) for k in range(len(steps))]
+
     def stage(index):
-        _, first_tile, second_tile = steps[index]
+        t, k = flat[index]
+        _, first_tile, second_tile = tiles[t][0][k]
         pltpu.matmul_push_rhs(first_tile(), index % 2, 0)
         pltpu.matmul_push_rhs(second_tile(), index % 2, 1)
 
-    def run(first_acc, second_acc):
+    def run(*accs):
+        def finish(t):
+            first, second = accs[t % 2], accs[2 + t % 2]
+            tiles[t][1](pltpu.matmul_pop(first), pltpu.matmul_pop(second))
+
         stage(0)
-        for index, (lhs, _, _) in enumerate(steps):
-            if index + 1 < len(steps):
+        for index, (t, k) in enumerate(flat):
+            if index + 1 < len(flat):
                 stage(index + 1)
-            left = lhs()
-            pltpu.matmul_acc_lhs(first_acc, left, index % 2)
-            pltpu.matmul_acc_lhs(second_acc, left, index % 2)
-        return pltpu.matmul_pop(first_acc), pltpu.matmul_pop(second_acc)
-
-    return pl.run_scoped(
-        run, pltpu.ACC(0)((rows, MXU), jnp.float32), pltpu.ACC(1)((rows, MXU), jnp.float32)
-    )
+            left = tiles[t][0][k][0]()
+            pltpu.matmul_acc_lhs(accs[t % 2], left, index % 2)
+            pltpu.matmul_acc_lhs(accs[2 + t % 2], left, index % 2)
+            if t and k == 1:
+                finish(t - 1)
+        finish(len(tiles) - 1)
+
+    kinds = [pltpu.ACC(unit)((rows, MXU), jnp.float32) for unit in (0, 0, 1, 1)]
+    pl.run_scoped(run, *kinds)
 
 
 def load_kernel(source_ref, held_ref, sem):
-    copies = [
-        pltpu.make_async_copy(source_ref.at[e], held_ref.at[e], sem.at[e])
-        for e in range(source_ref.shape[0])
-    ]
+    copies = copies_of(source_ref, held_ref, sem)
     for copy in copies:
         copy.start()
     for copy in copies:
@@ -243,7 +275,8 @@
     @pl.loop(0, experts)
     def _(e):
         weight = column_of(side, first_expert + e)
-        for tile in range(units // MXU):
+
+        def tile_of_units(tile):
             columns = pl.ds(tile * MXU, MXU)
 
             def step(k):
@@ -254,9 +287,12 @@
                     lambda: wu_ref[e, part, columns],
                 )
 
-            steps = [step(k) for k in range(depth // MXU)]
-            gate, up = paired_products(2 * rows, steps)
-            out_ref[e, :, columns] = silu_up(gate, up, scale, weight)
+            def finish(gate, up):
+                out_ref[e, :, columns] = silu_up(gate, up, scale, weight)
+
+            return [step(k) for k in range(depth // MXU)], finish
+
+        paired_products(2 * rows, [tile_of_units(tile) for tile in range(units // MXU)])
 
 
 def block_hidden(chunks, side, w_gate, w_up, after):
@@ -268,19 +304,20 @@
         [*chunks, side, w_gate, w_up],
         after,
         scratch=[pltpu.VMEM((2 * rows, depth), jnp.bfloat16)],
+        limit=4,
         work=weight_work(2 * rows, w_gate, w_up),
     )
 
 
-def block_down_kernel(half, h_ref, w_ref, own_ref, sib_ref):
+def block_down_kernel(half, h_ref, w_ref, own_ref, *sib_refs):
     rows, width = own_ref.shape
+    count = rows // len(sib_refs)
     experts, _, units = h_ref.shape
     here = lax.axis_index("tp")
     first = (here + half - 2 * half * here) * width
 
-    @pl.loop(0, width // (2 * MXU))
-    def _(tile):
-        start = pl.multiple_of(tile * (2 * MXU), 2 * MXU)
+    def tile_of_columns(tile):
+        start = tile * (2 * MXU)
 
         def step(e, k):
             part = pl.ds(k * MXU, MXU)
@@ -291,22 +328,30 @@
                 lambda: w_ref[e, part, at[1]],
             )
 
-        steps = [step(e, k) for e in range(experts) for k in range(units // MXU)]
-        for n, y in enumerate(paired_products(2 * rows, steps)):
-            columns = pl.ds(pl.multiple_of(start + n * MXU, MXU), MXU)
-            own_ref[:, columns] = y[:rows].astype(jnp.bfloat16)
-            sib_ref[:, columns] = y[rows:].astype(jnp.bfloat16)
-
-
-def block_down(half, hidden, w_down, after):
+        def finish(*products):
+            for n, y in enumerate(products):
+                columns = pl.ds(start + n * MXU, MXU)
+                own_ref[:, columns] = y[:rows].astype(jnp.bfloat16)
+                for m, sib_ref in enumerate(sib_refs):
+                    part = y[rows + m * count : rows + (m + 1) * count]
+                    sib_ref[:, columns] = part.astype(jnp.bfloat16)
+
+        return [step(e, k) for e in range(experts) for k in range(units // MXU)], finish
+
+    paired_products(2 * rows, [tile_of_columns(n) for n in range(width // (2 * MXU))])
+
+
+def block_down(half, hidden, w_down, after, parts=1):
     _, tokens, _ = hidden.shape
-    out = jax.ShapeDtypeStruct((tokens // 2, w_down.shape[2] // 2), jnp.bfloat16)
+    rows, width = tokens // 2, w_down.shape[2] // 2
+    out = jax.ShapeDtypeStruct((rows, width), jnp.bfloat16)
+    part = jax.ShapeDtypeStruct((rows // parts, width), jnp.bfloat16)
     return whole_call(
         functools.partial(block_down_kernel, half),
-        [out, out],
+        [out] + [part] * parts,
         [hidden, w_down],
         after,
-        work=weight_work(tokens // 2, w_down),
+        work=weight_work(rows, w_down),
     )
 
 
@@ -342,15 +387,18 @@
     small_shape = jax.ShapeDtypeStruct((side_rows, rows), jnp.float32)
     pair_shape = jax.ShapeDtypeStruct((side_rows, 2 * rows), jnp.float32)
     placed_shape = jax.ShapeDtypeStruct((rows, columns), jnp.bfloat16)
-    layer_input, stream, w_kv = [
-        pltpu.with_memory_space_constraint(x, pltpu.HBM) for x in (layer_input, stream, w_kv)
+    layer_input, stream, w_kv, w_down = [
+        pltpu.with_memory_space_constraint(x, pltpu.HBM)
+        for x in (layer_input, stream, w_kv, w_down)
     ]
 
-    rows_out, token = whole_call(opening_kernel, [row_shape], [stream, moe_norm])
+    rows_out, token = whole_call(
+        opening_kernel, [row_shape], [stream, moe_norm], limit=8
+    )
     lane, crossed = [rows_out, along(rows_out)], [across(rows_out)]
 
     small, token = whole_call(
-        stats_kernel, [small_shape], [layer_input, stream, rows_out, router.T], token
+        stats_kernel, [small_shape], [layer_input, stream, rows_out, router.T], token, limit=8
     )
     small_other = across(small)
     gate_held, token = loaded(w_gate, token)
@@ -362,64 +410,85 @@
         sides_kernel, [small_shape], [small, small_other, expert_ids.T], token
     )
     side_other = beside(side)
-    down_held, token = loaded(w_down, token)
+    kept, sent, down_held, token = whole_call(
+        rows_kernel,
+        [placed_shape, placed_shape, pltpu.VMEM(w_down.shape, w_down.dtype)],
+        [layer_input, attn_norm, w_kv, side, kv_owner.T, w_down],
+        token,
+        kinds=[pltpu.VMEM] * 5 + [pl.ANY],
+        scratch=[pltpu.SemaphoreType.DMA((w_down.shape[0],))],
+        limit=7,
+    )
     pair, token = whole_call(joined_kernel, [pair_shape], [side, side_other], token)
     sides = [pair]
-    for _ in range(chips - 1):
-        sides.append(along(sides[-1]))
+    for s in range(1, chips):
+        ahead = [(d, (d + 2 * s) % ep_count) for d in range(ep_count)]
+        sides.append(lax.ppermute(pair, "ep", ahead))
 
     hidden, own, back, swapped = [[None] * chips for _ in range(4)]
 
+    def chunks(s):
+        return (lane[s], crossed[s], beside(lane[s]), beside(crossed[s]))
+
     def up(s, after):
-        chunks = (lane[s], crossed[s], beside(lane[s]), beside(crossed[s]))
-        hidden[s], after = block_hidden(chunks, sides[s], gate_held, up_held, after)
+        hidden[s], after = block_hidden(chunks(s), sides[s], gate_held, up_held, after)
         return after
 
-    def down(s, arrays, after, meanwhile=lambda after: after):
-        kept, sent, after = block_down(1, hidden[s], down_held, after)
-        *arrays, sent, after = tied([*arrays, sent], after)
+    def down(s, arrays, after, meanwhile=lambda after: after, parts=1):
+        sent_parts = 1 if s else 2
+        kept, *sent, after = block_down(1, hidden[s], down_held, after, sent_parts)
+        *taken, after = tied([*arrays, *sent], after)
         own[s], back[s], after = block_down(0, hidden[s], down_held, after)
         after = meanwhile(after)
-        passed, after = summed([kept, beside(sent)], after)
-        swapped[s] = across(passed)
-        return *arrays, after
+        returned, swapped[s] = [beside(x) for x in taken[len(arrays) :]], []
+        if s == 0:
+            passed, after = whole_call(final_kernel, [row_shape], [kept, *returned], after)
+            swapped[s].append(across(passed))
+            return after
+        for n in range(parts):
+            count = rows // parts
+            passed, after = summed([kept, *returned], after, n * count, count)
+            swapped[s].append(across(passed))
+        return *taken[: len(arrays)], after
 
     def exchange(s, after):
         sent, after = tied([back[s]], after)
         back[s] = beside(sent)
         return after
 
-    def gather(s, after):
-        passed, after = summed([own[s], back[s], swapped[s]] + travelling, after)
-        travelling[:] = [along(passed)]
+    def gather(s, after, part=0):
+        count = swapped[s][part].shape[0]
+        terms = [own[s], back[s], swapped[s][part], *travelling[s]]
+        passed, after = summed(terms, after, part * count, count, weight_work(1, w_gate, w_up))
+        travelling[(s + 1) % chips].append(along(passed))
         return after
 
-    travelling = []
+    travelling = [[] for _ in range(chips)]
     token = up(0, token)
-    lane[2], crossed[1], token = tied([lane[2], crossed[1]], token)
+    lane[2], crossed[1], *sides[1:], token = tied([lane[2], crossed[1], *sides[1:]], token)
     lane.append(along(lane[2]))
     crossed.append(across(lane[2]))
-    kept, sent, token = whole_call(
-        rows_kernel,
-        [placed_shape, placed_shape],
-        [layer_input, attn_norm, w_kv, side, kv_owner.T],
-        token,
-        limit=10,
-    )
     token = up(1, token)
     lane[3], crossed[2], token = down(1, [lane[3], crossed[2]], token)
-    crossed.append(across(lane[3]))
+    crossed.append(along(crossed[2]))
     token = exchange(1, token)
     token = up(2, token)
     crossed[3], token = down(2, [crossed[3]], token, functools.partial(gather, 1))
     token = exchange(2, token)
     token = up(3, token)
-    arrived, token = down(3, [across(sent)], token, functools.partial(gather, 2))
+    arrived, token = down(3, [across(sent)], token, functools.partial(gather, 2), 2)
     token = exchange(3, token)
     kv_cache, token = whole_call(cache_kernel, [placed_shape], [kept, arrived, k_norm], token)
-    (token,) = down(0, [], token, functools.partial(gather, 3))
+    token = down(0, [], token, functools.partial(gather, 3))
+    token = gather(3, token, 1)
     token = exchange(0, token)
-    moe_out, _ = summed([own[0], back[0], swapped[0], *travelling], token)
+    moe_out, _ = whole_call(
+        final_kernel,
+        [row_shape],
+        [own[0], back[0], *swapped[0], *travelling[0]],
+        token,
+        limit=4,
+    )
     return moe_out, kv_cache.reshape(1, 1, rows, columns)
 
 

time: 141 us -> 138 us (0.979)
  Pallas kernels: 73.4 us -> 67.1 us
  waiting for transfers between devices: 33.9 us -> 36.6 us
    pallas_call x29 -> x30, Pallas kernels: 73.3 us -> 67.1 us  [whole_call(): pl.pallas_call(with_token, in_specs=[pl.BlockSpec(memory_space=kind) for...]
    ppermute x1, waiting for transfers between devices: 0.26 us -> 4.45 us  [ring_device(): lane.append(along(lane[2]))]
    ppermute x23 -> x26, waiting for transfers between devices: 33.2 us -> 32.1 us  [the longest x4 19.2 us: gather(): travelling[(s + 1) % chips].append(along(passed))]
    ppermute x23 -> x26, starting transfers between devices: 13.1 us -> 13.8 us  [the longest x5 5.83 us: down(): swapped[s].append(across(passed))]
  transfers between devices with their start and end apart: 36 -> 39, of which waited for: 10 -> 8; matrix products, arithmetic and copies ran while one was open for 0% -> 0% of each run, Pallas kernels for 50% -> 47%
where the time goes in v8:
time: 138 us; the launch traced here: 137 us
  Pallas kernels  67.1 us (49%)
  waiting for transfers between devices  36.6 us (27%)
  starting transfers between devices  26.4 us (19%)
  local copies, waits for them, and re-layouts  6.14 us (4%)
    pallas_call x30, Pallas kernels, whole_call(): pl.pallas_call(with_token, in_specs=[pl.BlockSpec(memory_space=kind) for...  67.1 us
    ppermute x4, waiting for transfers between devices, gather(): travelling[(s + 1) % chips].append(along(passed))  19.2 us
    ppermute x5, waiting for transfers between devices, down(): swapped[s].append(across(passed))  9.96 us
    unnamed x22, local copies, waits for them, and re-layouts  6.14 us
    ppermute x5, starting transfers between devices, down(): swapped[s].append(across(passed))  5.83 us
    ppermute x2, starting transfers between devices, ring_device(): lane, crossed = ([rows_out, along(rows_out)], [across(rows_out)])  4.57 us
    ppermute x1, waiting for transfers between devices, ring_device(): lane.append(along(lane[2]))  4.45 us
    ppermute x3, starting transfers between devices, ring_device(): sides.append(lax.ppermute(pair, 'ep', ahead))  4.06 us
  transfers between devices with their start and end apart: 39, of which 8 were waited for; matrix products, arithmetic and copies ran while one was open for 0% of the time, Pallas kernels for 47%

profile of v8, /device:TPU:0, one launch (start us, length us, event | category | flops | bytes accessed | tf_op | source)
XLA Modules:
  0.0 137.4 jit_solution(16363696263283496616)
XLA Ops:
  0.6 0.7 copy-done.3
  1.3 1.1 shard_map.131
  2.5 3.1 %collective-permute-start = (bf16[128,2048]{1,0:T(8,128)(2,1)S(1)}, bf16[128,2048]{1,0:T(8,128)(2,1)S(1)}, u32[]{:S(2)}, u32[]{:S(2)}) collective-permute-start(bf16[128,2048]{1,0:T(8,128)(2,1)S(1)} %get-tuple-element.103.refs_2_.refs_0_), channel_id=1, source_target_pairs={{0,4},{2,6},{4,8},{6,10},{8,12},{10,14},{12,0},{14,2},{1,5},{3,7},... | collective-permute-start | bytes 1572872 | tf_op jit(solution)/shard_map/ppermute | solution.py:398
  5.5 1.5 %collective-permute-start.1 = (bf16[128,2048]{1,0:T(8,128)(2,1)S(1)}, bf16[128,2048]{1,0:T(8,128)(2,1)S(1)}, u32[]{:S(2)}, u32[]{:S(2)}) collective-permute-start(bf16[128,2048]{1,0:T(8,128)(2,1)S(1)} %get-tuple-element.103.refs_2_.refs_0_), channel_id=1, source_target_pairs={{0,1},{1,0},{2,3},{3,2},{4,5},{5,4},{6,7},{7,6},{8,9},{9,8},{10,11... | collective-permute-start | bytes 1572872 | tf_op jit(solution)/shard_map/ppermute | solution.py:398
  7.0 0.8 copy-done.2
  7.9 1.5 %shard_map.132 = (f32[24,128]{1,0:T(8,128)S(1)}, f32[8,128]{1,0:T(8,128)S(1)}) custom-call(bf16[128,2048]{1,0:T(8,128)(2,1)} %refs_0_.9, bf16[128,2048]{1,0:T(8,128)(2,1)} %refs_1_.4, bf16[128,2048]{1,0:T(8,128)(2,1)S(1)} %get-tuple-element.103.refs_2_.refs_0_, bf16[16,2048]{1,0:T(8,128)(2,1)S(1)} %bitcast.6, f32[8,128]{1,0:T(8,128)S(1)} %get-tuple-element.104.refs_4_), custom_call_target="tpu_custom_call" | custom-call | flops 1 | bytes 1 | tf_op jit(solution)/shard_map/pallas_call | solution.py:65
  9.4 0.6 collective-permute-start.2
  10.0 4.7 %shard_map.133 = (bf16[2,4096,768]{2,1,0:T(8,128)(2,1)S(1)}, f32[8,128]{1,0:T(8,128)S(1)}) custom-call(bf16[2,4096,768]{2,1,0:T(8,128)(2,1)} %refs_0_.7, f32[8,128]{1,0:T(8,128)S(1)} %get-tuple-element.106.refs_1_), custom_call_target="tpu_custom_call" | custom-call | flops 12582912 | bytes 12582912 | tf_op jit(solution)/shard_map/pallas_call | solution.py:65
  14.7 4.6 %shard_map.134 = (bf16[2,4096,768]{2,1,0:T(8,128)(2,1)S(1)}, f32[8,128]{1,0:T(8,128)S(1)}) custom-call(bf16[2,4096,768]{2,1,0:T(8,128)(2,1)} %refs_0_.8, f32[8,128]{1,0:T(8,128)S(1)} %get-tuple-element.107.refs_1_), custom_call_target="tpu_custom_call" | custom-call | flops 12582912 | bytes 12582912 | tf_op jit(solution)/shard_map/pallas_call | solution.py:65
  19.3 4.6 %copy-done = bf16[2,4096,768]{2,1,0:T(8,128)(2,1)} copy-done((bf16[2,4096,768]{2,1,0:T(8,128)(2,1)}, bf16[2,4096,768]{2,1,0:T(8,128)(2,1)S(1)}, u32[]{:S(2)}) %copy-start) | copy-done | bytes 12582936
  23.9 0.6 collective-permute-start.4
  24.6 1.6 %collective-permute-start.7 = (bf16[128,2048]{1,0:T(8,128)(2,1)S(1)}, bf16[128,2048]{1,0:T(8,128)(2,1)S(1)}, u32[]{:S(2)}, u32[]{:S(2)}) collective-permute-start(bf16[128,2048]{1,0:T(8,128)(2,1)S(1)} %get-tuple-element.123.refs_0_), channel_id=1, source_target_pairs={{0,4},{2,6},{4,8},{6,10},{8,12},{10,14},{12,0},{14,2},{1,5},{3,7},... | collective-permute-start | bytes 1572872 | tf_op jit(solution)/shard_map/ppermute | solution.py:407
  26.2 1.5 %collective-permute-start.8 = (bf16[128,2048]{1,0:T(8,128)(2,1)S(1)}, bf16[128,2048]{1,0:T(8,128)(2,1)S(1)}, u32[]{:S(2)}, u32[]{:S(2)}) collective-permute-start(bf16[128,2048]{1,0:T(8,128)(2,1)S(1)} %get-tuple-element.123.refs_0_), channel_id=1, source_target_pairs={{0,1},{1,0},{2,3},{3,2},{4,5},{5,4},{6,7},{7,6},{8,9},{9,8},{10,11... | collective-permute-start | bytes 1572872 | tf_op jit(solution)/shard_map/ppermute | solution.py:408
  27.7 7.0 %shard_map.137 = (bf16[128,1024]{1,0:T(8,128)(2,1)S(1)}, bf16[128,1024]{1,0:T(8,128)(2,1)S(1)}, bf16[2,768,4096]{2,1,0:T(8,128)(2,1)S(1)}, f32[8,128]{1,0:T(8,128)S(1)}) custom-call(bf16[128,2048]{1,0:T(8,128)(2,1)} %refs_0_.9, bf16[2048]{0:T(1024)(128)(2,1)S(1)} %copy-done.4, bf16[2048,1024]{1,0:T(8,128)(2,1)} %refs_2_.2, ...), custom_call_target="tpu_custom_call" | custom-call | flops 1 | bytes 1 | tf_op jit(solution)/shard_map/pallas_call | solution.py:65
  34.8 2.0 %collective-permute-start.10 = (f32[24,256]{1,0:T(8,128)S(1)}, f32[24,256]{1,0:T(8,128)S(1)}, u32[]{:S(2)}, u32[]{:S(2)}) collective-permute-start(f32[24,256]{1,0:T(8,128)S(1)} %get-tuple-element.115.refs_4_), channel_id=1, source_target_pairs={{0,8},{2,10},{4,12},{6,14},{8,0},{10,2},{12,4},{14,6},{1,9},{3,11}... | collective-permute-start | bytes 73736 | tf_op jit(solution)/shard_map/ppermute | solution.py:426
  36.8 2.0 %collective-permute-start.11 = (f32[24,256]{1,0:T(8,128)S(1)}, f32[24,256]{1,0:T(8,128)S(1)}, u32[]{:S(2)}, u32[]{:S(2)}) collective-permute-start(f32[24,256]{1,0:T(8,128)S(1)} %get-tuple-element.115.refs_4_), channel_id=1, source_target_pairs={{0,12},{2,14},{4,0},{6,2},{8,4},{10,6},{12,8},{14,10},{1,13},{3,15... | collective-permute-start | bytes 73736 | tf_op jit(solution)/shard_map/ppermute | solution.py:426
  38.9 7.5 %shard_map.139 = (bf16[2,256,768]{2,1,0:T(8,128)(2,1)S(1)}, f32[8,128]{1,0:T(8,128)S(1)}) custom-call(bf16[128,2048]{1,0:T(8,128)(2,1)S(1)} %get-tuple-element.103.refs_2_.refs_0_, bf16[128,2048]{1,0:T(8,128)(2,1)S(1)} %get-tuple-element.109.refs_1_, bf16[128,2048]{1,0:T(8,128)(2,1)S(1)} %collective-permute-done.3.refs_2_, ...), custom_call_target="tpu_custom_call" | custom-call | flops 6442450944 | bytes 25165824 | tf_op jit(solution)/shard_map/pallas_call | solution.py:65
  46.5 0.5 collective-permute-start.15
  47.1 0.8 collective-permute-start.12
  47.9 1.2 collective-permute-start.13
  49.1 7.5 %shard_map.141 = (bf16[2,256,768]{2,1,0:T(8,128)(2,1)S(1)}, f32[8,128]{1,0:T(8,128)S(1)}) custom-call(bf16[128,2048]{1,0:T(8,128)(2,1)S(1)} %get-tuple-element.123.refs_0_, bf16[128,2048]{1,0:T(8,128)(2,1)S(1)} %get-tuple-element.126.refs_1_, bf16[128,2048]{1,0:T(8,128)(2,1)S(1)} %collective-permute-done.14.refs_2_, ...), custom_call_target="tpu_custom_call" | custom-call | flops 6442450944 | bytes 25165824 | tf_op jit(solution)/shard_map/pallas_call | solution.py:65
  56.6 1.9 %shard_map.142 = (bf16[128,2048]{1,0:T(8,128)(2,1)S(1)}, bf16[128,2048]{1,0:T(8,128)(2,1)S(1)}, f32[8,128]{1,0:T(8,128)S(1)}) custom-call(bf16[2,256,768]{2,1,0:T(8,128)(2,1)S(1)} %get-tuple-element.129.refs_0_, bf16[2,768,4096]{2,1,0:T(8,128)(2,1)S(1)} %get-tuple-element.120.refs_1_, f32[8,128]{1,0:T(8,128)S(1)} %get-tuple-element.130.refs_2_), custom_call_target="tpu_custom_call" | custom-call | flops 1610612736 | bytes 12582912 | tf_op jit(solution)/shard_map/pallas_call | solution.py:65
  58.5 4.5 %collective-permute-done.12.refs_0_ = bf16[128,2048]{1,0:T(8,128)(2,1)S(1)} collective-permute-done((bf16[128,2048]{1,0:T(8,128)(2,1)S(1)}, bf16[128,2048]{1,0:T(8,128)(2,1)S(1)}, u32[]{:S(2)}, u32[]{:S(2)}) %collective-permute-start.12) | collective-permute-done | bytes 524320 | tf_op jit(solution)/shard_map/ppermute | solution.py:469
  63.6 1.9 %shard_map.144 = (bf16[128,2048]{1,0:T(8,128)(2,1)S(1)}, bf16[128,2048]{1,0:T(8,128)(2,1)S(1)}, f32[8,128]{1,0:T(8,128)S(1)}) custom-call(bf16[2,256,768]{2,1,0:T(8,128)(2,1)S(1)} %get-tuple-element.129.refs_0_, bf16[2,768,4096]{2,1,0:T(8,128)(2,1)S(1)} %get-tuple-element.120.refs_1_, f32[8,128]{1,0:T(8,128)S(1)} %get-tuple-element.136.refs_2_), custom_call_target="tpu_custom_call" | custom-call | flops 1610612736 | bytes 12582912 | tf_op jit(solution)/shard_map/pallas_call | solution.py:65
  66.1 1.2 collective-permute-start.24
  67.3 7.5 %shard_map.147 = (bf16[2,256,768]{2,1,0:T(8,128)(2,1)S(1)}, f32[8,128]{1,0:T(8,128)S(1)}) custom-call(bf16[128,2048]{1,0:T(8,128)(2,1)S(1)} %get-tuple-element.125.refs_0_, bf16[128,2048]{1,0:T(8,128)(2,1)S(1)} %get-tuple-element.134.refs_1_, bf16[128,2048]{1,0:T(8,128)(2,1)S(1)} %collective-permute-done.17.refs_2_, ...), custom_call_target="tpu_custom_call" | custom-call | flops 6442450944 | bytes 25165824 | tf_op jit(solution)/shard_map/pallas_call | solution.py:65
  74.8 1.9 %shard_map.148 = (bf16[128,2048]{1,0:T(8,128)(2,1)S(1)}, bf16[128,2048]{1,0:T(8,128)(2,1)S(1)}, f32[8,128]{1,0:T(8,128)S(1)}) custom-call(bf16[2,256,768]{2,1,0:T(8,128)(2,1)S(1)} %get-tuple-element.143.refs_0_, bf16[2,768,4096]{2,1,0:T(8,128)(2,1)S(1)} %get-tuple-element.120.refs_1_, f32[8,128]{1,0:T(8,128)S(1)} %get-tuple-element.144.refs_2_), custom_call_target="tpu_custom_call" | custom-call | flops 1610612736 | bytes 12582912 | tf_op jit(solution)/shard_map/pallas_call | solution.py:65
  76.7 2.9 %collective-permute-done.16.refs_0_ = bf16[128,2048]{1,0:T(8,128)(2,1)S(1)} collective-permute-done((bf16[128,2048]{1,0:T(8,128)(2,1)S(1)}, bf16[128,2048]{1,0:T(8,128)(2,1)S(1)}, u32[]{:S(2)}, u32[]{:S(2)}) %collective-permute-start.16) | collective-permute-done | bytes 524320 | tf_op jit(solution)/shard_map/ppermute | solution.py:473
  79.6 0.5 collective-permute-start.20
  80.1 1.9 %shard_map.150 = (bf16[128,2048]{1,0:T(8,128)(2,1)S(1)}, bf16[128,2048]{1,0:T(8,128)(2,1)S(1)}, f32[8,128]{1,0:T(8,128)S(1)}) custom-call(bf16[2,256,768]{2,1,0:T(8,128)(2,1)S(1)} %get-tuple-element.143.refs_0_, bf16[2,768,4096]{2,1,0:T(8,128)(2,1)S(1)} %get-tuple-element.120.refs_1_, f32[8,128]{1,0:T(8,128)S(1)} %get-tuple-element.149.refs_2_), custom_call_target="tpu_custom_call" | custom-call | flops 1610612736 | bytes 12582912 | tf_op jit(solution)/shard_map/pallas_call | solution.py:65
  82.0 1.3 collective-permute-start.6
  84.0 0.8 collective-permute-start.27
  84.8 7.5 %shard_map.154 = (bf16[2,256,768]{2,1,0:T(8,128)(2,1)S(1)}, f32[8,128]{1,0:T(8,128)S(1)}) custom-call(bf16[128,2048]{1,0:T(8,128)(2,1)S(1)} %get-tuple-element.133.refs_0_, bf16[128,2048]{1,0:T(8,128)(2,1)S(1)} %get-tuple-element.147.refs_1_, bf16[128,2048]{1,0:T(8,128)(2,1)S(1)} %collective-permute-done.20.refs_2_, ...), custom_call_target="tpu_custom_call" | custom-call | flops 6442450944 | bytes 25165824 | tf_op jit(solution)/shard_map/pallas_call | solution.py:65
  92.3 1.9 %shard_map.155 = (bf16[128,2048]{1,0:T(8,128)(2,1)S(1)}, bf16[128,2048]{1,0:T(8,128)(2,1)S(1)}, f32[8,128]{1,0:T(8,128)S(1)}) custom-call(bf16[2,256,768]{2,1,0:T(8,128)(2,1)S(1)} %get-tuple-element.160.refs_0_, bf16[2,768,4096]{2,1,0:T(8,128)(2,1)S(1)} %get-tuple-element.120.refs_1_, f32[8,128]{1,0:T(8,128)S(1)} %get-tuple-element.161.refs_2_), custom_call_target="tpu_custom_call" | custom-call | flops 1610612736 | bytes 12582912 | tf_op jit(solution)/shard_map/pallas_call | solution.py:65
  94.3 1.9 %shard_map.157 = (bf16[128,2048]{1,0:T(8,128)(2,1)S(1)}, bf16[128,2048]{1,0:T(8,128)(2,1)S(1)}, f32[8,128]{1,0:T(8,128)S(1)}) custom-call(bf16[2,256,768]{2,1,0:T(8,128)(2,1)S(1)} %get-tuple-element.160.refs_0_, bf16[2,768,4096]{2,1,0:T(8,128)(2,1)S(1)} %get-tuple-element.120.refs_1_, f32[8,128]{1,0:T(8,128)S(1)} %get-tuple-element.165.refs_2_), custom_call_target="tpu_custom_call" | custom-call | flops 1610612736 | bytes 12582912 | tf_op jit(solution)/shard_map/pallas_call | solution.py:65
  96.1 5.9 %collective-permute-done.27.refs_2_ = bf16[128,2048]{1,0:T(8,128)(2,1)S(1)} collective-permute-done((bf16[128,2048]{1,0:T(8,128)(2,1)S(1)}, bf16[128,2048]{1,0:T(8,128)(2,1)S(1)}, u32[]{:S(2)}, u32[]{:S(2)}) %collective-permute-start.27) | collective-permute-done | bytes 524320 | tf_op jit(solution)/shard_map/ppermute | solution.py:451
  102.6 1.3 collective-permute-start.34
  103.9 0.9 shard_map.162
  104.8 1.9 %shard_map.163 = (bf16[128,2048]{1,0:T(8,128)(2,1)S(1)}, bf16[64,2048]{1,0:T(8,128)(2,1)S(1)}, bf16[64,2048]{1,0:T(8,128)(2,1)S(1)}, f32[8,128]{1,0:T(8,128)S(1)}) custom-call(bf16[2,256,768]{2,1,0:T(8,128)(2,1)S(1)} %get-tuple-element.119.refs_0_, bf16[2,768,4096]{2,1,0:T(8,128)(2,1)S(1)} %get-tuple-element.120.refs_1_, f32[8,128]{1,0:T(8,128)S(1)} %get-tuple-element.178.refs_2_), custom_call_target="tpu_custom_call" | custom-call | flops 1610612736 | bytes 12582912 | tf_op jit(solution)/shard_map/pallas_call | solution.py:65
  107.3 4.0 %collective-permute-done.34.refs_2_ = bf16[64,2048]{1,0:T(8,128)(2,1)S(1)} collective-permute-done((bf16[64,2048]{1,0:T(8,128)(2,1)S(1)}, bf16[64,2048]{1,0:T(8,128)(2,1)S(1)}, u32[]{:S(2)}, u32[]{:S(2)}) %collective-permute-start.34) | collective-permute-done | bytes 262176 | tf_op jit(solution)/shard_map/ppermute | solution.py:451
  111.3 1.2 collective-permute-start.30
  112.5 1.9 %shard_map.165 = (bf16[128,2048]{1,0:T(8,128)(2,1)S(1)}, bf16[128,2048]{1,0:T(8,128)(2,1)S(1)}, f32[8,128]{1,0:T(8,128)S(1)}) custom-call(bf16[2,256,768]{2,1,0:T(8,128)(2,1)S(1)} %get-tuple-element.119.refs_0_, bf16[2,768,4096]{2,1,0:T(8,128)(2,1)S(1)} %get-tuple-element.120.refs_1_, f32[8,128]{1,0:T(8,128)S(1)} %get-tuple-element.182.refs_2_), custom_call_target="tpu_custom_call" | custom-call | flops 1610612736 | bytes 12582912 | tf_op jit(solution)/shard_map/pallas_call | solution.py:65
  114.4 4.3 %collective-permute-done.31.refs_3_ = bf16[128,2048]{1,0:T(8,128)(2,1)S(1)} collective-permute-done((bf16[128,2048]{1,0:T(8,128)(2,1)S(1)}, bf16[128,2048]{1,0:T(8,128)(2,1)S(1)}, u32[]{:S(2)}, u32[]{:S(2)}) %collective-permute-start.31) | collective-permute-done | bytes 524320 | tf_op jit(solution)/shard_map/ppermute | solution.py:463
  119.3 1.3 collective-permute-start.36
  120.8 0.7 collective-permute-start.37
  121.5 10.0 %collective-permute-done.38.refs_4_ = bf16[64,2048]{1,0:T(8,128)(2,1)S(1)} collective-permute-done((bf16[64,2048]{1,0:T(8,128)(2,1)S(1)}, bf16[64,2048]{1,0:T(8,128)(2,1)S(1)}, u32[]{:S(2)}, u32[]{:S(2)}) %collective-permute-start.38) | collective-permute-done | bytes 262176 | tf_op jit(solution)/shard_map/ppermute | solution.py:463
  131.5 4.8 %collective-permute-done.37.refs_3_ = bf16[64,2048]{1,0:T(8,128)(2,1)S(1)} collective-permute-done((bf16[64,2048]{1,0:T(8,128)(2,1)S(1)}, bf16[64,2048]{1,0:T(8,128)(2,1)S(1)}, u32[]{:S(2)}, u32[]{:S(2)}) %collective-permute-start.37) | collective-permute-done | bytes 262176 | tf_op jit(solution)/shard_map/ppermute | solution.py:463
  136.3 1.1 shard_map.170
  (93 shorter events, 4.2 us)
Async XLA Ops:
  2.5 21.4 %collective-permute-start = (bf16[128,2048]{1,0:T(8,128)(2,1)S(1)}, bf16[128,2048]{1,0:T(8,128)(2,1)S(1)}, u32[]{:S(2)}, u32[]{:S(2)}) collective-permute-start(bf16[128,2048]{1,0:T(8,128)(2,1)S(1)} %get-tuple-element.103.refs_2_.refs_0_), channel_id=1, source_target_pairs={{0,4},{2,6},{4,8},{6,10},{8,12},{10,14},{12,0},{14,2},{1,5},{3,7},... | collective-permute-start | bytes 1572872 | tf_op jit(solution)/shard_map/ppermute | solution.py:398
  5.5 18.4 %collective-permute-start.1 = (bf16[128,2048]{1,0:T(8,128)(2,1)S(1)}, bf16[128,2048]{1,0:T(8,128)(2,1)S(1)}, u32[]{:S(2)}, u32[]{:S(2)}) collective-permute-start(bf16[128,2048]{1,0:T(8,128)(2,1)S(1)} %get-tuple-element.103.refs_2_.refs_0_), channel_id=1, source_target_pairs={{0,1},{1,0},{2,3},{3,2},{4,5},{5,4},{6,7},{7,6},{8,9},{9,8},{10,11... | collective-permute-start | bytes 1572872 | tf_op jit(solution)/shard_map/ppermute | solution.py:398
  9.4 14.5 %collective-permute-start.2 = (f32[24,128]{1,0:T(8,128)S(1)}, f32[24,128]{1,0:T(8,128)S(1)}, u32[]{:S(2)}, u32[]{:S(2)}) collective-permute-start(f32[24,128]{1,0:T(8,128)S(1)} %get-tuple-element.105.refs_0_), channel_id=1, source_target_pairs={{0,1},{1,0},{2,3},{3,2},{4,5},{5,4},{6,7},{7,6},{8,9},{9,8},{10,11... | collective-permute-start | bytes 36872 | tf_op jit(solution)/shard_map/ppermute | solution.py:403
  10.0 26.9 %collective-permute-start.3 = (bf16[128,2048]{1,0:T(8,128)(2,1)S(1)}, bf16[128,2048]{1,0:T(8,128)(2,1)S(1)}, u32[]{:S(2)}, u32[]{:S(2)}) collective-permute-start(bf16[128,2048]{1,0:T(8,128)(2,1)S(1)} %get-tuple-element.103.refs_2_.refs_0_), channel_id=1, source_target_pairs={{0,2},{2,0},{4,6},{6,4},{8,10},{10,8},{12,14},{14,12},{1,3},{3,1},... | collective-permute-start | bytes 1572872 | tf_op jit(solution)/shard_map/ppermute | solution.py:431
  10.0 14.5 %copy-start.5 = (s32[128,8]{0,1:T(8,128)S(1)}, s32[128,8]{0,1:T(8,128)}, u32[]{:S(2)}) copy-start(s32[128,8]{0,1:T(8,128)} %param.14) | copy-start | bytes 12292
  10.0 17.7 %copy-start.4 = (bf16[2048]{0:T(1024)(128)(2,1)S(1)}, bf16[2048]{0:T(1024)(128)(2,1)}, u32[]{:S(2)}) copy-start(bf16[2048]{0:T(1024)(128)(2,1)} %refs_1_.5) | copy-start | bytes 12292
  10.0 17.7 %copy-start.6 = (s32[128,1]{0,1:T(1,128)S(1)}, s32[128,1]{0,1:T(1,128)}, u32[]{:S(2)}) copy-start(s32[128,1]{0,1:T(1,128)} %param.15) | copy-start | bytes 1540
  19.3 4.6 %copy-start = (bf16[2,4096,768]{2,1,0:T(8,128)(2,1)}, bf16[2,4096,768]{2,1,0:T(8,128)(2,1)S(1)}, u32[]{:S(2)}) copy-start(bf16[2,4096,768]{2,1,0:T(8,128)(2,1)S(1)} %get-tuple-element.117.refs_6_) | copy-start | bytes 37748740
  23.9 15.0 %copy-start.1 = (bf16[2,4096,768]{2,1,0:T(8,128)(2,1)S(1)}, bf16[2,4096,768]{2,1,0:T(8,128)(2,1)}, u32[]{:S(2)}) copy-start(bf16[2,4096,768]{2,1,0:T(8,128)(2,1)} %copy-done) | copy-start | bytes 37748740
  23.9 14.9 %collective-permute-start.4 = (bf16[128,2048]{1,0:T(8,128)(2,1)S(1)}, bf16[128,2048]{1,0:T(8,128)(2,1)S(1)}, u32[]{:S(2)}, u32[]{:S(2)}) collective-permute-start(bf16[128,2048]{1,0:T(8,128)(2,1)S(1)} %get-tuple-element.109.refs_1_), channel_id=1, source_target_pairs={{0,2},{2,0},{4,6},{6,4},{8,10},{10,8},{12,14},{14,12},{1,3},{3,1},... | collective-permute-start | bytes 1572872 | tf_op jit(solution)/shard_map/ppermute | solution.py:431
  24.5 10.2 %collective-permute-start.5 = (f32[24,128]{1,0:T(8,128)S(1)}, f32[24,128]{1,0:T(8,128)S(1)}, u32[]{:S(2)}, u32[]{:S(2)}) collective-permute-start(f32[24,128]{1,0:T(8,128)S(1)} %get-tuple-element.112.refs_3_.refs_0_), channel_id=1, source_target_pairs={{0,2},{2,0},{4,6},{6,4},{8,10},{10,8},{12,14},{14,12},{1,3},{3,1},... | collective-permute-start | bytes 36872 | tf_op jit(solution)/shard_map/ppermute | solution.py:412
  24.6 21.9 %collective-permute-start.7 = (bf16[128,2048]{1,0:T(8,128)(2,1)S(1)}, bf16[128,2048]{1,0:T(8,128)(2,1)S(1)}, u32[]{:S(2)}, u32[]{:S(2)}) collective-permute-start(bf16[128,2048]{1,0:T(8,128)(2,1)S(1)} %get-tuple-element.123.refs_0_), channel_id=1, source_target_pairs={{0,4},{2,6},{4,8},{6,10},{8,12},{10,14},{12,0},{14,2},{1,5},{3,7},... | collective-permute-start | bytes 1572872 | tf_op jit(solution)/shard_map/ppermute | solution.py:407
  26.2 20.3 %collective-permute-start.8 = (bf16[128,2048]{1,0:T(8,128)(2,1)S(1)}, bf16[128,2048]{1,0:T(8,128)(2,1)S(1)}, u32[]{:S(2)}, u32[]{:S(2)}) collective-permute-start(bf16[128,2048]{1,0:T(8,128)(2,1)S(1)} %get-tuple-element.123.refs_0_), channel_id=1, source_target_pairs={{0,1},{1,0},{2,3},{3,2},{4,5},{5,4},{6,7},{7,6},{8,9},{9,8},{10,11... | collective-permute-start | bytes 1572872 | tf_op jit(solution)/shard_map/ppermute | solution.py:408
  34.8 11.6 %collective-permute-start.10 = (f32[24,256]{1,0:T(8,128)S(1)}, f32[24,256]{1,0:T(8,128)S(1)}, u32[]{:S(2)}, u32[]{:S(2)}) collective-permute-start(f32[24,256]{1,0:T(8,128)S(1)} %get-tuple-element.115.refs_4_), channel_id=1, source_target_pairs={{0,8},{2,10},{4,12},{6,14},{8,0},{10,2},{12,4},{14,6},{1,9},{3,11}... | collective-permute-start | bytes 73736 | tf_op jit(solution)/shard_map/ppermute | solution.py:426
  36.8 9.6 %collective-permute-start.11 = (f32[24,256]{1,0:T(8,128)S(1)}, f32[24,256]{1,0:T(8,128)S(1)}, u32[]{:S(2)}, u32[]{:S(2)}) collective-permute-start(f32[24,256]{1,0:T(8,128)S(1)} %get-tuple-element.115.refs_4_), channel_id=1, source_target_pairs={{0,12},{2,14},{4,0},{6,2},{8,4},{10,6},{12,8},{14,10},{1,13},{3,15... | collective-permute-start | bytes 73736 | tf_op jit(solution)/shard_map/ppermute | solution.py:426
  38.8 7.7 %collective-permute-start.9 = (f32[24,256]{1,0:T(8,128)S(1)}, f32[24,256]{1,0:T(8,128)S(1)}, u32[]{:S(2)}, u32[]{:S(2)}) collective-permute-start(f32[24,256]{1,0:T(8,128)S(1)} %get-tuple-element.115.refs_4_), channel_id=1, source_target_pairs={{0,4},{2,6},{4,8},{6,10},{8,12},{10,14},{12,0},{14,2},{1,5},{3,7},... | collective-permute-start | bytes 73736 | tf_op jit(solution)/shard_map/ppermute | solution.py:426
  46.4 2.7 %collective-permute-start.14 = (bf16[128,2048]{1,0:T(8,128)(2,1)S(1)}, bf16[128,2048]{1,0:T(8,128)(2,1)S(1)}, u32[]{:S(2)}, u32[]{:S(2)}) collective-permute-start(bf16[128,2048]{1,0:T(8,128)(2,1)S(1)} %get-tuple-element.123.refs_0_), channel_id=1, source_target_pairs={{0,2},{2,0},{4,6},{6,4},{8,10},{10,8},{12,14},{14,12},{1,3},{3,1},... | collective-permute-start | bytes 1572872 | tf_op jit(solution)/shard_map/ppermute | solution.py:431
  46.5 2.6 %collective-permute-start.15 = (bf16[128,2048]{1,0:T(8,128)(2,1)S(1)}, bf16[128,2048]{1,0:T(8,128)(2,1)S(1)}, u32[]{:S(2)}, u32[]{:S(2)}) collective-permute-start(bf16[128,2048]{1,0:T(8,128)(2,1)S(1)} %get-tuple-element.126.refs_1_), channel_id=1, source_target_pairs={{0,2},{2,0},{4,6},{6,4},{8,10},{10,8},{12,14},{14,12},{1,3},{3,1},... | collective-permute-start | bytes 1572872 | tf_op jit(solution)/shard_map/ppermute | solution.py:431
  47.1 15.9 %collective-permute-start.12 = (bf16[128,2048]{1,0:T(8,128)(2,1)S(1)}, bf16[128,2048]{1,0:T(8,128)(2,1)S(1)}, u32[]{:S(2)}, u32[]{:S(2)}) collective-permute-start(bf16[128,2048]{1,0:T(8,128)(2,1)S(1)} %get-tuple-element.125.refs_0_), channel_id=1, source_target_pairs={{0,4},{2,6},{4,8},{6,10},{8,12},{10,14},{12,0},{14,2},{1,5},{3,7},... | collective-permute-start | bytes 1572872 | tf_op jit(solution)/shard_map/ppermute | solution.py:469
  47.9 15.1 %collective-permute-start.13 = (bf16[128,2048]{1,0:T(8,128)(2,1)S(1)}, bf16[128,2048]{1,0:T(8,128)(2,1)S(1)}, u32[]{:S(2)}, u32[]{:S(2)}) collective-permute-start(bf16[128,2048]{1,0:T(8,128)(2,1)S(1)} %get-tuple-element.125.refs_0_), channel_id=1, source_target_pairs={{0,1},{1,0},{2,3},{3,2},{4,5},{5,4},{6,7},{7,6},{8,9},{9,8},{10,11... | collective-permute-start | bytes 1572872 | tf_op jit(solution)/shard_map/ppermute | solution.py:470
  56.6 10.7 %slice-start = ((s8[12582912]{0:T(1024)(128)(4,1)}), s8[4194304]{0:T(1024)(128)(4,1)S(1)}, s32[]{:S(2)}) async-start(s8[12582912]{0:T(1024)(128)(4,1)} %bitcast.4), calls=%async_computation | async-start | bytes 8388608
  56.6 10.7 %slice-start.1 = ((s8[12582912]{0:T(1024)(128)(4,1)}), s8[4194304]{0:T(1024)(128)(4,1)S(1)}, s32[]{:S(2)}) async-start(s8[12582912]{0:T(1024)(128)(4,1)} %bitcast.4), calls=%async_computation.1 | async-start | bytes 8388608
  63.0 2.5 %collective-permute-start.19 = (bf16[128,2048]{1,0:T(8,128)(2,1)S(1)}, bf16[128,2048]{1,0:T(8,128)(2,1)S(1)}, u32[]{:S(2)}, u32[]{:S(2)}) collective-permute-start(bf16[128,2048]{1,0:T(8,128)(2,1)S(1)} %get-tuple-element.139), channel_id=1, source_target_pairs={{0,2},{2,0},{4,6},{6,4},{8,10},{10,8},{12,14},{14,12},{1,3},{3,1},... | collective-permute-start | bytes 1572872 | tf_op jit(solution)/shard_map/ppermute | solution.py:443
  63.0 4.3 %collective-permute-start.17 = (bf16[128,2048]{1,0:T(8,128)(2,1)S(1)}, bf16[128,2048]{1,0:T(8,128)(2,1)S(1)}, u32[]{:S(2)}, u32[]{:S(2)}) collective-permute-start(bf16[128,2048]{1,0:T(8,128)(2,1)S(1)} %get-tuple-element.125.refs_0_), channel_id=1, source_target_pairs={{0,2},{2,0},{4,6},{6,4},{8,10},{10,8},{12,14},{14,12},{1,3},{3,1},... | collective-permute-start | bytes 1572872 | tf_op jit(solution)/shard_map/ppermute | solution.py:431
  63.5 3.8 %collective-permute-start.18 = (bf16[128,2048]{1,0:T(8,128)(2,1)S(1)}, bf16[128,2048]{1,0:T(8,128)(2,1)S(1)}, u32[]{:S(2)}, u32[]{:S(2)}) collective-permute-start(bf16[128,2048]{1,0:T(8,128)(2,1)S(1)} %get-tuple-element.134.refs_1_), channel_id=1, source_target_pairs={{0,2},{2,0},{4,6},{6,4},{8,10},{10,8},{12,14},{14,12},{1,3},{3,1},... | collective-permute-start | bytes 1572872 | tf_op jit(solution)/shard_map/ppermute | solution.py:431
  63.6 16.1 %collective-permute-start.16 = (bf16[128,2048]{1,0:T(8,128)(2,1)S(1)}, bf16[128,2048]{1,0:T(8,128)(2,1)S(1)}, u32[]{:S(2)}, u32[]{:S(2)}) collective-permute-start(bf16[128,2048]{1,0:T(8,128)(2,1)S(1)} %get-tuple-element.134.refs_1_), channel_id=1, source_target_pairs={{0,4},{2,6},{4,8},{6,10},{8,12},{10,14},{12,0},{14,2},{1,5},{3,7},... | collective-permute-start | bytes 1572872 | tf_op jit(solution)/shard_map/ppermute | solution.py:473
  63.6 3.8 %slice-start.2 = ((s8[12582912]{0:T(1024)(128)(4,1)}), s8[4194304]{0:T(1024)(128)(4,1)S(1)}, s32[]{:S(2)}) async-start(s8[12582912]{0:T(1024)(128)(4,1)} %bitcast.4), calls=%async_computation.2 | async-start | bytes 8388608
  65.6 16.4 %collective-permute-start.23 = (bf16[128,2048]{1,0:T(8,128)(2,1)S(1)}, bf16[128,2048]{1,0:T(8,128)(2,1)S(1)}, u32[]{:S(2)}, u32[]{:S(2)}) collective-permute-start(bf16[128,2048]{1,0:T(8,128)(2,1)S(1)} %get-tuple-element.154), channel_id=1, source_target_pairs={{0,2},{2,0},{4,6},{6,4},{8,10},{10,8},{12,14},{14,12},{1,3},{3,1},... | collective-permute-start | bytes 1572872 | tf_op jit(solution)/shard_map/ppermute | solution.py:456
  66.1 17.2 %collective-permute-start.24 = (bf16[128,2048]{1,0:T(8,128)(2,1)S(1)}, bf16[128,2048]{1,0:T(8,128)(2,1)S(1)}, u32[]{:S(2)}, u32[]{:S(2)}) collective-permute-start(bf16[128,2048]{1,0:T(8,128)(2,1)S(1)} %get-tuple-element.155), channel_id=1, source_target_pairs={{0,1},{1,0},{2,3},{3,2},{4,5},{5,4},{6,7},{7,6},{8,9},{9,8},{10,11... | collective-permute-start | bytes 1572872 | tf_op jit(solution)/shard_map/ppermute | solution.py:451
  79.6 3.9 %collective-permute-start.22 = (bf16[128,2048]{1,0:T(8,128)(2,1)S(1)}, bf16[128,2048]{1,0:T(8,128)(2,1)S(1)}, u32[]{:S(2)}, u32[]{:S(2)}) collective-permute-start(bf16[128,2048]{1,0:T(8,128)(2,1)S(1)} %get-tuple-element.152), channel_id=1, source_target_pairs={{0,2},{2,0},{4,6},{6,4},{8,10},{10,8},{12,14},{14,12},{1,3},{3,1},... | collective-permute-start | bytes 1572872 | tf_op jit(solution)/shard_map/ppermute | solution.py:443
  79.6 5.1 %collective-permute-start.20 = (bf16[128,2048]{1,0:T(8,128)(2,1)S(1)}, bf16[128,2048]{1,0:T(8,128)(2,1)S(1)}, u32[]{:S(2)}, u32[]{:S(2)}) collective-permute-start(bf16[128,2048]{1,0:T(8,128)(2,1)S(1)} %get-tuple-element.133.refs_0_), channel_id=1, source_target_pairs={{0,2},{2,0},{4,6},{6,4},{8,10},{10,8},{12,14},{14,12},{1,3},{3,1},... | collective-permute-start | bytes 1572872 | tf_op jit(solution)/shard_map/ppermute | solution.py:431
  80.1 4.6 %collective-permute-start.21 = (bf16[128,2048]{1,0:T(8,128)(2,1)S(1)}, bf16[128,2048]{1,0:T(8,128)(2,1)S(1)}, u32[]{:S(2)}, u32[]{:S(2)}) collective-permute-start(bf16[128,2048]{1,0:T(8,128)(2,1)S(1)} %get-tuple-element.147.refs_1_), channel_id=1, source_target_pairs={{0,2},{2,0},{4,6},{6,4},{8,10},{10,8},{12,14},{14,12},{1,3},{3,1},... | collective-permute-start | bytes 1572872 | tf_op jit(solution)/shard_map/ppermute | solution.py:431
  82.0 12.1 %collective-permute-start.6 = (bf16[128,1024]{1,0:T(8,128)(2,1)S(1)}, bf16[128,1024]{1,0:T(8,128)(2,1)S(1)}, u32[]{:S(2)}, u32[]{:S(2)}) collective-permute-start(bf16[128,1024]{1,0:T(8,128)(2,1)S(1)} %get-tuple-element.122), channel_id=1, source_target_pairs={{0,1},{1,0},{2,3},{3,2},{4,5},{5,4},{6,7},{7,6},{8,9},{9,8},{10,11... | collective-permute-start | bytes 786440 | tf_op jit(solution)/shard_map/ppermute | solution.py:479
  83.7 12.5 %collective-permute-start.26 = (bf16[128,2048]{1,0:T(8,128)(2,1)S(1)}, bf16[128,2048]{1,0:T(8,128)(2,1)S(1)}, u32[]{:S(2)}, u32[]{:S(2)}) collective-permute-start(bf16[128,2048]{1,0:T(8,128)(2,1)S(1)} %get-tuple-element.170), channel_id=1, source_target_pairs={{0,2},{2,0},{4,6},{6,4},{8,10},{10,8},{12,14},{14,12},{1,3},{3,1},... | collective-permute-start | bytes 1572872 | tf_op jit(solution)/shard_map/ppermute | solution.py:456
  84.0 18.1 %collective-permute-start.27 = (bf16[128,2048]{1,0:T(8,128)(2,1)S(1)}, bf16[128,2048]{1,0:T(8,128)(2,1)S(1)}, u32[]{:S(2)}, u32[]{:S(2)}) collective-permute-start(bf16[128,2048]{1,0:T(8,128)(2,1)S(1)} %get-tuple-element.171), channel_id=1, source_target_pairs={{0,1},{1,0},{2,3},{3,2},{4,5},{5,4},{6,7},{7,6},{8,9},{9,8},{10,11... | collective-permute-start | bytes 1572872 | tf_op jit(solution)/shard_map/ppermute | solution.py:451
  84.8 17.3 %collective-permute-start.28 = (bf16[128,2048]{1,0:T(8,128)(2,1)S(1)}, bf16[128,2048]{1,0:T(8,128)(2,1)S(1)}, u32[]{:S(2)}, u32[]{:S(2)}) collective-permute-start(bf16[128,2048]{1,0:T(8,128)(2,1)S(1)} %get-tuple-element.172), channel_id=1, source_target_pairs={{0,4},{2,6},{4,8},{6,10},{8,12},{10,14},{12,0},{14,2},{1,5},{3,7},... | collective-permute-start | bytes 1572872 | tf_op jit(solution)/shard_map/ppermute | solution.py:463
  94.1 9.8 %copy-start.7 = (bf16[128]{0:T(256)(128)(2,1)S(1)}, bf16[128]{0:T(256)(128)(2,1)}, u32[]{:S(2)}) copy-start(bf16[128]{0:T(256)(128)(2,1)} %refs_2_.3) | copy-start | bytes 772
  94.2 8.1 %collective-permute-start.25 = (bf16[128,2048]{1,0:T(8,128)(2,1)S(1)}, bf16[128,2048]{1,0:T(8,128)(2,1)S(1)}, u32[]{:S(2)}, u32[]{:S(2)}) collective-permute-start(bf16[128,2048]{1,0:T(8,128)(2,1)S(1)} %get-tuple-element.168), channel_id=1, source_target_pairs={{0,2},{2,0},{4,6},{6,4},{8,10},{10,8},{12,14},{14,12},{1,3},{3,1},... | collective-permute-start | bytes 1572872 | tf_op jit(solution)/shard_map/ppermute | solution.py:443
  102.5 11.9 %collective-permute-start.29 = (bf16[128,2048]{1,0:T(8,128)(2,1)S(1)}, bf16[128,2048]{1,0:T(8,128)(2,1)S(1)}, u32[]{:S(2)}, u32[]{:S(2)}) collective-permute-start(bf16[128,2048]{1,0:T(8,128)(2,1)S(1)} %get-tuple-element.186), channel_id=1, source_target_pairs={{0,2},{2,0},{4,6},{6,4},{8,10},{10,8},{12,14},{14,12},{1,3},{3,1},... | collective-permute-start | bytes 1572872 | tf_op jit(solution)/shard_map/ppermute | solution.py:456
  102.6 16.1 %collective-permute-start.31 = (bf16[128,2048]{1,0:T(8,128)(2,1)S(1)}, bf16[128,2048]{1,0:T(8,128)(2,1)S(1)}, u32[]{:S(2)}, u32[]{:S(2)}) collective-permute-start(bf16[128,2048]{1,0:T(8,128)(2,1)S(1)} %get-tuple-element.188), channel_id=1, source_target_pairs={{0,4},{2,6},{4,8},{6,10},{8,12},{10,14},{12,0},{14,2},{1,5},{3,7},... | collective-permute-start | bytes 1572872 | tf_op jit(solution)/shard_map/ppermute | solution.py:463
  102.6 8.6 %collective-permute-start.34 = (bf16[64,2048]{1,0:T(8,128)(2,1)S(1)}, bf16[64,2048]{1,0:T(8,128)(2,1)S(1)}, u32[]{:S(2)}, u32[]{:S(2)}) collective-permute-start(bf16[64,2048]{1,0:T(8,128)(2,1)S(1)} %get-tuple-element.192), channel_id=1, source_target_pairs={{0,1},{1,0},{2,3},{3,2},{4,5},{5,4},{6,7},{7,6},{8,9},{9,8},{10,11... | collective-permute-start | bytes 786440 | tf_op jit(solution)/shard_map/ppermute | solution.py:451
  106.7 12.1 %collective-permute-start.32 = (bf16[64,2048]{1,0:T(8,128)(2,1)S(1)}, bf16[64,2048]{1,0:T(8,128)(2,1)S(1)}, u32[]{:S(2)}, u32[]{:S(2)}) collective-permute-start(bf16[64,2048]{1,0:T(8,128)(2,1)S(1)} %get-tuple-element.190), channel_id=1, source_target_pairs={{0,2},{2,0},{4,6},{6,4},{8,10},{10,8},{12,14},{14,12},{1,3},{3,1},... | collective-permute-start | bytes 786440 | tf_op jit(solution)/shard_map/ppermute | solution.py:443
  106.8 12.0 %collective-permute-start.33 = (bf16[64,2048]{1,0:T(8,128)(2,1)S(1)}, bf16[64,2048]{1,0:T(8,128)(2,1)S(1)}, u32[]{:S(2)}, u32[]{:S(2)}) collective-permute-start(bf16[64,2048]{1,0:T(8,128)(2,1)S(1)} %get-tuple-element.191), channel_id=1, source_target_pairs={{0,2},{2,0},{4,6},{6,4},{8,10},{10,8},{12,14},{14,12},{1,3},{3,1},... | collective-permute-start | bytes 786440 | tf_op jit(solution)/shard_map/ppermute | solution.py:443
  111.3 7.8 %collective-permute-start.30 = (bf16[64,2048]{1,0:T(8,128)(2,1)S(1)}, bf16[64,2048]{1,0:T(8,128)(2,1)S(1)}, u32[]{:S(2)}, u32[]{:S(2)}) collective-permute-start(bf16[64,2048]{1,0:T(8,128)(2,1)S(1)} %get-tuple-element.187), channel_id=1, source_target_pairs={{0,1},{1,0},{2,3},{3,2},{4,5},{5,4},{6,7},{7,6},{8,9},{9,8},{10,11... | collective-permute-start | bytes 786440 | tf_op jit(solution)/shard_map/ppermute | solution.py:451
  119.2 17.2 %collective-permute-start.35 = (bf16[128,2048]{1,0:T(8,128)(2,1)S(1)}, bf16[128,2048]{1,0:T(8,128)(2,1)S(1)}, u32[]{:S(2)}, u32[]{:S(2)}) collective-permute-start(bf16[128,2048]{1,0:T(8,128)(2,1)S(1)} %get-tuple-element.197), channel_id=1, source_target_pairs={{0,2},{2,0},{4,6},{6,4},{8,10},{10,8},{12,14},{14,12},{1,3},{3,1},... | collective-permute-start | bytes 1572872 | tf_op jit(solution)/shard_map/ppermute | solution.py:456
  119.3 17.1 %collective-permute-start.36 = (bf16[128,2048]{1,0:T(8,128)(2,1)S(1)}, bf16[128,2048]{1,0:T(8,128)(2,1)S(1)}, u32[]{:S(2)}, u32[]{:S(2)}) collective-permute-start(bf16[128,2048]{1,0:T(8,128)(2,1)S(1)} %get-tuple-element.198), channel_id=1, source_target_pairs={{0,1},{1,0},{2,3},{3,2},{4,5},{5,4},{6,7},{7,6},{8,9},{9,8},{10,11... | collective-permute-start | bytes 1572872 | tf_op jit(solution)/shard_map/ppermute | solution.py:446
  120.5 10.9 %collective-permute-start.38 = (bf16[64,2048]{1,0:T(8,128)(2,1)S(1)}, bf16[64,2048]{1,0:T(8,128)(2,1)S(1)}, u32[]{:S(2)}, u32[]{:S(2)}) collective-permute-start(bf16[64,2048]{1,0:T(8,128)(2,1)S(1)} %get-tuple-element.200), channel_id=1, source_target_pairs={{0,4},{2,6},{4,8},{6,10},{8,12},{10,14},{12,0},{14,2},{1,5},{3,7},... | collective-permute-start | bytes 786440 | tf_op jit(solution)/shard_map/ppermute | solution.py:463
  120.8 15.5 %collective-permute-start.37 = (bf16[64,2048]{1,0:T(8,128)(2,1)S(1)}, bf16[64,2048]{1,0:T(8,128)(2,1)S(1)}, u32[]{:S(2)}, u32[]{:S(2)}) collective-permute-start(bf16[64,2048]{1,0:T(8,128)(2,1)S(1)} %get-tuple-element.199), channel_id=1, source_target_pairs={{0,4},{2,6},{4,8},{6,10},{8,12},{10,14},{12,0},{14,2},{1,5},{3,7},... | collective-permute-start | bytes 786440 | tf_op jit(solution)/shard_map/ppermute | solution.py:463
  (2 other events, 1.5 us)
